TPU v7x, 32 devices: a whole 2x2x4 slice. The times are simulated.
32 devices in a mesh: ctx: 8 (over y, x, core), head: 4 (over z).
Axes of the slice: x: 2, y: 2, z: 4, core: 2. Of those that a mesh axis runs over, the one named last changes fastest.
Arguments:
- queries: bfloat16 [2048, 4096], P('ctx', 'head'), may hold values from -6 to 6
- key_rows: bfloat16 [8192, 4096], P('ctx', 'head'), may hold values from -8 to 8
- value_rows: bfloat16 [8192, 4096], P('ctx', 'head'), may hold values from -4 to 4
- selected: int32 [2048, 4], P('ctx'), may hold values from 0 to 127, as said below
- out_grad: bfloat16 [2048, 4096], P('ctx', 'head'), may hold values from -6 to 6
- out_weight: bfloat16 [4096, 4096], P(None, 'head'), may hold values from -0.09375 to 0.09375
Outputs:
- query_grad: float32 [2048, 4096], P('ctx', 'head')
- key_grad: float32 [8192, 4096], P('ctx', 'head')
- value_grad: float32 [8192, 4096], P('ctx', 'head')
- weight_grad: float32 [4096, 4096], P('ctx', 'head')
Inputs may be any that keep to these rules, and one draw needn't show every extreme that they name: `selected`: each query names 4 different blocks. Among the queries of one index of ctx no block is named more than 16 times, and some blocks are named exactly 16 times by the queries of every index of ctx.
All inputs are finite; a program needn't handle non-finite values.
Results may differ from a plain program's by a relative error of at most 0.015.
Values may be sent and summed in bfloat16 or wider, within the bound.
No kernel may reach another device: no remote copies, remote signals or barrier semaphores. Data moves between devices by JAX's collectives and lax.ppermute only.
A program may use at most 128 MiB of HBM per device.

v0:
```python
import jax
import jax.numpy as jnp
from jax import lax
from jax.sharding import PartitionSpec as P

HD = 128
BLOCK = 64
TOPK = 4


def body(queries, key_rows, value_rows, selected, out_grad, out_weight):
    ctx_count = lax.axis_size("ctx")
    query_rows, feature_width = queries.shape
    head_count = feature_width // HD
    block_count = key_rows.shape[0] // BLOCK
    block_total = block_count * ctx_count
    capacity = 2 * query_rows * TOPK // block_total
    slot_total = block_total * capacity
    score_scale = HD ** (-0.5)
    grad_full = lax.all_gather(out_grad, "head", axis=1, tiled=True)
    grad_attn = jnp.dot(grad_full, out_weight, preferred_element_type=jnp.float32).astype(
        jnp.bfloat16
    )
    grad_heads = grad_attn.reshape(query_rows, head_count, HD)
    query_heads = queries.reshape(query_rows, head_count, HD)
    flat_blocks = selected.reshape(-1)
    entry_count = flat_blocks.shape[0]
    block_ids = jnp.arange(block_total, dtype=jnp.int32)
    block_onehot = flat_blocks[:, None] == block_ids[None, :]
    mark_local = key_rows.reshape(block_count, BLOCK, feature_width)[:, BLOCK - 1]
    mark_all = lax.all_gather(mark_local, "ctx", axis=0, tiled=True)
    chosen = jnp.dot(
        block_onehot.astype(jnp.bfloat16), mark_all, preferred_element_type=jnp.float32
    ).astype(jnp.bfloat16)
    chosen = chosen.reshape(query_rows, TOPK, head_count, HD)
    gate_logits = score_scale * jnp.einsum(
        "qhd,qthd->qth", query_heads, chosen, preferred_element_type=jnp.float32
    )
    gate_probs = jax.nn.softmax(gate_logits, axis=1)
    pushed = (gate_probs[..., None] * grad_heads.astype(jnp.float32)[:, None]).astype(jnp.bfloat16)
    repeated = jnp.broadcast_to(query_heads[:, None], pushed.shape)
    payload = jnp.stack([repeated, pushed], axis=2).reshape(entry_count, 2 * feature_width)
    entry_ids = jnp.arange(entry_count, dtype=jnp.int32)
    earlier = (flat_blocks[:, None] == flat_blocks[None, :]) & (
        entry_ids[None, :] < entry_ids[:, None]
    )
    slot_rank = jnp.sum(earlier.astype(jnp.int32), axis=1)
    slot_index = flat_blocks * capacity + slot_rank
    slot_ids = jnp.arange(slot_total, dtype=jnp.int32)
    slot_onehot = (slot_index[:, None] == slot_ids[None, :]).astype(jnp.bfloat16)
    outbox = jnp.einsum(
        "es,ef->sf", slot_onehot, payload, preferred_element_type=jnp.float32
    ).astype(jnp.bfloat16)
    outbox = outbox.reshape(ctx_count, block_count, capacity, 2, feature_width)
    received = lax.all_to_all(outbox, "ctx", split_axis=0, concat_axis=2, tiled=True)
    inbound = ctx_count * capacity
    received = received.reshape(block_count, inbound, 2, head_count, HD)
    asked_rows = received[:, :, 0]
    pushed_rows = received[:, :, 1]
    tiles_key = key_rows.reshape(block_count, BLOCK, head_count, HD)
    tiles_value = value_rows.reshape(block_count, BLOCK, head_count, HD)
    logits = score_scale * jnp.einsum(
        "pshd,pjhd->phsj", asked_rows, tiles_key, preferred_element_type=jnp.float32
    )
    attn_probs = jax.nn.softmax(logits, axis=-1)
    probs_low = attn_probs.astype(jnp.bfloat16)
    block_out = jnp.einsum(
        "phsj,pjhd->pshd", probs_low, tiles_value, preferred_element_type=jnp.float32
    ).astype(jnp.bfloat16)
    prob_grad = jnp.einsum(
        "pshd,pjhd->phsj", pushed_rows, tiles_value, preferred_element_type=jnp.float32
    )
    delta_term = jnp.einsum(
        "pshd,pshd->phs", pushed_rows, block_out, preferred_element_type=jnp.float32
    )
    score_grad = (attn_probs * (prob_grad - delta_term[..., None])).astype(jnp.bfloat16)
    query_part = (
        score_scale
        * jnp.einsum("phsj,pjhd->pshd", score_grad, tiles_key, preferred_element_type=jnp.float32)
    ).astype(jnp.bfloat16)
    value_grad = jnp.einsum(
        "phsj,pshd->pjhd", probs_low, pushed_rows, preferred_element_type=jnp.float32
    ).reshape(-1, feature_width)
    key_block = score_scale * jnp.einsum(
        "phsj,pshd->pjhd", score_grad, asked_rows, preferred_element_type=jnp.float32
    )
    answer = jnp.stack([block_out, query_part], axis=2).reshape(
        1, block_count, inbound, 2, feature_width
    )
    replies = lax.all_to_all(answer, "ctx", split_axis=2, concat_axis=0, tiled=True)
    replies = replies.reshape(slot_total, 2 * feature_width)
    replies = jnp.dot(slot_onehot, replies, preferred_element_type=jnp.float32).astype(jnp.bfloat16)
    replies = replies.reshape(query_rows, TOPK, 2, head_count, HD)
    back_out = replies[:, :, 0]
    back_query = replies[:, :, 1]
    attn_out = (
        jnp.sum(gate_probs[..., None] * back_out.astype(jnp.float32), axis=1)
        .astype(jnp.bfloat16)
        .reshape(query_rows, feature_width)
    )
    gate_diff = jnp.einsum(
        "qhd,qthd->qth", grad_heads, back_out, preferred_element_type=jnp.float32
    )
    gate_grad = gate_probs * (gate_diff - jnp.sum(gate_probs * gate_diff, axis=1, keepdims=True))
    query_grad = jnp.sum(back_query.astype(jnp.float32), axis=1) + score_scale * jnp.einsum(
        "qth,qthd->qhd", gate_grad, chosen.astype(jnp.float32)
    )
    query_grad = query_grad.reshape(query_rows, feature_width)
    mark_terms = score_scale * gate_grad[..., None] * query_heads.astype(jnp.float32)[:, None]
    mark_partial = jnp.einsum(
        "eb,ef->bf",
        block_onehot.astype(jnp.float32),
        mark_terms.reshape(entry_count, feature_width),
        precision=lax.Precision.HIGHEST,
        preferred_element_type=jnp.float32,
    )
    columns = lax.all_to_all(grad_full, "ctx", split_axis=1, concat_axis=0, tiled=True)
    weight_grad = jnp.einsum(
        "qd,qf->df",
        columns,
        lax.all_gather(attn_out, "ctx", axis=0, tiled=True),
        preferred_element_type=jnp.float32,
    )
    mark_sum = lax.psum_scatter(
        mark_partial.astype(jnp.bfloat16), "ctx", scatter_dimension=0, tiled=True
    ).astype(jnp.float32)
    key_block = key_block.reshape(block_count, BLOCK, feature_width)
    key_grad = key_block.at[:, BLOCK - 1].add(mark_sum).reshape(-1, feature_width)
    return (query_grad, key_grad, value_grad, weight_grad)


def solution(mesh):
    return jax.shard_map(
        body,
        mesh=mesh,
        in_specs=(
            P("ctx", "head"),
            P("ctx", "head"),
            P("ctx", "head"),
            P("ctx", None),
            P("ctx", "head"),
            P(None, "head"),
        ),
        out_specs=(P("ctx", "head"), P("ctx", "head"), P("ctx", "head"), P("ctx", "head")),
        check_vma=False,
    )
```

profile of v0, /device:TPU:0, one launch (start us, length us, event | category | flops | bytes accessed | tf_op | source)
XLA Modules:
  0.0 584.2 jit_solution(13803376210978599405)
XLA Ops:
  11.3 10.8 %all-gather = bf16[128,1,1024]{2,0,1:T(8,128)(2,1)S(1)} all-gather(bf16[16,1,1024]{2,0,1:T(8,128)(2,1)S(1)} %copy.71), channel_id=2, replica_groups=mesh['ctx'=8,'head'=4] {'ctx'}, dimensions={0}, use_global_device_ids=true | all-gather | bytes 294912 | tf_op jit(solution)/shard_map/all_gather | solution.py:31
  34.7 24.1 %all-gather.4.cloned.1.call-done = bf16[256,4096]{0,1:T(8,128)(2,1)} async-done(((bf16[256,1024]{0,1:T(8,128)(2,1)}), bf16[256,4096]{0,1:T(8,128)(2,1)}) %all-gather.4.cloned.1.call-update) | async-done | bytes 2097168 | tf_op jit(solution)/shard_map/all_gather | solution.py:20
  58.8 6.4 %convolution_convert_fusion.1 = bf16[256,1024]{1,0:T(8,128)(2,1)S(1)} fusion(bf16[256,4096]{0,1:T(8,128)(2,1)} %all-gather.4.cloned.1.call-done, bf16[4096,1024]{1,0:T(8,128)(2,1)} %param.13), kind=kOutput, calls=%fused_computation.59 | convolution fusion | flops 2147745792 | bytes 11010048 | tf_op jit(solution)/shard_map/dot_general | solution.py:21
  70.1 7.3 %reshape.151 = bf16[1024,2048]{1,0:T(8,128)(2,1)} reshape(bf16[256,4,2,8,128]{4,3,2,1,0:T(8,128)(2,1)} %pad_maximum_fusion.1) | data formatting | bytes 8388608 | tf_op jit(solution)/shard_map/reshape | solution.py:42
  77.4 13.6 %fusion.5 = bf16[2048,2048]{1,0:T(8,128)(2,1)} fusion(bf16[1024,2048]{1,0:T(8,128)(2,1)} %reshape.151, s32[1024]{0:T(1024)S(1)} %multiply_add_fusion.1), kind=kOutput, calls=%fused_computation.9 | convolution fusion | flops 8596226048 | bytes 12587008 | tf_op jit(solution)/shard_map/es,ef->sf/dot_general | solution.py:51
  91.0 14.5 %reshape.152 = bf16[8,16,16,2,1024]{4,3,2,1,0:T(2,128)(2,1)} reshape(bf16[2048,2048]{1,0:T(8,128)(2,1)} %fusion.5) | data formatting | bytes 16777216 | tf_op jit(solution)/shard_map/reshape | solution.py:54
  105.4 9.4 %copy.73 = bf16[8,16,16,2,1024]{4,2,3,1,0:T(8,128)(2,1)} copy(bf16[8,16,16,2,1024]{4,3,2,1,0:T(2,128)(2,1)} %reshape.152) | data formatting | bytes 16777216 | tf_op jit(solution)/shard_map/reshape | solution.py:54
  114.8 5.2 all-to-all-start
  124.4 89.7 %all-to-all-done = bf16[8,16,16,2,1024]{4,2,3,1,0:T(8,128)(2,1)} async-done(((bf16[8,16,16,2,1024]{4,2,3,1,0:T(8,128)(2,1)}), bf16[8,16,16,2,1024]{4,2,3,1,0:T(8,128)(2,1)}, u32[]{:S(2)}, u32[]{:S(2)}) %all-to-all-start) | async-done | bytes 8388640 | tf_op jit(solution)/shard_map/all_to_all | solution.py:55
  214.1 8.5 %copy.74 = bf16[1,16,8,16,2,1024]{5,3,2,4,1,0:T(8,128)(2,1)} copy(bf16[1,16,8,16,2,1024]{5,3,4,1,2,0:T(8,128)(2,1)} %bitcast.7) | data formatting | bytes 16777216 | tf_op jit(solution)/shard_map/all_to_all | solution.py:55
  222.7 8.8 %copy.112 = bf16[512,8,8,128]{3,2,1,0:T(8,128)(2,1)} copy(bf16[512,8,8,128]{3,1,2,0:T(8,128)(2,1)} %bitcast.150) | data formatting | bytes 16777216
  245.9 9.7 %copy.99 = f32[16,8,128,128]{2,3,1,0:T(8,128)} copy(f32[16,8,128,128]{3,2,1,0:T(8,128)} %bitcast_convert_fusion) | data formatting | bytes 16777216
  255.6 9.2 %multiply_reduce_fusion = (f32[16,8,128]{2,1,0:T(8,128)S(1)}, bf16[16,8,128,128]{2,3,1,0:T(8,128)(2,1)}) fusion(f32[16,8,128,128]{2,3,1,0:T(8,128)} %copy.99, bf16[16,64,8,128]{3,2,1,0:T(8,128)(2,1)} %bitcast.179, f32[16,8,128,64]{2,3,1,0:T(8,128)} %get-tuple-element.39, f32[16,8,128]{2,1,0:T(8,128)S(1)} %get-tuple-element.38), kind=kOutput, calls=%fused_computation.4 | convolution fusion | flops 278904832 | bytes 19005440 | tf_op jit(solution)/shard_map/phsj,pjhd->pshd/dot_general | solution.py:67
  271.3 20.8 %copy.82 = bf16[1,16,128,1,1024]{4,3,1,0,2:T(2,128)(2,1)} copy(bf16[1,16,128,1,1024]{2,4,1,3,0:T(8,128)(2,1)} %bitcast.158) | data formatting | bytes 8388608 | tf_op jit(solution)/shard_map/stack | solution.py:87
  292.1 20.7 %copy.81 = bf16[1,16,128,1,1024]{4,3,1,0,2:T(2,128)(2,1)} copy(bf16[1,16,128,1,1024]{2,4,1,3,0:T(8,128)(2,1)} %bitcast.170) | data formatting | bytes 8388608 | tf_op jit(solution)/shard_map/stack | solution.py:87
  312.8 21.4 %pad_maximum_fusion = bf16[1,16,128,2,1024]{4,3,1,0,2:T(2,128)(2,1)} fusion(bf16[1,16,128,1,1024]{4,3,1,0,2:T(2,128)(2,1)} %copy.82, bf16[1,16,128,1,1024]{4,3,1,0,2:T(2,128)(2,1)} %copy.81), kind=kLoop, calls=%fused_computation.3 | loop fusion | flops 16777216 | bytes 16777216 | tf_op jit(solution)/shard_map/stack | solution.py:87
  334.3 5.0 all-to-all-start.1
  340.0 93.3 %all-to-all-done.1 = bf16[1,16,128,2,1024]{4,3,1,0,2:T(2,128)(2,1)} async-done(((bf16[1,16,128,2,1024]{4,3,1,0,2:T(2,128)(2,1)}), bf16[1,16,128,2,1024]{4,3,1,0,2:T(2,128)(2,1)}, u32[]{:S(2)}, u32[]{:S(2)}) %all-to-all-start.1) | async-done | bytes 8388640 | tf_op jit(solution)/shard_map/all_to_all | solution.py:90
  433.3 11.3 %copy.83 = bf16[1,16,128,2,1024]{4,2,3,1,0:T(8,128)(2,1)} copy(bf16[1,16,128,2,1024]{4,3,1,0,2:T(2,128)(2,1)} %all-to-all-done.1) | data formatting | bytes 16777216 | tf_op jit(solution)/shard_map/all_to_all | solution.py:90
  444.6 16.5 %copy.84 = bf16[8,1,16,16,2,1024]{5,4,3,2,0,1:T(2,128)(2,1)} copy(bf16[8,1,16,16,2,1024]{5,3,0,4,2,1:T(8,128)(2,1)} %bitcast.151) | data formatting | bytes 16777216 | tf_op jit(solution)/shard_map/all_to_all | solution.py:90
  461.1 10.1 %copy.115 = bf16[256,8,2,1024]{3,1,2,0:T(8,128)(2,1)} copy(bf16[256,8,2,1024]{3,2,1,0:T(2,128)(2,1)} %bitcast.152) | data formatting | bytes 16777216
  471.2 11.5 %convert_bitcast_fusion = bf16[128,8,16,128]{3,1,2,0:T(8,128)(2,1)S(1)} fusion(bf16[2048,2048]{1,0:T(8,128)(2,1)} %bitcast.162, s32[1024]{0:T(1024)S(1)} %multiply_add_fusion.1), kind=kOutput, calls=%fused_computation.25 | convolution fusion | flops 8594128896 | bytes 12587008 | tf_op jit(solution)/shard_map/dot_general | solution.py:92
  502.1 31.1 %all_to_all.49 = bf16[256,8,512]{0,2,1:T(8,128)(2,1)} all-to-all(bf16[256,8,512]{0,2,1:T(8,128)(2,1)S(1)} %bitcast.161), channel_id=1, replica_groups=mesh['ctx'=8,'head'=4] {'ctx'}, dimensions={1} | all-to-all | bytes 4194304 | tf_op jit(solution)/shard_map/all_to_all | solution.py:117
  568.5 5.9 %convolution_bitcast_fusion = f32[512,1024]{0,1:T(8,128)} fusion(bf16[2048,1024]{1,0:T(8,128)(2,1)} %all-gather.6.cloned.1.call-done, bf16[2048,512]{1,0:T(8,128)(2,1)S(1)} %bitcast.164), kind=kOutput, calls=%fused_computation.54 | convolution fusion | flops 2147483648 | bytes 8388608 | tf_op jit(solution)/shard_map/qd,qf->df/dot_general | solution.py:118
  (104 shorter events, 104.8 us)
Async XLA Ops:
  7.2 51.6 %all-gather.4.cloned.1.call-start = ((), (), s32[]{:S(2)}) async-start(), calls=%async_computation.4 | async-start | bytes 2621440 | tf_op jit(solution)/shard_map/all_gather | solution.py:20
  9.3 14.2 %copy-start.12 = (bf16[256,1024]{1,0:T(8,128)(2,1)S(1)}, bf16[256,1024]{1,0:T(8,128)(2,1)}, u32[]{:S(2)}) copy-start(bf16[256,1024]{1,0:T(8,128)(2,1)} %param.8) | copy-start | bytes 1572868
  10.3 23.6 %copy-start.19 = (s32[1024]{0:T(1024)}, s32[1024]{0:T(1024)S(1)}, u32[]{:S(2)}) copy-start(s32[1024]{0:T(1024)S(1)} %reshape.147) | copy-start | bytes 12292
  23.5 6.5 %copy-start.14 = (bf16[128,8,8,128]{3,2,1,0:T(8,128)(2,1)}, bf16[128,8,8,128]{3,2,1,0:T(8,128)(2,1)S(1)}, u32[]{:S(2)}) copy-start(bf16[128,8,8,128]{3,2,1,0:T(8,128)(2,1)S(1)} %copy.110) | copy-start | bytes 6291460
  34.7 30.7 %copy-start.17 = (f32[256,4,8]{2,1,0:T(4,128)}, f32[256,4,8]{2,1,0:T(4,128)S(1)}, u32[]{:S(2)}) copy-start(f32[256,4,8]{2,1,0:T(4,128)S(1)} %fusion.51) | copy-start | bytes 98308
  114.8 99.3 %all-to-all-start = ((bf16[8,16,16,2,1024]{4,2,3,1,0:T(8,128)(2,1)}), bf16[8,16,16,2,1024]{4,2,3,1,0:T(8,128)(2,1)}, u32[]{:S(2)}, u32[]{:S(2)}) async-start(bf16[8,16,16,2,1024]{4,2,3,1,0:T(8,128)(2,1)} %copy.73), calls=%async_computation | async-start | bytes 16777216 | tf_op jit(solution)/shard_map/all_to_all | solution.py:55
  120.0 2.4 copy-start.13
  235.3 3.0 copy-start
  235.4 6.1 %copy-start.2 = (bf16[16,128,1,8,128]{4,3,1,2,0:T(8,128)(2,1)}, bf16[16,128,1,8,128]{4,3,1,2,0:T(8,128)(2,1)S(1)}, u32[]{:S(2)}) copy-start(bf16[16,128,1,8,128]{4,3,1,2,0:T(8,128)(2,1)S(1)} %get-tuple-element.37) | copy-start | bytes 12582916
  255.6 9.2 %copy-start.3 = (bf16[16,128,1,8,128]{4,3,1,2,0:T(8,128)(2,1)S(1)}, bf16[16,128,1,8,128]{4,3,1,2,0:T(8,128)(2,1)}, u32[]{:S(2)}) copy-start(bf16[16,128,1,8,128]{4,3,1,2,0:T(8,128)(2,1)} %copy-done.2) | copy-start | bytes 12582916
  255.6 9.2 %copy-start.10 = (f32[16,8,128,64]{2,3,1,0:T(8,128)S(1)}, f32[16,8,128,64]{2,3,1,0:T(8,128)}, u32[]{:S(2)}) copy-start(f32[16,8,128,64]{2,3,1,0:T(8,128)} %get-tuple-element.39) | copy-start | bytes 12582916
  255.6 9.2 %copy-start.16 = (bf16[128,8,8,128]{3,2,1,0:T(8,128)(2,1)S(1)}, bf16[128,8,8,128]{3,2,1,0:T(8,128)(2,1)}, u32[]{:S(2)}) copy-start(bf16[128,8,8,128]{3,2,1,0:T(8,128)(2,1)} %copy.114) | copy-start | bytes 6291460
  267.8 3.4 copy-start.6
  334.3 99.0 %all-to-all-start.1 = ((bf16[1,16,128,2,1024]{4,3,1,0,2:T(2,128)(2,1)}), bf16[1,16,128,2,1024]{4,3,1,0,2:T(2,128)(2,1)}, u32[]{:S(2)}, u32[]{:S(2)}) async-start(bf16[1,16,128,2,1024]{4,3,1,0,2:T(2,128)(2,1)} %pad_maximum_fusion), calls=%async_computation.1 | async-start | bytes 16777216 | tf_op jit(solution)/shard_map/all_to_all | solution.py:90
  339.2 222.2 %reduce-scatter.2.cloned.1.call-start = ((), (), s32[]{:S(2)}) async-start(), calls=%async_computation.5 | async-start | bytes 294912 | tf_op jit(solution)/shard_map/reduce_scatter | solution.py:124
  486.6 6.6 %copy-start.18 = (f32[256,4,8]{2,1,0:T(4,128)S(1)}, f32[256,4,8]{2,1,0:T(4,128)}, u32[]{:S(2)}) copy-start(f32[256,4,8]{2,1,0:T(4,128)} %copy-done.17) | copy-start | bytes 98308
  494.9 7.2 %copy-start.5 = (bf16[256,4096]{0,1:T(8,128)(2,1)S(1)}, bf16[256,4096]{0,1:T(8,128)(2,1)}, u32[]{:S(2)}) copy-start(bf16[256,4096]{0,1:T(8,128)(2,1)} %all-gather.4.cloned.1.call-done) | copy-start | bytes 6291460
  497.7 70.7 %all-gather.6.cloned.1.call-start = ((), (), s32[]{:S(2)}) async-start(), calls=%async_computation.6 | async-start | bytes 4718592 | tf_op jit(solution)/shard_map/all_gather | solution.py:121
  533.2 4.1 copy-start.7
  541.0 3.7 copy-start.4
  541.0 5.0 copy-start.11
  541.6 5.6 copy-start.9
  553.5 4.3 copy-start.15
  560.1 8.4 %copy-start.8 = (bf16[8,256,512]{2,1,0:T(8,128)(2,1)S(1)}, bf16[8,256,512]{2,1,0:T(8,128)(2,1)}, u32[]{:S(2)}) copy-start(bf16[8,256,512]{2,1,0:T(8,128)(2,1)} %copy.89) | copy-start | bytes 6291460
  (2 other events, 3.7 us)
Sparse Core Ops, SparseCore 0:
  10.1 48.6 all-gather.3
  497.9 31.8 reduce-scatter.1
  531.8 36.6 all-gather.5
where the time goes:
time: 594 us; the launch traced here: 584 us
  waiting for transfers between devices  211 us (36%)
  local copies, waits for them, and re-layouts  188 us (32%)
  matrix products  74.5 us (13%)
  other arithmetic  43.1 us (7%)
  blocking collectives  41.9 us (7%)
  between operations  14.7 us (2%)
  starting transfers between devices  10.3 us (2%)
    all_to_all x1, waiting for transfers between devices, body(): lax.all_to_all(answer, 'ctx', split_axis=2, concat_axis=0, tiled=True)  93.3 us
    all_to_all x1, waiting for transfers between devices, body(): lax.all_to_all(outbox, 'ctx', split_axis=0, concat_axis=2, tiled=True)  89.7 us
    unnamed x57, local copies, waits for them, and re-layouts  52.4 us
    another operation x2, local copies, waits for them, and re-layouts, body(): jnp.stack([block_out, query_part], axis=2)  41.6 us
    all_to_all x1, blocking collectives, body(): lax.all_to_all(grad_full, 'ctx', split_axis=1, concat_axis=0, tiled=True)  31.1 us
    all_to_all x2, local copies, waits for them, and re-layouts, body(): lax.all_to_all(answer, 'ctx', split_axis=2, concat_axis=0, tiled=True)  27.8 us
    all_gather x1, waiting for transfers between devices, body(): grad_full = lax.all_gather(out_grad, 'head', axis=1, tiled=True)  24.1 us
    reshape x2, local copies, waits for them, and re-layouts, body(): outbox = outbox.reshape(ctx_count, block_count, capacity, 2, feature_width)  23.9 us
  transfers between devices with their start and end apart: 5, of which 4 were waited for; matrix products, arithmetic and copies ran while one was open for 9% of the time, Pallas kernels for 0%

commit v1 on v0

v1 whole, which is shorter than its diff:
```python
import functools

import jax
import jax.numpy as jnp
from jax import lax
from jax.experimental import pallas as pl
from jax.experimental.pallas import tpu as pltpu
from jax.sharding import PartitionSpec as P

HD = 128
BLOCK = 64
TOPK = 4
F32 = jnp.float32
BF16 = jnp.bfloat16
VMEM_LIMIT = 56 * 1024 * 1024
NN = (((1,), (0,)), ((), ()))
NT = (((1,), (1,)), ((), ()))
TN = (((0,), (0,)), ((), ()))


def mm(a, b, dims=NN):
    return lax.dot_general(a, b, dims, preferred_element_type=F32)


def joined(items, axis):
    return items[0] if len(items) == 1 else jnp.concatenate(items, axis=axis)


def forward_kernel(chunks, span, cap, me_ref, sel_ref, mark_ref, k_ref, v_ref, *refs):
    q_refs = refs[:chunks]
    part_refs = refs[chunks : 2 * chunks]
    qg_ref, p_ref, gate_ref, hot_ref = refs[2 * chunks : 2 * chunks + 4]
    mask_ref, out_ref = refs[2 * chunks + 4 :]
    block_count, _, width = k_ref.shape
    block_total = mark_ref.shape[0]
    heads = width // HD
    rows = q_refs[0].shape[0]
    group_rows = rows * span
    groups = chunks // span
    me = me_ref[0]
    scale = HD ** (-0.5)
    base = me * block_count

    before = lax.broadcasted_iota(jnp.int32, (group_rows, group_rows), 0)
    after = lax.broadcasted_iota(jnp.int32, (group_rows, group_rows), 1)
    earlier = (before < after).astype(BF16)
    for g in range(groups):
        picked = joined([sel_ref[me ^ (g * span + i)] for i in range(span)], 1)
        own_ids = base + lax.broadcasted_iota(jnp.int32, (block_count, group_rows), 0)
        all_ids = lax.broadcasted_iota(jnp.int32, (block_total, group_rows), 0)
        own = picked[0:1, :] == own_ids
        named = picked[0:1, :] == all_ids
        for t in range(1, TOPK):
            own = own | (picked[t : t + 1, :] == own_ids)
            named = named | (picked[t : t + 1, :] == all_ids)
        own = jnp.where(own, 1.0, 0.0)
        rank = mm(own.astype(BF16), earlier)
        rank = jnp.where(own > 0.5, rank, -1.0)
        place = lax.broadcasted_iota(jnp.int32, (cap, group_rows), 0).astype(F32)
        hot = jnp.concatenate(
            [jnp.where(rank[b : b + 1, :] == place, 1.0, 0.0) for b in range(block_count)], axis=0
        ).astype(BF16)
        hot_ref[g] = hot
        named = jnp.where(named, 1.0, 0.0).astype(BF16)
        mask_ref[:, g * cap : (g + 1) * cap, :] = mm(hot, named, NT).reshape(
            block_count, cap, block_total
        )
        q_group = joined([q_refs[g * span + i][...] for i in range(span)], 0)
        qg_ref[:, g * cap : (g + 1) * cap, :] = (
            mm(hot, q_group).astype(BF16).reshape(block_count, cap, width)
        )

    def one_block(b, carry):
        mask = mask_ref[b].T > 0.5
        gates = []
        for h in range(heads):
            cols = slice(h * HD, (h + 1) * HD)
            q = qg_ref[b, :, cols]
            marks = jnp.where(mask, scale * mm(mark_ref[:, cols], q, NT), -1e30)
            top = jnp.max(marks, axis=0, keepdims=True)
            total = jnp.sum(jnp.exp(marks - top), axis=0, keepdims=True)
            logits = scale * mm(k_ref[b, :, cols], q, NT)
            gate = jnp.exp(jnp.minimum(logits[BLOCK - 1 :, :] - top, 0.0)) / total
            weight = jnp.exp(logits - jnp.max(logits, axis=0, keepdims=True))
            probs = weight * (1.0 / jnp.sum(weight, axis=0, keepdims=True))
            p_ref[b, h] = probs.astype(BF16)
            gates.append(gate)
            gated = (probs * gate).T.astype(BF16)
            out_ref[b, :, cols] = mm(gated, v_ref[b, :, cols]).astype(BF16)
        gate_ref[b] = jnp.concatenate(gates, axis=0)
        return carry

    lax.fori_loop(0, block_count, one_block, 0)

    for g in range(groups):
        hot = hot_ref[g]
        slots = out_ref[:, g * cap : (g + 1) * cap, :].reshape(block_count * cap, width)
        part = mm(hot, slots, TN).astype(BF16)
        for i in range(span):
            part_refs[g * span + i][...] = part[i * rows : (i + 1) * rows]


def backward_kernel(chunks, span, cap, hot_ref, qg_ref, p_ref, gate_ref, k_ref, v_ref, *refs):
    ga_refs = refs[:chunks]
    part_refs = refs[chunks : 2 * chunks]
    dk_ref, dv_ref = refs[2 * chunks : 2 * chunks + 2]
    gag_ref, dq_ref = refs[2 * chunks + 2 :]
    block_count, _, width = k_ref.shape
    heads = width // HD
    rows = ga_refs[0].shape[0]
    groups = chunks // span
    scale = HD ** (-0.5)

    for g in range(groups):
        ga_group = joined([ga_refs[g * span + i][...] for i in range(span)], 0)
        gag_ref[:, g * cap : (g + 1) * cap, :] = (
            mm(hot_ref[g], ga_group).astype(BF16).reshape(block_count, cap, width + HD)
        )
    last = lax.broadcasted_iota(jnp.int32, (BLOCK, groups * cap), 0) == BLOCK - 1

    def one_block(b, carry):
        dots = gag_ref[b, :, width:].astype(F32).T
        dots = dots[:heads] + dots[heads : 2 * heads]
        gates = gate_ref[b]
        for h in range(heads):
            cols = slice(h * HD, (h + 1) * HD)
            q = qg_ref[b, :, cols]
            ga = gag_ref[b, :, cols]
            probs = p_ref[b, h].astype(F32)
            gate = gates[h : h + 1, :]
            prob_grad = mm(v_ref[b, :, cols], ga, NT)
            delta = jnp.sum(probs * prob_grad, axis=0, keepdims=True)
            gated = probs * gate
            score = gated * (prob_grad - delta)
            score = score + jnp.where(last, gate * (delta - dots[h : h + 1, :]), 0.0)
            dv_ref[b, :, cols] = mm(gated.astype(BF16), ga)
            dk_ref[b, :, cols] = scale * mm(score.astype(BF16), q)
            dq_ref[b, :, cols] = (scale * mm(score.T.astype(BF16), k_ref[b, :, cols])).astype(BF16)
        return carry

    lax.fori_loop(0, block_count, one_block, 0)

    for g in range(groups):
        slots = dq_ref[:, g * cap : (g + 1) * cap, :].reshape(block_count * cap, width)
        part = mm(hot_ref[g], slots, TN).astype(BF16)
        for i in range(span):
            part_refs[g * span + i][...] = part[i * rows : (i + 1) * rows]


def swap(x, bits):
    count = lax.axis_size("ctx")
    return lax.ppermute(x, "ctx", [(i, i ^ bits) for i in range(count)])


def spread(x):
    count = lax.axis_size("ctx")
    pieces = [None] * count
    for m in range(0, count, 2):
        pieces[m] = swap(x, m) if m else x
    for m in range(0, count, 2):
        pieces[m + 1] = swap(pieces[m], 1)
    return pieces


def collect(parts):
    count = lax.axis_size("ctx")
    total = None
    for m in range(0, count, 2):
        both = parts[m].astype(F32) + swap(parts[m + 1], 1).astype(F32)
        term = swap(both.astype(BF16), m).astype(F32) if m else both
        total = term if total is None else total + term
    return total


def body(queries, key_rows, value_rows, selected, out_grad, out_weight):
    chunks = lax.axis_size("ctx")
    rows, width = queries.shape
    heads = width // HD
    block_count = key_rows.shape[0] // BLOCK
    block_total = block_count * chunks
    capacity = 2 * rows * TOPK // block_total
    span = max(1, 16 // capacity)
    cap = capacity * span
    groups = chunks // span
    slots = groups * cap
    me = lax.axis_index("ctx").astype(jnp.int32).reshape(1)
    keys = key_rows.reshape(block_count, BLOCK, width)
    values = value_rows.reshape(block_count, BLOCK, width)
    vmem = pl.BlockSpec(memory_space=pltpu.VMEM)

    queries_all = spread(queries)
    grad_full = lax.all_gather(out_grad, "head", axis=1, tiled=True)
    sel_all = lax.all_gather(selected.T, "ctx", axis=0)
    mark_all = lax.all_gather(keys[:, BLOCK - 1], "ctx", axis=0, tiled=True)

    outs = pl.pallas_call(
        functools.partial(forward_kernel, chunks, span, cap),
        out_shape=[jax.ShapeDtypeStruct((rows, width), BF16)] * chunks
        + [
            jax.ShapeDtypeStruct((block_count, slots, width), BF16),
            jax.ShapeDtypeStruct((block_count, heads, BLOCK, slots), BF16),
            jax.ShapeDtypeStruct((block_count, heads, slots), F32),
            jax.ShapeDtypeStruct((groups, block_count * cap, rows * span), BF16),
        ],
        in_specs=[pl.BlockSpec(memory_space=pltpu.SMEM)] + [vmem] * (4 + chunks),
        out_specs=[vmem] * (chunks + 4),
        scratch_shapes=[
            pltpu.VMEM((block_count, slots, block_total), F32),
            pltpu.VMEM((block_count, slots, width), BF16),
        ],
        compiler_params=pltpu.CompilerParams(vmem_limit_bytes=VMEM_LIMIT),
        name="forward",
    )(me, sel_all, mark_all, keys, values, *queries_all)
    attn_parts = outs[:chunks]
    q_slots, probs, gates, hot = outs[chunks:]

    grad_attn = jnp.dot(grad_full, out_weight, preferred_element_type=F32).astype(BF16)
    columns = lax.all_to_all(grad_full, "ctx", split_axis=1, concat_axis=0, tiled=True)

    attn_out = collect(attn_parts).astype(BF16)
    dots = jnp.sum(
        (grad_attn.astype(F32) * attn_out.astype(F32)).reshape(rows, heads, HD), axis=2
    )
    dots_high = dots.astype(BF16)
    dots_low = (dots - dots_high.astype(F32)).astype(BF16)
    spare = jnp.zeros((rows, HD - 2 * heads), BF16)
    grad_all = spread(jnp.concatenate([grad_attn, dots_high, dots_low, spare], axis=1))
    attn_all = lax.all_gather(attn_out, "ctx", axis=0, tiled=True)

    outs = pl.pallas_call(
        functools.partial(backward_kernel, chunks, span, cap),
        out_shape=[jax.ShapeDtypeStruct((rows, width), BF16)] * chunks
        + [jax.ShapeDtypeStruct((block_count, BLOCK, width), F32)] * 2,
        in_specs=[vmem] * (6 + chunks),
        out_specs=[vmem] * (chunks + 2),
        scratch_shapes=[
            pltpu.VMEM((block_count, slots, width + HD), BF16),
            pltpu.VMEM((block_count, slots, width), BF16),
        ],
        compiler_params=pltpu.CompilerParams(vmem_limit_bytes=VMEM_LIMIT),
        name="backward",
    )(hot, q_slots, probs, gates, keys, values, *grad_all)
    query_grad = collect(outs[:chunks])
    key_grad, value_grad = outs[chunks:]

    weight_grad = jnp.einsum(
        "qd,qf->df",
        columns,
        attn_all,
        preferred_element_type=F32,
    )
    return (
        query_grad,
        key_grad.reshape(-1, width),
        value_grad.reshape(-1, width),
        weight_grad,
    )


def solution(mesh):
    return jax.shard_map(
        body,
        mesh=mesh,
        in_specs=(
            P("ctx", "head"),
            P("ctx", "head"),
            P("ctx", "head"),
            P("ctx", None),
            P("ctx", "head"),
            P(None, "head"),
        ),
        out_specs=(P("ctx", "head"), P("ctx", "head"), P("ctx", "head"), P("ctx", "head")),
        check_vma=False,
    )
```

time: 594 us -> 291 us (0.49); the launches traced: 584 us -> 291 us
  local copies, waits for them, and re-layouts: 188 us -> 11.8 us
  waiting for transfers between devices: 211 us -> 110 us
  Pallas kernels: 0 us -> 85.6 us
  matrix products: 74.5 us -> 12.3 us
  other arithmetic: 43.1 us -> 14.2 us
  blocking collectives: 41.9 us -> 20.4 us
  starting transfers between devices: 10.3 us -> 21.9 us
    all_to_all x2 -> x1, waiting for transfers between devices: 183 us -> 18.3 us  [body(): lax.all_to_all(grad_full, 'ctx', split_axis=1, concat_axis=0, tiled=True)]
    ppermute x0 -> x28, waiting for transfers between devices: none -> 92.1 us  [swap(): return lax.ppermute(x, 'ctx', [(i, i ^ bits) for i in range(count)])]
    pallas_call x0 -> x2, Pallas kernels: none -> 85.6 us  [the longest x1 48.2 us: body(): pl.pallas_call(functools.partial(forward_kernel, chunks, span, cap), out_...]
    dot_general x15 -> x2, matrix products: 74.5 us -> 12.3 us  [the longest x1 6.37 us: body(): jnp.dot(grad_full, out_weight, preferred_element_type=F32).astype(BF16)]
    unnamed x57 -> x45, local copies, waits for them, and re-layouts: 52.4 us -> 7.86 us
    another operation x5 -> x0, local copies, waits for them, and re-layouts: 43.8 us -> none  [the longest x2 41.6 us: body(): jnp.stack([block_out, query_part], axis=2)]
    all_to_all x3 -> x0, local copies, waits for them, and re-layouts: 36.3 us -> none  [the longest x2 27.8 us: body(): lax.all_to_all(answer, 'ctx', split_axis=2, concat_axis=0, tiled=True)]
    reshape x6 -> x0, local copies, waits for them, and re-layouts: 32.5 us -> none  [the longest x2 23.9 us: body(): outbox = outbox.reshape(ctx_count, block_count, capacity, 2, feature_width)]
  transfers between devices with their start and end apart: 5 -> 31, of which waited for: 4 -> 13; matrix products, arithmetic and copies ran while one was open for 9% -> 8% of each run, Pallas kernels for 0% -> 29%
where the time goes in v1:
time: 291 us
  waiting for transfers between devices  110 us (38%)
  Pallas kernels  85.6 us (29%)
  starting transfers between devices  21.9 us (8%)
  blocking collectives  20.4 us (7%)
  between operations  14.3 us (5%)
  other arithmetic  14.2 us (5%)
  matrix products  12.3 us (4%)
  local copies, waits for them, and re-layouts  11.8 us (4%)
    ppermute x28, waiting for transfers between devices, swap(): return lax.ppermute(x, 'ctx', [(i, i ^ bits) for i in range(count)])  92.1 us
    pallas_call x1, Pallas kernels, body(): pl.pallas_call(functools.partial(forward_kernel, chunks, span, cap), out_...  48.2 us
    pallas_call x1, Pallas kernels, body(): pl.pallas_call(functools.partial(backward_kernel, chunks, span, cap), out...  37.4 us
    all_to_all x1, waiting for transfers between devices, body(): lax.all_to_all(grad_full, 'ctx', split_axis=1, concat_axis=0, tiled=True)  18.3 us
    ppermute x28, starting transfers between devices, swap(): return lax.ppermute(x, 'ctx', [(i, i ^ bits) for i in range(count)])  17.9 us
    all_gather x1, blocking collectives, body(): sel_all = lax.all_gather(selected.T, 'ctx', axis=0)  10.9 us
    all_gather x1, blocking collectives, body(): mark_all = lax.all_gather(keys[:, BLOCK - 1], 'ctx', axis=0, tiled=True)  9.55 us
    convert_element_type x6, other arithmetic, collect(): term = swap(both.astype(BF16), m).astype(F32) if m else both  8.43 us
  transfers between devices with their start and end apart: 31, of which 13 were waited for; matrix products, arithmetic and copies ran while one was open for 8% of the time, Pallas kernels for 29%

profile of v1, /device:TPU:0, one launch (start us, length us, event | category | flops | bytes accessed | tf_op | source)
XLA Modules:
  0.0 290.8 jit_solution(15322484114664105056)
XLA Ops:
  7.2 2.1 copy.20
  9.3 3.0 %collective-permute-start.3 = (bf16[256,1024]{1,0:T(8,128)(2,1)}, bf16[256,1024]{1,0:T(8,128)(2,1)S(1)}, u32[]{:S(2)}, u32[]{:S(2)}) collective-permute-start(bf16[256,1024]{1,0:T(8,128)(2,1)} %refs_0_.1), channel_id=1, source_target_pairs={{0,16},{4,20},{8,24},{12,28},{16,0},{20,4},{24,8},{28,12},{1,17},{... | collective-permute-start | bytes 1572872 | tf_op jit(solution)/shard_map/ppermute | solution.py:152
  13.9 10.6 %collective-permute-done.3.refs_4_ = bf16[256,1024]{1,0:T(8,128)(2,1)S(1)} collective-permute-done((bf16[256,1024]{1,0:T(8,128)(2,1)}, bf16[256,1024]{1,0:T(8,128)(2,1)S(1)}, u32[]{:S(2)}, u32[]{:S(2)}) %collective-permute-start.3) | collective-permute-done | bytes 524320 | tf_op jit(solution)/shard_map/ppermute | solution.py:152
  24.5 2.9 %collective-permute-done.1.refs_2_ = bf16[256,1024]{1,0:T(8,128)(2,1)S(1)} collective-permute-done((bf16[256,1024]{1,0:T(8,128)(2,1)}, bf16[256,1024]{1,0:T(8,128)(2,1)S(1)}, u32[]{:S(2)}, u32[]{:S(2)}) %collective-permute-start.1) | collective-permute-done | bytes 524320 | tf_op jit(solution)/shard_map/ppermute | solution.py:152
  27.4 9.6 %collective-permute-done.5.refs_6_ = bf16[256,1024]{1,0:T(8,128)(2,1)S(1)} collective-permute-done((bf16[256,1024]{1,0:T(8,128)(2,1)}, bf16[256,1024]{1,0:T(8,128)(2,1)S(1)}, u32[]{:S(2)}, u32[]{:S(2)}) %collective-permute-start.5) | collective-permute-done | bytes 524320 | tf_op jit(solution)/shard_map/ppermute | solution.py:152
  38.2 10.9 %all-gather.2.sel_ref = s32[8,4,256]{2,1,0:T(4,128)} all-gather(s32[1,4,256]{2,1,0:T(4,128)} %bitcast.30), channel_id=2, replica_groups=mesh['ctx'=8,'head'=4] {'ctx'}, dimensions={0}, use_global_device_ids=true | all-gather | bytes 36864 | tf_op jit(solution)/shard_map/all_gather | solution.py:193
  49.1 9.5 %all-gather.1 = bf16[128,1,1024]{2,0,1:T(8,128)(2,1)} all-gather(bf16[16,1,1024]{2,0,1:T(8,128)(2,1)S(1)} %copy.19), channel_id=3, replica_groups=mesh['ctx'=8,'head'=4] {'ctx'}, dimensions={0}, use_global_device_ids=true | all-gather | bytes 294912 | tf_op jit(solution)/shard_map/all_gather | solution.py:194
  59.8 48.2 %forward.1 = (bf16[256,1024]{1,0:T(8,128)(2,1)}, bf16[256,1024]{1,0:T(8,128)(2,1)}, bf16[256,1024]{1,0:T(8,128)(2,1)}, bf16[256,1024]{1,0:T(8,128)(2,1)}, bf16[2...) custom-call(s32[1]{0:T(128)} %bitcast.me_ref, ...), custom_call_target="tpu_custom_call" | custom-call | tf_op jit(solution)/shard_map/forward/pallas_call | solution.py:196
  112.8 2.0 add_convert_fusion.5
  118.0 6.4 %convolution_convert_fusion = bf16[256,1024]{1,0:T(8,128)(2,1)S(1)} fusion(bf16[256,4096]{0,1:T(8,128)(2,1)} %all-gather.6.cloned.1.call-done, bf16[4096,1024]{1,0:T(8,128)(2,1)} %param.11), kind=kOutput, calls=%fused_computation.1 | convolution fusion | flops 2147745792 | bytes 11010048 | tf_op jit(solution)/shard_map/dot_general | solution.py:217
  126.3 13.9 %collective-permute-done.11 = bf16[256,1024]{1,0:T(8,128)(2,1)S(1)} collective-permute-done((bf16[256,1024]{1,0:T(8,128)(2,1)}, bf16[256,1024]{1,0:T(8,128)(2,1)S(1)}, u32[]{:S(2)}, u32[]{:S(2)}) %collective-permute-start.11) | collective-permute-done | bytes 524320 | tf_op jit(solution)/shard_map/ppermute | solution.py:152
  140.9 2.6 multiply_bitcast_fusion
  148.1 19.3 %collective-permute-done.19.refs_6_ = bf16[256,1152]{1,0:T(8,128)(2,1)S(1)} collective-permute-done((bf16[256,1152]{1,0:T(8,128)(2,1)S(1)}, bf16[256,1152]{1,0:T(8,128)(2,1)S(1)}, u32[]{:S(2)}, u32[]{:S(2)}) %collective-permute-start.19) | collective-permute-done | bytes 589856 | tf_op jit(solution)/shard_map/ppermute | solution.py:152
  167.4 10.8 %collective-permute-done.17.refs_4_ = bf16[256,1152]{1,0:T(8,128)(2,1)S(1)} collective-permute-done((bf16[256,1152]{1,0:T(8,128)(2,1)S(1)}, bf16[256,1152]{1,0:T(8,128)(2,1)S(1)}, u32[]{:S(2)}, u32[]{:S(2)}) %collective-permute-start.17) | collective-permute-done | bytes 589856 | tf_op jit(solution)/shard_map/ppermute | solution.py:152
  181.9 37.4 %backward.1 = (bf16[256,1024]{1,0:T(8,128)(2,1)}, bf16[256,1024]{1,0:T(8,128)(2,1)}, bf16[256,1024]{1,0:T(8,128)(2,1)}, bf16[256,1024]{1,0:T(8,128)(2,1)}, bf16[...) custom-call(bf16[8,256,256]{2,1,0:T(8,128)(2,1)} %get-tuple-element., ...), custom_call_target="tpu_custom_call" | custom-call | tf_op jit(solution)/shard_map/backward/pallas_call | solution.py:230
  219.5 4.0 %all-to-all-start = ((bf16[256,8,512]{0,2,1:T(8,128)(2,1)}), bf16[256,8,512]{0,2,1:T(8,128)(2,1)S(1)}, u32[]{:S(2)}, u32[]{:S(2)}) async-start(bf16[256,8,512]{0,2,1:T(8,128)(2,1)} %bitcast.8), calls=%async_computation | async-start | bytes 4194304 | tf_op jit(solution)/shard_map/all_to_all | solution.py:218
  224.3 2.2 add_convert_fusion.2
  232.0 18.3 %all-to-all-done = bf16[256,8,512]{0,2,1:T(8,128)(2,1)S(1)} async-done(((bf16[256,8,512]{0,2,1:T(8,128)(2,1)}), bf16[256,8,512]{0,2,1:T(8,128)(2,1)S(1)}, u32[]{:S(2)}, u32[]{:S(2)}) %all-to-all-start) | async-done | bytes 2097184 | tf_op jit(solution)/shard_map/all_to_all | solution.py:218
  250.3 2.4 copy.21
  252.7 8.0 %collective-permute-done.23 = bf16[256,1024]{1,0:T(8,128)(2,1)} collective-permute-done((bf16[256,1024]{1,0:T(8,128)(2,1)}, bf16[256,1024]{1,0:T(8,128)(2,1)}, u32[]{:S(2)}, u32[]{:S(2)}) %collective-permute-start.23) | collective-permute-done | bytes 524320 | tf_op jit(solution)/shard_map/ppermute | solution.py:152
  260.7 11.7 %collective-permute-done.27 = bf16[256,1024]{1,0:T(8,128)(2,1)} collective-permute-done((bf16[256,1024]{1,0:T(8,128)(2,1)}, bf16[256,1024]{1,0:T(8,128)(2,1)}, u32[]{:S(2)}, u32[]{:S(2)}) %collective-permute-start.27) | collective-permute-done | bytes 524320 | tf_op jit(solution)/shard_map/ppermute | solution.py:152
  272.4 2.8 convert_add_fusion
  275.2 5.9 %convolution_bitcast_fusion = f32[512,1024]{0,1:T(8,128)} fusion(bf16[2048,1024]{1,0:T(8,128)(2,1)} %all-gather.8.cloned.1.call-done, bf16[2048,512]{1,0:T(8,128)(2,1)S(1)} %bitcast.25), kind=kOutput, calls=%fused_computation | convolution fusion | flops 2147483648 | bytes 8388608 | tf_op jit(solution)/shard_map/qd,qf->df/dot_general | solution.py:246
  281.1 2.9 copy.22
  (106 shorter events, 29.3 us)
Async XLA Ops:
  7.2 110.9 %all-gather.6.cloned.1.call-start = ((), (), s32[]{:S(2)}) async-start(), calls=%async_computation.1 | async-start | bytes 2621440 | tf_op jit(solution)/shard_map/all_gather | solution.py:192
  9.3 265.9 %all-gather.8.cloned.1.call-start = ((), (), s32[]{:S(2)}) async-start(), calls=%async_computation.2 | async-start | bytes 4718592 | tf_op jit(solution)/shard_map/all_gather | solution.py:228
  9.3 15.2 %collective-permute-start.3 = (bf16[256,1024]{1,0:T(8,128)(2,1)}, bf16[256,1024]{1,0:T(8,128)(2,1)S(1)}, u32[]{:S(2)}, u32[]{:S(2)}) collective-permute-start(bf16[256,1024]{1,0:T(8,128)(2,1)} %refs_0_.1), channel_id=1, source_target_pairs={{0,16},{4,20},{8,24},{12,28},{16,0},{20,4},{24,8},{28,12},{1,17},{... | collective-permute-start | bytes 1572872 | tf_op jit(solution)/shard_map/ppermute | solution.py:152
  12.4 15.1 %collective-permute-start.1 = (bf16[256,1024]{1,0:T(8,128)(2,1)}, bf16[256,1024]{1,0:T(8,128)(2,1)S(1)}, u32[]{:S(2)}, u32[]{:S(2)}) collective-permute-start(bf16[256,1024]{1,0:T(8,128)(2,1)} %refs_0_.1), channel_id=1, source_target_pairs={{0,8},{4,12},{8,0},{12,4},{16,24},{20,28},{24,16},{28,20},{1,9},{5... | collective-permute-start | bytes 1572872 | tf_op jit(solution)/shard_map/ppermute | solution.py:152
  13.9 23.1 %collective-permute-start.5 = (bf16[256,1024]{1,0:T(8,128)(2,1)}, bf16[256,1024]{1,0:T(8,128)(2,1)S(1)}, u32[]{:S(2)}, u32[]{:S(2)}) collective-permute-start(bf16[256,1024]{1,0:T(8,128)(2,1)} %refs_0_.1), channel_id=1, source_target_pairs={{0,24},{4,28},{8,16},{12,20},{16,8},{20,12},{24,0},{28,4},{1,25},{... | collective-permute-start | bytes 1572872 | tf_op jit(solution)/shard_map/ppermute | solution.py:152
  13.9 44.7 %collective-permute-start = (bf16[256,1024]{1,0:T(8,128)(2,1)}, bf16[256,1024]{1,0:T(8,128)(2,1)S(1)}, u32[]{:S(2)}, u32[]{:S(2)}) collective-permute-start(bf16[256,1024]{1,0:T(8,128)(2,1)} %refs_0_.1), channel_id=1, source_target_pairs={{0,4},{4,0},{8,12},{12,8},{16,20},{20,16},{24,28},{28,24},{1,5},{5... | collective-permute-start | bytes 1572872 | tf_op jit(solution)/shard_map/ppermute | solution.py:152
  24.5 34.1 %collective-permute-start.4 = (bf16[256,1024]{1,0:T(8,128)(2,1)S(1)}, bf16[256,1024]{1,0:T(8,128)(2,1)S(1)}, u32[]{:S(2)}, u32[]{:S(2)}) collective-permute-start(bf16[256,1024]{1,0:T(8,128)(2,1)S(1)} %collective-permute-done.3.refs_4_), channel_id=1, source_target_pairs={{0,4},{4,0},{8,12},{12,8},{16,20},{20,16},{24,28},{28,24},{1,5},{5... | collective-permute-start | bytes 1572872 | tf_op jit(solution)/shard_map/ppermute | solution.py:152
  27.4 31.2 %collective-permute-start.2 = (bf16[256,1024]{1,0:T(8,128)(2,1)S(1)}, bf16[256,1024]{1,0:T(8,128)(2,1)S(1)}, u32[]{:S(2)}, u32[]{:S(2)}) collective-permute-start(bf16[256,1024]{1,0:T(8,128)(2,1)S(1)} %collective-permute-done.1.refs_2_), channel_id=1, source_target_pairs={{0,4},{4,0},{8,12},{12,8},{16,20},{20,16},{24,28},{28,24},{1,5},{5... | collective-permute-start | bytes 1572872 | tf_op jit(solution)/shard_map/ppermute | solution.py:152
  37.0 21.7 %collective-permute-start.6 = (bf16[256,1024]{1,0:T(8,128)(2,1)S(1)}, bf16[256,1024]{1,0:T(8,128)(2,1)}, u32[]{:S(2)}, u32[]{:S(2)}) collective-permute-start(bf16[256,1024]{1,0:T(8,128)(2,1)S(1)} %collective-permute-done.5.refs_6_), channel_id=1, source_target_pairs={{0,4},{4,0},{8,12},{12,8},{16,20},{20,16},{24,28},{28,24},{1,5},{5... | collective-permute-start | bytes 1572872 | tf_op jit(solution)/shard_map/ppermute | solution.py:152
  108.6 15.8 %collective-permute-start.7 = (bf16[256,1024]{1,0:T(8,128)(2,1)}, bf16[256,1024]{1,0:T(8,128)(2,1)S(1)}, u32[]{:S(2)}, u32[]{:S(2)}) collective-permute-start(bf16[256,1024]{1,0:T(8,128)(2,1)} %get-tuple-element.31), channel_id=1, source_target_pairs={{0,4},{4,0},{8,12},{12,8},{16,20},{20,16},{24,28},{28,24},{1,5},{5... | collective-permute-start | bytes 1572872 | tf_op jit(solution)/shard_map/ppermute | solution.py:152
  108.9 6.6 %collective-permute-start.12 = (bf16[256,1024]{1,0:T(8,128)(2,1)}, bf16[256,1024]{1,0:T(8,128)(2,1)S(1)}, u32[]{:S(2)}, u32[]{:S(2)}) collective-permute-start(bf16[256,1024]{1,0:T(8,128)(2,1)} %get-tuple-element.37), channel_id=1, source_target_pairs={{0,4},{4,0},{8,12},{12,8},{16,20},{20,16},{24,28},{28,24},{1,5},{5... | collective-permute-start | bytes 1572872 | tf_op jit(solution)/shard_map/ppermute | solution.py:152
  111.5 14.8 %collective-permute-start.9 = (bf16[256,1024]{1,0:T(8,128)(2,1)S(1)}, bf16[256,1024]{1,0:T(8,128)(2,1)S(1)}, u32[]{:S(2)}, u32[]{:S(2)}) collective-permute-start(bf16[256,1024]{1,0:T(8,128)(2,1)S(1)} %add_convert_fusion.6), channel_id=1, source_target_pairs={{0,8},{4,12},{8,0},{12,4},{16,24},{20,28},{24,16},{28,20},{1,9},{5... | collective-permute-start | bytes 1572872 | tf_op jit(solution)/shard_map/ppermute | solution.py:152
  114.8 25.3 %collective-permute-start.11 = (bf16[256,1024]{1,0:T(8,128)(2,1)}, bf16[256,1024]{1,0:T(8,128)(2,1)S(1)}, u32[]{:S(2)}, u32[]{:S(2)}) collective-permute-start(bf16[256,1024]{1,0:T(8,128)(2,1)} %add_convert_fusion.5), channel_id=1, source_target_pairs={{0,16},{4,20},{8,24},{12,28},{16,0},{20,4},{24,8},{28,12},{1,17},{... | collective-permute-start | bytes 1572872 | tf_op jit(solution)/shard_map/ppermute | solution.py:152
  116.6 23.6 %collective-permute-start.13 = (bf16[256,1024]{1,0:T(8,128)(2,1)}, bf16[256,1024]{1,0:T(8,128)(2,1)}, u32[]{:S(2)}, u32[]{:S(2)}) collective-permute-start(bf16[256,1024]{1,0:T(8,128)(2,1)} %add_convert_fusion.4), channel_id=1, source_target_pairs={{0,24},{4,28},{8,16},{12,20},{16,8},{20,12},{24,0},{28,4},{1,25},{... | collective-permute-start | bytes 1572872 | tf_op jit(solution)/shard_map/ppermute | solution.py:152
  144.5 22.9 %collective-permute-start.19 = (bf16[256,1152]{1,0:T(8,128)(2,1)S(1)}, bf16[256,1152]{1,0:T(8,128)(2,1)S(1)}, u32[]{:S(2)}, u32[]{:S(2)}) collective-permute-start(bf16[256,1152]{1,0:T(8,128)(2,1)S(1)} %concatenate.3.refs_0_), channel_id=1, source_target_pairs={{0,24},{4,28},{8,16},{12,20},{16,8},{20,12},{24,0},{28,4},{1,25},{... | collective-permute-start | bytes 1769480 | tf_op jit(solution)/shard_map/ppermute | solution.py:152
  146.1 32.2 %collective-permute-start.17 = (bf16[256,1152]{1,0:T(8,128)(2,1)S(1)}, bf16[256,1152]{1,0:T(8,128)(2,1)S(1)}, u32[]{:S(2)}, u32[]{:S(2)}) collective-permute-start(bf16[256,1152]{1,0:T(8,128)(2,1)S(1)} %concatenate.3.refs_0_), channel_id=1, source_target_pairs={{0,16},{4,20},{8,24},{12,28},{16,0},{20,4},{24,8},{28,12},{1,17},{... | collective-permute-start | bytes 1769480 | tf_op jit(solution)/shard_map/ppermute | solution.py:152
  146.8 31.4 %collective-permute-start.15 = (bf16[256,1152]{1,0:T(8,128)(2,1)S(1)}, bf16[256,1152]{1,0:T(8,128)(2,1)S(1)}, u32[]{:S(2)}, u32[]{:S(2)}) collective-permute-start(bf16[256,1152]{1,0:T(8,128)(2,1)S(1)} %concatenate.3.refs_0_), channel_id=1, source_target_pairs={{0,8},{4,12},{8,0},{12,4},{16,24},{20,28},{24,16},{28,20},{1,9},{5... | collective-permute-start | bytes 1769480 | tf_op jit(solution)/shard_map/ppermute | solution.py:152
  148.1 30.6 %collective-permute-start.14 = (bf16[256,1152]{1,0:T(8,128)(2,1)S(1)}, bf16[256,1152]{1,0:T(8,128)(2,1)S(1)}, u32[]{:S(2)}, u32[]{:S(2)}) collective-permute-start(bf16[256,1152]{1,0:T(8,128)(2,1)S(1)} %concatenate.3.refs_0_), channel_id=1, source_target_pairs={{0,4},{4,0},{8,12},{12,8},{16,20},{20,16},{24,28},{28,24},{1,5},{5... | collective-permute-start | bytes 1769480 | tf_op jit(solution)/shard_map/ppermute | solution.py:152
  167.4 11.3 %collective-permute-start.20 = (bf16[256,1152]{1,0:T(8,128)(2,1)S(1)}, bf16[256,1152]{1,0:T(8,128)(2,1)S(1)}, u32[]{:S(2)}, u32[]{:S(2)}) collective-permute-start(bf16[256,1152]{1,0:T(8,128)(2,1)S(1)} %collective-permute-done.19.refs_6_), channel_id=1, source_target_pairs={{0,4},{4,0},{8,12},{12,8},{16,20},{20,16},{24,28},{28,24},{1,5},{5... | collective-permute-start | bytes 1769480 | tf_op jit(solution)/shard_map/ppermute | solution.py:152
  219.5 30.8 %all-to-all-start = ((bf16[256,8,512]{0,2,1:T(8,128)(2,1)}), bf16[256,8,512]{0,2,1:T(8,128)(2,1)S(1)}, u32[]{:S(2)}, u32[]{:S(2)}) async-start(bf16[256,8,512]{0,2,1:T(8,128)(2,1)} %bitcast.8), calls=%async_computation | async-start | bytes 4194304 | tf_op jit(solution)/shard_map/all_to_all | solution.py:218
  223.8 28.9 %collective-permute-start.21 = (bf16[256,1024]{1,0:T(8,128)(2,1)}, bf16[256,1024]{1,0:T(8,128)(2,1)S(1)}, u32[]{:S(2)}, u32[]{:S(2)}) collective-permute-start(bf16[256,1024]{1,0:T(8,128)(2,1)} %get-tuple-element.39), channel_id=1, source_target_pairs={{0,4},{4,0},{8,12},{12,8},{16,20},{20,16},{24,28},{28,24},{1,5},{5... | collective-permute-start | bytes 1572872 | tf_op jit(solution)/shard_map/ppermute | solution.py:152
  226.5 34.2 %collective-permute-start.23 = (bf16[256,1024]{1,0:T(8,128)(2,1)}, bf16[256,1024]{1,0:T(8,128)(2,1)}, u32[]{:S(2)}, u32[]{:S(2)}) collective-permute-start(bf16[256,1024]{1,0:T(8,128)(2,1)} %add_convert_fusion.2), channel_id=1, source_target_pairs={{0,8},{4,12},{8,0},{12,4},{16,24},{20,28},{24,16},{28,20},{1,9},{5... | collective-permute-start | bytes 1572872 | tf_op jit(solution)/shard_map/ppermute | solution.py:152
  229.0 31.7 %collective-permute-start.25 = (bf16[256,1024]{1,0:T(8,128)(2,1)}, bf16[256,1024]{1,0:T(8,128)(2,1)}, u32[]{:S(2)}, u32[]{:S(2)}) collective-permute-start(bf16[256,1024]{1,0:T(8,128)(2,1)} %add_convert_fusion.1), channel_id=1, source_target_pairs={{0,16},{4,20},{8,24},{12,28},{16,0},{20,4},{24,8},{28,12},{1,17},{... | collective-permute-start | bytes 1572872 | tf_op jit(solution)/shard_map/ppermute | solution.py:152
  231.5 40.9 %collective-permute-start.27 = (bf16[256,1024]{1,0:T(8,128)(2,1)}, bf16[256,1024]{1,0:T(8,128)(2,1)}, u32[]{:S(2)}, u32[]{:S(2)}) collective-permute-start(bf16[256,1024]{1,0:T(8,128)(2,1)} %add_convert_fusion), channel_id=1, source_target_pairs={{0,24},{4,28},{8,16},{12,20},{16,8},{20,12},{24,0},{28,4},{1,25},{... | collective-permute-start | bytes 1572872 | tf_op jit(solution)/shard_map/ppermute | solution.py:152
  (28 other events, 272.8 us)
Sparse Core Ops, SparseCore 0:
  9.6 48.6 all-gather.5
  143.7 48.4 all-gather.7

commit v2 on v1

v2 whole, which is shorter than its diff:
```python
import functools

import jax
import jax.numpy as jnp
from jax import lax
from jax.experimental import pallas as pl
from jax.experimental.pallas import tpu as pltpu
from jax.sharding import PartitionSpec as P

HD = 128
BLOCK = 64
TOPK = 4
F32 = jnp.float32
BF16 = jnp.bfloat16
VMEM_LIMIT = 40 * 1024 * 1024
NN = (((1,), (0,)), ((), ()))
NT = (((1,), (1,)), ((), ()))
TN = (((0,), (0,)), ((), ()))


def mm(a, b, dims=NN):
    return lax.dot_general(a, b, dims, preferred_element_type=F32)


def joined(items, axis):
    return items[0] if len(items) == 1 else jnp.concatenate(items, axis=axis)


def diagonal(pair):
    zero = jnp.zeros((pair.shape[0], HD), pair.dtype)
    top = jnp.concatenate([pair[:, :HD], zero], axis=1)
    low = jnp.concatenate([zero, pair[:, HD:]], axis=1)
    return jnp.concatenate([top, low], axis=0)


def gate_kernel(sel_ref, mark_ref, q_ref, aux_ref):
    block_total, width = mark_ref.shape
    rows = q_ref.shape[0]
    heads = width // HD
    scale = HD ** (-0.5)
    ids = lax.broadcasted_iota(jnp.int32, (block_total, rows), 0)
    picks = [sel_ref[t : t + 1, :] == ids for t in range(TOPK)]
    chosen = picks[0]
    for t in range(1, TOPK):
        chosen = chosen | picks[t]
    bias = jnp.where(chosen, 0.0, -1e30)
    gates = [[None] * heads for _ in range(TOPK)]
    for h in range(heads):
        cols = slice(h * HD, (h + 1) * HD)
        logits = scale * mm(mark_ref[:, cols], q_ref[:, cols], NT) + bias
        weight = jnp.exp(logits - jnp.max(logits, axis=0, keepdims=True))
        inverse = 1.0 / jnp.sum(weight, axis=0, keepdims=True)
        for t in range(TOPK):
            gates[t][h] = inverse * jnp.sum(
                jnp.where(picks[t], weight, 0.0), axis=0, keepdims=True
            )
    high = (sel_ref[...] >> 4).astype(F32)
    low = (sel_ref[...] & 15).astype(F32)
    lines = [gates[t][h] for t in range(TOPK) for h in range(heads)] + [high, low]
    lines.append(jnp.zeros((HD - TOPK * heads - 2 * TOPK, rows), F32))
    aux_ref[...] = jnp.concatenate(lines, axis=0).astype(BF16)


def block_ids(aux, heads):
    at = TOPK * heads
    return 16.0 * aux[at : at + TOPK] + aux[at + TOPK : at + 2 * TOPK]


def forward_kernel(chunks, span, cap, me_ref, aux_ref, k_ref, v_ref, *refs):
    q_refs = refs[:chunks]
    even_refs = refs[chunks : chunks + chunks // 2]
    odd_ref, qg_ref, p_ref, gate_ref, hot_ref = refs[chunks + chunks // 2 : chunks + chunks // 2 + 5]
    auxg_ref, out_ref = refs[chunks + chunks // 2 + 5 :]
    block_count, _, width = k_ref.shape
    heads = width // HD
    rows = q_refs[0].shape[0]
    group_rows = rows * span
    groups = chunks // span
    me = me_ref[0]
    rate = HD ** (-0.5) * 1.4426950408889634
    base = me * block_count

    before = lax.broadcasted_iota(jnp.int32, (group_rows, group_rows), 0)
    after = lax.broadcasted_iota(jnp.int32, (group_rows, group_rows), 1)
    earlier = (before < after).astype(BF16)
    own_ids = (base + lax.broadcasted_iota(jnp.int32, (block_count, group_rows), 0)).astype(F32)
    place = lax.broadcasted_iota(jnp.int32, (cap, group_rows), 0).astype(F32)
    for g in range(groups):
        aux = joined([aux_ref[me ^ (g * span + i)] for i in range(span)], 1)
        picked = block_ids(aux.astype(F32), heads)
        own = picked[0:1, :] == own_ids
        for t in range(1, TOPK):
            own = own | (picked[t : t + 1, :] == own_ids)
        own = jnp.where(own, 1.0, 0.0)
        rank = jnp.where(own > 0.5, mm(own.astype(BF16), earlier), -1.0)
        hot = jnp.concatenate(
            [jnp.where(rank[b : b + 1, :] == place, 1.0, 0.0) for b in range(block_count)], axis=0
        ).astype(BF16)
        hot_ref[g] = hot
        auxg_ref[:, g * cap : (g + 1) * cap, :] = mm(hot, aux, NT).reshape(block_count, cap, HD)
        q_group = joined([q_refs[g * span + i][...] for i in range(span)], 0)
        qg_ref[:, g * cap : (g + 1) * cap, :] = (
            mm(hot, q_group).astype(BF16).reshape(block_count, cap, width)
        )

    def one_block(b, carry):
        pairs = [slice(p * 2 * HD, (p + 1) * 2 * HD) for p in range(heads // 2)]
        logits = [mm(diagonal(k_ref[b, :, cols]), qg_ref[b, :, cols], NT) for cols in pairs]
        wide = [diagonal(v_ref[b, :, cols]) for cols in pairs]
        aux = auxg_ref[b].T
        ids = block_ids(aux, heads)
        mine = (base + b).astype(F32)
        gates = jnp.where(ids[0:1] == mine, aux[:heads], 0.0)
        for t in range(1, TOPK):
            gates = gates + jnp.where(
                ids[t : t + 1] == mine, aux[t * heads : (t + 1) * heads], 0.0
            )
        probs, gated = [], []
        for p in range(heads // 2):
            for i in range(2):
                part = logits[p][i * BLOCK : (i + 1) * BLOCK]
                weight = jnp.exp2(rate * (part - jnp.max(part, axis=0, keepdims=True)))
                inverse = 1.0 / jnp.sum(weight, axis=0, keepdims=True)
                gate = gates[2 * p + i : 2 * p + i + 1, :]
                probs.append((weight * inverse).astype(BF16))
                gated.append((weight * (inverse * gate)).astype(BF16))
        outs = [
            mm(jnp.concatenate(gated[2 * p : 2 * p + 2], axis=0), wide[p], TN).astype(BF16)
            for p in range(heads // 2)
        ]
        gate_ref[b] = gates
        for p in range(heads // 2):
            p_ref[b, p] = jnp.concatenate(probs[2 * p : 2 * p + 2], axis=0)
            out_ref[b, :, pairs[p]] = outs[p]
        return carry

    lax.fori_loop(0, block_count, one_block, 0)

    for g in range(groups):
        slots = out_ref[:, g * cap : (g + 1) * cap, :].reshape(block_count * cap, width)
        part = mm(hot_ref[g], slots, TN).astype(BF16)
        for i in range(span):
            m = g * span + i
            target = odd_ref.at[m // 2] if m % 2 else even_refs[m // 2]
            target[...] = part[i * rows : (i + 1) * rows]


def finish_kernel(*refs):
    *term_refs, ga_ref, attn_ref, ext_ref = refs
    rows, width = ga_ref.shape
    heads = width // HD
    lane = lax.broadcasted_iota(jnp.int32, (rows, HD), 1)
    high = jnp.zeros((rows, HD), F32)
    low = jnp.zeros((rows, HD), F32)
    ext_ref[:, :width] = ga_ref[...]
    for h in range(heads):
        cols = slice(h * HD, (h + 1) * HD)
        total = term_refs[0][:, cols].astype(F32)
        for ref in term_refs[1:]:
            total = total + ref[:, cols].astype(F32)
        attn_ref[:, cols] = total.astype(BF16)
        dots = jnp.sum(total * ga_ref[:, cols].astype(F32), axis=1, keepdims=True)
        upper = dots.astype(BF16).astype(F32)
        high = jnp.where(lane == h, upper, high)
        low = jnp.where(lane == heads + h, dots - upper, low)
    ext_ref[:, width:] = (high + low).astype(BF16)


def backward_kernel(chunks, span, cap, hot_ref, qg_ref, p_ref, gate_ref, k_ref, v_ref, *refs):
    ga_refs = refs[:chunks]
    even_refs = refs[chunks : chunks + chunks // 2]
    odd_ref, dk_ref, dv_ref = refs[chunks + chunks // 2 : chunks + chunks // 2 + 3]
    gag_ref, dq_ref = refs[chunks + chunks // 2 + 3 :]
    block_count, _, width = k_ref.shape
    heads = width // HD
    rows = ga_refs[0].shape[0]
    groups = chunks // span
    scale = HD ** (-0.5)

    for g in range(groups):
        ga_group = joined([ga_refs[g * span + i][...] for i in range(span)], 0)
        gag_ref[:, g * cap : (g + 1) * cap, :] = (
            mm(hot_ref[g], ga_group).astype(BF16).reshape(block_count, cap, width + HD)
        )
    last = lax.broadcasted_iota(jnp.int32, (BLOCK, groups * cap), 0) == BLOCK - 1

    def one_block(b, carry):
        pairs = [slice(p * 2 * HD, (p + 1) * 2 * HD) for p in range(heads // 2)]
        q = [qg_ref[b, :, cols] for cols in pairs]
        ga = [gag_ref[b, :, cols] for cols in pairs]
        grads = [mm(diagonal(v_ref[b, :, cols]), ga[p], NT) for p, cols in enumerate(pairs)]
        wide = [diagonal(k_ref[b, :, cols]) for cols in pairs]
        probs = [p_ref[b, p].astype(F32) for p in range(heads // 2)]
        gates = gate_ref[b]
        dots = gag_ref[b, :, width:].astype(F32).T
        dots = dots[:heads] + dots[heads : 2 * heads]
        gated, score = [], []
        for p in range(heads // 2):
            for i in range(2):
                at = slice(i * BLOCK, (i + 1) * BLOCK)
                h = 2 * p + i
                gate = gates[h : h + 1, :]
                grad = grads[p][at]
                delta = jnp.sum(probs[p][at] * grad, axis=0, keepdims=True)
                weight = probs[p][at] * gate
                extra = jnp.where(last, scale * gate * (delta - dots[h : h + 1, :]), 0.0)
                score.append((weight * (scale * (grad - delta)) + extra).astype(BF16))
                gated.append(weight.astype(BF16))
        for p, cols in enumerate(pairs):
            both = jnp.concatenate(gated[2 * p : 2 * p + 2], axis=0)
            scores = jnp.concatenate(score[2 * p : 2 * p + 2], axis=0)
            dv = mm(both, ga[p])
            dk = mm(scores, q[p])
            dq = mm(scores, wide[p], TN).astype(BF16)
            dv_ref[b, :, cols] = jnp.concatenate([dv[:BLOCK, :HD], dv[BLOCK:, HD:]], axis=1)
            dk_ref[b, :, cols] = jnp.concatenate([dk[:BLOCK, :HD], dk[BLOCK:, HD:]], axis=1)
            dq_ref[b, :, cols] = dq
        return carry

    lax.fori_loop(0, block_count, one_block, 0)

    for g in range(groups):
        slots = dq_ref[:, g * cap : (g + 1) * cap, :].reshape(block_count * cap, width)
        part = mm(hot_ref[g], slots, TN).astype(BF16)
        for i in range(span):
            m = g * span + i
            target = odd_ref.at[m // 2] if m % 2 else even_refs[m // 2]
            target[...] = part[i * rows : (i + 1) * rows]


def weight_kernel(chips, me_ref, *refs):
    slabs, attns = refs[:chips], refs[chips : 2 * chips]
    own_ref, other_ref = refs[2 * chips :]
    half = own_ref.shape[0]
    core = me_ref[0] % 2
    attn = jnp.concatenate([ref[...] for ref in attns], axis=0)

    def side(which):
        cols = pl.ds(pl.multiple_of(which * half, half), half)
        return mm(jnp.concatenate([ref[:, cols] for ref in slabs], axis=0), attn, TN)

    own_ref[...] = side(core)
    other_ref[...] = side(1 - core).astype(BF16)


def swap(x, bits):
    count = lax.axis_size("ctx")
    return lax.ppermute(x, "ctx", [(i, i ^ bits) for i in range(count)])


def after(x, *others):
    return lax.optimization_barrier((x, *others))[0]


def chip_terms(evens, odd):
    received = swap(odd, 1)
    terms = [evens[0], received[0]]
    for j in range(1, len(evens)):
        both = evens[j].astype(F32) + received[j].astype(F32)
        terms.append(swap(both.astype(BF16), 2 * j))
    return terms


def body(queries, key_rows, value_rows, selected, out_grad, out_weight):
    chunks = lax.axis_size("ctx")
    chips = chunks // 2
    rows, width = queries.shape
    features = out_weight.shape[0]
    heads = width // HD
    block_count = key_rows.shape[0] // BLOCK
    block_total = block_count * chunks
    capacity = 2 * rows * TOPK // block_total
    span = max(1, 16 // capacity)
    cap = capacity * span
    groups = chunks // span
    slots = groups * cap
    index = lax.axis_index("ctx").astype(jnp.int32)
    me = index.reshape(1)
    keys = key_rows.reshape(block_count, BLOCK, width)
    values = value_rows.reshape(block_count, BLOCK, width)
    vmem = pl.BlockSpec(memory_space=pltpu.VMEM)
    smem = pl.BlockSpec(memory_space=pltpu.SMEM)
    params = pltpu.CompilerParams(vmem_limit_bytes=VMEM_LIMIT)

    def shaped(shape, kind=BF16):
        return jax.ShapeDtypeStruct(shape, kind)

    grad_full = lax.all_gather(out_grad, "head", axis=0)
    query_chips = [queries] + [swap(queries, 2 * j) for j in range(1, chips)]
    mark_all = lax.all_gather(keys[:, BLOCK - 1], "ctx", axis=0, tiled=True)
    aux = pl.pallas_call(
        gate_kernel,
        out_shape=shaped((HD, rows)),
        in_specs=[vmem] * 3,
        out_specs=vmem,
        compiler_params=params,
        name="gates",
    )(selected.T, mark_all, queries)
    aux_all = lax.all_gather(aux, "ctx", axis=0)
    query_all = []
    for piece in query_chips:
        query_all += [piece, swap(after(piece, aux_all), 1)]

    outs = pl.pallas_call(
        functools.partial(forward_kernel, chunks, span, cap),
        out_shape=[shaped((rows, width))] * chips
        + [
            shaped((chips, rows, width)),
            shaped((block_count, slots, width)),
            shaped((block_count, heads // 2, 2 * BLOCK, slots)),
            shaped((block_count, heads, slots), F32),
            shaped((groups, block_count * cap, rows * span)),
        ],
        in_specs=[smem] + [vmem] * (3 + chunks),
        out_specs=[vmem] * (chips + 5),
        scratch_shapes=[
            pltpu.VMEM((block_count, slots, HD), F32),
            pltpu.VMEM((block_count, slots, width), BF16),
        ],
        compiler_params=params,
        name="forward",
    )(me, aux_all, keys, values, *query_all)
    q_slots, probs, gates, hot = outs[chips + 1 :]

    grad_attn = jnp.einsum(
        "zqf,zfd->qd",
        grad_full,
        out_weight.reshape(features // width, width, width),
        preferred_element_type=F32,
    ).astype(BF16)
    terms = chip_terms(outs[:chips], outs[chips])
    attn_out, extended = pl.pallas_call(
        finish_kernel,
        out_shape=[shaped((rows, width)), shaped((rows, width + HD))],
        in_specs=[vmem] * (len(terms) + 1),
        out_specs=[vmem] * 2,
        compiler_params=params,
        name="finish",
    )(*terms, grad_attn)
    grad_chips = [extended] + [swap(extended, 2 * j) for j in range(1, chips)]
    grad_all = []
    for piece in grad_chips:
        grad_all += [piece, swap(piece, 1)]

    share = features // chips
    slabs, attns = [], [attn_out]
    for j in range(chips):
        first = ((index // 2) ^ j) * share
        slab = lax.dynamic_slice(
            grad_full, (first // width, 0, first % width), (1, rows, share)
        ).reshape(rows, share)
        slabs.append(swap(after(slab, *grad_chips), 2 * j) if j else slab)
    for j in range(1, chips):
        attns.append(swap(after(attn_out, *grad_chips), 2 * j))

    outs = pl.pallas_call(
        functools.partial(backward_kernel, chunks, span, cap),
        out_shape=[shaped((rows, width))] * chips
        + [shaped((chips, rows, width))]
        + [shaped((block_count, BLOCK, width), F32)] * 2,
        in_specs=[vmem] * (6 + chunks),
        out_specs=[vmem] * (chips + 3),
        scratch_shapes=[
            pltpu.VMEM((block_count, slots, width + HD), BF16),
            pltpu.VMEM((block_count, slots, width), BF16),
        ],
        compiler_params=params,
        name="backward",
    )(hot, q_slots, probs, gates, keys, values, *grad_all)
    key_grad, value_grad = outs[chips + 1 :]
    terms = chip_terms(outs[:chips], outs[chips])
    query_grad = terms[0].astype(F32)
    for term in terms[1:]:
        query_grad = query_grad + term.astype(F32)

    weight_own, weight_other = pl.pallas_call(
        functools.partial(weight_kernel, chips),
        out_shape=[shaped((share // 2, width), F32), shaped((share // 2, width))],
        in_specs=[smem] + [vmem] * (2 * chips),
        out_specs=[vmem] * 2,
        compiler_params=params,
        name="weight",
    )(me, *slabs, *attns)
    weight_grad = weight_own + swap(weight_other, 1).astype(F32)
    return (
        query_grad,
        key_grad.reshape(-1, width),
        value_grad.reshape(-1, width),
        weight_grad,
    )


def solution(mesh):
    return jax.shard_map(
        body,
        mesh=mesh,
        in_specs=(
            P("ctx", "head"),
            P("ctx", "head"),
            P("ctx", "head"),
            P("ctx", None),
            P("ctx", "head"),
            P(None, "head"),
        ),
        out_specs=(P("ctx", "head"), P("ctx", "head"), P("ctx", "head"), P("ctx", "head")),
        check_vma=False,
    )
```

time: 291 us -> 253 us (0.87)
  Pallas kernels: 85.6 us -> 41.1 us
  blocking collectives: 20.4 us -> 35.9 us
  other arithmetic: 14.2 us -> 7.68 us
  matrix products: 12.3 us -> 6.4 us
  starting transfers between devices: 21.9 us -> 27.1 us
  local copies, waits for them, and re-layouts: 11.8 us -> 8.03 us
    pallas_call x1, Pallas kernels: 48.2 us -> 16.3 us  [body(): pl.pallas_call(functools.partial(forward_kernel, chunks, span, cap), out_...]
    pallas_call x1, Pallas kernels: 37.4 us -> 18.4 us  [body(): pl.pallas_call(functools.partial(backward_kernel, chunks, span, cap), out...]
    all_to_all x1 -> x0, waiting for transfers between devices: 18.3 us -> none  [body(): lax.all_to_all(grad_full, 'ctx', split_axis=1, concat_axis=0, tiled=True)]
    all_gather x1, blocking collectives: 9.55 us -> 27.2 us  [body(): mark_all = lax.all_gather(keys[:, BLOCK - 1], 'ctx', axis=0, tiled=True)]
    all_gather x2 -> x1, waiting for transfers between devices: 0.01 us -> 17.4 us  [body(): grad_full = lax.all_gather(out_grad, 'head', axis=0)]
    ppermute x28 -> x29, starting transfers between devices: 17.9 us -> 27.1 us  [swap(): return lax.ppermute(x, 'ctx', [(i, i ^ bits) for i in range(count)])]
    pallas_call x0 -> x3, Pallas kernels: none -> 6.47 us  [the longest x1 2.4 us: body(): pl.pallas_call(functools.partial(weight_kernel, chips), out_shape=[shaped...]
    dot_general x2 -> x1, matrix products: 12.3 us -> 6.4 us  [body(): jnp.einsum('zqf,zfd->qd', grad_full, out_weight.reshape(features // width...]
  transfers between devices with their start and end apart: 31 -> 30, of which waited for: 13 -> 15; matrix products, arithmetic and copies ran while one was open for 8% -> 6% of each run, Pallas kernels for 29% -> 8%
where the time goes in v2:
time: 253 us
  waiting for transfers between devices  112 us (44%)
  Pallas kernels  41.1 us (16%)
  blocking collectives  35.9 us (14%)
  starting transfers between devices  27.1 us (11%)
  between operations  14.2 us (6%)
  local copies, waits for them, and re-layouts  8.03 us (3%)
  other arithmetic  7.68 us (3%)
  matrix products  6.4 us (3%)
    ppermute x29, waiting for transfers between devices, swap(): return lax.ppermute(x, 'ctx', [(i, i ^ bits) for i in range(count)])  95 us
    all_gather x1, blocking collectives, body(): mark_all = lax.all_gather(keys[:, BLOCK - 1], 'ctx', axis=0, tiled=True)  27.2 us
    ppermute x29, starting transfers between devices, swap(): return lax.ppermute(x, 'ctx', [(i, i ^ bits) for i in range(count)])  27.1 us
    pallas_call x1, Pallas kernels, body(): pl.pallas_call(functools.partial(backward_kernel, chunks, span, cap), out...  18.4 us
    all_gather x1, waiting for transfers between devices, body(): grad_full = lax.all_gather(out_grad, 'head', axis=0)  17.4 us
    pallas_call x1, Pallas kernels, body(): pl.pallas_call(functools.partial(forward_kernel, chunks, span, cap), out_...  16.3 us
    all_gather x1, blocking collectives, body(): aux_all = lax.all_gather(aux, 'ctx', axis=0)  8.67 us
    dot_general x1, matrix products, body(): jnp.einsum('zqf,zfd->qd', grad_full, out_weight.reshape(features // width...  6.4 us
  transfers between devices with their start and end apart: 30, of which 15 were waited for; matrix products, arithmetic and copies ran while one was open for 6% of the time, Pallas kernels for 8%

profile of v2, /device:TPU:0, one launch (start us, length us, event | category | flops | bytes accessed | tf_op | source)
XLA Modules:
  0.0 252.9 jit_solution(5052928557689668935)
XLA Ops:
  7.2 3.0 %collective-permute-start.1 = (bf16[256,1024]{1,0:T(8,128)(2,1)}, bf16[256,1024]{1,0:T(8,128)(2,1)S(1)}, u32[]{:S(2)}, u32[]{:S(2)}) collective-permute-start(bf16[256,1024]{1,0:T(8,128)(2,1)} %refs_0_.1), channel_id=1, source_target_pairs={{0,8},{4,12},{8,0},{12,4},{16,24},{20,28},{24,16},{28,20},{1,9},{5... | collective-permute-start | bytes 1572872 | tf_op jit(solution)/shard_map/ppermute | solution.py:248
  12.8 27.2 %all-gather = bf16[128,1,1024]{2,0,1:T(8,128)(2,1)S(1)} all-gather(bf16[16,1,1024]{2,0,1:T(8,128)(2,1)S(1)} %copy.10), channel_id=2, replica_groups=mesh['ctx'=8,'head'=4] {'ctx'}, dimensions={0}, use_global_device_ids=true | all-gather | bytes 294912 | tf_op jit(solution)/shard_map/all_gather | solution.py:290
  40.7 2.0 gates.1
  42.8 8.7 %all-gather.1 = bf16[1024,256]{1,0:T(8,128)(2,1)S(1)} all-gather(bf16[128,256]{1,0:T(8,128)(2,1)S(1)} %gates.1), channel_id=3, replica_groups=mesh['ctx'=8,'head'=4] {'ctx'}, dimensions={0}, use_global_device_ids=true | all-gather | bytes 589824 | tf_op jit(solution)/shard_map/all_gather | solution.py:299
  55.9 16.3 %forward.1 = (bf16[256,1024]{1,0:T(8,128)(2,1)S(1)}, bf16[256,1024]{1,0:T(8,128)(2,1)S(1)}, bf16[256,1024]{1,0:T(8,128)(2,1)S(1)}, bf16[256,1024]{1,0:T(8,128)(2...) custom-call(s32[1]{0:T(128)} %bitcast.me_ref, ...), custom_call_target="tpu_custom_call" | custom-call | tf_op jit(solution)/shard_map/forward/pallas_call | solution.py:304
  72.7 3.8 %collective-permute-done.7 = bf16[4,256,1024]{2,1,0:T(8,128)(2,1)S(1)} collective-permute-done((bf16[4,256,1024]{2,1,0:T(8,128)(2,1)S(1)}, bf16[4,256,1024]{2,1,0:T(8,128)(2,1)S(1)}, u32[]{:S(2)}, u32[]{:S(2)}) %collective-permute-start.7) | collective-permute-done | bytes 2097184 | tf_op jit(solution)/shard_map/ppermute | solution.py:248
  79.6 1.7 collective-permute-start.8
  81.6 17.4 %all-gather.5.cloned.1.call-done = bf16[1024,1024]{1,0:T(8,128)(2,1)} async-done(((bf16[256,1024]{1,0:T(8,128)(2,1)}), bf16[1024,1024]{1,0:T(8,128)(2,1)}) %all-gather.5.cloned.1.call-update) | async-done | bytes 2097168 | tf_op jit(solution)/shard_map/all_gather | solution.py:288
  99.1 6.4 %fusion.refs_5_ = bf16[256,1024]{1,0:T(8,128)(2,1)S(1)} fusion(bf16[4,256,1024]{2,1,0:T(8,128)(2,1)} %bitcast.69, bf16[4,1024,1024]{2,1,0:T(8,128)(2,1)} %bitcast.71), kind=kOutput, calls=%fused_computation.2 | convolution fusion | flops 2147745792 | bytes 11010048 | tf_op jit(solution)/shard_map/zqf,zfd->qd/dot_general | solution.py:325
  107.6 2.0 finish.1
  113.2 12.7 %collective-permute-done.12.refs_2_ = bf16[256,1152]{1,0:T(8,128)(2,1)S(1)} collective-permute-done((bf16[256,1152]{1,0:T(8,128)(2,1)S(1)}, bf16[256,1152]{1,0:T(8,128)(2,1)S(1)}, u32[]{:S(2)}, u32[]{:S(2)}) %collective-permute-start.12) | collective-permute-done | bytes 589856 | tf_op jit(solution)/shard_map/ppermute | solution.py:248
  125.9 12.7 %collective-permute-done.14.refs_4_ = bf16[256,1152]{1,0:T(8,128)(2,1)S(1)} collective-permute-done((bf16[256,1152]{1,0:T(8,128)(2,1)S(1)}, bf16[256,1152]{1,0:T(8,128)(2,1)S(1)}, u32[]{:S(2)}, u32[]{:S(2)}) %collective-permute-start.14) | collective-permute-done | bytes 589856 | tf_op jit(solution)/shard_map/ppermute | solution.py:248
  141.5 18.4 %backward.1 = (bf16[256,1024]{1,0:T(8,128)(2,1)S(1)}, bf16[256,1024]{1,0:T(8,128)(2,1)S(1)}, bf16[256,1024]{1,0:T(8,128)(2,1)S(1)}, bf16[256,1024]{1,0:T(8,128)(...) custom-call(bf16[8,256,256]{2,1,0:T(8,128)(2,1)S(1)} %copy-done.4, ...), custom_call_target="tpu_custom_call" | custom-call | tf_op jit(solution)/shard_map/backward/pallas_call | solution.py:356
  164.5 1.7 dynamic-slice_bitcast_fusion
  169.3 7.9 %collective-permute-done.25.refs_5_ = bf16[256,1024]{1,0:T(8,128)(2,1)S(1)} collective-permute-done((bf16[256,1024]{1,0:T(8,128)(2,1)S(1)}, bf16[256,1024]{1,0:T(8,128)(2,1)S(1)}, u32[]{:S(2)}, u32[]{:S(2)}) %collective-permute-start.25) | collective-permute-done | bytes 524320 | tf_op jit(solution)/shard_map/ppermute | solution.py:248
  178.7 19.8 %collective-permute-done.26.refs_6_ = bf16[256,1024]{1,0:T(8,128)(2,1)S(1)} collective-permute-done((bf16[256,1024]{1,0:T(8,128)(2,1)S(1)}, bf16[256,1024]{1,0:T(8,128)(2,1)S(1)}, u32[]{:S(2)}, u32[]{:S(2)}) %collective-permute-start.26) | collective-permute-done | bytes 524320 | tf_op jit(solution)/shard_map/ppermute | solution.py:248
  198.5 2.4 collective-permute-start.22
  200.9 10.4 %collective-permute-done.23.refs_2_ = bf16[256,1024]{1,0:T(8,128)(2,1)S(1)} collective-permute-done((bf16[256,1024]{1,0:T(8,128)(2,1)S(1)}, bf16[256,1024]{1,0:T(8,128)(2,1)S(1)}, u32[]{:S(2)}, u32[]{:S(2)}) %collective-permute-start.23) | collective-permute-done | bytes 524320 | tf_op jit(solution)/shard_map/ppermute | solution.py:248
  211.3 2.4 weight.1
  213.8 2.0 fusion.3
  217.4 2.6 %collective-permute-start.20 = (bf16[256,1024]{1,0:T(8,128)(2,1)S(1)}, bf16[256,1024]{1,0:T(8,128)(2,1)S(1)}, u32[]{:S(2)}, u32[]{:S(2)}) collective-permute-start(bf16[256,1024]{1,0:T(8,128)(2,1)S(1)} %get-tuple-element.66), channel_id=1, source_target_pairs={{0,16},{4,20},{8,24},{12,28},{16,0},{20,4},{24,8},{28,12},{1,17},{... | collective-permute-start | bytes 1572872 | tf_op jit(solution)/shard_map/ppermute | solution.py:248
  221.7 9.0 %collective-permute-done.19 = bf16[256,1024]{1,0:T(8,128)(2,1)S(1)} collective-permute-done((bf16[256,1024]{1,0:T(8,128)(2,1)S(1)}, bf16[256,1024]{1,0:T(8,128)(2,1)S(1)}, u32[]{:S(2)}, u32[]{:S(2)}) %collective-permute-start.19) | collective-permute-done | bytes 524320 | tf_op jit(solution)/shard_map/ppermute | solution.py:248
  230.7 12.9 %collective-permute-done.20 = bf16[256,1024]{1,0:T(8,128)(2,1)S(1)} collective-permute-done((bf16[256,1024]{1,0:T(8,128)(2,1)S(1)}, bf16[256,1024]{1,0:T(8,128)(2,1)S(1)}, u32[]{:S(2)}, u32[]{:S(2)}) %collective-permute-start.20) | collective-permute-done | bytes 524320 | tf_op jit(solution)/shard_map/ppermute | solution.py:248
  243.6 2.4 fusion.6
  (85 shorter events, 32.7 us)
Async XLA Ops:
  7.2 91.9 %all-gather.5.cloned.1.call-start = ((), (), s32[]{:S(2)}) async-start(), calls=%async_computation | async-start | bytes 2621440 | tf_op jit(solution)/shard_map/all_gather | solution.py:288
  7.2 44.6 %collective-permute-start.1 = (bf16[256,1024]{1,0:T(8,128)(2,1)}, bf16[256,1024]{1,0:T(8,128)(2,1)S(1)}, u32[]{:S(2)}, u32[]{:S(2)}) collective-permute-start(bf16[256,1024]{1,0:T(8,128)(2,1)} %refs_0_.1), channel_id=1, source_target_pairs={{0,8},{4,12},{8,0},{12,4},{16,24},{20,28},{24,16},{28,20},{1,9},{5... | collective-permute-start | bytes 1572872 | tf_op jit(solution)/shard_map/ppermute | solution.py:248
  10.2 41.7 %collective-permute-start.3 = (bf16[256,1024]{1,0:T(8,128)(2,1)}, bf16[256,1024]{1,0:T(8,128)(2,1)}, u32[]{:S(2)}, u32[]{:S(2)}) collective-permute-start(bf16[256,1024]{1,0:T(8,128)(2,1)} %refs_0_.1), channel_id=1, source_target_pairs={{0,16},{4,20},{8,24},{12,28},{16,0},{20,4},{24,8},{28,12},{1,17},{... | collective-permute-start | bytes 1572872 | tf_op jit(solution)/shard_map/ppermute | solution.py:248
  11.7 40.6 %collective-permute-start.5 = (bf16[256,1024]{1,0:T(8,128)(2,1)}, bf16[256,1024]{1,0:T(8,128)(2,1)}, u32[]{:S(2)}, u32[]{:S(2)}) collective-permute-start(bf16[256,1024]{1,0:T(8,128)(2,1)} %refs_0_.1), channel_id=1, source_target_pairs={{0,24},{4,28},{8,16},{12,20},{16,8},{20,12},{24,0},{28,4},{1,25},{... | collective-permute-start | bytes 1572872 | tf_op jit(solution)/shard_map/ppermute | solution.py:248
  72.2 4.2 %collective-permute-start.7 = (bf16[4,256,1024]{2,1,0:T(8,128)(2,1)S(1)}, bf16[4,256,1024]{2,1,0:T(8,128)(2,1)S(1)}, u32[]{:S(2)}, u32[]{:S(2)}) collective-permute-start(bf16[4,256,1024]{2,1,0:T(8,128)(2,1)S(1)} %get-tuple-element.41), channel_id=1, source_target_pairs={{0,4},{4,0},{8,12},{12,8},{16,20},{20,16},{24,28},{28,24},{1,5},{5... | collective-permute-start | bytes 6291464 | tf_op jit(solution)/shard_map/ppermute | solution.py:248
  78.0 27.4 %collective-permute-start.10 = (bf16[256,1024]{1,0:T(8,128)(2,1)}, bf16[256,1024]{1,0:T(8,128)(2,1)S(1)}, u32[]{:S(2)}, u32[]{:S(2)}) collective-permute-start(bf16[256,1024]{1,0:T(8,128)(2,1)} %get-tuple-element.67), channel_id=1, source_target_pairs={{0,24},{4,28},{8,16},{12,20},{16,8},{20,12},{24,0},{28,4},{1,25},{... | collective-permute-start | bytes 1572872 | tf_op jit(solution)/shard_map/ppermute | solution.py:248
  79.6 26.7 %collective-permute-start.8 = (bf16[256,1024]{1,0:T(8,128)(2,1)}, bf16[256,1024]{1,0:T(8,128)(2,1)}, u32[]{:S(2)}, u32[]{:S(2)}) collective-permute-start(bf16[256,1024]{1,0:T(8,128)(2,1)} %get-tuple-element.69), channel_id=1, source_target_pairs={{0,8},{4,12},{8,0},{12,4},{16,24},{20,28},{24,16},{28,20},{1,9},{5... | collective-permute-start | bytes 1572872 | tf_op jit(solution)/shard_map/ppermute | solution.py:248
  81.3 25.0 %collective-permute-start.9 = (bf16[256,1024]{1,0:T(8,128)(2,1)}, bf16[256,1024]{1,0:T(8,128)(2,1)}, u32[]{:S(2)}, u32[]{:S(2)}) collective-permute-start(bf16[256,1024]{1,0:T(8,128)(2,1)} %get-tuple-element.68), channel_id=1, source_target_pairs={{0,16},{4,20},{8,24},{12,28},{16,0},{20,4},{24,8},{28,12},{1,17},{... | collective-permute-start | bytes 1572872 | tf_op jit(solution)/shard_map/ppermute | solution.py:248
  109.7 16.3 %collective-permute-start.12 = (bf16[256,1152]{1,0:T(8,128)(2,1)S(1)}, bf16[256,1152]{1,0:T(8,128)(2,1)S(1)}, u32[]{:S(2)}, u32[]{:S(2)}) collective-permute-start(bf16[256,1152]{1,0:T(8,128)(2,1)S(1)} %get-tuple-element.45.refs_0_), channel_id=1, source_target_pairs={{0,8},{4,12},{8,0},{12,4},{16,24},{20,28},{24,16},{28,20},{1,9},{5... | collective-permute-start | bytes 1769480 | tf_op jit(solution)/shard_map/ppermute | solution.py:248
  111.3 27.4 %collective-permute-start.14 = (bf16[256,1152]{1,0:T(8,128)(2,1)S(1)}, bf16[256,1152]{1,0:T(8,128)(2,1)S(1)}, u32[]{:S(2)}, u32[]{:S(2)}) collective-permute-start(bf16[256,1152]{1,0:T(8,128)(2,1)S(1)} %get-tuple-element.45.refs_0_), channel_id=1, source_target_pairs={{0,16},{4,20},{8,24},{12,28},{16,0},{20,4},{24,8},{28,12},{1,17},{... | collective-permute-start | bytes 1769480 | tf_op jit(solution)/shard_map/ppermute | solution.py:248
  112.8 25.9 %collective-permute-start.16 = (bf16[256,1152]{1,0:T(8,128)(2,1)S(1)}, bf16[256,1152]{1,0:T(8,128)(2,1)S(1)}, u32[]{:S(2)}, u32[]{:S(2)}) collective-permute-start(bf16[256,1152]{1,0:T(8,128)(2,1)S(1)} %get-tuple-element.45.refs_0_), channel_id=1, source_target_pairs={{0,24},{4,28},{8,16},{12,20},{16,8},{20,12},{24,0},{28,4},{1,25},{... | collective-permute-start | bytes 1769480 | tf_op jit(solution)/shard_map/ppermute | solution.py:248
  113.2 26.0 %collective-permute-start.11 = (bf16[256,1152]{1,0:T(8,128)(2,1)S(1)}, bf16[256,1152]{1,0:T(8,128)(2,1)S(1)}, u32[]{:S(2)}, u32[]{:S(2)}) collective-permute-start(bf16[256,1152]{1,0:T(8,128)(2,1)S(1)} %get-tuple-element.45.refs_0_), channel_id=1, source_target_pairs={{0,4},{4,0},{8,12},{12,8},{16,20},{20,16},{24,28},{28,24},{1,5},{5... | collective-permute-start | bytes 1769480 | tf_op jit(solution)/shard_map/ppermute | solution.py:248
  125.9 13.2 %collective-permute-start.13 = (bf16[256,1152]{1,0:T(8,128)(2,1)S(1)}, bf16[256,1152]{1,0:T(8,128)(2,1)S(1)}, u32[]{:S(2)}, u32[]{:S(2)}) collective-permute-start(bf16[256,1152]{1,0:T(8,128)(2,1)S(1)} %collective-permute-done.12.refs_2_), channel_id=1, source_target_pairs={{0,4},{4,0},{8,12},{12,8},{16,20},{20,16},{24,28},{28,24},{1,5},{5... | collective-permute-start | bytes 1769480 | tf_op jit(solution)/shard_map/ppermute | solution.py:248
  162.3 51.5 %collective-permute-start.18 = (bf16[4,256,1024]{2,1,0:T(8,128)(2,1)}, bf16[4,256,1024]{2,1,0:T(8,128)(2,1)}, u32[]{:S(2)}, u32[]{:S(2)}) collective-permute-start(bf16[4,256,1024]{2,1,0:T(8,128)(2,1)} %get-tuple-element.47), channel_id=1, source_target_pairs={{0,4},{4,0},{8,12},{12,8},{16,20},{20,16},{24,28},{28,24},{1,5},{5... | collective-permute-start | bytes 6291464 | tf_op jit(solution)/shard_map/ppermute | solution.py:248
  162.4 14.8 %collective-permute-start.25 = (bf16[256,1024]{1,0:T(8,128)(2,1)S(1)}, bf16[256,1024]{1,0:T(8,128)(2,1)S(1)}, u32[]{:S(2)}, u32[]{:S(2)}) collective-permute-start(bf16[256,1024]{1,0:T(8,128)(2,1)S(1)} %get-tuple-element.57.refs_4_), channel_id=1, source_target_pairs={{0,8},{4,12},{8,0},{12,4},{16,24},{20,28},{24,16},{28,20},{1,9},{5... | collective-permute-start | bytes 1572872 | tf_op jit(solution)/shard_map/ppermute | solution.py:248
  162.8 35.6 %collective-permute-start.26 = (bf16[256,1024]{1,0:T(8,128)(2,1)S(1)}, bf16[256,1024]{1,0:T(8,128)(2,1)S(1)}, u32[]{:S(2)}, u32[]{:S(2)}) collective-permute-start(bf16[256,1024]{1,0:T(8,128)(2,1)S(1)} %get-tuple-element.57.refs_4_), channel_id=1, source_target_pairs={{0,16},{4,20},{8,24},{12,28},{16,0},{20,4},{24,8},{28,12},{1,17},{... | collective-permute-start | bytes 1572872 | tf_op jit(solution)/shard_map/ppermute | solution.py:248
  166.3 34.6 %collective-permute-start.27 = (bf16[256,1024]{1,0:T(8,128)(2,1)S(1)}, bf16[256,1024]{1,0:T(8,128)(2,1)S(1)}, u32[]{:S(2)}, u32[]{:S(2)}) collective-permute-start(bf16[256,1024]{1,0:T(8,128)(2,1)S(1)} %get-tuple-element.57.refs_4_), channel_id=1, source_target_pairs={{0,24},{4,28},{8,16},{12,20},{16,8},{20,12},{24,0},{28,4},{1,25},{... | collective-permute-start | bytes 1572872 | tf_op jit(solution)/shard_map/ppermute | solution.py:248
  167.7 33.2 %collective-permute-start.24 = (bf16[256,1024]{1,0:T(8,128)(2,1)S(1)}, bf16[256,1024]{1,0:T(8,128)(2,1)S(1)}, u32[]{:S(2)}, u32[]{:S(2)}) collective-permute-start(bf16[256,1024]{1,0:T(8,128)(2,1)S(1)} %get-tuple-element.55), channel_id=1, source_target_pairs={{0,24},{4,28},{8,16},{12,20},{16,8},{20,12},{24,0},{28,4},{1,25},{... | collective-permute-start | bytes 1572872 | tf_op jit(solution)/shard_map/ppermute | solution.py:248
  177.2 34.1 %collective-permute-start.23 = (bf16[256,1024]{1,0:T(8,128)(2,1)S(1)}, bf16[256,1024]{1,0:T(8,128)(2,1)S(1)}, u32[]{:S(2)}, u32[]{:S(2)}) collective-permute-start(bf16[256,1024]{1,0:T(8,128)(2,1)S(1)} %get-tuple-element.54), channel_id=1, source_target_pairs={{0,16},{4,20},{8,24},{12,28},{16,0},{20,4},{24,8},{28,12},{1,17},{... | collective-permute-start | bytes 1572872 | tf_op jit(solution)/shard_map/ppermute | solution.py:248
  198.5 12.8 %collective-permute-start.22 = (bf16[256,1024]{1,0:T(8,128)(2,1)S(1)}, bf16[256,1024]{1,0:T(8,128)(2,1)S(1)}, u32[]{:S(2)}, u32[]{:S(2)}) collective-permute-start(bf16[256,1024]{1,0:T(8,128)(2,1)S(1)} %get-tuple-element.53), channel_id=1, source_target_pairs={{0,8},{4,12},{8,0},{12,4},{16,24},{20,28},{24,16},{28,20},{1,9},{5... | collective-permute-start | bytes 1572872 | tf_op jit(solution)/shard_map/ppermute | solution.py:248
  213.7 6.4 %collective-permute-start.28 = (bf16[512,1024]{1,0:T(8,128)(2,1)S(1)}, bf16[512,1024]{1,0:T(8,128)(2,1)S(1)}, u32[]{:S(2)}, u32[]{:S(2)}) collective-permute-start(bf16[512,1024]{1,0:T(8,128)(2,1)S(1)} %get-tuple-element.59), channel_id=1, source_target_pairs={{0,4},{4,0},{8,12},{12,8},{16,20},{20,16},{24,28},{28,24},{1,5},{5... | collective-permute-start | bytes 3145736 | tf_op jit(solution)/shard_map/ppermute | solution.py:248
  215.9 14.8 %collective-permute-start.19 = (bf16[256,1024]{1,0:T(8,128)(2,1)S(1)}, bf16[256,1024]{1,0:T(8,128)(2,1)S(1)}, u32[]{:S(2)}, u32[]{:S(2)}) collective-permute-start(bf16[256,1024]{1,0:T(8,128)(2,1)S(1)} %get-tuple-element.64), channel_id=1, source_target_pairs={{0,8},{4,12},{8,0},{12,4},{16,24},{20,28},{24,16},{28,20},{1,9},{5... | collective-permute-start | bytes 1572872 | tf_op jit(solution)/shard_map/ppermute | solution.py:248
  217.4 26.1 %collective-permute-start.20 = (bf16[256,1024]{1,0:T(8,128)(2,1)S(1)}, bf16[256,1024]{1,0:T(8,128)(2,1)S(1)}, u32[]{:S(2)}, u32[]{:S(2)}) collective-permute-start(bf16[256,1024]{1,0:T(8,128)(2,1)S(1)} %get-tuple-element.66), channel_id=1, source_target_pairs={{0,16},{4,20},{8,24},{12,28},{16,0},{20,4},{24,8},{28,12},{1,17},{... | collective-permute-start | bytes 1572872 | tf_op jit(solution)/shard_map/ppermute | solution.py:248
  220.1 23.5 %collective-permute-start.21 = (bf16[256,1024]{1,0:T(8,128)(2,1)S(1)}, bf16[256,1024]{1,0:T(8,128)(2,1)S(1)}, u32[]{:S(2)}, u32[]{:S(2)}) collective-permute-start(bf16[256,1024]{1,0:T(8,128)(2,1)S(1)} %get-tuple-element.65), channel_id=1, source_target_pairs={{0,24},{4,28},{8,16},{12,20},{16,8},{20,12},{24,0},{28,4},{1,25},{... | collective-permute-start | bytes 1572872 | tf_op jit(solution)/shard_map/ppermute | solution.py:248
  (22 other events, 175.4 us)
Sparse Core Ops, SparseCore 0:
  52.6 46.3 all-gather.4

commit v3 on v2

--- a/solution.py
+++ b/solution.py
@@ -26,6 +26,26 @@
     return items[0] if len(items) == 1 else jnp.concatenate(items, axis=axis)
 
 
+def dealt(refs, counts):
+    lists, at = [], 0
+    for count in counts:
+        lists.append(refs[at : at + count])
+        at += count
+    return lists, refs[at:]
+
+
+def whole(refs):
+    return joined([ref[...] for ref in refs], 0)
+
+
+def added(terms, cols):
+    total = None
+    for refs in terms:
+        term = joined([ref[:, cols].astype(F32) for ref in refs], 0)
+        total = term if total is None else total + term
+    return total
+
+
 def diagonal(pair):
     zero = jnp.zeros((pair.shape[0], HD), pair.dtype)
     top = jnp.concatenate([pair[:, :HD], zero], axis=1)
@@ -33,9 +53,14 @@
     return jnp.concatenate([top, low], axis=0)
 
 
-def gate_kernel(sel_ref, mark_ref, q_ref, aux_ref):
-    block_total, width = mark_ref.shape
+def gate_kernel(me_ref, sel_ref, mine_ref, other_ref, q_ref, aux_ref, mark_ref):
+    chips, block_count, width = mine_ref.shape
+    block_total = 2 * chips * block_count
     rows = q_ref.shape[0]
+    me = me_ref[0]
+    for j in range(chips):
+        mark_ref[me ^ (2 * j)] = mine_ref[j]
+        mark_ref[me ^ (2 * j + 1)] = other_ref[j]
     heads = width // HD
     scale = HD ** (-0.5)
     ids = lax.broadcasted_iota(jnp.int32, (block_total, rows), 0)
@@ -47,7 +72,8 @@
     gates = [[None] * heads for _ in range(TOPK)]
     for h in range(heads):
         cols = slice(h * HD, (h + 1) * HD)
-        logits = scale * mm(mark_ref[:, cols], q_ref[:, cols], NT) + bias
+        marks = mark_ref[:, :, cols].reshape(block_total, HD)
+        logits = scale * mm(marks, q_ref[:, cols], NT) + bias
         weight = jnp.exp(logits - jnp.max(logits, axis=0, keepdims=True))
         inverse = 1.0 / jnp.sum(weight, axis=0, keepdims=True)
         for t in range(TOPK):
@@ -66,14 +92,15 @@
     return 16.0 * aux[at : at + TOPK] + aux[at + TOPK : at + 2 * TOPK]
 
 
-def forward_kernel(chunks, span, cap, me_ref, aux_ref, k_ref, v_ref, *refs):
-    q_refs = refs[:chunks]
-    even_refs = refs[chunks : chunks + chunks // 2]
-    odd_ref, qg_ref, p_ref, gate_ref, hot_ref = refs[chunks + chunks // 2 : chunks + chunks // 2 + 5]
-    auxg_ref, out_ref = refs[chunks + chunks // 2 + 5 :]
+def forward_kernel(counts, span, cap, me_ref, mine_ref, other_ref, k_ref, v_ref, *refs):
+    chunks = len(counts)
+    q_refs, refs = dealt(refs, counts)
+    part_refs, refs = refs[:chunks], refs[chunks:]
+    qg_ref, p_ref, gate_ref, hot_ref, auxg_ref, out_ref = refs
+    aux_refs = [(other_ref if m % 2 else mine_ref).at[m // 2] for m in range(chunks)]
     block_count, _, width = k_ref.shape
     heads = width // HD
-    rows = q_refs[0].shape[0]
+    rows = part_refs[0].shape[0]
     group_rows = rows * span
     groups = chunks // span
     me = me_ref[0]
@@ -86,7 +113,7 @@
     own_ids = (base + lax.broadcasted_iota(jnp.int32, (block_count, group_rows), 0)).astype(F32)
     place = lax.broadcasted_iota(jnp.int32, (cap, group_rows), 0).astype(F32)
     for g in range(groups):
-        aux = joined([aux_ref[me ^ (g * span + i)] for i in range(span)], 1)
+        aux = joined([aux_refs[g * span + i][...] for i in range(span)], 1)
         picked = block_ids(aux.astype(F32), heads)
         own = picked[0:1, :] == own_ids
         for t in range(1, TOPK):
@@ -98,7 +125,7 @@
         ).astype(BF16)
         hot_ref[g] = hot
         auxg_ref[:, g * cap : (g + 1) * cap, :] = mm(hot, aux, NT).reshape(block_count, cap, HD)
-        q_group = joined([q_refs[g * span + i][...] for i in range(span)], 0)
+        q_group = joined([whole(q_refs[g * span + i]) for i in range(span)], 0)
         qg_ref[:, g * cap : (g + 1) * cap, :] = (
             mm(hot, q_group).astype(BF16).reshape(block_count, cap, width)
         )
@@ -140,13 +167,47 @@
         slots = out_ref[:, g * cap : (g + 1) * cap, :].reshape(block_count * cap, width)
         part = mm(hot_ref[g], slots, TN).astype(BF16)
         for i in range(span):
-            m = g * span + i
-            target = odd_ref.at[m // 2] if m % 2 else even_refs[m // 2]
-            target[...] = part[i * rows : (i + 1) * rows]
-
-
-def finish_kernel(*refs):
-    *term_refs, ga_ref, attn_ref, ext_ref = refs
+            part_refs[g * span + i][...] = part[i * rows : (i + 1) * rows]
+
+
+def grad_kernel(lines, chips, at_ref, w_ref, *refs):
+    own_ref, up_refs, down_refs = refs[0], refs[1:lines], refs[lines : 2 * lines - 1]
+    ga_ref, slab_refs = refs[2 * lines - 1], refs[2 * lines : 2 * lines + chips]
+    full_ref, w_buf, sems = refs[2 * lines + chips :]
+    width = own_ref.shape[1]
+    share = slab_refs[0].shape[1]
+    line, chip = at_ref[0], at_ref[1]
+    copies = [
+        pltpu.make_async_copy(w_ref.at[pl.ds(i * width, width)], w_buf.at[i], sems.at[i])
+        for i in range(lines)
+    ]
+    for copy in copies:
+        copy.start()
+    full_ref[line] = own_ref[...]
+    for d in range(1, lines):
+
+        @pl.when(line >= d)
+        def _():
+            full_ref[line - d] = up_refs[d - 1][...]
+
+        @pl.when(line + d < lines)
+        def _():
+            full_ref[line + d] = down_refs[d - 1][...]
+
+    for j in range(chips):
+        first = (chip ^ j) * share
+        cols = pl.ds(pl.multiple_of(first % width, HD), share)
+        slab_refs[j][...] = full_ref[first // width, :, cols]
+    total = None
+    for i in range(lines):
+        copies[i].wait()
+        term = mm(full_ref[i], w_buf[i])
+        total = term if total is None else total + term
+    ga_ref[...] = total.astype(BF16)
+
+
+def finish_kernel(counts, *refs):
+    terms, (ga_ref, attn_ref, ext_ref) = dealt(refs, counts)
     rows, width = ga_ref.shape
     heads = width // HD
     lane = lax.broadcasted_iota(jnp.int32, (rows, HD), 1)
@@ -155,9 +216,7 @@
     ext_ref[:, :width] = ga_ref[...]
     for h in range(heads):
         cols = slice(h * HD, (h + 1) * HD)
-        total = term_refs[0][:, cols].astype(F32)
-        for ref in term_refs[1:]:
-            total = total + ref[:, cols].astype(F32)
+        total = added(terms, cols)
         attn_ref[:, cols] = total.astype(BF16)
         dots = jnp.sum(total * ga_ref[:, cols].astype(F32), axis=1, keepdims=True)
         upper = dots.astype(BF16).astype(F32)
@@ -166,19 +225,26 @@
     ext_ref[:, width:] = (high + low).astype(BF16)
 
 
-def backward_kernel(chunks, span, cap, hot_ref, qg_ref, p_ref, gate_ref, k_ref, v_ref, *refs):
-    ga_refs = refs[:chunks]
-    even_refs = refs[chunks : chunks + chunks // 2]
-    odd_ref, dk_ref, dv_ref = refs[chunks + chunks // 2 : chunks + chunks // 2 + 3]
-    gag_ref, dq_ref = refs[chunks + chunks // 2 + 3 :]
+def total_kernel(counts, *refs):
+    terms, (out_ref,) = dealt(refs, counts)
+    for h in range(out_ref.shape[1] // HD):
+        cols = slice(h * HD, (h + 1) * HD)
+        out_ref[:, cols] = added(terms, cols)
+
+
+def backward_kernel(counts, span, cap, hot_ref, qg_ref, p_ref, gate_ref, k_ref, v_ref, *refs):
+    chunks = len(counts)
+    ga_refs, refs = dealt(refs, counts)
+    part_refs, refs = refs[:chunks], refs[chunks:]
+    dk_ref, dv_ref, gag_ref, dq_ref = refs
     block_count, _, width = k_ref.shape
     heads = width // HD
-    rows = ga_refs[0].shape[0]
+    rows = part_refs[0].shape[0]
     groups = chunks // span
     scale = HD ** (-0.5)
 
     for g in range(groups):
-        ga_group = joined([ga_refs[g * span + i][...] for i in range(span)], 0)
+        ga_group = joined([whole(ga_refs[g * span + i]) for i in range(span)], 0)
         gag_ref[:, g * cap : (g + 1) * cap, :] = (
             mm(hot_ref[g], ga_group).astype(BF16).reshape(block_count, cap, width + HD)
         )
@@ -223,21 +289,20 @@
         slots = dq_ref[:, g * cap : (g + 1) * cap, :].reshape(block_count * cap, width)
         part = mm(hot_ref[g], slots, TN).astype(BF16)
         for i in range(span):
-            m = g * span + i
-            target = odd_ref.at[m // 2] if m % 2 else even_refs[m // 2]
-            target[...] = part[i * rows : (i + 1) * rows]
-
-
-def weight_kernel(chips, me_ref, *refs):
-    slabs, attns = refs[:chips], refs[chips : 2 * chips]
-    own_ref, other_ref = refs[2 * chips :]
+            part_refs[g * span + i][...] = part[i * rows : (i + 1) * rows]
+
+
+def weight_kernel(counts, me_ref, *refs):
+    chips = len(counts)
+    slabs = refs[:chips]
+    attns, (own_ref, other_ref) = dealt(refs[chips:], counts)
     half = own_ref.shape[0]
     core = me_ref[0] % 2
-    attn = jnp.concatenate([ref[...] for ref in attns], axis=0)
+    attn = joined([whole(pieces) for pieces in attns], 0)
 
     def side(which):
         cols = pl.ds(pl.multiple_of(which * half, half), half)
-        return mm(jnp.concatenate([ref[:, cols] for ref in slabs], axis=0), attn, TN)
+        return mm(joined([ref[:, cols] for ref in slabs], 0), attn, TN)
 
     own_ref[...] = side(core)
     other_ref[...] = side(1 - core).astype(BF16)
@@ -252,20 +317,60 @@
     return lax.optimization_barrier((x, *others))[0]
 
 
-def chip_terms(evens, odd):
-    received = swap(odd, 1)
-    terms = [evens[0], received[0]]
-    for j in range(1, len(evens)):
-        both = evens[j].astype(F32) + received[j].astype(F32)
-        terms.append(swap(both.astype(BF16), 2 * j))
-    return terms
+def flat(lists):
+    return [x for pieces in lists for x in pieces]
+
+
+def spread_chips(x):
+    chips = lax.axis_size("ctx") // 2
+    if chips != 4:
+        return [[x]] + [[swap(x, 2 * j)] for j in range(1, chips)]
+    half = x.shape[0] // 2
+    top, low = x[:half], x[half:]
+    x_top, y_low = swap(top, 2), swap(low, 4)
+    x_low, y_top = swap(low, 2), swap(top, 4)
+    return [[x], [x_top, x_low], [y_top, y_low], [swap(x_top, 4), swap(y_low, 2)]]
+
+
+def collect_chips(parts):
+    chips = len(parts) // 2
+    received = [None] * chips
+    for j in reversed(range(chips)):
+        received[j] = swap(parts[2 * j + 1], 1)
+
+    def both(j, rows, extra=None):
+        total = parts[2 * j][rows].astype(F32) + received[j][rows].astype(F32)
+        if extra is not None:
+            total = total + extra.astype(F32)
+        return total.astype(BF16)
+
+    terms = [[parts[0]], [received[0]]]
+    if chips != 4:
+        return terms + [[swap(both(j, slice(None)), 2 * j)] for j in range(1, chips)]
+    half = parts[0].shape[0] // 2
+    top, low = slice(0, half), slice(half, None)
+    x_far, y_far = swap(both(3, top), 2), swap(both(3, low), 4)
+    x_top, y_low = swap(both(1, top), 2), swap(both(2, low), 4)
+    x_low, y_top = swap(both(1, low, y_far), 2), swap(both(2, top, x_far), 4)
+    return terms + [[x_top, x_low], [y_top, y_low]]
+
+
+def spread_line(x):
+    lines = lax.axis_size("head")
+    ups, downs = [x], [x]
+    for d in range(1, lines):
+        ups.append(lax.ppermute(ups[-1], "head", [(i, i + 1) for i in range(d - 1, lines - 1)]))
+        downs.append(lax.ppermute(downs[-1], "head", [(i, i - 1) for i in range(1, lines - d + 1)]))
+    return ups[1:], downs[1:]
 
 
 def body(queries, key_rows, value_rows, selected, out_grad, out_weight):
     chunks = lax.axis_size("ctx")
     chips = chunks // 2
+    lines = lax.axis_size("head")
     rows, width = queries.shape
     features = out_weight.shape[0]
+    share = features // chips
     heads = width // HD
     block_count = key_rows.shape[0] // BLOCK
     block_total = block_count * chunks
@@ -276,6 +381,7 @@
     slots = groups * cap
     index = lax.axis_index("ctx").astype(jnp.int32)
     me = index.reshape(1)
+    at = jnp.stack([lax.axis_index("head").astype(jnp.int32), index // 2])
     keys = key_rows.reshape(block_count, BLOCK, width)
     values = value_rows.reshape(block_count, BLOCK, width)
     vmem = pl.BlockSpec(memory_space=pltpu.VMEM)
@@ -285,102 +391,107 @@
     def shaped(shape, kind=BF16):
         return jax.ShapeDtypeStruct(shape, kind)
 
-    grad_full = lax.all_gather(out_grad, "head", axis=0)
-    query_chips = [queries] + [swap(queries, 2 * j) for j in range(1, chips)]
-    mark_all = lax.all_gather(keys[:, BLOCK - 1], "ctx", axis=0, tiled=True)
+    marks = keys[:, BLOCK - 1]
+    marks = jnp.stack([marks] + [swap(marks, 2 * j) for j in range(1, chips)])
+    ups, downs = spread_line(out_grad)
+    query_chips = spread_chips(queries)
     aux = pl.pallas_call(
         gate_kernel,
         out_shape=shaped((HD, rows)),
-        in_specs=[vmem] * 3,
+        in_specs=[smem] + [vmem] * 4,
         out_specs=vmem,
+        scratch_shapes=[pltpu.VMEM((chunks, block_count, width), BF16)],
         compiler_params=params,
         name="gates",
-    )(selected.T, mark_all, queries)
-    aux_all = lax.all_gather(aux, "ctx", axis=0)
+    )(me, selected.T, marks, swap(marks, 1), queries)
+    aux = jnp.stack([aux] + [swap(aux, 2 * j) for j in range(1, chips)])
     query_all = []
-    for piece in query_chips:
-        query_all += [piece, swap(after(piece, aux_all), 1)]
+    for pieces in query_chips:
+        query_all += [pieces, [swap(piece, 1) for piece in pieces]]
 
     outs = pl.pallas_call(
-        functools.partial(forward_kernel, chunks, span, cap),
-        out_shape=[shaped((rows, width))] * chips
+        functools.partial(forward_kernel, [len(pieces) for pieces in query_all], span, cap),
+        out_shape=[shaped((rows, width))] * chunks
         + [
-            shaped((chips, rows, width)),
             shaped((block_count, slots, width)),
             shaped((block_count, heads // 2, 2 * BLOCK, slots)),
             shaped((block_count, heads, slots), F32),
             shaped((groups, block_count * cap, rows * span)),
         ],
-        in_specs=[smem] + [vmem] * (3 + chunks),
-        out_specs=[vmem] * (chips + 5),
+        in_specs=[smem] + [vmem] * (4 + len(flat(query_all))),
+        out_specs=[vmem] * (chunks + 4),
         scratch_shapes=[
             pltpu.VMEM((block_count, slots, HD), F32),
             pltpu.VMEM((block_count, slots, width), BF16),
         ],
         compiler_params=params,
         name="forward",
-    )(me, aux_all, keys, values, *query_all)
-    q_slots, probs, gates, hot = outs[chips + 1 :]
-
-    grad_attn = jnp.einsum(
-        "zqf,zfd->qd",
-        grad_full,
-        out_weight.reshape(features // width, width, width),
-        preferred_element_type=F32,
-    ).astype(BF16)
-    terms = chip_terms(outs[:chips], outs[chips])
+    )(me, aux, swap(aux, 1), keys, values, *flat(query_all))
+    q_slots, probs, gates, hot = outs[chunks:]
+
+    grad_attn, *slabs = pl.pallas_call(
+        functools.partial(grad_kernel, lines, chips),
+        out_shape=[shaped((rows, width))] + [shaped((rows, share))] * chips,
+        in_specs=[smem, pl.BlockSpec(memory_space=pl.ANY)] + [vmem] * (2 * lines - 1),
+        out_specs=[vmem] * (1 + chips),
+        scratch_shapes=[
+            pltpu.VMEM((lines, rows, width), BF16),
+            pltpu.VMEM((lines, width, width), BF16),
+            pltpu.SemaphoreType.DMA((lines,)),
+        ],
+        compiler_params=params,
+        name="grad",
+    )(at, out_weight, out_grad, *ups, *downs)
+    terms = collect_chips(outs[:chunks])
     attn_out, extended = pl.pallas_call(
-        finish_kernel,
+        functools.partial(finish_kernel, [len(pieces) for pieces in terms]),
         out_shape=[shaped((rows, width)), shaped((rows, width + HD))],
-        in_specs=[vmem] * (len(terms) + 1),
+        in_specs=[vmem] * (len(flat(terms)) + 1),
         out_specs=[vmem] * 2,
         compiler_params=params,
         name="finish",
-    )(*terms, grad_attn)
-    grad_chips = [extended] + [swap(extended, 2 * j) for j in range(1, chips)]
+    )(*flat(terms), grad_attn)
+    grad_chips = spread_chips(extended)
     grad_all = []
-    for piece in grad_chips:
-        grad_all += [piece, swap(piece, 1)]
-
-    share = features // chips
-    slabs, attns = [], [attn_out]
-    for j in range(chips):
-        first = ((index // 2) ^ j) * share
-        slab = lax.dynamic_slice(
-            grad_full, (first // width, 0, first % width), (1, rows, share)
-        ).reshape(rows, share)
-        slabs.append(swap(after(slab, *grad_chips), 2 * j) if j else slab)
-    for j in range(1, chips):
-        attns.append(swap(after(attn_out, *grad_chips), 2 * j))
+    for pieces in grad_chips:
+        grad_all += [pieces, [swap(piece, 1) for piece in pieces]]
+
+    arrived = flat(grad_chips)
+    attns = spread_chips(after(attn_out, *arrived))
+    slabs = [slabs[0]] + [swap(after(slabs[j], *arrived), 2 * j) for j in range(1, chips)]
 
     outs = pl.pallas_call(
-        functools.partial(backward_kernel, chunks, span, cap),
-        out_shape=[shaped((rows, width))] * chips
-        + [shaped((chips, rows, width))]
+        functools.partial(backward_kernel, [len(pieces) for pieces in grad_all], span, cap),
+        out_shape=[shaped((rows, width))] * chunks
         + [shaped((block_count, BLOCK, width), F32)] * 2,
-        in_specs=[vmem] * (6 + chunks),
-        out_specs=[vmem] * (chips + 3),
+        in_specs=[vmem] * (6 + len(flat(grad_all))),
+        out_specs=[vmem] * (chunks + 2),
         scratch_shapes=[
             pltpu.VMEM((block_count, slots, width + HD), BF16),
             pltpu.VMEM((block_count, slots, width), BF16),
         ],
         compiler_params=params,
         name="backward",
-    )(hot, q_slots, probs, gates, keys, values, *grad_all)
-    key_grad, value_grad = outs[chips + 1 :]
-    terms = chip_terms(outs[:chips], outs[chips])
-    query_grad = terms[0].astype(F32)
-    for term in terms[1:]:
-        query_grad = query_grad + term.astype(F32)
+    )(hot, q_slots, probs, gates, keys, values, *flat(grad_all))
+    key_grad, value_grad = outs[chunks:]
+    terms = collect_chips(outs[:chunks])
+    query_grad = pl.pallas_call(
+        functools.partial(total_kernel, [len(pieces) for pieces in terms]),
+        out_shape=shaped((rows, width), F32),
+        in_specs=[vmem] * len(flat(terms)),
+        out_specs=vmem,
+        compiler_params=params,
+        name="total",
+    )(*flat(terms))
 
     weight_own, weight_other = pl.pallas_call(
-        functools.partial(weight_kernel, chips),
+        functools.partial(weight_kernel, [len(pieces) for pieces in attns]),
         out_shape=[shaped((share // 2, width), F32), shaped((share // 2, width))],
-        in_specs=[smem] + [vmem] * (2 * chips),
+        in_specs=[smem] + [vmem] * (chips + len(flat(attns))),
         out_specs=[vmem] * 2,
         compiler_params=params,
         name="weight",
-    )(me, *slabs, *attns)
+    )(me, *slabs, *flat(attns))
     weight_grad = weight_own + swap(weight_other, 1).astype(F32)
     return (
         query_grad,

time: 253 us -> 210 us (0.83)
  blocking collectives: 35.9 us -> 0 us
  starting transfers between devices: 27.1 us -> 53.2 us
  waiting for transfers between devices: 112 us -> 95.2 us
  between operations: 14.2 us -> 1.08 us
  matrix products: 6.4 us -> 0 us
  local copies, waits for them, and re-layouts: 8.03 us -> 12 us
  other arithmetic: 7.68 us -> 4.64 us
    all_gather x2 -> x0, blocking collectives: 35.9 us -> none  [the longest x1 27.2 us: body(): mark_all = lax.all_gather(keys[:, BLOCK - 1], 'ctx', axis=0, tiled=True)]
    all_gather x1 -> x0, waiting for transfers between devices: 17.4 us -> none  [body(): grad_full = lax.all_gather(out_grad, 'head', axis=0)]
    ppermute x29 -> x64, starting transfers between devices: 27.1 us -> 44.4 us  [swap(): return lax.ppermute(x, 'ctx', [(i, i ^ bits) for i in range(count)])]
    ppermute x0 -> x6, waiting for transfers between devices: none -> 16.9 us  [the longest x3 16.9 us: spread_line(): lax.ppermute(downs[-1], 'head', [(i, i - 1) for i in range(1, lines - d +...]
    ppermute x29 -> x64, waiting for transfers between devices: 95 us -> 78.3 us  [swap(): return lax.ppermute(x, 'ctx', [(i, i ^ bits) for i in range(count)])]
    ppermute x0 -> x6, starting transfers between devices: none -> 8.75 us  [the longest x3 4.89 us: spread_line(): lax.ppermute(ups[-1], 'head', [(i, i + 1) for i in range(d - 1, lines - 1)])]
    dot_general x1 -> x0, matrix products: 6.4 us -> none  [body(): jnp.einsum('zqf,zfd->qd', grad_full, out_weight.reshape(features // width...]
    unnamed x32 -> x43, local copies, waits for them, and re-layouts: 5.23 us -> 10.7 us
  transfers between devices with their start and end apart: 30 -> 70, of which waited for: 15 -> 29; matrix products, arithmetic and copies ran while one was open for 6% -> 1% of each run, Pallas kernels for 8% -> 19%
where the time goes in v3:
time: 210 us; the launch traced here: 209 us
  waiting for transfers between devices  95.2 us (45%)
  starting transfers between devices  53.2 us (25%)
  Pallas kernels  42.7 us (20%)
  local copies, waits for them, and re-layouts  12 us (6%)
  other arithmetic  4.64 us (2%)
    ppermute x64, waiting for transfers between devices, swap(): return lax.ppermute(x, 'ctx', [(i, i ^ bits) for i in range(count)])  78.3 us
    ppermute x64, starting transfers between devices, swap(): return lax.ppermute(x, 'ctx', [(i, i ^ bits) for i in range(count)])  44.4 us
    ppermute x3, waiting for transfers between devices, spread_line(): lax.ppermute(downs[-1], 'head', [(i, i - 1) for i in range(1, lines - d +...  16.9 us
    pallas_call x1, Pallas kernels, body(): pl.pallas_call(functools.partial(backward_kernel, [len(pieces) for pieces...  16.5 us
    pallas_call x1, Pallas kernels, body(): pl.pallas_call(functools.partial(forward_kernel, [len(pieces) for pieces...  14.1 us
    unnamed x43, local copies, waits for them, and re-layouts  10.7 us
    pallas_call x1, Pallas kernels, body(): pl.pallas_call(functools.partial(grad_kernel, lines, chips), out_shape=[s...  5.23 us
    ppermute x3, starting transfers between devices, spread_line(): lax.ppermute(ups[-1], 'head', [(i, i + 1) for i in range(d - 1, lines - 1)])  4.89 us
  transfers between devices with their start and end apart: 70, of which 29 were waited for; matrix products, arithmetic and copies ran while one was open for 1% of the time, Pallas kernels for 19%

profile of v3, /device:TPU:0, one launch (start us, length us, event | category | flops | bytes accessed | tf_op | source)
XLA Modules:
  0.0 208.9 jit_solution(8202959891469621688)
XLA Ops:
  1.8 3.0 %collective-permute-start = (bf16[16,1024]{1,0:T(8,128)(2,1)S(1)}, bf16[16,1024]{1,0:T(8,128)(2,1)S(1)}, u32[]{:S(2)}, u32[]{:S(2)}) collective-permute-start(bf16[16,1024]{1,0:T(8,128)(2,1)S(1)} %bitcast.27), channel_id=1, source_target_pairs={{0,8},{4,12},{8,0},{12,4},{16,24},{20,28},{24,16},{28,20},{1,9},{5... | collective-permute-start | bytes 98312 | tf_op jit(solution)/shard_map/ppermute | solution.py:313
  6.7 2.0 collective-permute-done.1
  8.8 2.4 %collective-permute-done.2 = bf16[16,1024]{1,0:T(8,128)(2,1)S(1)} collective-permute-done((bf16[16,1024]{1,0:T(8,128)(2,1)S(1)}, bf16[16,1024]{1,0:T(8,128)(2,1)S(1)}, u32[]{:S(2)}, u32[]{:S(2)}) %collective-permute-start.2) | collective-permute-done | bytes 32800 | tf_op jit(solution)/shard_map/ppermute | solution.py:313
  16.0 2.9 %collective-permute-start.6 = (bf16[128,256]{1,0:T(8,128)(2,1)S(1)}, bf16[128,256]{1,0:T(8,128)(2,1)S(1)}, u32[]{:S(2)}, u32[]{:S(2)}) collective-permute-start(bf16[128,256]{1,0:T(8,128)(2,1)S(1)} %gates.1), channel_id=1, source_target_pairs={{0,24},{4,28},{8,16},{12,20},{16,8},{20,12},{24,0},{28,4},{1,25},{... | collective-permute-start | bytes 196616 | tf_op jit(solution)/shard_map/ppermute | solution.py:313
  23.2 9.7 %collective-permute-done.9.refs_2_ = bf16[128,1024]{1,0:T(8,128)(2,1)S(1)} collective-permute-done((bf16[128,1024]{1,0:T(8,128)(2,1)S(1)}, bf16[128,1024]{1,0:T(8,128)(2,1)S(1)}, u32[]{:S(2)}, u32[]{:S(2)}) %collective-permute-start.9) | collective-permute-done | bytes 262176 | tf_op jit(solution)/shard_map/ppermute | solution.py:313
  35.5 4.3 %collective-permute-done.17.refs_10_ = bf16[128,1024]{1,0:T(8,128)(2,1)S(1)} collective-permute-done((bf16[128,1024]{1,0:T(8,128)(2,1)S(1)}, bf16[128,1024]{1,0:T(8,128)(2,1)S(1)}, u32[]{:S(2)}, u32[]{:S(2)}) %collective-permute-start.17) | collective-permute-done | bytes 262176 | tf_op jit(solution)/shard_map/ppermute | solution.py:313
  41.3 3.5 %collective-permute-start.31 = (bf16[256,1024]{1,0:T(8,128)(2,1)}, bf16[256,1024]{1,0:T(8,128)(2,1)S(1)}, u32[]{:S(2)}, u32[]{:S(2)}) collective-permute-start(bf16[256,1024]{1,0:T(8,128)(2,1)} %refs_0_.3), channel_id=1, source_target_pairs={{0,1},{1,2},{2,3},{4,5},{5,6},{6,7},{8,9},{9,10},{10,11},{12,13},{... | collective-permute-start | bytes 1572872 | tf_op jit(solution)/shard_map/ppermute | solution.py:362
  46.2 14.1 %forward.1 = (bf16[256,1024]{1,0:T(8,128)(2,1)S(1)}, bf16[256,1024]{1,0:T(8,128)(2,1)}, bf16[256,1024]{1,0:T(8,128)(2,1)S(1)}, bf16[256,1024]{1,0:T(8,128)(2,1)S...) custom-call(s32[1]{0:T(128)} %bitcast.me_ref, ...), custom_call_target="tpu_custom_call" | custom-call | tf_op jit(solution)/shard_map/forward/pallas_call | solution.py:412
  64.8 15.9 %collective-permute-done.35.refs_5_ = bf16[256,1024]{1,0:T(8,128)(2,1)S(1)} collective-permute-done((bf16[256,1024]{1,0:T(8,128)(2,1)S(1)}, bf16[256,1024]{1,0:T(8,128)(2,1)S(1)}, u32[]{:S(2)}, u32[]{:S(2)}) %collective-permute-start.35) | collective-permute-done | bytes 524320 | tf_op jit(solution)/shard_map/ppermute | solution.py:363
  85.1 6.2 %collective-permute-done.25 = bf16[128,1024]{1,0:T(8,128)(2,1)S(1)} collective-permute-done((bf16[128,1024]{1,0:T(8,128)(2,1)S(1)}, bf16[128,1024]{1,0:T(8,128)(2,1)S(1)}, u32[]{:S(2)}, u32[]{:S(2)}) %collective-permute-start.25) | collective-permute-done | bytes 262176 | tf_op jit(solution)/shard_map/ppermute | solution.py:313
  105.2 5.2 %grad.1 = (bf16[256,1024]{1,0:T(8,128)(2,1)S(1)}, bf16[256,1024]{1,0:T(8,128)(2,1)S(1)}, bf16[256,1024]{1,0:T(8,128)(2,1)S(1)}, bf16[256,1024]{1,0:T(8,128)(2,1)S(1)}, bf16[256,1024]{1,0:T(8,128)(2,1)S(1)}) custom-call(s32[2]{0:T(128)S(1)} %pad_add_fusion.at_ref, bf16[4096,1024]{1,0:T(8,128)(2,1)} %w_ref.1, bf16[256,1024]{1,0:T(8,128)(2,1)S(1)} %copy-done.5, ...), custom_call_target="tpu_custom_call" | custom-call | tf_op jit(solution)/shard_map/grad/pallas_call | solution.py:432
  110.5 2.1 %finish.1 = (bf16[256,1024]{1,0:T(8,128)(2,1)S(1)}, bf16[256,1152]{1,0:T(8,128)(2,1)S(1)}) custom-call(bf16[256,1024]{1,0:T(8,128)(2,1)S(1)} %copy-done.7, bf16[256,1024]{1,0:T(8,128)(2,1)} %collective-permute-done.21.refs_1_, bf16[128,1024]{1,0:T(8,128)(2,1)} %collective-permute-done.23.refs_2_, bf16[128,1024]{1,0:T(8,128)(2,1)} %collective-permute-done.26.refs_3_, ...), custom_call_target="tpu_custom_call" | custom-call | tf_op jit(solution)/shard_map/finish/pallas_call | solution.py:446
  116.8 5.9 %collective-permute-done.38.refs_2_ = bf16[128,1152]{1,0:T(8,128)(2,1)S(1)} collective-permute-done((bf16[128,1152]{1,0:T(8,128)(2,1)S(1)}, bf16[128,1152]{1,0:T(8,128)(2,1)S(1)}, u32[]{:S(2)}, u32[]{:S(2)}) %collective-permute-start.38) | collective-permute-done | bytes 294944 | tf_op jit(solution)/shard_map/ppermute | solution.py:313
  124.7 4.3 %collective-permute-done.39.refs_3_ = bf16[128,1152]{1,0:T(8,128)(2,1)S(1)} collective-permute-done((bf16[128,1152]{1,0:T(8,128)(2,1)S(1)}, bf16[128,1152]{1,0:T(8,128)(2,1)S(1)}, u32[]{:S(2)}, u32[]{:S(2)}) %collective-permute-start.39) | collective-permute-done | bytes 294944 | tf_op jit(solution)/shard_map/ppermute | solution.py:313
  130.2 3.5 %collective-permute-done.46.refs_10_ = bf16[128,1152]{1,0:T(8,128)(2,1)S(1)} collective-permute-done((bf16[128,1152]{1,0:T(8,128)(2,1)S(1)}, bf16[128,1152]{1,0:T(8,128)(2,1)S(1)}, u32[]{:S(2)}, u32[]{:S(2)}) %collective-permute-start.46) | collective-permute-done | bytes 294944 | tf_op jit(solution)/shard_map/ppermute | solution.py:313
  137.8 5.7 %collective-permute-done.63.refs_5_ = bf16[128,1024]{1,0:T(8,128)(2,1)S(1)} collective-permute-done((bf16[128,1024]{1,0:T(8,128)(2,1)S(1)}, bf16[128,1024]{1,0:T(8,128)(2,1)S(1)}, u32[]{:S(2)}, u32[]{:S(2)}) %collective-permute-start.63) | collective-permute-done | bytes 262176 | tf_op jit(solution)/shard_map/ppermute | solution.py:313
  145.6 2.6 %collective-permute-done.64.refs_6_ = bf16[128,1024]{1,0:T(8,128)(2,1)S(1)} collective-permute-done((bf16[128,1024]{1,0:T(8,128)(2,1)S(1)}, bf16[128,1024]{1,0:T(8,128)(2,1)S(1)}, u32[]{:S(2)}, u32[]{:S(2)}) %collective-permute-start.64) | collective-permute-done | bytes 262176 | tf_op jit(solution)/shard_map/ppermute | solution.py:313
  151.7 16.5 %backward.1 = (bf16[256,1024]{1,0:T(8,128)(2,1)S(1)}, bf16[256,1024]{1,0:T(8,128)(2,1)S(1)}, bf16[256,1024]{1,0:T(8,128)(2,1)S(1)}, bf16[256,1024]{1,0:T(8,128)(...) custom-call(bf16[8,256,256]{2,1,0:T(8,128)(2,1)S(1)} %get-tuple-elem, ...), custom_call_target="tpu_custom_call" | custom-call | tf_op jit(solution)/shard_map/backward/pallas_call | solution.py:463
  170.4 7.8 %collective-permute-done.68.refs_10_ = bf16[128,1024]{1,0:T(8,128)(2,1)S(1)} collective-permute-done((bf16[128,1024]{1,0:T(8,128)(2,1)S(1)}, bf16[128,1024]{1,0:T(8,128)(2,1)S(1)}, u32[]{:S(2)}, u32[]{:S(2)}) %collective-permute-start.68) | collective-permute-done | bytes 262176 | tf_op jit(solution)/shard_map/ppermute | solution.py:313
  178.8 2.4 %weight.1 = (f32[512,1024]{1,0:T(8,128)S(1)}, bf16[512,1024]{1,0:T(8,128)(2,1)S(1)}) custom-call(s32[1]{0:T(128)} %bitcast.me_ref, bf16[256,1024]{1,0:T(8,128)(2,1)S(1)} %get-tuple-element.63.refs_0_, bf16[256,1024]{1,0:T(8,128)(2,1)S(1)} %collective-permute-done.60.refs_1_, bf16[256,1024]{1,0:T(8,128)(2,1)S(1)} %collective-permute-done.61.refs_2_, ...), custom_call_target="tpu_custom_call" | custom-call | tf_op jit(solution)/shard_map/weight/pallas_call | solution.py:487
  183.8 6.4 %collective-permute-done.57 = bf16[128,1024]{1,0:T(8,128)(2,1)S(1)} collective-permute-done((bf16[128,1024]{1,0:T(8,128)(2,1)S(1)}, bf16[128,1024]{1,0:T(8,128)(2,1)S(1)}, u32[]{:S(2)}, u32[]{:S(2)}) %collective-permute-start.57) | collective-permute-done | bytes 262176 | tf_op jit(solution)/shard_map/ppermute | solution.py:313
  194.9 4.8 %collective-permute-done.58.refs_4_ = bf16[128,1024]{1,0:T(8,128)(2,1)S(1)} collective-permute-done((bf16[128,1024]{1,0:T(8,128)(2,1)S(1)}, bf16[128,1024]{1,0:T(8,128)(2,1)S(1)}, u32[]{:S(2)}, u32[]{:S(2)}) %collective-permute-start.58) | collective-permute-done | bytes 262176 | tf_op jit(solution)/shard_map/ppermute | solution.py:313
  199.8 4.3 %collective-permute-done.59.refs_5_ = bf16[128,1024]{1,0:T(8,128)(2,1)S(1)} collective-permute-done((bf16[128,1024]{1,0:T(8,128)(2,1)S(1)}, bf16[128,1024]{1,0:T(8,128)(2,1)S(1)}, u32[]{:S(2)}, u32[]{:S(2)}) %collective-permute-start.59) | collective-permute-done | bytes 262176 | tf_op jit(solution)/shard_map/ppermute | solution.py:313
  204.1 1.8 collective-permute-done.55.refs_3_
  (180 shorter events, 70.2 us)
Async XLA Ops:
  18.9 15.0 %collective-permute-start.14 = (bf16[128,1024]{1,0:T(8,128)(2,1)S(1)}, bf16[128,1024]{1,0:T(8,128)(2,1)S(1)}, u32[]{:S(2)}, u32[]{:S(2)}) collective-permute-start(bf16[128,1024]{1,0:T(8,128)(2,1)S(1)} %get-tuple-element.90), channel_id=1, source_target_pairs={{0,16},{4,20},{8,24},{12,28},{16,0},{20,4},{24,8},{28,12},{1,17},{... | collective-permute-start | bytes 786440 | tf_op jit(solution)/shard_map/ppermute | solution.py:313
  19.5 15.4 %collective-permute-start.10 = (bf16[128,1024]{1,0:T(8,128)(2,1)S(1)}, bf16[128,1024]{1,0:T(8,128)(2,1)S(1)}, u32[]{:S(2)}, u32[]{:S(2)}) collective-permute-start(bf16[128,1024]{1,0:T(8,128)(2,1)S(1)} %get-tuple-element.90), channel_id=1, source_target_pairs={{0,8},{4,12},{8,0},{12,4},{16,24},{20,28},{24,16},{28,20},{1,9},{5... | collective-permute-start | bytes 786440 | tf_op jit(solution)/shard_map/ppermute | solution.py:313
  41.3 19.0 %collective-permute-start.31 = (bf16[256,1024]{1,0:T(8,128)(2,1)}, bf16[256,1024]{1,0:T(8,128)(2,1)S(1)}, u32[]{:S(2)}, u32[]{:S(2)}) collective-permute-start(bf16[256,1024]{1,0:T(8,128)(2,1)} %refs_0_.3), channel_id=1, source_target_pairs={{0,1},{1,2},{2,3},{4,5},{5,6},{6,7},{8,9},{9,10},{10,11},{12,13},{... | collective-permute-start | bytes 1572872 | tf_op jit(solution)/shard_map/ppermute | solution.py:362
  44.8 16.2 %collective-permute-start.34 = (bf16[256,1024]{1,0:T(8,128)(2,1)}, bf16[256,1024]{1,0:T(8,128)(2,1)S(1)}, u32[]{:S(2)}, u32[]{:S(2)}) collective-permute-start(bf16[256,1024]{1,0:T(8,128)(2,1)} %refs_0_.3), channel_id=1, source_target_pairs={{1,0},{2,1},{3,2},{5,4},{6,5},{7,6},{9,8},{10,9},{11,10},{13,12},{... | collective-permute-start | bytes 1572872 | tf_op jit(solution)/shard_map/ppermute | solution.py:363
  61.1 19.6 %collective-permute-start.35 = (bf16[256,1024]{1,0:T(8,128)(2,1)S(1)}, bf16[256,1024]{1,0:T(8,128)(2,1)S(1)}, u32[]{:S(2)}, u32[]{:S(2)}) collective-permute-start(bf16[256,1024]{1,0:T(8,128)(2,1)S(1)} %collective-permute-done.34.refs_4_), channel_id=1, source_target_pairs={{1,0},{2,1},{5,4},{6,5},{9,8},{10,9},{13,12},{14,13},{17,16},{18,1... | collective-permute-start | bytes 1572872 | tf_op jit(solution)/shard_map/ppermute | solution.py:363
  62.4 19.6 %collective-permute-start.27 = (bf16[256,1024]{1,0:T(8,128)(2,1)S(1)}, bf16[256,1024]{1,0:T(8,128)(2,1)S(1)}, u32[]{:S(2)}, u32[]{:S(2)}) collective-permute-start(bf16[256,1024]{1,0:T(8,128)(2,1)S(1)} %get-tuple-element.50), channel_id=1, source_target_pairs={{0,4},{4,0},{8,12},{12,8},{16,20},{20,16},{24,28},{28,24},{1,5},{5... | collective-permute-start | bytes 1572872 | tf_op jit(solution)/shard_map/ppermute | solution.py:313
  62.9 21.0 %collective-permute-start.22 = (bf16[256,1024]{1,0:T(8,128)(2,1)S(1)}, bf16[256,1024]{1,0:T(8,128)(2,1)S(1)}, u32[]{:S(2)}, u32[]{:S(2)}) collective-permute-start(bf16[256,1024]{1,0:T(8,128)(2,1)S(1)} %get-tuple-element.46), channel_id=1, source_target_pairs={{0,4},{4,0},{8,12},{12,8},{16,20},{20,16},{24,28},{28,24},{1,5},{5... | collective-permute-start | bytes 1572872 | tf_op jit(solution)/shard_map/ppermute | solution.py:313
  63.2 19.7 %collective-permute-start.28 = (bf16[128,1024]{1,0:T(8,128)(2,1)S(1)}, bf16[128,1024]{1,0:T(8,128)(2,1)S(1)}, u32[]{:S(2)}, u32[]{:S(2)}) collective-permute-start(bf16[128,1024]{1,0:T(8,128)(2,1)S(1)} %get-tuple-element.82), channel_id=1, source_target_pairs={{0,8},{4,12},{8,0},{12,4},{16,24},{20,28},{24,16},{28,20},{1,9},{5... | collective-permute-start | bytes 786440 | tf_op jit(solution)/shard_map/ppermute | solution.py:313
  64.1 29.0 %collective-permute-start.33 = (bf16[256,1024]{1,0:T(8,128)(2,1)S(1)}, bf16[256,1024]{1,0:T(8,128)(2,1)S(1)}, u32[]{:S(2)}, u32[]{:S(2)}) collective-permute-start(bf16[256,1024]{1,0:T(8,128)(2,1)S(1)} %collective-permute-done.32.refs_2_), channel_id=1, source_target_pairs={{2,3},{6,7},{10,11},{14,15},{18,19},{22,23},{26,27},{30,31}} | collective-permute-start | bytes 1572872 | tf_op jit(solution)/shard_map/ppermute | solution.py:362
  80.7 15.4 %collective-permute-start.36 = (bf16[256,1024]{1,0:T(8,128)(2,1)S(1)}, bf16[256,1024]{1,0:T(8,128)(2,1)S(1)}, u32[]{:S(2)}, u32[]{:S(2)}) collective-permute-start(bf16[256,1024]{1,0:T(8,128)(2,1)S(1)} %collective-permute-done.35.refs_5_), channel_id=1, source_target_pairs={{1,0},{5,4},{9,8},{13,12},{17,16},{21,20},{25,24},{29,28}} | collective-permute-start | bytes 1572872 | tf_op jit(solution)/shard_map/ppermute | solution.py:363
  82.9 27.5 %collective-permute-start.21 = (bf16[256,1024]{1,0:T(8,128)(2,1)}, bf16[256,1024]{1,0:T(8,128)(2,1)}, u32[]{:S(2)}, u32[]{:S(2)}) collective-permute-start(bf16[256,1024]{1,0:T(8,128)(2,1)} %get-tuple-element.44), channel_id=1, source_target_pairs={{0,4},{4,0},{8,12},{12,8},{16,20},{20,16},{24,28},{28,24},{1,5},{5... | collective-permute-start | bytes 1572872 | tf_op jit(solution)/shard_map/ppermute | solution.py:313
  83.9 26.5 %collective-permute-start.29 = (bf16[128,1024]{1,0:T(8,128)(2,1)}, bf16[128,1024]{1,0:T(8,128)(2,1)S(1)}, u32[]{:S(2)}, u32[]{:S(2)}) collective-permute-start(bf16[128,1024]{1,0:T(8,128)(2,1)} %get-tuple-element.81), channel_id=1, source_target_pairs={{0,16},{4,20},{8,24},{12,28},{16,0},{20,4},{24,8},{28,12},{1,17},{... | collective-permute-start | bytes 786440 | tf_op jit(solution)/shard_map/ppermute | solution.py:313
  91.3 19.1 %collective-permute-start.30 = (bf16[128,1024]{1,0:T(8,128)(2,1)}, bf16[128,1024]{1,0:T(8,128)(2,1)}, u32[]{:S(2)}, u32[]{:S(2)}) collective-permute-start(bf16[128,1024]{1,0:T(8,128)(2,1)} %get-tuple-element.80), channel_id=1, source_target_pairs={{0,16},{4,20},{8,24},{12,28},{16,0},{20,4},{24,8},{28,12},{1,17},{... | collective-permute-start | bytes 786440 | tf_op jit(solution)/shard_map/ppermute | solution.py:313
  94.0 16.4 %collective-permute-start.23 = (bf16[128,1024]{1,0:T(8,128)(2,1)}, bf16[128,1024]{1,0:T(8,128)(2,1)}, u32[]{:S(2)}, u32[]{:S(2)}) collective-permute-start(bf16[128,1024]{1,0:T(8,128)(2,1)} %get-tuple-element.85), channel_id=1, source_target_pairs={{0,8},{4,12},{8,0},{12,4},{16,24},{20,28},{24,16},{28,20},{1,9},{5... | collective-permute-start | bytes 786440 | tf_op jit(solution)/shard_map/ppermute | solution.py:313
  114.7 14.3 %collective-permute-start.39 = (bf16[128,1152]{1,0:T(8,128)(2,1)S(1)}, bf16[128,1152]{1,0:T(8,128)(2,1)S(1)}, u32[]{:S(2)}, u32[]{:S(2)}) collective-permute-start(bf16[128,1152]{1,0:T(8,128)(2,1)S(1)} %get-tuple-element.86), channel_id=1, source_target_pairs={{0,8},{4,12},{8,0},{12,4},{16,24},{20,28},{24,16},{28,20},{1,9},{5... | collective-permute-start | bytes 884744 | tf_op jit(solution)/shard_map/ppermute | solution.py:313
  115.8 14.4 %collective-permute-start.42 = (bf16[128,1152]{1,0:T(8,128)(2,1)S(1)}, bf16[128,1152]{1,0:T(8,128)(2,1)S(1)}, u32[]{:S(2)}, u32[]{:S(2)}) collective-permute-start(bf16[128,1152]{1,0:T(8,128)(2,1)S(1)} %get-tuple-element.87), channel_id=1, source_target_pairs={{0,16},{4,20},{8,24},{12,28},{16,0},{20,4},{24,8},{28,12},{1,17},{... | collective-permute-start | bytes 884744 | tf_op jit(solution)/shard_map/ppermute | solution.py:313
  135.3 14.2 %collective-permute-start.48 = (bf16[128,1152]{1,0:T(8,128)(2,1)S(1)}, bf16[128,1152]{1,0:T(8,128)(2,1)S(1)}, u32[]{:S(2)}, u32[]{:S(2)}) collective-permute-start(bf16[128,1152]{1,0:T(8,128)(2,1)S(1)} %collective-permute-done.46.refs_10_), channel_id=1, source_target_pairs={{0,4},{4,0},{8,12},{12,8},{16,20},{20,16},{24,28},{28,24},{1,5},{5... | collective-permute-start | bytes 884744 | tf_op jit(solution)/shard_map/ppermute | solution.py:313
  135.7 14.8 %collective-permute-start.49 = (bf16[128,1152]{1,0:T(8,128)(2,1)S(1)}, bf16[128,1152]{1,0:T(8,128)(2,1)S(1)}, u32[]{:S(2)}, u32[]{:S(2)}) collective-permute-start(bf16[128,1152]{1,0:T(8,128)(2,1)S(1)} %collective-permute-done.47.refs_11_), channel_id=1, source_target_pairs={{0,4},{4,0},{8,12},{12,8},{16,20},{20,16},{24,28},{28,24},{1,5},{5... | collective-permute-start | bytes 884744 | tf_op jit(solution)/shard_map/ppermute | solution.py:313
  143.5 24.7 %collective-permute-start.65 = (bf16[128,1024]{1,0:T(8,128)(2,1)S(1)}, bf16[128,1024]{1,0:T(8,128)(2,1)S(1)}, u32[]{:S(2)}, u32[]{:S(2)}) collective-permute-start(bf16[128,1024]{1,0:T(8,128)(2,1)S(1)} %get-tuple-element.89), channel_id=1, source_target_pairs={{0,16},{4,20},{8,24},{12,28},{16,0},{20,4},{24,8},{28,12},{1,17},{... | collective-permute-start | bytes 786440 | tf_op jit(solution)/shard_map/ppermute | solution.py:313
  144.5 25.1 %collective-permute-start.67 = (bf16[128,1024]{1,0:T(8,128)(2,1)S(1)}, bf16[128,1024]{1,0:T(8,128)(2,1)S(1)}, u32[]{:S(2)}, u32[]{:S(2)}) collective-permute-start(bf16[128,1024]{1,0:T(8,128)(2,1)S(1)} %collective-permute-done.63.refs_5_), channel_id=1, source_target_pairs={{0,16},{4,20},{8,24},{12,28},{16,0},{20,4},{24,8},{28,12},{1,17},{... | collective-permute-start | bytes 786440 | tf_op jit(solution)/shard_map/ppermute | solution.py:313
  148.2 30.1 %collective-permute-start.62 = (bf16[256,1024]{1,0:T(8,128)(2,1)S(1)}, bf16[256,1024]{1,0:T(8,128)(2,1)S(1)}, u32[]{:S(2)}, u32[]{:S(2)}) collective-permute-start(bf16[256,1024]{1,0:T(8,128)(2,1)S(1)} %get-tuple-element.69), channel_id=1, source_target_pairs={{0,24},{4,28},{8,16},{12,20},{16,8},{20,12},{24,0},{28,4},{1,25},{... | collective-permute-start | bytes 1572872 | tf_op jit(solution)/shard_map/ppermute | solution.py:313
  149.5 29.3 %collective-permute-start.61 = (bf16[256,1024]{1,0:T(8,128)(2,1)S(1)}, bf16[256,1024]{1,0:T(8,128)(2,1)S(1)}, u32[]{:S(2)}, u32[]{:S(2)}) collective-permute-start(bf16[256,1024]{1,0:T(8,128)(2,1)S(1)} %get-tuple-element.67), channel_id=1, source_target_pairs={{0,16},{4,20},{8,24},{12,28},{16,0},{20,4},{24,8},{28,12},{1,17},{... | collective-permute-start | bytes 1572872 | tf_op jit(solution)/shard_map/ppermute | solution.py:313
  150.5 28.3 %collective-permute-start.60 = (bf16[256,1024]{1,0:T(8,128)(2,1)S(1)}, bf16[256,1024]{1,0:T(8,128)(2,1)S(1)}, u32[]{:S(2)}, u32[]{:S(2)}) collective-permute-start(bf16[256,1024]{1,0:T(8,128)(2,1)S(1)} %get-tuple-element.65), channel_id=1, source_target_pairs={{0,8},{4,12},{8,0},{12,4},{16,24},{20,28},{24,16},{28,20},{1,9},{5... | collective-permute-start | bytes 1572872 | tf_op jit(solution)/shard_map/ppermute | solution.py:313
  181.2 26.0 %collective-permute-start.69 = (bf16[512,1024]{1,0:T(8,128)(2,1)S(1)}, bf16[512,1024]{1,0:T(8,128)(2,1)S(1)}, u32[]{:S(2)}, u32[]{:S(2)}) collective-permute-start(bf16[512,1024]{1,0:T(8,128)(2,1)S(1)} %get-tuple-element.73), channel_id=1, source_target_pairs={{0,4},{4,0},{8,12},{12,8},{16,20},{20,16},{24,28},{28,24},{1,5},{5... | collective-permute-start | bytes 3145736 | tf_op jit(solution)/shard_map/ppermute | solution.py:313
  (67 other events, 671.2 us)

commit v4 on v3

--- a/solution.py
+++ b/solution.py
@@ -12,7 +12,7 @@
 TOPK = 4
 F32 = jnp.float32
 BF16 = jnp.bfloat16
-VMEM_LIMIT = 40 * 1024 * 1024
+MIB = 1024 * 1024
 NN = (((1,), (0,)), ((), ()))
 NT = (((1,), (1,)), ((), ()))
 TN = (((0,), (0,)), ((), ()))
@@ -34,8 +34,29 @@
     return lists, refs[at:]
 
 
-def whole(refs):
-    return joined([ref[...] for ref in refs], 0)
+def loads(lists, buf, sems):
+    copies, at = [], 0
+    for i, refs in enumerate(lists):
+        mine, row = [], 0
+        for ref in refs:
+            rows = ref.shape[0]
+            mine.append(
+                pltpu.make_async_copy(ref, buf.at[i, pl.ds(row, rows)], sems.at[at])
+            )
+            row += rows
+            at += 1
+        copies.append(mine)
+    return copies
+
+
+def start(copies):
+    for copy in copies:
+        copy.start()
+
+
+def wait(copies):
+    for copy in copies:
+        copy.wait()
 
 
 def added(terms, cols):
@@ -92,11 +113,25 @@
     return 16.0 * aux[at : at + TOPK] + aux[at + TOPK : at + 2 * TOPK]
 
 
-def forward_kernel(counts, span, cap, me_ref, mine_ref, other_ref, k_ref, v_ref, *refs):
+def forward_kernel(counts, span, cap, me_ref, mine_ref, other_ref, k_any, v_any, *refs):
     chunks = len(counts)
     q_refs, refs = dealt(refs, counts)
     part_refs, refs = refs[:chunks], refs[chunks:]
-    qg_ref, p_ref, gate_ref, hot_ref, auxg_ref, out_ref = refs
+    qg_any, p_any, gate_ref, hot_any = refs[:4]
+    q_buf, k_ref, v_ref, qg_ref, p_ref, hot_ref, auxg_ref, out_ref, in_sems, kv_sems, out_sems = refs[4:]
+    q_copies = loads(q_refs, q_buf, in_sems)
+    kv_copies = [
+        pltpu.make_async_copy(k_any, k_ref, kv_sems.at[0]),
+        pltpu.make_async_copy(v_any, v_ref, kv_sems.at[1]),
+    ]
+    out_copies = [
+        pltpu.make_async_copy(qg_ref, qg_any, out_sems.at[chunks]),
+        pltpu.make_async_copy(hot_ref, hot_any, out_sems.at[chunks + 1]),
+        pltpu.make_async_copy(p_ref, p_any, out_sems.at[chunks + 2]),
+    ]
+    for copies in q_copies:
+        start(copies)
+    start(kv_copies)
     aux_refs = [(other_ref if m % 2 else mine_ref).at[m // 2] for m in range(chunks)]
     block_count, _, width = k_ref.shape
     heads = width // HD
@@ -125,10 +160,15 @@
         ).astype(BF16)
         hot_ref[g] = hot
         auxg_ref[:, g * cap : (g + 1) * cap, :] = mm(hot, aux, NT).reshape(block_count, cap, HD)
-        q_group = joined([whole(q_refs[g * span + i]) for i in range(span)], 0)
+        for i in range(span):
+            wait(q_copies[g * span + i])
+        q_group = joined([q_buf[g * span + i] for i in range(span)], 0)
         qg_ref[:, g * cap : (g + 1) * cap, :] = (
             mm(hot, q_group).astype(BF16).reshape(block_count, cap, width)
         )
+
+    start(out_copies[:2])
+    wait(kv_copies)
 
     def one_block(b, carry):
         pairs = [slice(p * 2 * HD, (p + 1) * 2 * HD) for p in range(heads // 2)]
@@ -162,38 +202,49 @@
         return carry
 
     lax.fori_loop(0, block_count, one_block, 0)
+    start(out_copies[2:])
 
     for g in range(groups):
         slots = out_ref[:, g * cap : (g + 1) * cap, :].reshape(block_count * cap, width)
         part = mm(hot_ref[g], slots, TN).astype(BF16)
         for i in range(span):
-            part_refs[g * span + i][...] = part[i * rows : (i + 1) * rows]
+            m = g * span + i
+            q_buf[m] = part[i * rows : (i + 1) * rows]
+            copy = pltpu.make_async_copy(q_buf.at[m], part_refs[m], out_sems.at[m])
+            copy.start()
+            out_copies.append(copy)
+    wait(out_copies)
 
 
 def grad_kernel(lines, chips, at_ref, w_ref, *refs):
     own_ref, up_refs, down_refs = refs[0], refs[1:lines], refs[lines : 2 * lines - 1]
     ga_ref, slab_refs = refs[2 * lines - 1], refs[2 * lines : 2 * lines + chips]
-    full_ref, w_buf, sems = refs[2 * lines + chips :]
+    full_ref, w_buf, sems, piece_sems = refs[2 * lines + chips :]
     width = own_ref.shape[1]
     share = slab_refs[0].shape[1]
     line, chip = at_ref[0], at_ref[1]
+
+    def placed(ref, i):
+        return pltpu.make_async_copy(ref, full_ref.at[i], piece_sems.at[i])
+
+    placed(own_ref, line).start()
+    for d in range(1, lines):
+
+        @pl.when(line >= d)
+        def _():
+            placed(up_refs[d - 1], line - d).start()
+
+        @pl.when(line + d < lines)
+        def _():
+            placed(down_refs[d - 1], line + d).start()
+
     copies = [
         pltpu.make_async_copy(w_ref.at[pl.ds(i * width, width)], w_buf.at[i], sems.at[i])
         for i in range(lines)
     ]
-    for copy in copies:
-        copy.start()
-    full_ref[line] = own_ref[...]
-    for d in range(1, lines):
-
-        @pl.when(line >= d)
-        def _():
-            full_ref[line - d] = up_refs[d - 1][...]
-
-        @pl.when(line + d < lines)
-        def _():
-            full_ref[line + d] = down_refs[d - 1][...]
-
+    start(copies)
+    for i in range(lines):
+        placed(own_ref, i).wait()
     for j in range(chips):
         first = (chip ^ j) * share
         cols = pl.ds(pl.multiple_of(first % width, HD), share)
@@ -232,25 +283,52 @@
         out_ref[:, cols] = added(terms, cols)
 
 
-def backward_kernel(counts, span, cap, hot_ref, qg_ref, p_ref, gate_ref, k_ref, v_ref, *refs):
+def backward_kernel(counts, span, cap, gate_ref, hot_any, qg_any, p_any, k_any, v_any, *refs):
     chunks = len(counts)
     ga_refs, refs = dealt(refs, counts)
     part_refs, refs = refs[:chunks], refs[chunks:]
-    dk_ref, dv_ref, gag_ref, dq_ref = refs
+    dk_any, dv_any = refs[:2]
+    ga_buf, hot_ref, qg_ref, p_ref, k_ref, v_ref, gag_ref, dq_ref, dk_ref, dv_ref = refs[2:12]
+    in_sems, hot_sem, block_sems, out_sems, part_sems = refs[12:]
+    ga_copies = loads(ga_refs, ga_buf, in_sems)
+    hot_copy = pltpu.make_async_copy(hot_any, hot_ref, hot_sem.at[0])
+    hot_copy.start()
+    for copies in ga_copies:
+        start(copies)
+
+    def block_loads(b):
+        pairs = ((qg_any, qg_ref), (p_any, p_ref), (k_any, k_ref), (v_any, v_ref))
+        return [
+            pltpu.make_async_copy(far.at[b], near.at[b], block_sems.at[i, b])
+            for i, (far, near) in enumerate(pairs)
+        ]
+
+    def block_stores(b):
+        return [
+            pltpu.make_async_copy(dk_ref.at[b], dk_any.at[b], out_sems.at[0, b]),
+            pltpu.make_async_copy(dv_ref.at[b], dv_any.at[b], out_sems.at[1, b]),
+        ]
+
     block_count, _, width = k_ref.shape
     heads = width // HD
     rows = part_refs[0].shape[0]
     groups = chunks // span
     scale = HD ** (-0.5)
 
+    for b in range(block_count):
+        start(block_loads(b))
+    hot_copy.wait()
     for g in range(groups):
-        ga_group = joined([whole(ga_refs[g * span + i]) for i in range(span)], 0)
+        for i in range(span):
+            wait(ga_copies[g * span + i])
+        ga_group = joined([ga_buf[g * span + i] for i in range(span)], 0)
         gag_ref[:, g * cap : (g + 1) * cap, :] = (
             mm(hot_ref[g], ga_group).astype(BF16).reshape(block_count, cap, width + HD)
         )
     last = lax.broadcasted_iota(jnp.int32, (BLOCK, groups * cap), 0) == BLOCK - 1
 
     def one_block(b, carry):
+        wait(block_loads(b))
         pairs = [slice(p * 2 * HD, (p + 1) * 2 * HD) for p in range(heads // 2)]
         q = [qg_ref[b, :, cols] for cols in pairs]
         ga = [gag_ref[b, :, cols] for cols in pairs]
@@ -281,15 +359,27 @@
             dv_ref[b, :, cols] = jnp.concatenate([dv[:BLOCK, :HD], dv[BLOCK:, HD:]], axis=1)
             dk_ref[b, :, cols] = jnp.concatenate([dk[:BLOCK, :HD], dk[BLOCK:, HD:]], axis=1)
             dq_ref[b, :, cols] = dq
+        start(block_stores(b))
         return carry
 
     lax.fori_loop(0, block_count, one_block, 0)
+
+    part_copies = []
 
     for g in range(groups):
         slots = dq_ref[:, g * cap : (g + 1) * cap, :].reshape(block_count * cap, width)
         part = mm(hot_ref[g], slots, TN).astype(BF16)
         for i in range(span):
-            part_refs[g * span + i][...] = part[i * rows : (i + 1) * rows]
+            m = g * span + i
+            ga_buf[m, :, :width] = part[i * rows : (i + 1) * rows]
+            copy = pltpu.make_async_copy(
+                ga_buf.at[m, :, pl.ds(0, width)], part_refs[m], part_sems.at[m]
+            )
+            copy.start()
+            part_copies.append(copy)
+    for b in range(block_count):
+        wait(block_stores(b))
+    wait(part_copies)
 
 
 def weight_kernel(counts, me_ref, *refs):
@@ -298,7 +388,7 @@
     attns, (own_ref, other_ref) = dealt(refs[chips:], counts)
     half = own_ref.shape[0]
     core = me_ref[0] % 2
-    attn = joined([whole(pieces) for pieces in attns], 0)
+    attn = joined([ref[...] for pieces in attns for ref in pieces], 0)
 
     def side(which):
         cols = pl.ds(pl.multiple_of(which * half, half), half)
@@ -332,11 +422,11 @@
     return [[x], [x_top, x_low], [y_top, y_low], [swap(x_top, 4), swap(y_low, 2)]]
 
 
-def collect_chips(parts):
+def collect_chips(parts, *before):
     chips = len(parts) // 2
     received = [None] * chips
     for j in reversed(range(chips)):
-        received[j] = swap(parts[2 * j + 1], 1)
+        received[j] = after(swap(parts[2 * j + 1], 1), *before)
 
     def both(j, rows, extra=None):
         total = parts[2 * j][rows].astype(F32) + received[j][rows].astype(F32)
@@ -346,13 +436,14 @@
 
     terms = [[parts[0]], [received[0]]]
     if chips != 4:
-        return terms + [[swap(both(j, slice(None)), 2 * j)] for j in range(1, chips)]
+        terms += [[swap(both(j, slice(None)), 2 * j)] for j in range(1, chips)]
+        return terms, terms[2][0]
     half = parts[0].shape[0] // 2
     top, low = slice(0, half), slice(half, None)
     x_far, y_far = swap(both(3, top), 2), swap(both(3, low), 4)
     x_top, y_low = swap(both(1, top), 2), swap(both(2, low), 4)
     x_low, y_top = swap(both(1, low, y_far), 2), swap(both(2, top, x_far), 4)
-    return terms + [[x_top, x_low], [y_top, y_low]]
+    return terms + [[x_top, x_low], [y_top, y_low]], y_far
 
 
 def spread_line(x):
@@ -386,7 +477,10 @@
     values = value_rows.reshape(block_count, BLOCK, width)
     vmem = pl.BlockSpec(memory_space=pltpu.VMEM)
     smem = pl.BlockSpec(memory_space=pltpu.SMEM)
-    params = pltpu.CompilerParams(vmem_limit_bytes=VMEM_LIMIT)
+    anywhere = pl.BlockSpec(memory_space=pl.ANY)
+
+    def limit(mib):
+        return pltpu.CompilerParams(vmem_limit_bytes=mib * MIB)
 
     def shaped(shape, kind=BF16):
         return jax.ShapeDtypeStruct(shape, kind)
@@ -395,18 +489,19 @@
     marks = jnp.stack([marks] + [swap(marks, 2 * j) for j in range(1, chips)])
     ups, downs = spread_line(out_grad)
     query_chips = spread_chips(queries)
+    first = [query_chips[1][0], query_chips[-1][0] if chips != 4 else query_chips[2][1]]
     aux = pl.pallas_call(
         gate_kernel,
         out_shape=shaped((HD, rows)),
         in_specs=[smem] + [vmem] * 4,
         out_specs=vmem,
         scratch_shapes=[pltpu.VMEM((chunks, block_count, width), BF16)],
-        compiler_params=params,
+        compiler_params=limit(24),
         name="gates",
-    )(me, selected.T, marks, swap(marks, 1), queries)
+    )(me, selected.T, after(marks, *first), swap(marks, 1), queries)
     aux = jnp.stack([aux] + [swap(aux, 2 * j) for j in range(1, chips)])
-    query_all = []
-    for pieces in query_chips:
+    query_all = [[queries], [swap(after(queries, ups[0], downs[0]), 1)]]
+    for pieces in query_chips[1:]:
         query_all += [pieces, [swap(piece, 1) for piece in pieces]]
 
     outs = pl.pallas_call(
@@ -418,37 +513,47 @@
             shaped((block_count, heads, slots), F32),
             shaped((groups, block_count * cap, rows * span)),
         ],
-        in_specs=[smem] + [vmem] * (4 + len(flat(query_all))),
-        out_specs=[vmem] * (chunks + 4),
+        in_specs=[smem] + [vmem] * 2 + [anywhere] * (2 + len(flat(query_all))),
+        out_specs=[anywhere] * (chunks + 2) + [vmem, anywhere],
         scratch_shapes=[
+            pltpu.VMEM((chunks, rows, width), BF16),
+            pltpu.VMEM((block_count, BLOCK, width), BF16),
+            pltpu.VMEM((block_count, BLOCK, width), BF16),
+            pltpu.VMEM((block_count, slots, width), BF16),
+            pltpu.VMEM((block_count, heads // 2, 2 * BLOCK, slots), BF16),
+            pltpu.VMEM((groups, block_count * cap, rows * span), BF16),
             pltpu.VMEM((block_count, slots, HD), F32),
             pltpu.VMEM((block_count, slots, width), BF16),
+            pltpu.SemaphoreType.DMA((len(flat(query_all)),)),
+            pltpu.SemaphoreType.DMA((2,)),
+            pltpu.SemaphoreType.DMA((chunks + 3,)),
         ],
-        compiler_params=params,
+        compiler_params=limit(36),
         name="forward",
-    )(me, aux, swap(aux, 1), keys, values, *flat(query_all))
+    )(after(me, *ups[:2], *downs[:2]), aux, swap(aux, 1), keys, values, *flat(query_all))
     q_slots, probs, gates, hot = outs[chunks:]
 
     grad_attn, *slabs = pl.pallas_call(
         functools.partial(grad_kernel, lines, chips),
         out_shape=[shaped((rows, width))] + [shaped((rows, share))] * chips,
-        in_specs=[smem, pl.BlockSpec(memory_space=pl.ANY)] + [vmem] * (2 * lines - 1),
+        in_specs=[smem] + [anywhere] * (2 * lines),
         out_specs=[vmem] * (1 + chips),
         scratch_shapes=[
             pltpu.VMEM((lines, rows, width), BF16),
             pltpu.VMEM((lines, width, width), BF16),
             pltpu.SemaphoreType.DMA((lines,)),
+            pltpu.SemaphoreType.DMA((lines,)),
         ],
-        compiler_params=params,
+        compiler_params=limit(24),
         name="grad",
     )(at, out_weight, out_grad, *ups, *downs)
-    terms = collect_chips(outs[:chunks])
+    terms, _ = collect_chips(outs[:chunks], grad_attn)
     attn_out, extended = pl.pallas_call(
         functools.partial(finish_kernel, [len(pieces) for pieces in terms]),
         out_shape=[shaped((rows, width)), shaped((rows, width + HD))],
         in_specs=[vmem] * (len(flat(terms)) + 1),
         out_specs=[vmem] * 2,
-        compiler_params=params,
+        compiler_params=limit(24),
         name="finish",
     )(*flat(terms), grad_attn)
     grad_chips = spread_chips(extended)
@@ -456,31 +561,44 @@
     for pieces in grad_chips:
         grad_all += [pieces, [swap(piece, 1) for piece in pieces]]
 
-    arrived = flat(grad_chips)
-    attns = spread_chips(after(attn_out, *arrived))
+    arrived = flat(grad_chips[1:3])
+    attns = [[attn_out]] + [[swap(after(attn_out, *arrived), 2 * j)] for j in range(1, chips)]
     slabs = [slabs[0]] + [swap(after(slabs[j], *arrived), 2 * j) for j in range(1, chips)]
 
     outs = pl.pallas_call(
         functools.partial(backward_kernel, [len(pieces) for pieces in grad_all], span, cap),
         out_shape=[shaped((rows, width))] * chunks
         + [shaped((block_count, BLOCK, width), F32)] * 2,
-        in_specs=[vmem] * (6 + len(flat(grad_all))),
-        out_specs=[vmem] * (chunks + 2),
+        in_specs=[vmem] + [anywhere] * (5 + len(flat(grad_all))),
+        out_specs=[anywhere] * (chunks + 2),
         scratch_shapes=[
+            pltpu.VMEM((chunks, rows, width + HD), BF16),
+            pltpu.VMEM((groups, block_count * cap, rows * span), BF16),
+            pltpu.VMEM((block_count, slots, width), BF16),
+            pltpu.VMEM((block_count, heads // 2, 2 * BLOCK, slots), BF16),
+            pltpu.VMEM((block_count, BLOCK, width), BF16),
+            pltpu.VMEM((block_count, BLOCK, width), BF16),
             pltpu.VMEM((block_count, slots, width + HD), BF16),
             pltpu.VMEM((block_count, slots, width), BF16),
+            pltpu.VMEM((block_count, BLOCK, width), F32),
+            pltpu.VMEM((block_count, BLOCK, width), F32),
+            pltpu.SemaphoreType.DMA((len(flat(grad_all)),)),
+            pltpu.SemaphoreType.DMA((1,)),
+            pltpu.SemaphoreType.DMA((4, block_count)),
+            pltpu.SemaphoreType.DMA((2, block_count)),
+            pltpu.SemaphoreType.DMA((chunks,)),
         ],
-        compiler_params=params,
+        compiler_params=limit(44),
         name="backward",
-    )(hot, q_slots, probs, gates, keys, values, *flat(grad_all))
+    )(gates, hot, q_slots, probs, keys, values, *flat(grad_all))
     key_grad, value_grad = outs[chunks:]
-    terms = collect_chips(outs[:chunks])
+    terms, far = collect_chips(outs[:chunks])
     query_grad = pl.pallas_call(
         functools.partial(total_kernel, [len(pieces) for pieces in terms]),
         out_shape=shaped((rows, width), F32),
         in_specs=[vmem] * len(flat(terms)),
         out_specs=vmem,
-        compiler_params=params,
+        compiler_params=limit(24),
         name="total",
     )(*flat(terms))
 
@@ -489,9 +607,9 @@
         out_shape=[shaped((share // 2, width), F32), shaped((share // 2, width))],
         in_specs=[smem] + [vmem] * (chips + len(flat(attns))),
         out_specs=[vmem] * 2,
-        compiler_params=params,
+        compiler_params=limit(24),
         name="weight",
-    )(me, *slabs, *flat(attns))
+    )(after(me, far), *slabs, *flat(attns))
     weight_grad = weight_own + swap(weight_other, 1).astype(F32)
     return (
         query_grad,

time: 210 us -> 253 us (1.20)
  waiting for transfers between devices: 95.2 us -> 127 us
  local copies, waits for them, and re-layouts: 12 us -> 21.7 us
    ppermute x64 -> x61, waiting for transfers between devices: 78.3 us -> 120 us  [swap(): return lax.ppermute(x, 'ctx', [(i, i ^ bits) for i in range(count)])]
    ppermute x3, waiting for transfers between devices: 16.9 us -> 7.1 us  [spread_line(): lax.ppermute(downs[-1], 'head', [(i, i - 1) for i in range(1, lines - d +...]
    unnamed x43 -> x49, local copies, waits for them, and re-layouts: 10.7 us -> 18.6 us
    pallas_call x1, Pallas kernels: 14.1 us -> 16.8 us  [body(): pl.pallas_call(functools.partial(forward_kernel, [len(pieces) for pieces...]
    ppermute x64 -> x61, starting transfers between devices: 44.4 us -> 42.9 us  [swap(): return lax.ppermute(x, 'ctx', [(i, i ^ bits) for i in range(count)])]
  transfers between devices with their start and end apart: 70 -> 67, of which waited for: 29 -> 27; matrix products, arithmetic and copies ran while one was open for 1% -> 1% of each run, Pallas kernels for 19% -> 11%
where the time goes in v4:
time: 253 us; the launch traced here: 251 us
  waiting for transfers between devices  127 us (50%)
  starting transfers between devices  53.2 us (21%)
  Pallas kernels  45.1 us (18%)
  local copies, waits for them, and re-layouts  21.7 us (9%)
  other arithmetic  3.04 us (1%)
    ppermute x61, waiting for transfers between devices, swap(): return lax.ppermute(x, 'ctx', [(i, i ^ bits) for i in range(count)])  120 us
    ppermute x61, starting transfers between devices, swap(): return lax.ppermute(x, 'ctx', [(i, i ^ bits) for i in range(count)])  42.9 us
    unnamed x49, local copies, waits for them, and re-layouts  18.6 us
    pallas_call x1, Pallas kernels, body(): pl.pallas_call(functools.partial(backward_kernel, [len(pieces) for pieces...  17.2 us
    pallas_call x1, Pallas kernels, body(): pl.pallas_call(functools.partial(forward_kernel, [len(pieces) for pieces...  16.8 us
    ppermute x3, waiting for transfers between devices, spread_line(): lax.ppermute(downs[-1], 'head', [(i, i - 1) for i in range(1, lines - d +...  7.1 us
    ppermute x3, starting transfers between devices, spread_line(): lax.ppermute(ups[-1], 'head', [(i, i + 1) for i in range(d - 1, lines - 1)])  6.46 us
  transfers between devices with their start and end apart: 67, of which 27 were waited for; matrix products, arithmetic and copies ran while one was open for 1% of the time, Pallas kernels for 11%

profile of v4, /device:TPU:0, one launch (start us, length us, event | category | flops | bytes accessed | tf_op | source)
XLA Modules:
  0.0 251.3 jit_solution(13271878279141994541)
XLA Ops:
  2.6 2.9 %collective-permute-start.7 = (bf16[128,1024]{1,0:T(8,128)(2,1)}, bf16[128,1024]{1,0:T(8,128)(2,1)S(1)}, u32[]{:S(2)}, u32[]{:S(2)}) collective-permute-start(bf16[128,1024]{1,0:T(8,128)(2,1)} %get-tuple-element.105), channel_id=1, source_target_pairs={{0,8},{4,12},{8,0},{12,4},{16,24},{20,28},{24,16},{28,20},{1,9},{5... | collective-permute-start | bytes 786440 | tf_op jit(solution)/shard_map/ppermute | solution.py:403
  5.6 3.5 %collective-permute-start = (bf16[256,1024]{1,0:T(8,128)(2,1)}, bf16[256,1024]{1,0:T(8,128)(2,1)S(1)}, u32[]{:S(2)}, u32[]{:S(2)}) collective-permute-start(bf16[256,1024]{1,0:T(8,128)(2,1)} %refs_0_.3), channel_id=1, source_target_pairs={{0,1},{1,2},{2,3},{4,5},{5,6},{6,7},{8,9},{9,10},{10,11},{12,13},{... | collective-permute-start | bytes 1572872 | tf_op jit(solution)/shard_map/ppermute | solution.py:453
  13.6 4.4 %collective-permute-done.6 = bf16[16,1024]{1,0:T(8,128)(2,1)S(1)} collective-permute-done((bf16[16,1024]{1,0:T(8,128)(2,1)S(1)}, bf16[16,1024]{1,0:T(8,128)(2,1)S(1)}, u32[]{:S(2)}, u32[]{:S(2)}) %collective-permute-start.6) | collective-permute-done | bytes 32800 | tf_op jit(solution)/shard_map/ppermute | solution.py:403
  18.5 3.4 %collective-permute-done.5 = bf16[16,1024]{1,0:T(8,128)(2,1)S(1)} collective-permute-done((bf16[16,1024]{1,0:T(8,128)(2,1)S(1)}, bf16[16,1024]{1,0:T(8,128)(2,1)S(1)}, u32[]{:S(2)}, u32[]{:S(2)}) %collective-permute-start.5) | collective-permute-done | bytes 32800 | tf_op jit(solution)/shard_map/ppermute | solution.py:403
  22.5 3.7 %collective-permute-done.4 = bf16[16,1024]{1,0:T(8,128)(2,1)S(1)} collective-permute-done((bf16[16,1024]{1,0:T(8,128)(2,1)S(1)}, bf16[16,1024]{1,0:T(8,128)(2,1)S(1)}, u32[]{:S(2)}, u32[]{:S(2)}) %collective-permute-start.4) | collective-permute-done | bytes 32800 | tf_op jit(solution)/shard_map/ppermute | solution.py:403
  45.4 6.1 %collective-permute-done.21.refs_10_ = bf16[128,1024]{1,0:T(8,128)(2,1)S(1)} collective-permute-done((bf16[128,1024]{1,0:T(8,128)(2,1)S(1)}, bf16[128,1024]{1,0:T(8,128)(2,1)S(1)}, u32[]{:S(2)}, u32[]{:S(2)}) %collective-permute-start.21) | collective-permute-done | bytes 262176 | tf_op jit(solution)/shard_map/ppermute | solution.py:403
  53.3 7.1 %collective-permute-done.3.refs_5_ = bf16[256,1024]{1,0:T(8,128)(2,1)} collective-permute-done((bf16[256,1024]{1,0:T(8,128)(2,1)S(1)}, bf16[256,1024]{1,0:T(8,128)(2,1)}, u32[]{:S(2)}, u32[]{:S(2)}) %collective-permute-start.3) | collective-permute-done | bytes 524320 | tf_op jit(solution)/shard_map/ppermute | solution.py:454
  65.8 16.8 %forward.1 = (bf16[256,1024]{1,0:T(8,128)(2,1)S(1)}, bf16[256,1024]{1,0:T(8,128)(2,1)S(1)}, bf16[256,1024]{1,0:T(8,128)(2,1)S(1)}, bf16[256,1024]{1,0:T(8,128)(2...) custom-call(s32[1]{0:T(128)} %bitcast.me_ref, ...), custom_call_target="tpu_custom_call" | custom-call | tf_op jit(solution)/shard_map/forward/pallas_call | solution.py:507
  90.7 3.4 %copy-done.1 = bf16[4096,1024]{1,0:T(8,128)(2,1)S(1)} copy-done((bf16[4096,1024]{1,0:T(8,128)(2,1)S(1)}, bf16[4096,1024]{1,0:T(8,128)(2,1)}, u32[]{:S(2)}) %copy-start.1) | copy-done | bytes 8388632
  97.2 4.8 %grad.1 = (bf16[256,1024]{1,0:T(8,128)(2,1)S(1)}, bf16[256,1024]{1,0:T(8,128)(2,1)S(1)}, bf16[256,1024]{1,0:T(8,128)(2,1)S(1)}, bf16[256,1024]{1,0:T(8,128)(2,1)S(1)}, bf16[256,1024]{1,0:T(8,128)(2,1)S(1)}) custom-call(s32[2]{0:T(128)S(1)} %pad_add_fusion.at_ref, bf16[4096,1024]{1,0:T(8,128)(2,1)S(1)} %copy-done.1, bf16[256,1024]{1,0:T(8,128)(2,1)S(1)} %copy-done.6, ...), custom_call_target="tpu_custom_call" | custom-call | tf_op jit(solution)/shard_map/grad/pallas_call | solution.py:536
  104.5 6.1 %collective-permute-done.31 = bf16[128,1024]{1,0:T(8,128)(2,1)S(1)} collective-permute-done((bf16[128,1024]{1,0:T(8,128)(2,1)S(1)}, bf16[128,1024]{1,0:T(8,128)(2,1)S(1)}, u32[]{:S(2)}, u32[]{:S(2)}) %collective-permute-start.31) | collective-permute-done | bytes 262176 | tf_op jit(solution)/shard_map/ppermute | solution.py:403
  115.2 4.9 %collective-permute-done.29.refs_2_ = bf16[128,1024]{1,0:T(8,128)(2,1)S(1)} collective-permute-done((bf16[128,1024]{1,0:T(8,128)(2,1)S(1)}, bf16[128,1024]{1,0:T(8,128)(2,1)S(1)}, u32[]{:S(2)}, u32[]{:S(2)}) %collective-permute-start.29) | collective-permute-done | bytes 262176 | tf_op jit(solution)/shard_map/ppermute | solution.py:403
  120.1 3.7 %collective-permute-done.32.refs_3_ = bf16[128,1024]{1,0:T(8,128)(2,1)S(1)} collective-permute-done((bf16[128,1024]{1,0:T(8,128)(2,1)S(1)}, bf16[128,1024]{1,0:T(8,128)(2,1)S(1)}, u32[]{:S(2)}, u32[]{:S(2)}) %collective-permute-start.32) | collective-permute-done | bytes 262176 | tf_op jit(solution)/shard_map/ppermute | solution.py:403
  130.5 5.7 %collective-permute-done.38.refs_2_ = bf16[128,1152]{1,0:T(8,128)(2,1)S(1)} collective-permute-done((bf16[128,1152]{1,0:T(8,128)(2,1)S(1)}, bf16[128,1152]{1,0:T(8,128)(2,1)S(1)}, u32[]{:S(2)}, u32[]{:S(2)}) %collective-permute-start.38) | collective-permute-done | bytes 294944 | tf_op jit(solution)/shard_map/ppermute | solution.py:403
  136.2 3.2 %collective-permute-done.39.refs_3_ = bf16[128,1152]{1,0:T(8,128)(2,1)S(1)} collective-permute-done((bf16[128,1152]{1,0:T(8,128)(2,1)S(1)}, bf16[128,1152]{1,0:T(8,128)(2,1)S(1)}, u32[]{:S(2)}, u32[]{:S(2)}) %collective-permute-start.39) | collective-permute-done | bytes 294944 | tf_op jit(solution)/shard_map/ppermute | solution.py:403
  142.6 6.2 %collective-permute-done.46.refs_10_ = bf16[128,1152]{1,0:T(8,128)(2,1)S(1)} collective-permute-done((bf16[128,1152]{1,0:T(8,128)(2,1)S(1)}, bf16[128,1152]{1,0:T(8,128)(2,1)S(1)}, u32[]{:S(2)}, u32[]{:S(2)}) %collective-permute-start.46) | collective-permute-done | bytes 294944 | tf_op jit(solution)/shard_map/ppermute | solution.py:403
  151.3 17.2 %backward.1 = (bf16[256,1024]{1,0:T(8,128)(2,1)S(1)}, bf16[256,1024]{1,0:T(8,128)(2,1)S(1)}, bf16[256,1024]{1,0:T(8,128)(2,1)S(1)}, bf16[256,1024]{1,0:T(8,128)(...) custom-call(f32[16,8,128]{2,1,0:T(8,128)S(1)} %get-tuple-element.50., ...), custom_call_target="tpu_custom_call" | custom-call | tf_op jit(solution)/shard_map/backward/pallas_call | solution.py:568
  174.3 9.2 %collective-permute-done.60.refs_1_ = bf16[256,1024]{1,0:T(8,128)(2,1)S(1)} collective-permute-done((bf16[256,1024]{1,0:T(8,128)(2,1)S(1)}, bf16[256,1024]{1,0:T(8,128)(2,1)S(1)}, u32[]{:S(2)}, u32[]{:S(2)}) %collective-permute-start.60) | collective-permute-done | bytes 524320 | tf_op jit(solution)/shard_map/ppermute | solution.py:403
  185.2 10.4 %collective-permute-done.61.refs_2_ = bf16[256,1024]{1,0:T(8,128)(2,1)S(1)} collective-permute-done((bf16[256,1024]{1,0:T(8,128)(2,1)S(1)}, bf16[256,1024]{1,0:T(8,128)(2,1)S(1)}, u32[]{:S(2)}, u32[]{:S(2)}) %collective-permute-start.61) | collective-permute-done | bytes 524320 | tf_op jit(solution)/shard_map/ppermute | solution.py:403
  196.8 26.0 %collective-permute-done.54 = bf16[128,1024]{1,0:T(8,128)(2,1)S(1)} collective-permute-done((bf16[128,1024]{1,0:T(8,128)(2,1)S(1)}, bf16[128,1024]{1,0:T(8,128)(2,1)S(1)}, u32[]{:S(2)}, u32[]{:S(2)}) %collective-permute-start.54) | collective-permute-done | bytes 262176 | tf_op jit(solution)/shard_map/ppermute | solution.py:403
  229.4 5.6 %collective-permute-done.57 = bf16[128,1024]{1,0:T(8,128)(2,1)S(1)} collective-permute-done((bf16[128,1024]{1,0:T(8,128)(2,1)S(1)}, bf16[128,1024]{1,0:T(8,128)(2,1)S(1)}, u32[]{:S(2)}, u32[]{:S(2)}) %collective-permute-start.57) | collective-permute-done | bytes 262176 | tf_op jit(solution)/shard_map/ppermute | solution.py:403
  237.3 3.3 %collective-permute-done.52.refs_2_ = bf16[128,1024]{1,0:T(8,128)(2,1)S(1)} collective-permute-done((bf16[128,1024]{1,0:T(8,128)(2,1)S(1)}, bf16[128,1024]{1,0:T(8,128)(2,1)S(1)}, u32[]{:S(2)}, u32[]{:S(2)}) %collective-permute-start.52) | collective-permute-done | bytes 262176 | tf_op jit(solution)/shard_map/ppermute | solution.py:403
  240.6 5.2 %collective-permute-done.55.refs_3_ = bf16[128,1024]{1,0:T(8,128)(2,1)S(1)} collective-permute-done((bf16[128,1024]{1,0:T(8,128)(2,1)S(1)}, bf16[128,1024]{1,0:T(8,128)(2,1)S(1)}, u32[]{:S(2)}, u32[]{:S(2)}) %collective-permute-start.55) | collective-permute-done | bytes 262176 | tf_op jit(solution)/shard_map/ppermute | solution.py:403
  245.8 2.6 %collective-permute-done.59.refs_5_ = bf16[128,1024]{1,0:T(8,128)(2,1)S(1)} collective-permute-done((bf16[128,1024]{1,0:T(8,128)(2,1)S(1)}, bf16[128,1024]{1,0:T(8,128)(2,1)S(1)}, u32[]{:S(2)}, u32[]{:S(2)}) %collective-permute-start.59) | collective-permute-done | bytes 262176 | tf_op jit(solution)/shard_map/ppermute | solution.py:403
  (179 shorter events, 84.9 us)
Async XLA Ops:
  2.6 24.1 %collective-permute-start.7 = (bf16[128,1024]{1,0:T(8,128)(2,1)}, bf16[128,1024]{1,0:T(8,128)(2,1)S(1)}, u32[]{:S(2)}, u32[]{:S(2)}) collective-permute-start(bf16[128,1024]{1,0:T(8,128)(2,1)} %get-tuple-element.105), channel_id=1, source_target_pairs={{0,8},{4,12},{8,0},{12,4},{16,24},{20,28},{24,16},{28,20},{1,9},{5... | collective-permute-start | bytes 786440 | tf_op jit(solution)/shard_map/ppermute | solution.py:403
  5.6 33.6 %collective-permute-start = (bf16[256,1024]{1,0:T(8,128)(2,1)}, bf16[256,1024]{1,0:T(8,128)(2,1)S(1)}, u32[]{:S(2)}, u32[]{:S(2)}) collective-permute-start(bf16[256,1024]{1,0:T(8,128)(2,1)} %refs_0_.3), channel_id=1, source_target_pairs={{0,1},{1,2},{2,3},{4,5},{5,6},{6,7},{8,9},{9,10},{10,11},{12,13},{... | collective-permute-start | bytes 1572872 | tf_op jit(solution)/shard_map/ppermute | solution.py:453
  9.1 31.6 %collective-permute-start.2 = (bf16[256,1024]{1,0:T(8,128)(2,1)}, bf16[256,1024]{1,0:T(8,128)(2,1)S(1)}, u32[]{:S(2)}, u32[]{:S(2)}) collective-permute-start(bf16[256,1024]{1,0:T(8,128)(2,1)} %refs_0_.3), channel_id=1, source_target_pairs={{1,0},{2,1},{3,2},{5,4},{6,5},{7,6},{9,8},{10,9},{11,10},{13,12},{... | collective-permute-start | bytes 1572872 | tf_op jit(solution)/shard_map/ppermute | solution.py:454
  10.4 16.9 %collective-permute-start.8 = (bf16[128,1024]{1,0:T(8,128)(2,1)}, bf16[128,1024]{1,0:T(8,128)(2,1)}, u32[]{:S(2)}, u32[]{:S(2)}) collective-permute-start(bf16[128,1024]{1,0:T(8,128)(2,1)} %get-tuple-element.104), channel_id=1, source_target_pairs={{0,16},{4,20},{8,24},{12,28},{16,0},{20,4},{24,8},{28,12},{1,17},{... | collective-permute-start | bytes 786440 | tf_op jit(solution)/shard_map/ppermute | solution.py:403
  39.2 13.5 %collective-permute-start.1 = (bf16[256,1024]{1,0:T(8,128)(2,1)S(1)}, bf16[256,1024]{1,0:T(8,128)(2,1)}, u32[]{:S(2)}, u32[]{:S(2)}) collective-permute-start(bf16[256,1024]{1,0:T(8,128)(2,1)S(1)} %collective-permute-done.refs_1_), channel_id=1, source_target_pairs={{1,2},{2,3},{5,6},{6,7},{9,10},{10,11},{13,14},{14,15},{17,18},{18... | collective-permute-start | bytes 1572872 | tf_op jit(solution)/shard_map/ppermute | solution.py:453
  40.7 19.7 %collective-permute-start.3 = (bf16[256,1024]{1,0:T(8,128)(2,1)S(1)}, bf16[256,1024]{1,0:T(8,128)(2,1)}, u32[]{:S(2)}, u32[]{:S(2)}) collective-permute-start(bf16[256,1024]{1,0:T(8,128)(2,1)S(1)} %collective-permute-done.2.refs_4_), channel_id=1, source_target_pairs={{1,0},{2,1},{5,4},{6,5},{9,8},{10,9},{13,12},{14,13},{17,16},{18,1... | collective-permute-start | bytes 1572872 | tf_op jit(solution)/shard_map/ppermute | solution.py:454
  45.4 17.8 %collective-permute-start.14 = (bf16[256,1024]{1,0:T(8,128)(2,1)S(1)}, bf16[256,1024]{1,0:T(8,128)(2,1)S(1)}, u32[]{:S(2)}, u32[]{:S(2)}) collective-permute-start(bf16[256,1024]{1,0:T(8,128)(2,1)S(1)} %copy-done.3), channel_id=1, source_target_pairs={{0,4},{4,0},{8,12},{12,8},{16,20},{20,16},{24,28},{28,24},{1,5},{5... | collective-permute-start | bytes 1572872 | tf_op jit(solution)/shard_map/ppermute | solution.py:403
  60.4 30.4 %collective-permute-start.26 = (bf16[256,1024]{1,0:T(8,128)(2,1)}, bf16[256,1024]{1,0:T(8,128)(2,1)}, u32[]{:S(2)}, u32[]{:S(2)}) collective-permute-start(bf16[256,1024]{1,0:T(8,128)(2,1)} %collective-permute-done.1.refs_2_), channel_id=1, source_target_pairs={{2,3},{6,7},{10,11},{14,15},{18,19},{22,23},{26,27},{30,31}} | collective-permute-start | bytes 1572872 | tf_op jit(solution)/shard_map/ppermute | solution.py:453
  61.9 28.9 %collective-permute-start.27 = (bf16[256,1024]{1,0:T(8,128)(2,1)}, bf16[256,1024]{1,0:T(8,128)(2,1)}, u32[]{:S(2)}, u32[]{:S(2)}) collective-permute-start(bf16[256,1024]{1,0:T(8,128)(2,1)} %collective-permute-done.3.refs_5_), channel_id=1, source_target_pairs={{1,0},{5,4},{9,8},{13,12},{17,16},{21,20},{25,24},{29,28}} | collective-permute-start | bytes 1572872 | tf_op jit(solution)/shard_map/ppermute | solution.py:454
  89.6 12.5 %collective-permute-start.30 = (bf16[256,1024]{1,0:T(8,128)(2,1)}, bf16[256,1024]{1,0:T(8,128)(2,1)S(1)}, u32[]{:S(2)}, u32[]{:S(2)}) collective-permute-start(bf16[256,1024]{1,0:T(8,128)(2,1)} %get-tuple-element.62), channel_id=1, source_target_pairs={{0,4},{4,0},{8,12},{12,8},{16,20},{20,16},{24,28},{28,24},{1,5},{5... | collective-permute-start | bytes 1572872 | tf_op jit(solution)/shard_map/ppermute | solution.py:403
  90.1 14.3 %collective-permute-start.28 = (bf16[256,1024]{1,0:T(8,128)(2,1)}, bf16[256,1024]{1,0:T(8,128)(2,1)S(1)}, u32[]{:S(2)}, u32[]{:S(2)}) collective-permute-start(bf16[256,1024]{1,0:T(8,128)(2,1)} %copy-done.23), channel_id=1, source_target_pairs={{0,4},{4,0},{8,12},{12,8},{16,20},{20,16},{24,28},{28,24},{1,5},{5... | collective-permute-start | bytes 1572872 | tf_op jit(solution)/shard_map/ppermute | solution.py:403
  90.1 14.3 %collective-permute-start.33 = (bf16[256,1024]{1,0:T(8,128)(2,1)}, bf16[256,1024]{1,0:T(8,128)(2,1)S(1)}, u32[]{:S(2)}, u32[]{:S(2)}) collective-permute-start(bf16[256,1024]{1,0:T(8,128)(2,1)} %copy-done.22), channel_id=1, source_target_pairs={{0,4},{4,0},{8,12},{12,8},{16,20},{20,16},{24,28},{28,24},{1,5},{5... | collective-permute-start | bytes 1572872 | tf_op jit(solution)/shard_map/ppermute | solution.py:403
  130.5 19.3 %collective-permute-start.37 = (bf16[256,1152]{1,0:T(8,128)(2,1)S(1)}, bf16[256,1152]{1,0:T(8,128)(2,1)S(1)}, u32[]{:S(2)}, u32[]{:S(2)}) collective-permute-start(bf16[256,1152]{1,0:T(8,128)(2,1)S(1)} %get-tuple-element.67.refs_0_), channel_id=1, source_target_pairs={{0,4},{4,0},{8,12},{12,8},{16,20},{20,16},{24,28},{28,24},{1,5},{5... | collective-permute-start | bytes 1769480 | tf_op jit(solution)/shard_map/ppermute | solution.py:403
  168.7 14.8 %collective-permute-start.60 = (bf16[256,1024]{1,0:T(8,128)(2,1)S(1)}, bf16[256,1024]{1,0:T(8,128)(2,1)S(1)}, u32[]{:S(2)}, u32[]{:S(2)}) collective-permute-start(bf16[256,1024]{1,0:T(8,128)(2,1)S(1)} %get-tuple-element.81), channel_id=1, source_target_pairs={{0,8},{4,12},{8,0},{12,4},{16,24},{20,28},{24,16},{28,20},{1,9},{5... | collective-permute-start | bytes 1572872 | tf_op jit(solution)/shard_map/ppermute | solution.py:403
  169.6 26.0 %collective-permute-start.61 = (bf16[256,1024]{1,0:T(8,128)(2,1)S(1)}, bf16[256,1024]{1,0:T(8,128)(2,1)S(1)}, u32[]{:S(2)}, u32[]{:S(2)}) collective-permute-start(bf16[256,1024]{1,0:T(8,128)(2,1)S(1)} %get-tuple-element.83), channel_id=1, source_target_pairs={{0,16},{4,20},{8,24},{12,28},{16,0},{20,4},{24,8},{28,12},{1,17},{... | collective-permute-start | bytes 1572872 | tf_op jit(solution)/shard_map/ppermute | solution.py:403
  170.8 26.0 %collective-permute-start.62 = (bf16[256,1024]{1,0:T(8,128)(2,1)S(1)}, bf16[256,1024]{1,0:T(8,128)(2,1)S(1)}, u32[]{:S(2)}, u32[]{:S(2)}) collective-permute-start(bf16[256,1024]{1,0:T(8,128)(2,1)S(1)} %get-tuple-element.85), channel_id=1, source_target_pairs={{0,24},{4,28},{8,16},{12,20},{16,8},{20,12},{24,0},{28,4},{1,25},{... | collective-permute-start | bytes 1572872 | tf_op jit(solution)/shard_map/ppermute | solution.py:403
  172.2 50.6 %collective-permute-start.63 = (bf16[256,1024]{1,0:T(8,128)(2,1)S(1)}, bf16[256,1024]{1,0:T(8,128)(2,1)S(1)}, u32[]{:S(2)}, u32[]{:S(2)}) collective-permute-start(bf16[256,1024]{1,0:T(8,128)(2,1)S(1)} %get-tuple-element.87.refs_4_), channel_id=1, source_target_pairs={{0,8},{4,12},{8,0},{12,4},{16,24},{20,28},{24,16},{28,20},{1,9},{5... | collective-permute-start | bytes 1572872 | tf_op jit(solution)/shard_map/ppermute | solution.py:403
  173.1 49.7 %collective-permute-start.64 = (bf16[256,1024]{1,0:T(8,128)(2,1)S(1)}, bf16[256,1024]{1,0:T(8,128)(2,1)S(1)}, u32[]{:S(2)}, u32[]{:S(2)}) collective-permute-start(bf16[256,1024]{1,0:T(8,128)(2,1)S(1)} %get-tuple-element.87.refs_4_), channel_id=1, source_target_pairs={{0,16},{4,20},{8,24},{12,28},{16,0},{20,4},{24,8},{28,12},{1,17},{... | collective-permute-start | bytes 1572872 | tf_op jit(solution)/shard_map/ppermute | solution.py:403
  183.5 39.3 %collective-permute-start.65 = (bf16[256,1024]{1,0:T(8,128)(2,1)S(1)}, bf16[256,1024]{1,0:T(8,128)(2,1)S(1)}, u32[]{:S(2)}, u32[]{:S(2)}) collective-permute-start(bf16[256,1024]{1,0:T(8,128)(2,1)S(1)} %get-tuple-element.87.refs_4_), channel_id=1, source_target_pairs={{0,24},{4,28},{8,16},{12,20},{16,8},{20,12},{24,0},{28,4},{1,25},{... | collective-permute-start | bytes 1572872 | tf_op jit(solution)/shard_map/ppermute | solution.py:403
  195.6 27.2 %collective-permute-start.54 = (bf16[128,1024]{1,0:T(8,128)(2,1)S(1)}, bf16[128,1024]{1,0:T(8,128)(2,1)S(1)}, u32[]{:S(2)}, u32[]{:S(2)}) collective-permute-start(bf16[128,1024]{1,0:T(8,128)(2,1)S(1)} %get-tuple-element.93), channel_id=1, source_target_pairs={{0,16},{4,20},{8,24},{12,28},{16,0},{20,4},{24,8},{28,12},{1,17},{... | collective-permute-start | bytes 786440 | tf_op jit(solution)/shard_map/ppermute | solution.py:403
  196.8 30.2 %collective-permute-start.51 = (bf16[256,1024]{1,0:T(8,128)(2,1)S(1)}, bf16[256,1024]{1,0:T(8,128)(2,1)S(1)}, u32[]{:S(2)}, u32[]{:S(2)}) collective-permute-start(bf16[256,1024]{1,0:T(8,128)(2,1)S(1)} %get-tuple-element.71), channel_id=1, source_target_pairs={{0,4},{4,0},{8,12},{12,8},{16,20},{20,16},{24,28},{28,24},{1,5},{5... | collective-permute-start | bytes 1572872 | tf_op jit(solution)/shard_map/ppermute | solution.py:403
  225.2 24.4 %collective-permute-start.66 = (bf16[512,1024]{1,0:T(8,128)(2,1)S(1)}, bf16[512,1024]{1,0:T(8,128)(2,1)S(1)}, u32[]{:S(2)}, u32[]{:S(2)}) collective-permute-start(bf16[512,1024]{1,0:T(8,128)(2,1)S(1)} %get-tuple-element.89), channel_id=1, source_target_pairs={{0,4},{4,0},{8,12},{12,8},{16,20},{20,16},{24,28},{28,24},{1,5},{5... | collective-permute-start | bytes 3145736 | tf_op jit(solution)/shard_map/ppermute | solution.py:403
  227.3 13.3 %collective-permute-start.52 = (bf16[128,1024]{1,0:T(8,128)(2,1)S(1)}, bf16[128,1024]{1,0:T(8,128)(2,1)S(1)}, u32[]{:S(2)}, u32[]{:S(2)}) collective-permute-start(bf16[128,1024]{1,0:T(8,128)(2,1)S(1)} %get-tuple-element.95), channel_id=1, source_target_pairs={{0,8},{4,12},{8,0},{12,4},{16,24},{20,28},{24,16},{28,20},{1,9},{5... | collective-permute-start | bytes 786440 | tf_op jit(solution)/shard_map/ppermute | solution.py:403
  228.2 17.6 %collective-permute-start.55 = (bf16[128,1024]{1,0:T(8,128)(2,1)S(1)}, bf16[128,1024]{1,0:T(8,128)(2,1)S(1)}, u32[]{:S(2)}, u32[]{:S(2)}) collective-permute-start(bf16[128,1024]{1,0:T(8,128)(2,1)S(1)} %get-tuple-element.94), channel_id=1, source_target_pairs={{0,8},{4,12},{8,0},{12,4},{16,24},{20,28},{24,16},{28,20},{1,9},{5... | collective-permute-start | bytes 786440 | tf_op jit(solution)/shard_map/ppermute | solution.py:403
  (67 other events, 486.1 us)

commit v5 on v3

--- a/solution.py
+++ b/solution.py
@@ -12,7 +12,9 @@
 TOPK = 4
 F32 = jnp.float32
 BF16 = jnp.bfloat16
-VMEM_LIMIT = 40 * 1024 * 1024
+MIB = 1024 * 1024
+PAD = 16
+LOW = -(2.0**99)
 NN = (((1,), (0,)), ((), ()))
 NT = (((1,), (1,)), ((), ()))
 TN = (((0,), (0,)), ((), ()))
@@ -34,6 +36,11 @@
     return lists, refs[at:]
 
 
+def start(copies):
+    for copy in copies:
+        copy.start()
+
+
 def whole(refs):
     return joined([ref[...] for ref in refs], 0)
 
@@ -53,68 +60,39 @@
     return jnp.concatenate([top, low], axis=0)
 
 
-def gate_kernel(me_ref, sel_ref, mine_ref, other_ref, q_ref, aux_ref, mark_ref):
-    chips, block_count, width = mine_ref.shape
-    block_total = 2 * chips * block_count
-    rows = q_ref.shape[0]
-    me = me_ref[0]
-    for j in range(chips):
-        mark_ref[me ^ (2 * j)] = mine_ref[j]
-        mark_ref[me ^ (2 * j + 1)] = other_ref[j]
-    heads = width // HD
-    scale = HD ** (-0.5)
-    ids = lax.broadcasted_iota(jnp.int32, (block_total, rows), 0)
-    picks = [sel_ref[t : t + 1, :] == ids for t in range(TOPK)]
-    chosen = picks[0]
-    for t in range(1, TOPK):
-        chosen = chosen | picks[t]
-    bias = jnp.where(chosen, 0.0, -1e30)
-    gates = [[None] * heads for _ in range(TOPK)]
-    for h in range(heads):
-        cols = slice(h * HD, (h + 1) * HD)
-        marks = mark_ref[:, :, cols].reshape(block_total, HD)
-        logits = scale * mm(marks, q_ref[:, cols], NT) + bias
-        weight = jnp.exp(logits - jnp.max(logits, axis=0, keepdims=True))
-        inverse = 1.0 / jnp.sum(weight, axis=0, keepdims=True)
-        for t in range(TOPK):
-            gates[t][h] = inverse * jnp.sum(
-                jnp.where(picks[t], weight, 0.0), axis=0, keepdims=True
-            )
-    high = (sel_ref[...] >> 4).astype(F32)
-    low = (sel_ref[...] & 15).astype(F32)
-    lines = [gates[t][h] for t in range(TOPK) for h in range(heads)] + [high, low]
-    lines.append(jnp.zeros((HD - TOPK * heads - 2 * TOPK, rows), F32))
-    aux_ref[...] = jnp.concatenate(lines, axis=0).astype(BF16)
-
-
-def block_ids(aux, heads):
-    at = TOPK * heads
-    return 16.0 * aux[at : at + TOPK] + aux[at + TOPK : at + 2 * TOPK]
-
-
-def forward_kernel(counts, span, cap, me_ref, mine_ref, other_ref, k_ref, v_ref, *refs):
+def pack_kernel(sel_ref, q_ref, out_ref):
+    rows, width = q_ref.shape
+    out_ref[:rows] = q_ref[...]
+    digits = [(sel_ref[...] >> 4).astype(F32), (sel_ref[...] & 15).astype(F32)]
+    if width > 2 * rows:
+        digits.append(jnp.zeros((TOPK, width - 2 * rows), F32))
+    lines = [jnp.concatenate(digits, axis=1), jnp.zeros((PAD - TOPK, width), F32)]
+    out_ref[rows:] = jnp.concatenate(lines, axis=0).astype(BF16)
+
+
+def forward_kernel(counts, span, cap, me_ref, mark_ref, k_ref, v_ref, *refs):
     chunks = len(counts)
     q_refs, refs = dealt(refs, counts)
     part_refs, refs = refs[:chunks], refs[chunks:]
-    qg_ref, p_ref, gate_ref, hot_ref, auxg_ref, out_ref = refs
-    aux_refs = [(other_ref if m % 2 else mine_ref).at[m // 2] for m in range(chunks)]
+    qg_ref, p_ref, logit_ref, hot_ref, topg_ref, out_ref = refs
     block_count, _, width = k_ref.shape
     heads = width // HD
     rows = part_refs[0].shape[0]
     group_rows = rows * span
     groups = chunks // span
-    me = me_ref[0]
-    rate = HD ** (-0.5) * 1.4426950408889634
-    base = me * block_count
+    scale = HD ** (-0.5)
+    rate = scale * 1.4426950408889634
+    base = me_ref[0] * block_count
 
     before = lax.broadcasted_iota(jnp.int32, (group_rows, group_rows), 0)
-    after = lax.broadcasted_iota(jnp.int32, (group_rows, group_rows), 1)
-    earlier = (before < after).astype(BF16)
+    later = lax.broadcasted_iota(jnp.int32, (group_rows, group_rows), 1)
+    earlier = (before < later).astype(BF16)
     own_ids = (base + lax.broadcasted_iota(jnp.int32, (block_count, group_rows), 0)).astype(F32)
     place = lax.broadcasted_iota(jnp.int32, (cap, group_rows), 0).astype(F32)
     for g in range(groups):
-        aux = joined([aux_refs[g * span + i][...] for i in range(span)], 1)
-        picked = block_ids(aux.astype(F32), heads)
+        packs = [whole(q_refs[g * span + i]) for i in range(span)]
+        digits = [pack[rows : rows + PAD].astype(F32)[:TOPK] for pack in packs]
+        picked = joined([16.0 * d[:, :rows] + d[:, rows : 2 * rows] for d in digits], 1)
         own = picked[0:1, :] == own_ids
         for t in range(1, TOPK):
             own = own | (picked[t : t + 1, :] == own_ids)
@@ -124,8 +102,24 @@
             [jnp.where(rank[b : b + 1, :] == place, 1.0, 0.0) for b in range(block_count)], axis=0
         ).astype(BF16)
         hot_ref[g] = hot
-        auxg_ref[:, g * cap : (g + 1) * cap, :] = mm(hot, aux, NT).reshape(block_count, cap, HD)
-        q_group = joined([whole(q_refs[g * span + i]) for i in range(span)], 0)
+        q_group = joined([pack[:rows] for pack in packs], 0)
+        tops, sums = [], []
+        for h in range(heads):
+            cols = slice(h * HD, (h + 1) * HD)
+            marks = scale * mm(mark_ref[:, cols], q_group[:, cols], NT)
+            marks = jnp.where(own > 0.5, marks, LOW)
+            top = jnp.max(marks, axis=0, keepdims=True).astype(BF16).astype(F32)
+            tops.append(top)
+            sums.append(jnp.sum(own * jnp.exp(marks - top), axis=0, keepdims=True))
+        tops, sums = jnp.concatenate(tops, axis=0), jnp.concatenate(sums, axis=0)
+        upper = sums.astype(BF16).astype(F32)
+        spare = jnp.zeros((HD - 3 * heads, group_rows), F32)
+        tail = jnp.concatenate([tops, upper, sums - upper, spare], axis=0)
+        topg_ref[:, g * cap : (g + 1) * cap, :] = mm(hot, tail.astype(BF16), NT).reshape(
+            block_count, cap, HD
+        )
+        for i in range(span):
+            part_refs[g * span + i][:, width:] = tail[:, i * rows : (i + 1) * rows].T.astype(BF16)
         qg_ref[:, g * cap : (g + 1) * cap, :] = (
             mm(hot, q_group).astype(BF16).reshape(block_count, cap, width)
         )
@@ -134,14 +128,12 @@
         pairs = [slice(p * 2 * HD, (p + 1) * 2 * HD) for p in range(heads // 2)]
         logits = [mm(diagonal(k_ref[b, :, cols]), qg_ref[b, :, cols], NT) for cols in pairs]
         wide = [diagonal(v_ref[b, :, cols]) for cols in pairs]
-        aux = auxg_ref[b].T
-        ids = block_ids(aux, heads)
-        mine = (base + b).astype(F32)
-        gates = jnp.where(ids[0:1] == mine, aux[:heads], 0.0)
-        for t in range(1, TOPK):
-            gates = gates + jnp.where(
-                ids[t : t + 1] == mine, aux[t * heads : (t + 1) * heads], 0.0
-            )
+        tops = topg_ref[b].T[:heads]
+        marks = scale * jnp.concatenate(
+            [logits[h // 2][(h % 2 + 1) * BLOCK - 1 : (h % 2 + 1) * BLOCK] for h in range(heads)],
+            axis=0,
+        )
+        gates = jnp.exp(marks - tops)
         probs, gated = [], []
         for p in range(heads // 2):
             for i in range(2):
@@ -155,7 +147,7 @@
             mm(jnp.concatenate(gated[2 * p : 2 * p + 2], axis=0), wide[p], TN).astype(BF16)
             for p in range(heads // 2)
         ]
-        gate_ref[b] = gates
+        logit_ref[b] = marks
         for p in range(heads // 2):
             p_ref[b, p] = jnp.concatenate(probs[2 * p : 2 * p + 2], axis=0)
             out_ref[b, :, pairs[p]] = outs[p]
@@ -167,33 +159,93 @@
         slots = out_ref[:, g * cap : (g + 1) * cap, :].reshape(block_count * cap, width)
         part = mm(hot_ref[g], slots, TN).astype(BF16)
         for i in range(span):
-            part_refs[g * span + i][...] = part[i * rows : (i + 1) * rows]
+            part_refs[g * span + i][:, :width] = part[i * rows : (i + 1) * rows]
+
+
+def blend(terms, heads):
+    width = heads * HD
+    tails = [joined([ref[rows, width:] for ref, rows in term], 0).astype(F32) for term in terms]
+    top = tails[0]
+    for tail in tails[1:]:
+        top = jnp.maximum(top, tail)
+    tops, sums, columns = [], [], []
+    for h in range(heads):
+        cols = slice(h * HD, (h + 1) * HD)
+        peak = top[:, h : h + 1]
+        total, column = None, None
+        for term, tail in zip(terms, tails):
+            factor = jnp.exp(tail[:, h : h + 1] - peak)
+            low = 2 * heads + h
+            share = factor * (tail[:, heads + h : heads + h + 1] + tail[:, low : low + 1])
+            part = factor * joined([ref[rows, cols] for ref, rows in term], 0).astype(F32)
+            total = share if total is None else total + share
+            column = part if column is None else column + part
+        tops.append(peak)
+        sums.append(total)
+        columns.append(column)
+    return tops, sums, columns
+
+
+def tailed(groups, rows):
+    lane = lax.broadcasted_iota(jnp.int32, (rows, HD), 1)
+    tail = jnp.zeros((rows, HD), F32)
+    at = 0
+    for group in groups:
+        for column in group:
+            tail = jnp.where(lane == at, column, tail)
+            at += 1
+    return tail.astype(BF16)
+
+
+def digits_of(columns, count):
+    groups = []
+    for _ in range(count):
+        upper = [column.astype(BF16).astype(F32) for column in columns]
+        groups.append(upper)
+        columns = [column - part for column, part in zip(columns, upper)]
+    return groups
+
+
+def merge_kernel(plan, heads, *refs):
+    ins, outs = refs[: len(refs) - len(plan)], refs[len(refs) - len(plan) :]
+    for terms, out_ref in zip(plan, outs):
+        tops, sums, columns = blend(
+            [[(ins[i], pl.ds(first, count))] for i, first, count in terms], heads
+        )
+        for h in range(heads):
+            out_ref[:, h * HD : (h + 1) * HD] = columns[h].astype(BF16)
+        out_ref[:, heads * HD :] = tailed([tops] + digits_of(sums, 2), out_ref.shape[0])
 
 
 def grad_kernel(lines, chips, at_ref, w_ref, *refs):
     own_ref, up_refs, down_refs = refs[0], refs[1:lines], refs[lines : 2 * lines - 1]
     ga_ref, slab_refs = refs[2 * lines - 1], refs[2 * lines : 2 * lines + chips]
-    full_ref, w_buf, sems = refs[2 * lines + chips :]
+    full_ref, w_buf, sems, piece_sems = refs[2 * lines + chips :]
     width = own_ref.shape[1]
     share = slab_refs[0].shape[1]
     line, chip = at_ref[0], at_ref[1]
+
+    def placed(ref, i):
+        return pltpu.make_async_copy(ref, full_ref.at[i], piece_sems.at[i])
+
+    placed(own_ref, line).start()
+    for d in range(1, lines):
+
+        @pl.when(line >= d)
+        def _():
+            placed(up_refs[d - 1], line - d).start()
+
+        @pl.when(line + d < lines)
+        def _():
+            placed(down_refs[d - 1], line + d).start()
+
     copies = [
         pltpu.make_async_copy(w_ref.at[pl.ds(i * width, width)], w_buf.at[i], sems.at[i])
         for i in range(lines)
     ]
-    for copy in copies:
-        copy.start()
-    full_ref[line] = own_ref[...]
-    for d in range(1, lines):
-
-        @pl.when(line >= d)
-        def _():
-            full_ref[line - d] = up_refs[d - 1][...]
-
-        @pl.when(line + d < lines)
-        def _():
-            full_ref[line + d] = down_refs[d - 1][...]
-
+    start(copies)
+    for i in range(lines):
+        placed(own_ref, i).wait()
     for j in range(chips):
         first = (chip ^ j) * share
         cols = pl.ds(pl.multiple_of(first % width, HD), share)
@@ -210,19 +262,18 @@
     terms, (ga_ref, attn_ref, ext_ref) = dealt(refs, counts)
     rows, width = ga_ref.shape
     heads = width // HD
-    lane = lax.broadcasted_iota(jnp.int32, (rows, HD), 1)
-    high = jnp.zeros((rows, HD), F32)
-    low = jnp.zeros((rows, HD), F32)
+    tops, sums, columns = blend(
+        [[(ref, slice(None)) for ref in pieces] for pieces in terms], heads
+    )
     ext_ref[:, :width] = ga_ref[...]
+    dots, levels = [], []
     for h in range(heads):
         cols = slice(h * HD, (h + 1) * HD)
-        total = added(terms, cols)
+        total = columns[h] * (1.0 / sums[h])
         attn_ref[:, cols] = total.astype(BF16)
-        dots = jnp.sum(total * ga_ref[:, cols].astype(F32), axis=1, keepdims=True)
-        upper = dots.astype(BF16).astype(F32)
-        high = jnp.where(lane == h, upper, high)
-        low = jnp.where(lane == heads + h, dots - upper, low)
-    ext_ref[:, width:] = (high + low).astype(BF16)
+        dots.append(jnp.sum(total * ga_ref[:, cols].astype(F32), axis=1, keepdims=True))
+        levels.append(tops[h] + jnp.log(sums[h]))
+    ext_ref[:, width:] = tailed(digits_of(dots, 2) + digits_of(levels, 3), rows)
 
 
 def total_kernel(counts, *refs):
@@ -232,7 +283,7 @@
         out_ref[:, cols] = added(terms, cols)
 
 
-def backward_kernel(counts, span, cap, hot_ref, qg_ref, p_ref, gate_ref, k_ref, v_ref, *refs):
+def backward_kernel(counts, span, cap, hot_ref, qg_ref, p_ref, logit_ref, k_ref, v_ref, *refs):
     chunks = len(counts)
     ga_refs, refs = dealt(refs, counts)
     part_refs, refs = refs[:chunks], refs[chunks:]
@@ -257,9 +308,10 @@
         grads = [mm(diagonal(v_ref[b, :, cols]), ga[p], NT) for p, cols in enumerate(pairs)]
         wide = [diagonal(k_ref[b, :, cols]) for cols in pairs]
         probs = [p_ref[b, p].astype(F32) for p in range(heads // 2)]
-        gates = gate_ref[b]
-        dots = gag_ref[b, :, width:].astype(F32).T
-        dots = dots[:heads] + dots[heads : 2 * heads]
+        tail = gag_ref[b, :, width:].astype(F32).T
+        tail = [tail[i * heads : (i + 1) * heads] for i in range(5)]
+        dots = tail[0] + tail[1]
+        gates = jnp.exp(jnp.minimum(logit_ref[b] - (tail[2] + tail[3] + tail[4]), 0.0))
         gated, score = [], []
         for p in range(heads // 2):
             for i in range(2):
@@ -321,22 +373,31 @@
     return [x for pieces in lists for x in pieces]
 
 
-def spread_chips(x):
+def spread_chips(x, half):
     chips = lax.axis_size("ctx") // 2
+    near = [swap(x, 2 * j) for j in range(1, chips)] if chips != 4 else [swap(x, 2), swap(x, 4)]
     if chips != 4:
-        return [[x]] + [[swap(x, 2 * j)] for j in range(1, chips)]
-    half = x.shape[0] // 2
-    top, low = x[:half], x[half:]
-    x_top, y_low = swap(top, 2), swap(low, 4)
-    x_low, y_top = swap(low, 2), swap(top, 4)
-    return [[x], [x_top, x_low], [y_top, y_low], [swap(x_top, 4), swap(y_low, 2)]]
-
-
-def collect_chips(parts):
-    chips = len(parts) // 2
-    received = [None] * chips
-    for j in reversed(range(chips)):
-        received[j] = swap(parts[2 * j + 1], 1)
+        return [[x]] + [[piece] for piece in near]
+    far = [swap(near[0][:half], 4), swap(near[1][half:], 2)]
+    return [[x], [near[0]], [near[1]], far]
+
+
+def with_cores(lists, own):
+    both = [lists[0], [swap(own, 1)]]
+    for pieces in lists[1:]:
+        both += [pieces, [swap(piece, 1) for piece in pieces]]
+    return both
+
+
+def from_core(parts, *before):
+    received = [None] * (len(parts) // 2)
+    for j in reversed(range(len(received))):
+        received[j] = after(swap(parts[2 * j + 1], 1), *before)
+    return received
+
+
+def collect_chips(parts, received):
+    chips = len(received)
 
     def both(j, rows, extra=None):
         total = parts[2 * j][rows].astype(F32) + received[j][rows].astype(F32)
@@ -352,6 +413,45 @@
     x_far, y_far = swap(both(3, top), 2), swap(both(3, low), 4)
     x_top, y_low = swap(both(1, top), 2), swap(both(2, low), 4)
     x_low, y_top = swap(both(1, low, y_far), 2), swap(both(2, top, x_far), 4)
+    return terms + [[x_top, x_low], [y_top, y_low]]
+
+
+def merge_chips(parts, received, heads):
+    chips = len(received)
+    rows = parts[0].shape[0]
+    half = rows // 2
+
+    def merged(ins, plan):
+        return pl.pallas_call(
+            functools.partial(merge_kernel, plan, heads),
+            out_shape=[
+                jax.ShapeDtypeStruct((terms[0][2], ins[0].shape[1]), BF16) for terms in plan
+            ],
+            in_specs=[pl.BlockSpec(memory_space=pltpu.VMEM)] * len(ins),
+            out_specs=[pl.BlockSpec(memory_space=pltpu.VMEM)] * len(plan),
+            compiler_params=pltpu.CompilerParams(vmem_limit_bytes=24 * MIB),
+            name="merge",
+        )(*ins)
+
+    terms = [[parts[0]], [received[0]]]
+    if chips != 4:
+        for j in range(1, chips):
+            (both,) = merged([parts[2 * j], received[j]], [[(0, 0, rows), (1, 0, rows)]])
+            terms.append([swap(both, 2 * j)])
+        return terms
+    top, low = (0, half), (half, half)
+    x_far, y_far = merged(
+        [parts[6], received[3]], [[(0, *top), (1, *top)], [(0, *low), (1, *low)]]
+    )
+    x_far, y_far = swap(x_far, 2), swap(y_far, 4)
+    ins = [parts[2], received[1], parts[4], received[2]]
+    x_top, y_low = merged(ins, [[(0, *top), (1, *top)], [(2, *low), (3, *low)]])
+    x_top, y_low = swap(x_top, 2), swap(y_low, 4)
+    x_low, y_top = merged(
+        ins + [y_far, x_far],
+        [[(0, *low), (1, *low), (4, *top)], [(2, *top), (3, *top), (5, *top)]],
+    )
+    x_low, y_top = swap(x_low, 2), swap(y_top, 4)
     return terms + [[x_top, x_low], [y_top, y_low]]
 
 
@@ -386,78 +486,74 @@
     values = value_rows.reshape(block_count, BLOCK, width)
     vmem = pl.BlockSpec(memory_space=pltpu.VMEM)
     smem = pl.BlockSpec(memory_space=pltpu.SMEM)
-    params = pltpu.CompilerParams(vmem_limit_bytes=VMEM_LIMIT)
+    anywhere = pl.BlockSpec(memory_space=pl.ANY)
+
+    def limit(mib):
+        return pltpu.CompilerParams(vmem_limit_bytes=mib * MIB)
 
     def shaped(shape, kind=BF16):
         return jax.ShapeDtypeStruct(shape, kind)
 
-    marks = keys[:, BLOCK - 1]
-    marks = jnp.stack([marks] + [swap(marks, 2 * j) for j in range(1, chips)])
     ups, downs = spread_line(out_grad)
-    query_chips = spread_chips(queries)
-    aux = pl.pallas_call(
-        gate_kernel,
-        out_shape=shaped((HD, rows)),
-        in_specs=[smem] + [vmem] * 4,
+    packed = pl.pallas_call(
+        pack_kernel,
+        out_shape=shaped((rows + PAD, width)),
+        in_specs=[vmem] * 2,
         out_specs=vmem,
-        scratch_shapes=[pltpu.VMEM((chunks, block_count, width), BF16)],
-        compiler_params=params,
-        name="gates",
-    )(me, selected.T, marks, swap(marks, 1), queries)
-    aux = jnp.stack([aux] + [swap(aux, 2 * j) for j in range(1, chips)])
-    query_all = []
-    for pieces in query_chips:
-        query_all += [pieces, [swap(piece, 1) for piece in pieces]]
+        compiler_params=limit(8),
+        name="pack",
+    )(selected.T, queries)
+    query_chips = spread_chips(packed, rows // 2)
+    query_all = with_cores(query_chips, after(packed, ups[0], downs[0]))
 
     outs = pl.pallas_call(
         functools.partial(forward_kernel, [len(pieces) for pieces in query_all], span, cap),
-        out_shape=[shaped((rows, width))] * chunks
+        out_shape=[shaped((rows, width + HD))] * chunks
         + [
             shaped((block_count, slots, width)),
             shaped((block_count, heads // 2, 2 * BLOCK, slots)),
             shaped((block_count, heads, slots), F32),
             shaped((groups, block_count * cap, rows * span)),
         ],
-        in_specs=[smem] + [vmem] * (4 + len(flat(query_all))),
+        in_specs=[smem] + [vmem] * (3 + len(flat(query_all))),
         out_specs=[vmem] * (chunks + 4),
         scratch_shapes=[
             pltpu.VMEM((block_count, slots, HD), F32),
             pltpu.VMEM((block_count, slots, width), BF16),
         ],
-        compiler_params=params,
+        compiler_params=limit(40),
         name="forward",
-    )(me, aux, swap(aux, 1), keys, values, *flat(query_all))
-    q_slots, probs, gates, hot = outs[chunks:]
+    )(after(me, *ups[:2], *downs[:2]), keys[:, BLOCK - 1], keys, values, *flat(query_all))
+    q_slots, probs, logits, hot = outs[chunks:]
 
     grad_attn, *slabs = pl.pallas_call(
         functools.partial(grad_kernel, lines, chips),
         out_shape=[shaped((rows, width))] + [shaped((rows, share))] * chips,
-        in_specs=[smem, pl.BlockSpec(memory_space=pl.ANY)] + [vmem] * (2 * lines - 1),
+        in_specs=[smem] + [anywhere] * (2 * lines),
         out_specs=[vmem] * (1 + chips),
         scratch_shapes=[
             pltpu.VMEM((lines, rows, width), BF16),
             pltpu.VMEM((lines, width, width), BF16),
             pltpu.SemaphoreType.DMA((lines,)),
+            pltpu.SemaphoreType.DMA((lines,)),
         ],
-        compiler_params=params,
+        compiler_params=limit(24),
         name="grad",
     )(at, out_weight, out_grad, *ups, *downs)
-    terms = collect_chips(outs[:chunks])
+    terms = merge_chips(outs[:chunks], from_core(outs[:chunks], grad_attn), heads)
     attn_out, extended = pl.pallas_call(
         functools.partial(finish_kernel, [len(pieces) for pieces in terms]),
         out_shape=[shaped((rows, width)), shaped((rows, width + HD))],
         in_specs=[vmem] * (len(flat(terms)) + 1),
         out_specs=[vmem] * 2,
-        compiler_params=params,
+        compiler_params=limit(24),
         name="finish",
     )(*flat(terms), grad_attn)
-    grad_chips = spread_chips(extended)
-    grad_all = []
-    for pieces in grad_chips:
-        grad_all += [pieces, [swap(piece, 1) for piece in pieces]]
-
-    arrived = flat(grad_chips)
-    attns = spread_chips(after(attn_out, *arrived))
+    grad_chips = spread_chips(extended, rows // 2)
+    grad_all = with_cores(grad_chips, extended)
+
+    arrived = flat(grad_chips[1:3])
+    attns = [[attn_out]] + [[swap(after(attn_out, *arrived), 2 * j)] for j in range(1, chips)]
     slabs = [slabs[0]] + [swap(after(slabs[j], *arrived), 2 * j) for j in range(1, chips)]
 
     outs = pl.pallas_call(
@@ -470,17 +566,17 @@
             pltpu.VMEM((block_count, slots, width + HD), BF16),
             pltpu.VMEM((block_count, slots, width), BF16),
         ],
-        compiler_params=params,
+        compiler_params=limit(44),
         name="backward",
-    )(hot, q_slots, probs, gates, keys, values, *flat(grad_all))
+    )(hot, q_slots, probs, logits, keys, values, *flat(grad_all))
     key_grad, value_grad = outs[chunks:]
-    terms = collect_chips(outs[:chunks])
+    terms = collect_chips(outs[:chunks], from_core(outs[:chunks], *flat(attns[1:])))
     query_grad = pl.pallas_call(
         functools.partial(total_kernel, [len(pieces) for pieces in terms]),
         out_shape=shaped((rows, width), F32),
         in_specs=[vmem] * len(flat(terms)),
         out_specs=vmem,
-        compiler_params=params,
+        compiler_params=limit(24),
         name="total",
     )(*flat(terms))
 
@@ -489,9 +585,9 @@
         out_shape=[shaped((share // 2, width), F32), shaped((share // 2, width))],
         in_specs=[smem] + [vmem] * (chips + len(flat(attns))),
         out_specs=[vmem] * 2,
-        compiler_params=params,
+        compiler_params=limit(24),
         name="weight",
-    )(me, *slabs, *flat(attns))
+    )(after(me, terms[2][0], terms[-1][-1]), *slabs, *flat(attns))
     weight_grad = weight_own + swap(weight_other, 1).astype(F32)
     return (
         query_grad,

time: 210 us -> 229 us (1.090)
  Pallas kernels: 42.7 us -> 55.6 us
  waiting for transfers between devices: 95.2 us -> 104 us
  local copies, waits for them, and re-layouts: 12 us -> 20.7 us
  starting transfers between devices: 53.2 us -> 44.8 us
    ppermute x64 -> x45, starting transfers between devices: 44.4 us -> 35.2 us  [swap(): return lax.ppermute(x, 'ctx', [(i, i ^ bits) for i in range(count)])]
    ppermute x3, waiting for transfers between devices: 16.9 us -> 26.1 us  [spread_line(): lax.ppermute(downs[-1], 'head', [(i, i - 1) for i in range(1, lines - d +...]
    unnamed x43 -> x51, local copies, waits for them, and re-layouts: 10.7 us -> 19.6 us
    pallas_call x1 -> x4, Pallas kernels: 1 us -> 6.92 us  [the longest x3 6.88 us: merged(): pl.pallas_call(functools.partial(merge_kernel, plan, heads), out_shape=[j...]
    pallas_call x1, Pallas kernels: 14.1 us -> 18.4 us  [body(): pl.pallas_call(functools.partial(forward_kernel, [len(pieces) for pieces...]
    ppermute x64 -> x45, waiting for transfers between devices: 78.3 us -> 78.2 us  [swap(): return lax.ppermute(x, 'ctx', [(i, i ^ bits) for i in range(count)])]
  transfers between devices with their start and end apart: 70 -> 51, of which waited for: 29 -> 19; matrix products, arithmetic and copies ran while one was open for 1% -> 1% of each run, Pallas kernels for 19% -> 14%
where the time goes in v5:
time: 229 us
  waiting for transfers between devices  104 us (45%)
  Pallas kernels  55.6 us (24%)
  starting transfers between devices  44.8 us (20%)
  local copies, waits for them, and re-layouts  20.7 us (9%)
  other arithmetic  2.37 us (1%)
    ppermute x45, waiting for transfers between devices, swap(): return lax.ppermute(x, 'ctx', [(i, i ^ bits) for i in range(count)])  78.2 us
    ppermute x45, starting transfers between devices, swap(): return lax.ppermute(x, 'ctx', [(i, i ^ bits) for i in range(count)])  35.2 us
    ppermute x3, waiting for transfers between devices, spread_line(): lax.ppermute(downs[-1], 'head', [(i, i - 1) for i in range(1, lines - d +...  26.1 us
    unnamed x51, local copies, waits for them, and re-layouts  19.6 us
    pallas_call x1, Pallas kernels, body(): pl.pallas_call(functools.partial(backward_kernel, [len(pieces) for pieces...  18.8 us
    pallas_call x1, Pallas kernels, body(): pl.pallas_call(functools.partial(forward_kernel, [len(pieces) for pieces...  18.4 us
    pallas_call x3, Pallas kernels, merged(): pl.pallas_call(functools.partial(merge_kernel, plan, heads), out_shape=[j...  6.88 us
    ppermute x3, starting transfers between devices, spread_line(): lax.ppermute(ups[-1], 'head', [(i, i + 1) for i in range(d - 1, lines - 1)])  5.69 us
  transfers between devices with their start and end apart: 51, of which 19 were waited for; matrix products, arithmetic and copies ran while one was open for 1% of the time, Pallas kernels for 14%

profile of v5, /device:TPU:0, one launch (start us, length us, event | category | flops | bytes accessed | tf_op | source)
XLA Modules:
  0.0 228.6 jit_solution(902708086443472272)
XLA Ops:
  2.6 3.0 %collective-permute-start.7 = (bf16[272,1024]{1,0:T(8,128)(2,1)S(1)}, bf16[272,1024]{1,0:T(8,128)(2,1)S(1)}, u32[]{:S(2)}, u32[]{:S(2)}) collective-permute-start(bf16[272,1024]{1,0:T(8,128)(2,1)S(1)} %pack.1.refs_0_), channel_id=1, source_target_pairs={{0,16},{4,20},{8,24},{12,28},{16,0},{20,4},{24,8},{28,12},{1,17},{... | collective-permute-start | bytes 1671176 | tf_op jit(solution)/shard_map/ppermute | solution.py:365
  7.1 3.5 %collective-permute-start = (bf16[256,1024]{1,0:T(8,128)(2,1)}, bf16[256,1024]{1,0:T(8,128)(2,1)S(1)}, u32[]{:S(2)}, u32[]{:S(2)}) collective-permute-start(bf16[256,1024]{1,0:T(8,128)(2,1)} %refs_0_.1), channel_id=1, source_target_pairs={{0,1},{1,2},{2,3},{4,5},{5,6},{6,7},{8,9},{9,10},{10,11},{12,13},{... | collective-permute-start | bytes 1572872 | tf_op jit(solution)/shard_map/ppermute | solution.py:462
  11.9 6.3 %collective-permute-done.7.refs_4_ = bf16[272,1024]{1,0:T(8,128)(2,1)S(1)} collective-permute-done((bf16[272,1024]{1,0:T(8,128)(2,1)S(1)}, bf16[272,1024]{1,0:T(8,128)(2,1)S(1)}, u32[]{:S(2)}, u32[]{:S(2)}) %collective-permute-start.7) | collective-permute-done | bytes 557088 | tf_op jit(solution)/shard_map/ppermute | solution.py:365
  29.5 12.1 %collective-permute-done.3.refs_5_ = bf16[256,1024]{1,0:T(8,128)(2,1)} collective-permute-done((bf16[256,1024]{1,0:T(8,128)(2,1)S(1)}, bf16[256,1024]{1,0:T(8,128)(2,1)}, u32[]{:S(2)}, u32[]{:S(2)}) %collective-permute-start.3) | collective-permute-done | bytes 524320 | tf_op jit(solution)/shard_map/ppermute | solution.py:463
  46.6 18.4 %forward.1 = (bf16[256,1152]{1,0:T(8,128)(2,1)S(1)}, bf16[256,1152]{1,0:T(8,128)(2,1)S(1)}, bf16[256,1152]{1,0:T(8,128)(2,1)S(1)}, bf16[256,1152]{1,0:T(8,128)(2...) custom-call(s32[1]{0:T(128)} %bitcast.me_ref, ...), custom_call_target="tpu_custom_call" | custom-call | tf_op jit(solution)/shard_map/forward/pallas_call | solution.py:509
  72.9 13.3 %collective-permute-done.15.refs_6_ = bf16[256,1024]{1,0:T(8,128)(2,1)} collective-permute-done((bf16[256,1024]{1,0:T(8,128)(2,1)}, bf16[256,1024]{1,0:T(8,128)(2,1)}, u32[]{:S(2)}, u32[]{:S(2)}) %collective-permute-start.15) | collective-permute-done | bytes 524320 | tf_op jit(solution)/shard_map/ppermute | solution.py:463
  86.2 3.4 %copy-done.1 = bf16[4096,1024]{1,0:T(8,128)(2,1)S(1)} copy-done((bf16[4096,1024]{1,0:T(8,128)(2,1)S(1)}, bf16[4096,1024]{1,0:T(8,128)(2,1)}, u32[]{:S(2)}) %copy-start.1) | copy-done | bytes 8388632
  93.7 4.6 %grad.1 = (bf16[256,1024]{1,0:T(8,128)(2,1)S(1)}, bf16[256,1024]{1,0:T(8,128)(2,1)S(1)}, bf16[256,1024]{1,0:T(8,128)(2,1)S(1)}, bf16[256,1024]{1,0:T(8,128)(2,1)S(1)}, bf16[256,1024]{1,0:T(8,128)(2,1)S(1)}) custom-call(s32[2]{0:T(128)S(1)} %pad_add_fusion.at_ref, bf16[4096,1024]{1,0:T(8,128)(2,1)S(1)} %copy-done.1, bf16[256,1024]{1,0:T(8,128)(2,1)S(1)} %copy-done.13, ...), custom_call_target="tpu_custom_call" | custom-call | tf_op jit(solution)/shard_map/grad/pallas_call | solution.py:529
  98.4 2.8 %merge.4 = (bf16[128,1152]{1,0:T(8,128)(2,1)S(1)}, bf16[128,1152]{1,0:T(8,128)(2,1)S(1)}) custom-call(bf16[256,1152]{1,0:T(8,128)(2,1)S(1)} %copy-done.10, bf16[256,1152]{1,0:T(8,128)(2,1)} %collective-permute-done.19.refs_1_), custom_call_target="tpu_custom_call" | custom-call | tf_op jit(solution)/shard_map/merge/pallas_call | solution.py:425
  107.2 4.0 %collective-permute-done.20.refs_4_ = bf16[128,1152]{1,0:T(8,128)(2,1)S(1)} collective-permute-done((bf16[128,1152]{1,0:T(8,128)(2,1)S(1)}, bf16[128,1152]{1,0:T(8,128)(2,1)S(1)}, u32[]{:S(2)}, u32[]{:S(2)}) %collective-permute-start.20) | collective-permute-done | bytes 294944 | tf_op jit(solution)/shard_map/ppermute | solution.py:365
  111.7 2.3 %merge.5 = (bf16[128,1152]{1,0:T(8,128)(2,1)S(1)}, bf16[128,1152]{1,0:T(8,128)(2,1)S(1)}) custom-call(bf16[256,1152]{1,0:T(8,128)(2,1)S(1)} %get-tuple-element.66.refs_0_, bf16[256,1152]{1,0:T(8,128)(2,1)S(1)} %collective-permute-done.16.refs_1_, bf16[256,1152]{1,0:T(8,128)(2,1)S(1)} %get-tuple-element.69.refs_2_, ...), custom_call_target="tpu_custom_call" | custom-call | tf_op jit(solution)/shard_map/merge/pallas_call | solution.py:425
  116.2 1.9 collective-permute-done.18.refs_2_
  118.0 4.6 %collective-permute-done.22.refs_3_ = bf16[128,1152]{1,0:T(8,128)(2,1)S(1)} collective-permute-done((bf16[128,1152]{1,0:T(8,128)(2,1)S(1)}, bf16[128,1152]{1,0:T(8,128)(2,1)S(1)}, u32[]{:S(2)}, u32[]{:S(2)}) %collective-permute-start.22) | collective-permute-done | bytes 294944 | tf_op jit(solution)/shard_map/ppermute | solution.py:365
  122.6 3.2 %finish.1 = (bf16[256,1024]{1,0:T(8,128)(2,1)S(1)}, bf16[256,1152]{1,0:T(8,128)(2,1)S(1)}) custom-call(bf16[256,1152]{1,0:T(8,128)(2,1)S(1)} %copy-done.12, bf16[256,1152]{1,0:T(8,128)(2,1)S(1)} %collective-permute-done.13.refs_1_, bf16[128,1152]{1,0:T(8,128)(2,1)S(1)} %collective-permute-done.18.refs_2_, ...), custom_call_target="tpu_custom_call" | custom-call | tf_op jit(solution)/shard_map/finish/pallas_call | solution.py:544
  127.9 11.5 %collective-permute-done.26.refs_2_ = bf16[256,1152]{1,0:T(8,128)(2,1)S(1)} collective-permute-done((bf16[256,1152]{1,0:T(8,128)(2,1)S(1)}, bf16[256,1152]{1,0:T(8,128)(2,1)S(1)}, u32[]{:S(2)}, u32[]{:S(2)}) %collective-permute-start.26) | collective-permute-done | bytes 589856 | tf_op jit(solution)/shard_map/ppermute | solution.py:365
  142.2 4.4 %collective-permute-done.30.refs_6_ = bf16[128,1152]{1,0:T(8,128)(2,1)S(1)} collective-permute-done((bf16[128,1152]{1,0:T(8,128)(2,1)S(1)}, bf16[128,1152]{1,0:T(8,128)(2,1)S(1)}, u32[]{:S(2)}, u32[]{:S(2)}) %collective-permute-start.30) | collective-permute-done | bytes 294944 | tf_op jit(solution)/shard_map/ppermute | solution.py:365
  146.6 4.0 %collective-permute-done.31.refs_7_ = bf16[128,1152]{1,0:T(8,128)(2,1)S(1)} collective-permute-done((bf16[128,1152]{1,0:T(8,128)(2,1)S(1)}, bf16[128,1152]{1,0:T(8,128)(2,1)S(1)}, u32[]{:S(2)}, u32[]{:S(2)}) %collective-permute-start.31) | collective-permute-done | bytes 294944 | tf_op jit(solution)/shard_map/ppermute | solution.py:365
  151.2 2.1 collective-permute-start.36
  154.1 18.8 %backward.1 = (bf16[256,1024]{1,0:T(8,128)(2,1)S(1)}, bf16[256,1024]{1,0:T(8,128)(2,1)S(1)}, bf16[256,1024]{1,0:T(8,128)(2,1)S(1)}, bf16[256,1024]{1,0:T(8,128)(...) custom-call(bf16[8,256,256]{2,1,0:T(8,128)(2,1)S(1)} %copy-done.8, ...), custom_call_target="tpu_custom_call" | custom-call | tf_op jit(solution)/shard_map/backward/pallas_call | solution.py:559
  173.4 3.4 %collective-permute-done.36.refs_6_ = bf16[256,1024]{1,0:T(8,128)(2,1)S(1)} collective-permute-done((bf16[256,1024]{1,0:T(8,128)(2,1)S(1)}, bf16[256,1024]{1,0:T(8,128)(2,1)S(1)}, u32[]{:S(2)}, u32[]{:S(2)}) %collective-permute-start.36) | collective-permute-done | bytes 524320 | tf_op jit(solution)/shard_map/ppermute | solution.py:365
  182.7 3.7 %collective-permute-done.41 = bf16[128,1024]{1,0:T(8,128)(2,1)S(1)} collective-permute-done((bf16[128,1024]{1,0:T(8,128)(2,1)S(1)}, bf16[128,1024]{1,0:T(8,128)(2,1)S(1)}, u32[]{:S(2)}, u32[]{:S(2)}) %collective-permute-start.41) | collective-permute-done | bytes 262176 | tf_op jit(solution)/shard_map/ppermute | solution.py:365
  189.0 25.3 %collective-permute-done.39.refs_2_ = bf16[128,1024]{1,0:T(8,128)(2,1)S(1)} collective-permute-done((bf16[128,1024]{1,0:T(8,128)(2,1)S(1)}, bf16[128,1024]{1,0:T(8,128)(2,1)S(1)}, u32[]{:S(2)}, u32[]{:S(2)}) %collective-permute-start.39) | collective-permute-done | bytes 262176 | tf_op jit(solution)/shard_map/ppermute | solution.py:365
  214.3 2.4 %weight.1 = (f32[512,1024]{1,0:T(8,128)S(1)}, bf16[512,1024]{1,0:T(8,128)(2,1)S(1)}) custom-call(s32[1]{0:T(128)} %bitcast.me_ref, bf16[256,1024]{1,0:T(8,128)(2,1)S(1)} %get-tuple-element.99.refs_0_, bf16[256,1024]{1,0:T(8,128)(2,1)S(1)} %collective-permute-done.47.refs_1_, bf16[256,1024]{1,0:T(8,128)(2,1)S(1)} %collective-permute-done.48.refs_2_, ...), custom_call_target="tpu_custom_call" | custom-call | tf_op jit(solution)/shard_map/weight/pallas_call | solution.py:583
  220.2 5.4 %collective-permute-done.42.refs_3_ = bf16[128,1024]{1,0:T(8,128)(2,1)S(1)} collective-permute-done((bf16[128,1024]{1,0:T(8,128)(2,1)S(1)}, bf16[128,1024]{1,0:T(8,128)(2,1)S(1)}, u32[]{:S(2)}, u32[]{:S(2)}) %collective-permute-start.42) | collective-permute-done | bytes 262176 | tf_op jit(solution)/shard_map/ppermute | solution.py:365
  (149 shorter events, 63.4 us)
Async XLA Ops:
  2.6 15.7 %collective-permute-start.7 = (bf16[272,1024]{1,0:T(8,128)(2,1)S(1)}, bf16[272,1024]{1,0:T(8,128)(2,1)S(1)}, u32[]{:S(2)}, u32[]{:S(2)}) collective-permute-start(bf16[272,1024]{1,0:T(8,128)(2,1)S(1)} %pack.1.refs_0_), channel_id=1, source_target_pairs={{0,16},{4,20},{8,24},{12,28},{16,0},{20,4},{24,8},{28,12},{1,17},{... | collective-permute-start | bytes 1671176 | tf_op jit(solution)/shard_map/ppermute | solution.py:365
  5.6 14.4 %collective-permute-start.5 = (bf16[272,1024]{1,0:T(8,128)(2,1)S(1)}, bf16[272,1024]{1,0:T(8,128)(2,1)}, u32[]{:S(2)}, u32[]{:S(2)}) collective-permute-start(bf16[272,1024]{1,0:T(8,128)(2,1)S(1)} %pack.1.refs_0_), channel_id=1, source_target_pairs={{0,8},{4,12},{8,0},{12,4},{16,24},{20,28},{24,16},{28,20},{1,9},{5... | collective-permute-start | bytes 1671176 | tf_op jit(solution)/shard_map/ppermute | solution.py:365
  7.1 15.5 %collective-permute-start = (bf16[256,1024]{1,0:T(8,128)(2,1)}, bf16[256,1024]{1,0:T(8,128)(2,1)S(1)}, u32[]{:S(2)}, u32[]{:S(2)}) collective-permute-start(bf16[256,1024]{1,0:T(8,128)(2,1)} %refs_0_.1), channel_id=1, source_target_pairs={{0,1},{1,2},{2,3},{4,5},{5,6},{6,7},{8,9},{9,10},{10,11},{12,13},{... | collective-permute-start | bytes 1572872 | tf_op jit(solution)/shard_map/ppermute | solution.py:462
  10.6 14.9 %collective-permute-start.2 = (bf16[256,1024]{1,0:T(8,128)(2,1)}, bf16[256,1024]{1,0:T(8,128)(2,1)S(1)}, u32[]{:S(2)}, u32[]{:S(2)}) collective-permute-start(bf16[256,1024]{1,0:T(8,128)(2,1)} %refs_0_.1), channel_id=1, source_target_pairs={{1,0},{2,1},{3,2},{5,4},{6,5},{7,6},{9,8},{10,9},{11,10},{13,12},{... | collective-permute-start | bytes 1572872 | tf_op jit(solution)/shard_map/ppermute | solution.py:463
  25.5 16.1 %collective-permute-start.3 = (bf16[256,1024]{1,0:T(8,128)(2,1)S(1)}, bf16[256,1024]{1,0:T(8,128)(2,1)}, u32[]{:S(2)}, u32[]{:S(2)}) collective-permute-start(bf16[256,1024]{1,0:T(8,128)(2,1)S(1)} %collective-permute-done.2.refs_4_), channel_id=1, source_target_pairs={{1,0},{2,1},{5,4},{6,5},{9,8},{10,9},{13,12},{14,13},{17,16},{18,1... | collective-permute-start | bytes 1572872 | tf_op jit(solution)/shard_map/ppermute | solution.py:463
  27.6 14.1 %collective-permute-start.4 = (bf16[272,1024]{1,0:T(8,128)(2,1)S(1)}, bf16[272,1024]{1,0:T(8,128)(2,1)}, u32[]{:S(2)}, u32[]{:S(2)}) collective-permute-start(bf16[272,1024]{1,0:T(8,128)(2,1)S(1)} %pack.1.refs_0_), channel_id=1, source_target_pairs={{0,4},{4,0},{8,12},{12,8},{16,20},{20,16},{24,28},{28,24},{1,5},{5... | collective-permute-start | bytes 1671176 | tf_op jit(solution)/shard_map/ppermute | solution.py:365
  28.2 15.3 %collective-permute-start.6 = (bf16[272,1024]{1,0:T(8,128)(2,1)}, bf16[272,1024]{1,0:T(8,128)(2,1)}, u32[]{:S(2)}, u32[]{:S(2)}) collective-permute-start(bf16[272,1024]{1,0:T(8,128)(2,1)} %collective-permute-done.5.refs_2_), channel_id=1, source_target_pairs={{0,4},{4,0},{8,12},{12,8},{16,20},{20,16},{24,28},{28,24},{1,5},{5... | collective-permute-start | bytes 1671176 | tf_op jit(solution)/shard_map/ppermute | solution.py:365
  28.2 15.3 %collective-permute-start.8 = (bf16[272,1024]{1,0:T(8,128)(2,1)S(1)}, bf16[272,1024]{1,0:T(8,128)(2,1)}, u32[]{:S(2)}, u32[]{:S(2)}) collective-permute-start(bf16[272,1024]{1,0:T(8,128)(2,1)S(1)} %collective-permute-done.7.refs_4_), channel_id=1, source_target_pairs={{0,4},{4,0},{8,12},{12,8},{16,20},{20,16},{24,28},{28,24},{1,5},{5... | collective-permute-start | bytes 1671176 | tf_op jit(solution)/shard_map/ppermute | solution.py:365
  28.7 14.8 %collective-permute-start.12 = (bf16[144,1024]{1,0:T(8,128)(2,1)S(1)}, bf16[144,1024]{1,0:T(8,128)(2,1)}, u32[]{:S(2)}, u32[]{:S(2)}) collective-permute-start(bf16[144,1024]{1,0:T(8,128)(2,1)S(1)} %collective-permute-done.10.refs_7_), channel_id=1, source_target_pairs={{0,4},{4,0},{8,12},{12,8},{16,20},{20,16},{24,28},{28,24},{1,5},{5... | collective-permute-start | bytes 884744 | tf_op jit(solution)/shard_map/ppermute | solution.py:365
  68.9 29.4 %collective-permute-start.19 = (bf16[256,1152]{1,0:T(8,128)(2,1)}, bf16[256,1152]{1,0:T(8,128)(2,1)}, u32[]{:S(2)}, u32[]{:S(2)}) collective-permute-start(bf16[256,1152]{1,0:T(8,128)(2,1)} %get-tuple-element.74), channel_id=1, source_target_pairs={{0,4},{4,0},{8,12},{12,8},{16,20},{20,16},{24,28},{28,24},{1,5},{5... | collective-permute-start | bytes 1769480 | tf_op jit(solution)/shard_map/ppermute | solution.py:365
  69.8 16.4 %collective-permute-start.15 = (bf16[256,1024]{1,0:T(8,128)(2,1)}, bf16[256,1024]{1,0:T(8,128)(2,1)}, u32[]{:S(2)}, u32[]{:S(2)}) collective-permute-start(bf16[256,1024]{1,0:T(8,128)(2,1)} %collective-permute-done.3.refs_5_), channel_id=1, source_target_pairs={{1,0},{5,4},{9,8},{13,12},{17,16},{21,20},{25,24},{29,28}} | collective-permute-start | bytes 1572872 | tf_op jit(solution)/shard_map/ppermute | solution.py:463
  71.1 31.8 %collective-permute-start.16 = (bf16[256,1152]{1,0:T(8,128)(2,1)}, bf16[256,1152]{1,0:T(8,128)(2,1)S(1)}, u32[]{:S(2)}, u32[]{:S(2)}) collective-permute-start(bf16[256,1152]{1,0:T(8,128)(2,1)} %get-tuple-element.67), channel_id=1, source_target_pairs={{0,4},{4,0},{8,12},{12,8},{16,20},{20,16},{24,28},{28,24},{1,5},{5... | collective-permute-start | bytes 1769480 | tf_op jit(solution)/shard_map/ppermute | solution.py:365
  71.5 31.4 %collective-permute-start.17 = (bf16[256,1152]{1,0:T(8,128)(2,1)}, bf16[256,1152]{1,0:T(8,128)(2,1)S(1)}, u32[]{:S(2)}, u32[]{:S(2)}) collective-permute-start(bf16[256,1152]{1,0:T(8,128)(2,1)} %get-tuple-element.70), channel_id=1, source_target_pairs={{0,4},{4,0},{8,12},{12,8},{16,20},{20,16},{24,28},{28,24},{1,5},{5... | collective-permute-start | bytes 1769480 | tf_op jit(solution)/shard_map/ppermute | solution.py:365
  72.5 43.7 %collective-permute-start.13 = (bf16[256,1152]{1,0:T(8,128)(2,1)}, bf16[256,1152]{1,0:T(8,128)(2,1)S(1)}, u32[]{:S(2)}, u32[]{:S(2)}) collective-permute-start(bf16[256,1152]{1,0:T(8,128)(2,1)} %copy-done.24), channel_id=1, source_target_pairs={{0,4},{4,0},{8,12},{12,8},{16,20},{20,16},{24,28},{28,24},{1,5},{5... | collective-permute-start | bytes 1769480 | tf_op jit(solution)/shard_map/ppermute | solution.py:365
  127.0 14.1 %collective-permute-start.28 = (bf16[256,1152]{1,0:T(8,128)(2,1)S(1)}, bf16[256,1152]{1,0:T(8,128)(2,1)S(1)}, u32[]{:S(2)}, u32[]{:S(2)}) collective-permute-start(bf16[256,1152]{1,0:T(8,128)(2,1)S(1)} %get-tuple-element.81.refs_0_), channel_id=1, source_target_pairs={{0,16},{4,20},{8,24},{12,28},{16,0},{20,4},{24,8},{28,12},{1,17},{... | collective-permute-start | bytes 1769480 | tf_op jit(solution)/shard_map/ppermute | solution.py:365
  127.9 22.7 %collective-permute-start.25 = (bf16[256,1152]{1,0:T(8,128)(2,1)S(1)}, bf16[256,1152]{1,0:T(8,128)(2,1)S(1)}, u32[]{:S(2)}, u32[]{:S(2)}) collective-permute-start(bf16[256,1152]{1,0:T(8,128)(2,1)S(1)} %get-tuple-element.81.refs_0_), channel_id=1, source_target_pairs={{0,4},{4,0},{8,12},{12,8},{16,20},{20,16},{24,28},{28,24},{1,5},{5... | collective-permute-start | bytes 1769480 | tf_op jit(solution)/shard_map/ppermute | solution.py:365
  150.6 22.8 %collective-permute-start.35 = (bf16[256,1024]{1,0:T(8,128)(2,1)S(1)}, bf16[256,1024]{1,0:T(8,128)(2,1)S(1)}, u32[]{:S(2)}, u32[]{:S(2)}) collective-permute-start(bf16[256,1024]{1,0:T(8,128)(2,1)S(1)} %get-tuple-element.85.refs_4_), channel_id=1, source_target_pairs={{0,8},{4,12},{8,0},{12,4},{16,24},{20,28},{24,16},{28,20},{1,9},{5... | collective-permute-start | bytes 1572872 | tf_op jit(solution)/shard_map/ppermute | solution.py:365
  151.2 25.6 %collective-permute-start.36 = (bf16[256,1024]{1,0:T(8,128)(2,1)S(1)}, bf16[256,1024]{1,0:T(8,128)(2,1)S(1)}, u32[]{:S(2)}, u32[]{:S(2)}) collective-permute-start(bf16[256,1024]{1,0:T(8,128)(2,1)S(1)} %get-tuple-element.85.refs_4_), channel_id=1, source_target_pairs={{0,16},{4,20},{8,24},{12,28},{16,0},{20,4},{24,8},{28,12},{1,17},{... | collective-permute-start | bytes 1572872 | tf_op jit(solution)/shard_map/ppermute | solution.py:365
  153.2 23.5 %collective-permute-start.37 = (bf16[256,1024]{1,0:T(8,128)(2,1)S(1)}, bf16[256,1024]{1,0:T(8,128)(2,1)S(1)}, u32[]{:S(2)}, u32[]{:S(2)}) collective-permute-start(bf16[256,1024]{1,0:T(8,128)(2,1)S(1)} %get-tuple-element.85.refs_4_), channel_id=1, source_target_pairs={{0,24},{4,28},{8,16},{12,20},{16,8},{20,12},{24,0},{28,4},{1,25},{... | collective-permute-start | bytes 1572872 | tf_op jit(solution)/shard_map/ppermute | solution.py:365
  179.2 35.1 %collective-permute-start.47 = (bf16[256,1024]{1,0:T(8,128)(2,1)S(1)}, bf16[256,1024]{1,0:T(8,128)(2,1)S(1)}, u32[]{:S(2)}, u32[]{:S(2)}) collective-permute-start(bf16[256,1024]{1,0:T(8,128)(2,1)S(1)} %get-tuple-element.101), channel_id=1, source_target_pairs={{0,8},{4,12},{8,0},{12,4},{16,24},{20,28},{24,16},{28,20},{1,9},{5... | collective-permute-start | bytes 1572872 | tf_op jit(solution)/shard_map/ppermute | solution.py:365
  180.8 33.5 %collective-permute-start.48 = (bf16[256,1024]{1,0:T(8,128)(2,1)S(1)}, bf16[256,1024]{1,0:T(8,128)(2,1)S(1)}, u32[]{:S(2)}, u32[]{:S(2)}) collective-permute-start(bf16[256,1024]{1,0:T(8,128)(2,1)S(1)} %get-tuple-element.103), channel_id=1, source_target_pairs={{0,16},{4,20},{8,24},{12,28},{16,0},{20,4},{24,8},{28,12},{1,17},{... | collective-permute-start | bytes 1572872 | tf_op jit(solution)/shard_map/ppermute | solution.py:365
  181.1 33.2 %collective-permute-start.49 = (bf16[256,1024]{1,0:T(8,128)(2,1)S(1)}, bf16[256,1024]{1,0:T(8,128)(2,1)S(1)}, u32[]{:S(2)}, u32[]{:S(2)}) collective-permute-start(bf16[256,1024]{1,0:T(8,128)(2,1)S(1)} %get-tuple-element.105), channel_id=1, source_target_pairs={{0,24},{4,28},{8,16},{12,20},{16,8},{20,12},{24,0},{28,4},{1,25},{... | collective-permute-start | bytes 1572872 | tf_op jit(solution)/shard_map/ppermute | solution.py:365
  186.5 27.7 %collective-permute-start.39 = (bf16[128,1024]{1,0:T(8,128)(2,1)S(1)}, bf16[128,1024]{1,0:T(8,128)(2,1)S(1)}, u32[]{:S(2)}, u32[]{:S(2)}) collective-permute-start(bf16[128,1024]{1,0:T(8,128)(2,1)S(1)} %get-tuple-element.113), channel_id=1, source_target_pairs={{0,8},{4,12},{8,0},{12,4},{16,24},{20,28},{24,16},{28,20},{1,9},{5... | collective-permute-start | bytes 786440 | tf_op jit(solution)/shard_map/ppermute | solution.py:365
  188.3 26.0 %collective-permute-start.46 = (bf16[128,1024]{1,0:T(8,128)(2,1)S(1)}, bf16[128,1024]{1,0:T(8,128)(2,1)S(1)}, u32[]{:S(2)}, u32[]{:S(2)}) collective-permute-start(bf16[128,1024]{1,0:T(8,128)(2,1)S(1)} %get-tuple-element.108), channel_id=1, source_target_pairs={{0,16},{4,20},{8,24},{12,28},{16,0},{20,4},{24,8},{28,12},{1,17},{... | collective-permute-start | bytes 786440 | tf_op jit(solution)/shard_map/ppermute | solution.py:365
  (52 other events, 414.3 us)

commit v6 on v5

--- a/solution.py
+++ b/solution.py
@@ -89,6 +89,16 @@
     earlier = (before < later).astype(BF16)
     own_ids = (base + lax.broadcasted_iota(jnp.int32, (block_count, group_rows), 0)).astype(F32)
     place = lax.broadcasted_iota(jnp.int32, (cap, group_rows), 0).astype(F32)
+    zero = jnp.zeros((block_count, HD), BF16)
+    wide_marks = jnp.concatenate(
+        [
+            jnp.concatenate(
+                [mark_ref[:, i * HD : (i + 1) * HD] if i == h else zero for i in range(heads)], axis=1
+            )
+            for h in range(heads)
+        ],
+        axis=0,
+    )
     for g in range(groups):
         packs = [whole(q_refs[g * span + i]) for i in range(span)]
         digits = [pack[rows : rows + PAD].astype(F32)[:TOPK] for pack in packs]
@@ -104,13 +114,12 @@
         hot_ref[g] = hot
         q_group = joined([pack[:rows] for pack in packs], 0)
         tops, sums = [], []
+        marks = scale * mm(wide_marks, q_group, NT)
         for h in range(heads):
-            cols = slice(h * HD, (h + 1) * HD)
-            marks = scale * mm(mark_ref[:, cols], q_group[:, cols], NT)
-            marks = jnp.where(own > 0.5, marks, LOW)
-            top = jnp.max(marks, axis=0, keepdims=True).astype(BF16).astype(F32)
+            mark = jnp.where(own > 0.5, marks[h * block_count : (h + 1) * block_count], LOW)
+            top = jnp.max(mark, axis=0, keepdims=True).astype(BF16).astype(F32)
             tops.append(top)
-            sums.append(jnp.sum(own * jnp.exp(marks - top), axis=0, keepdims=True))
+            sums.append(jnp.sum(own * jnp.exp(mark - top), axis=0, keepdims=True))
         tops, sums = jnp.concatenate(tops, axis=0), jnp.concatenate(sums, axis=0)
         upper = sums.astype(BF16).astype(F32)
         spare = jnp.zeros((HD - 3 * heads, group_rows), F32)
@@ -217,43 +226,17 @@
         out_ref[:, heads * HD :] = tailed([tops] + digits_of(sums, 2), out_ref.shape[0])
 
 
-def grad_kernel(lines, chips, at_ref, w_ref, *refs):
-    own_ref, up_refs, down_refs = refs[0], refs[1:lines], refs[lines : 2 * lines - 1]
-    ga_ref, slab_refs = refs[2 * lines - 1], refs[2 * lines : 2 * lines + chips]
-    full_ref, w_buf, sems, piece_sems = refs[2 * lines + chips :]
-    width = own_ref.shape[1]
-    share = slab_refs[0].shape[1]
-    line, chip = at_ref[0], at_ref[1]
-
-    def placed(ref, i):
-        return pltpu.make_async_copy(ref, full_ref.at[i], piece_sems.at[i])
-
-    placed(own_ref, line).start()
-    for d in range(1, lines):
-
-        @pl.when(line >= d)
-        def _():
-            placed(up_refs[d - 1], line - d).start()
-
-        @pl.when(line + d < lines)
-        def _():
-            placed(down_refs[d - 1], line + d).start()
-
+def grad_kernel(w_ref, full_ref, ga_ref, w_buf, sems):
+    parts, step = w_buf.shape[0], w_buf.shape[1]
     copies = [
-        pltpu.make_async_copy(w_ref.at[pl.ds(i * width, width)], w_buf.at[i], sems.at[i])
-        for i in range(lines)
+        pltpu.make_async_copy(w_ref.at[pl.ds(i * step, step)], w_buf.at[i], sems.at[i])
+        for i in range(parts)
     ]
     start(copies)
-    for i in range(lines):
-        placed(own_ref, i).wait()
-    for j in range(chips):
-        first = (chip ^ j) * share
-        cols = pl.ds(pl.multiple_of(first % width, HD), share)
-        slab_refs[j][...] = full_ref[first // width, :, cols]
     total = None
-    for i in range(lines):
+    for i in range(parts):
         copies[i].wait()
-        term = mm(full_ref[i], w_buf[i])
+        term = mm(full_ref[i * step : (i + 1) * step], w_buf[i], TN)
         total = term if total is None else total + term
     ga_ref[...] = total.astype(BF16)
 
@@ -344,20 +327,11 @@
             part_refs[g * span + i][...] = part[i * rows : (i + 1) * rows]
 
 
-def weight_kernel(counts, me_ref, *refs):
-    chips = len(counts)
-    slabs = refs[:chips]
-    attns, (own_ref, other_ref) = dealt(refs[chips:], counts)
-    half = own_ref.shape[0]
-    core = me_ref[0] % 2
-    attn = joined([whole(pieces) for pieces in attns], 0)
-
-    def side(which):
-        cols = pl.ds(pl.multiple_of(which * half, half), half)
-        return mm(joined([ref[:, cols] for ref in slabs], 0), attn, TN)
-
-    own_ref[...] = side(core)
-    other_ref[...] = side(1 - core).astype(BF16)
+def weight_kernel(counts, me_ref, cols_ref, *refs):
+    attns, (out_ref,) = dealt(refs, counts)
+    me = me_ref[0]
+    columns = joined([cols_ref[me ^ m] for m in range(len(counts))], 1)
+    out_ref[...] = mm(columns, joined([whole(pieces) for pieces in attns], 0))
 
 
 def swap(x, bits):
@@ -373,12 +347,12 @@
     return [x for pieces in lists for x in pieces]
 
 
-def spread_chips(x, half):
+def spread_chips(x, half, *before):
     chips = lax.axis_size("ctx") // 2
     near = [swap(x, 2 * j) for j in range(1, chips)] if chips != 4 else [swap(x, 2), swap(x, 4)]
     if chips != 4:
         return [[x]] + [[piece] for piece in near]
-    far = [swap(near[0][:half], 4), swap(near[1][half:], 2)]
+    far = [swap(after(near[0][:half], *before), 4), swap(after(near[1][half:], *before), 2)]
     return [[x], [near[0]], [near[1]], far]
 
 
@@ -416,7 +390,7 @@
     return terms + [[x_top, x_low], [y_top, y_low]]
 
 
-def merge_chips(parts, received, heads):
+def merge_chips(parts, received, heads, *before):
     chips = len(received)
     rows = parts[0].shape[0]
     half = rows // 2
@@ -448,29 +422,18 @@
     x_top, y_low = merged(ins, [[(0, *top), (1, *top)], [(2, *low), (3, *low)]])
     x_top, y_low = swap(x_top, 2), swap(y_low, 4)
     x_low, y_top = merged(
-        ins + [y_far, x_far],
+        ins + [after(y_far, *before), x_far],
         [[(0, *low), (1, *low), (4, *top)], [(2, *top), (3, *top), (5, *top)]],
     )
     x_low, y_top = swap(x_low, 2), swap(y_top, 4)
     return terms + [[x_top, x_low], [y_top, y_low]]
 
 
-def spread_line(x):
-    lines = lax.axis_size("head")
-    ups, downs = [x], [x]
-    for d in range(1, lines):
-        ups.append(lax.ppermute(ups[-1], "head", [(i, i + 1) for i in range(d - 1, lines - 1)]))
-        downs.append(lax.ppermute(downs[-1], "head", [(i, i - 1) for i in range(1, lines - d + 1)]))
-    return ups[1:], downs[1:]
-
-
 def body(queries, key_rows, value_rows, selected, out_grad, out_weight):
     chunks = lax.axis_size("ctx")
     chips = chunks // 2
-    lines = lax.axis_size("head")
     rows, width = queries.shape
     features = out_weight.shape[0]
-    share = features // chips
     heads = width // HD
     block_count = key_rows.shape[0] // BLOCK
     block_total = block_count * chunks
@@ -481,7 +444,6 @@
     slots = groups * cap
     index = lax.axis_index("ctx").astype(jnp.int32)
     me = index.reshape(1)
-    at = jnp.stack([lax.axis_index("head").astype(jnp.int32), index // 2])
     keys = key_rows.reshape(block_count, BLOCK, width)
     values = value_rows.reshape(block_count, BLOCK, width)
     vmem = pl.BlockSpec(memory_space=pltpu.VMEM)
@@ -494,7 +456,8 @@
     def shaped(shape, kind=BF16):
         return jax.ShapeDtypeStruct(shape, kind)
 
-    ups, downs = spread_line(out_grad)
+    grad_full = lax.all_gather(out_grad.T, "head", axis=0, tiled=True)
+    columns = lax.all_to_all(grad_full, "ctx", split_axis=0, concat_axis=0, tiled=True)
     packed = pl.pallas_call(
         pack_kernel,
         out_shape=shaped((rows + PAD, width)),
@@ -504,7 +467,7 @@
         name="pack",
     )(selected.T, queries)
     query_chips = spread_chips(packed, rows // 2)
-    query_all = with_cores(query_chips, after(packed, ups[0], downs[0]))
+    query_all = with_cores(query_chips, packed)
 
     outs = pl.pallas_call(
         functools.partial(forward_kernel, [len(pieces) for pieces in query_all], span, cap),
@@ -523,24 +486,22 @@
         ],
         compiler_params=limit(40),
         name="forward",
-    )(after(me, *ups[:2], *downs[:2]), keys[:, BLOCK - 1], keys, values, *flat(query_all))
+    )(me, keys[:, BLOCK - 1], keys, values, *flat(query_all))
     q_slots, probs, logits, hot = outs[chunks:]
 
-    grad_attn, *slabs = pl.pallas_call(
-        functools.partial(grad_kernel, lines, chips),
-        out_shape=[shaped((rows, width))] + [shaped((rows, share))] * chips,
-        in_specs=[smem] + [anywhere] * (2 * lines),
-        out_specs=[vmem] * (1 + chips),
+    grad_attn = pl.pallas_call(
+        grad_kernel,
+        out_shape=shaped((rows, width)),
+        in_specs=[anywhere, vmem],
+        out_specs=vmem,
         scratch_shapes=[
-            pltpu.VMEM((lines, rows, width), BF16),
-            pltpu.VMEM((lines, width, width), BF16),
-            pltpu.SemaphoreType.DMA((lines,)),
-            pltpu.SemaphoreType.DMA((lines,)),
+            pltpu.VMEM((features // width, width, width), BF16),
+            pltpu.SemaphoreType.DMA((features // width,)),
         ],
         compiler_params=limit(24),
         name="grad",
-    )(at, out_weight, out_grad, *ups, *downs)
-    terms = merge_chips(outs[:chunks], from_core(outs[:chunks], grad_attn), heads)
+    )(out_weight, grad_full)
+    terms = merge_chips(outs[:chunks], from_core(outs[:chunks]), heads, grad_attn)
     attn_out, extended = pl.pallas_call(
         functools.partial(finish_kernel, [len(pieces) for pieces in terms]),
         out_shape=[shaped((rows, width)), shaped((rows, width + HD))],
@@ -549,12 +510,10 @@
         compiler_params=limit(24),
         name="finish",
     )(*flat(terms), grad_attn)
-    grad_chips = spread_chips(extended, rows // 2)
+    grad_chips = spread_chips(extended, rows // 2, columns)
     grad_all = with_cores(grad_chips, extended)
-
     arrived = flat(grad_chips[1:3])
     attns = [[attn_out]] + [[swap(after(attn_out, *arrived), 2 * j)] for j in range(1, chips)]
-    slabs = [slabs[0]] + [swap(after(slabs[j], *arrived), 2 * j) for j in range(1, chips)]
 
     outs = pl.pallas_call(
         functools.partial(backward_kernel, [len(pieces) for pieces in grad_all], span, cap),
@@ -580,15 +539,15 @@
         name="total",
     )(*flat(terms))
 
-    weight_own, weight_other = pl.pallas_call(
+    attns = with_cores(attns, attn_out)
+    weight_grad = pl.pallas_call(
         functools.partial(weight_kernel, [len(pieces) for pieces in attns]),
-        out_shape=[shaped((share // 2, width), F32), shaped((share // 2, width))],
-        in_specs=[smem] + [vmem] * (chips + len(flat(attns))),
-        out_specs=[vmem] * 2,
+        out_shape=shaped((features // chunks, width), F32),
+        in_specs=[smem] + [vmem] * (1 + len(flat(attns))),
+        out_specs=vmem,
         compiler_params=limit(24),
         name="weight",
-    )(after(me, terms[2][0], terms[-1][-1]), *slabs, *flat(attns))
-    weight_grad = weight_own + swap(weight_other, 1).astype(F32)
+    )(after(me, *flat(terms)), columns.reshape(chunks, features // chunks, rows), *flat(attns))
     return (
         query_grad,
         key_grad.reshape(-1, width),

time: 229 us -> 212 us (0.926)
  between operations: 0.95 us -> 14.3 us
  waiting for transfers between devices: 104 us -> 92.1 us
  local copies, waits for them, and re-layouts: 20.7 us -> 9.73 us
  starting transfers between devices: 44.8 us -> 37.2 us
    ppermute x6 -> x0, waiting for transfers between devices: 26.1 us -> none  [the longest x3 26.1 us: spread_line(): lax.ppermute(downs[-1], 'head', [(i, i - 1) for i in range(1, lines - d +...]
    all_gather x0 -> x1, waiting for transfers between devices: none -> 19.9 us  [body(): grad_full = lax.all_gather(out_grad.T, 'head', axis=0, tiled=True)]
    unnamed x51 -> x26, local copies, waits for them, and re-layouts: 19.6 us -> 7.2 us
    ppermute x6 -> x0, starting transfers between devices: 9.55 us -> none  [the longest x3 5.69 us: spread_line(): lax.ppermute(ups[-1], 'head', [(i, i + 1) for i in range(d - 1, lines - 1)])]
    ppermute x45, waiting for transfers between devices: 78.2 us -> 72.1 us  [swap(): return lax.ppermute(x, 'ctx', [(i, i ^ bits) for i in range(count)])]
    all_to_all x0 -> x1, starting transfers between devices: none -> 4.48 us  [body(): lax.all_to_all(grad_full, 'ctx', split_axis=0, concat_axis=0, tiled=True)]
    pallas_call x1, Pallas kernels: 2.39 us -> 5.25 us  [body(): pl.pallas_call(functools.partial(weight_kernel, [len(pieces) for pieces i...]
    ppermute x45, starting transfers between devices: 35.2 us -> 32.7 us  [swap(): return lax.ppermute(x, 'ctx', [(i, i ^ bits) for i in range(count)])]
  transfers between devices with their start and end apart: 51 -> 47, of which waited for: 19 -> 16; matrix products, arithmetic and copies ran while one was open for 1% -> 2% of each run, Pallas kernels for 14% -> 25%
where the time goes in v6:
time: 212 us
  waiting for transfers between devices  92.1 us (43%)
  Pallas kernels  57.8 us (27%)
  starting transfers between devices  37.2 us (18%)
  between operations  14.3 us (7%)
  local copies, waits for them, and re-layouts  9.73 us (5%)
    ppermute x45, waiting for transfers between devices, swap(): return lax.ppermute(x, 'ctx', [(i, i ^ bits) for i in range(count)])  72.1 us
    ppermute x45, starting transfers between devices, swap(): return lax.ppermute(x, 'ctx', [(i, i ^ bits) for i in range(count)])  32.7 us
    all_gather x1, waiting for transfers between devices, body(): grad_full = lax.all_gather(out_grad.T, 'head', axis=0, tiled=True)  19.9 us
    pallas_call x1, Pallas kernels, body(): pl.pallas_call(functools.partial(forward_kernel, [len(pieces) for pieces...  19.6 us
    pallas_call x1, Pallas kernels, body(): pl.pallas_call(functools.partial(backward_kernel, [len(pieces) for pieces...  19.2 us
    unnamed x26, local copies, waits for them, and re-layouts  7.2 us
    pallas_call x3, Pallas kernels, merged(): pl.pallas_call(functools.partial(merge_kernel, plan, heads), out_shape=[j...  5.82 us
    pallas_call x1, Pallas kernels, body(): pl.pallas_call(functools.partial(weight_kernel, [len(pieces) for pieces i...  5.25 us
  transfers between devices with their start and end apart: 47, of which 16 were waited for; matrix products, arithmetic and copies ran while one was open for 2% of the time, Pallas kernels for 25%

profile of v6, /device:TPU:0, one launch (start us, length us, event | category | flops | bytes accessed | tf_op | source)
XLA Modules:
  0.0 211.8 jit_solution(7477099061915451001)
XLA Ops:
  7.2 2.0 copy.11
  11.1 3.0 %collective-permute-start.3 = (bf16[272,1024]{1,0:T(8,128)(2,1)S(1)}, bf16[272,1024]{1,0:T(8,128)(2,1)S(1)}, u32[]{:S(2)}, u32[]{:S(2)}) collective-permute-start(bf16[272,1024]{1,0:T(8,128)(2,1)S(1)} %pack.1.refs_0_), channel_id=1, source_target_pairs={{0,16},{4,20},{8,24},{12,28},{16,0},{20,4},{24,8},{28,12},{1,17},{... | collective-permute-start | bytes 1671176 | tf_op jit(solution)/shard_map/ppermute | solution.py:339
  15.6 11.1 %collective-permute-done.3.refs_4_ = bf16[272,1024]{1,0:T(8,128)(2,1)S(1)} collective-permute-done((bf16[272,1024]{1,0:T(8,128)(2,1)S(1)}, bf16[272,1024]{1,0:T(8,128)(2,1)S(1)}, u32[]{:S(2)}, u32[]{:S(2)}) %collective-permute-start.3) | collective-permute-done | bytes 557088 | tf_op jit(solution)/shard_map/ppermute | solution.py:339
  31.6 3.5 %collective-permute-done.6.refs_7_ = bf16[144,1024]{1,0:T(8,128)(2,1)S(1)} collective-permute-done((bf16[144,1024]{1,0:T(8,128)(2,1)S(1)}, bf16[144,1024]{1,0:T(8,128)(2,1)S(1)}, u32[]{:S(2)}, u32[]{:S(2)}) %collective-permute-start.6) | collective-permute-done | bytes 294944 | tf_op jit(solution)/shard_map/ppermute | solution.py:339
  35.1 3.8 %collective-permute-done.5.refs_6_ = bf16[128,1024]{1,0:T(8,128)(2,1)} collective-permute-done((bf16[128,1024]{1,0:T(8,128)(2,1)S(1)}, bf16[128,1024]{1,0:T(8,128)(2,1)}, u32[]{:S(2)}, u32[]{:S(2)}) %collective-permute-start.5) | collective-permute-done | bytes 262176 | tf_op jit(solution)/shard_map/ppermute | solution.py:339
  38.9 19.9 %all-gather.2.cloned.1.call-done.full_ref = bf16[4096,256]{1,0:T(8,128)(2,1)} async-done(((bf16[1024,256]{1,0:T(8,128)(2,1)}), bf16[4096,256]{1,0:T(8,128)(2,1)}) %all-gather.2.cloned.1.call-update) | async-done | bytes 2097168 | tf_op jit(solution)/shard_map/all_gather | solution.py:459
  58.8 4.5 %all-to-all-start = ((bf16[8,512,256]{2,1,0:T(8,128)(2,1)}), bf16[8,512,256]{2,1,0:T(8,128)(2,1)}, u32[]{:S(2)}, u32[]{:S(2)}) async-start(bf16[8,512,256]{2,1,0:T(8,128)(2,1)} %bitcast.15), calls=%async_computation | async-start | bytes 4194304 | tf_op jit(solution)/shard_map/all_to_all | solution.py:460
  63.5 19.6 %forward.1 = (bf16[256,1152]{1,0:T(8,128)(2,1)S(1)}, bf16[256,1152]{1,0:T(8,128)(2,1)S(1)}, bf16[256,1152]{1,0:T(8,128)(2,1)S(1)}, bf16[256,1152]{1,0:T(8,128)(2...) custom-call(s32[1]{0:T(128)} %bitcast.me_ref, ...), custom_call_target="tpu_custom_call" | custom-call | tf_op jit(solution)/shard_map/forward/pallas_call | solution.py:472
  86.9 2.0 collective-permute-start.14
  92.9 3.4 %copy-done.1 = bf16[4096,1024]{1,0:T(8,128)(2,1)S(1)} copy-done((bf16[4096,1024]{1,0:T(8,128)(2,1)S(1)}, bf16[4096,1024]{1,0:T(8,128)(2,1)}, u32[]{:S(2)}) %copy-start.1) | copy-done | bytes 8388632
  96.2 3.5 %grad.1.refs_6_ = bf16[256,1024]{1,0:T(8,128)(2,1)S(1)} custom-call(bf16[4096,1024]{1,0:T(8,128)(2,1)S(1)} %copy-done.1, bf16[4096,256]{1,0:T(8,128)(2,1)S(1)} %copy-done.2), custom_call_target="tpu_custom_call" | custom-call | tf_op jit(solution)/shard_map/grad/pallas_call | solution.py:492
  99.8 2.3 %merge.5 = (bf16[128,1152]{1,0:T(8,128)(2,1)S(1)}, bf16[128,1152]{1,0:T(8,128)(2,1)S(1)}) custom-call(bf16[256,1152]{1,0:T(8,128)(2,1)S(1)} %get-tuple-element.49.refs_0_, bf16[256,1152]{1,0:T(8,128)(2,1)S(1)} %collective-permute-done.10.refs_1_, bf16[256,1152]{1,0:T(8,128)(2,1)S(1)} %get-tuple-element.51.refs_2_, ...), custom_call_target="tpu_custom_call" | custom-call | tf_op jit(solution)/shard_map/merge/pallas_call | solution.py:399
  102.1 1.9 collective-permute-start.16
  105.5 5.7 %collective-permute-done.16.refs_3_ = bf16[128,1152]{1,0:T(8,128)(2,1)S(1)} collective-permute-done((bf16[128,1152]{1,0:T(8,128)(2,1)S(1)}, bf16[128,1152]{1,0:T(8,128)(2,1)S(1)}, u32[]{:S(2)}, u32[]{:S(2)}) %collective-permute-start.16) | collective-permute-done | bytes 294944 | tf_op jit(solution)/shard_map/ppermute | solution.py:339
  112.6 3.1 %finish.1 = (bf16[256,1024]{1,0:T(8,128)(2,1)S(1)}, bf16[256,1152]{1,0:T(8,128)(2,1)S(1)}) custom-call(bf16[256,1152]{1,0:T(8,128)(2,1)S(1)} %get-tuple-element.47.refs_0_, bf16[256,1152]{1,0:T(8,128)(2,1)S(1)} %collective-permute-done.9.refs_1_, bf16[128,1152]{1,0:T(8,128)(2,1)S(1)} %collective-permute-done.12.refs_2_, ...), custom_call_target="tpu_custom_call" | custom-call | tf_op jit(solution)/shard_map/finish/pallas_call | solution.py:505
  117.9 12.0 %collective-permute-done.20.refs_2_ = bf16[256,1152]{1,0:T(8,128)(2,1)S(1)} collective-permute-done((bf16[256,1152]{1,0:T(8,128)(2,1)S(1)}, bf16[256,1152]{1,0:T(8,128)(2,1)S(1)}, u32[]{:S(2)}, u32[]{:S(2)}) %collective-permute-start.20) | collective-permute-done | bytes 589856 | tf_op jit(solution)/shard_map/ppermute | solution.py:339
  133.9 7.0 %collective-permute-done.24.refs_6_ = bf16[128,1152]{1,0:T(8,128)(2,1)S(1)} collective-permute-done((bf16[128,1152]{1,0:T(8,128)(2,1)}, bf16[128,1152]{1,0:T(8,128)(2,1)S(1)}, u32[]{:S(2)}, u32[]{:S(2)}) %collective-permute-start.24) | collective-permute-done | bytes 294944 | tf_op jit(solution)/shard_map/ppermute | solution.py:339
  145.7 19.2 %backward.1 = (bf16[256,1024]{1,0:T(8,128)(2,1)S(1)}, bf16[256,1024]{1,0:T(8,128)(2,1)S(1)}, bf16[256,1024]{1,0:T(8,128)(2,1)S(1)}, bf16[256,1024]{1,0:T(8,128)(...) custom-call(bf16[8,256,256]{2,1,0:T(8,128)(2,1)S(1)} %copy-done.5, ...), custom_call_target="tpu_custom_call" | custom-call | tf_op jit(solution)/shard_map/backward/pallas_call | solution.py:518
  165.4 3.3 %collective-permute-done.30.refs_4_ = bf16[256,1024]{1,0:T(8,128)(2,1)S(1)} collective-permute-done((bf16[256,1024]{1,0:T(8,128)(2,1)}, bf16[256,1024]{1,0:T(8,128)(2,1)S(1)}, u32[]{:S(2)}, u32[]{:S(2)}) %collective-permute-start.30) | collective-permute-done | bytes 524320 | tf_op jit(solution)/shard_map/ppermute | solution.py:339
  170.7 5.2 %collective-permute-done.35 = bf16[128,1024]{1,0:T(8,128)(2,1)S(1)} collective-permute-done((bf16[128,1024]{1,0:T(8,128)(2,1)S(1)}, bf16[128,1024]{1,0:T(8,128)(2,1)S(1)}, u32[]{:S(2)}, u32[]{:S(2)}) %collective-permute-start.35) | collective-permute-done | bytes 262176 | tf_op jit(solution)/shard_map/ppermute | solution.py:339
  180.9 4.6 %collective-permute-done.33.refs_2_ = bf16[128,1024]{1,0:T(8,128)(2,1)S(1)} collective-permute-done((bf16[128,1024]{1,0:T(8,128)(2,1)S(1)}, bf16[128,1024]{1,0:T(8,128)(2,1)S(1)}, u32[]{:S(2)}, u32[]{:S(2)}) %collective-permute-start.33) | collective-permute-done | bytes 262176 | tf_op jit(solution)/shard_map/ppermute | solution.py:339
  185.5 4.2 %collective-permute-done.36.refs_3_ = bf16[128,1024]{1,0:T(8,128)(2,1)S(1)} collective-permute-done((bf16[128,1024]{1,0:T(8,128)(2,1)S(1)}, bf16[128,1024]{1,0:T(8,128)(2,1)S(1)}, u32[]{:S(2)}, u32[]{:S(2)}) %collective-permute-start.36) | collective-permute-done | bytes 262176 | tf_op jit(solution)/shard_map/ppermute | solution.py:339
  191.0 7.4 %collective-permute-done.40.refs_5_ = bf16[128,1024]{1,0:T(8,128)(2,1)S(1)} collective-permute-done((bf16[128,1024]{1,0:T(8,128)(2,1)S(1)}, bf16[128,1024]{1,0:T(8,128)(2,1)S(1)}, u32[]{:S(2)}, u32[]{:S(2)}) %collective-permute-start.40) | collective-permute-done | bytes 262176 | tf_op jit(solution)/shard_map/ppermute | solution.py:339
  199.7 5.2 %weight.1 = f32[512,1024]{1,0:T(8,128)} custom-call(s32[1]{0:T(128)} %bitcast.me_ref, bf16[8,512,256]{2,1,0:T(8,128)(2,1)} %all-to-all-done.cols_ref, bf16[256,1024]{1,0:T(8,128)(2,1)S(1)} %copy-done.7, bf16[256,1024]{1,0:T(8,128)(2,1)S(1)} %collective-permute-done.41.refs_1_, bf16[256,1024]{1,0:T(8,128)(2,1)S(1)} %collective-permute-done.29.refs_2_, ...), custom_call_target="tpu_custom_call" | custom-call | tf_op jit(solution)/shard_map/weight/pallas_call | solution.py:543
  (115 shorter events, 40.1 us)
Async XLA Ops:
  7.2 51.6 %all-gather.2.cloned.1.call-start = ((), (), s32[]{:S(2)}) async-start(), calls=%async_computation.1 | async-start | bytes 2621440 | tf_op jit(solution)/shard_map/all_gather | solution.py:459
  11.1 15.7 %collective-permute-start.3 = (bf16[272,1024]{1,0:T(8,128)(2,1)S(1)}, bf16[272,1024]{1,0:T(8,128)(2,1)S(1)}, u32[]{:S(2)}, u32[]{:S(2)}) collective-permute-start(bf16[272,1024]{1,0:T(8,128)(2,1)S(1)} %pack.1.refs_0_), channel_id=1, source_target_pairs={{0,16},{4,20},{8,24},{12,28},{16,0},{20,4},{24,8},{28,12},{1,17},{... | collective-permute-start | bytes 1671176 | tf_op jit(solution)/shard_map/ppermute | solution.py:339
  14.1 14.4 %collective-permute-start.1 = (bf16[272,1024]{1,0:T(8,128)(2,1)S(1)}, bf16[272,1024]{1,0:T(8,128)(2,1)}, u32[]{:S(2)}, u32[]{:S(2)}) collective-permute-start(bf16[272,1024]{1,0:T(8,128)(2,1)S(1)} %pack.1.refs_0_), channel_id=1, source_target_pairs={{0,8},{4,12},{8,0},{12,4},{16,24},{20,28},{24,16},{28,20},{1,9},{5... | collective-permute-start | bytes 1671176 | tf_op jit(solution)/shard_map/ppermute | solution.py:339
  28.5 34.9 %collective-permute-start = (bf16[272,1024]{1,0:T(8,128)(2,1)S(1)}, bf16[272,1024]{1,0:T(8,128)(2,1)}, u32[]{:S(2)}, u32[]{:S(2)}) collective-permute-start(bf16[272,1024]{1,0:T(8,128)(2,1)S(1)} %pack.1.refs_0_), channel_id=1, source_target_pairs={{0,4},{4,0},{8,12},{12,8},{16,20},{20,16},{24,28},{28,24},{1,5},{5... | collective-permute-start | bytes 1671176 | tf_op jit(solution)/shard_map/ppermute | solution.py:339
  28.5 34.9 %collective-permute-start.2 = (bf16[272,1024]{1,0:T(8,128)(2,1)}, bf16[272,1024]{1,0:T(8,128)(2,1)}, u32[]{:S(2)}, u32[]{:S(2)}) collective-permute-start(bf16[272,1024]{1,0:T(8,128)(2,1)} %collective-permute-done.1.refs_2_), channel_id=1, source_target_pairs={{0,4},{4,0},{8,12},{12,8},{16,20},{20,16},{24,28},{28,24},{1,5},{5... | collective-permute-start | bytes 1671176 | tf_op jit(solution)/shard_map/ppermute | solution.py:339
  29.0 34.4 %collective-permute-start.4 = (bf16[272,1024]{1,0:T(8,128)(2,1)S(1)}, bf16[272,1024]{1,0:T(8,128)(2,1)}, u32[]{:S(2)}, u32[]{:S(2)}) collective-permute-start(bf16[272,1024]{1,0:T(8,128)(2,1)S(1)} %collective-permute-done.3.refs_4_), channel_id=1, source_target_pairs={{0,4},{4,0},{8,12},{12,8},{16,20},{20,16},{24,28},{28,24},{1,5},{5... | collective-permute-start | bytes 1671176 | tf_op jit(solution)/shard_map/ppermute | solution.py:339
  35.1 28.4 %collective-permute-start.8 = (bf16[144,1024]{1,0:T(8,128)(2,1)S(1)}, bf16[144,1024]{1,0:T(8,128)(2,1)}, u32[]{:S(2)}, u32[]{:S(2)}) collective-permute-start(bf16[144,1024]{1,0:T(8,128)(2,1)S(1)} %collective-permute-done.6.refs_7_), channel_id=1, source_target_pairs={{0,4},{4,0},{8,12},{12,8},{16,20},{20,16},{24,28},{28,24},{1,5},{5... | collective-permute-start | bytes 884744 | tf_op jit(solution)/shard_map/ppermute | solution.py:339
  38.9 24.5 %collective-permute-start.7 = (bf16[128,1024]{1,0:T(8,128)(2,1)}, bf16[128,1024]{1,0:T(8,128)(2,1)}, u32[]{:S(2)}, u32[]{:S(2)}) collective-permute-start(bf16[128,1024]{1,0:T(8,128)(2,1)} %collective-permute-done.5.refs_6_), channel_id=1, source_target_pairs={{0,4},{4,0},{8,12},{12,8},{16,20},{20,16},{24,28},{28,24},{1,5},{5... | collective-permute-start | bytes 786440 | tf_op jit(solution)/shard_map/ppermute | solution.py:339
  58.8 73.0 %all-to-all-start = ((bf16[8,512,256]{2,1,0:T(8,128)(2,1)}), bf16[8,512,256]{2,1,0:T(8,128)(2,1)}, u32[]{:S(2)}, u32[]{:S(2)}) async-start(bf16[8,512,256]{2,1,0:T(8,128)(2,1)} %bitcast.15), calls=%async_computation | async-start | bytes 4194304 | tf_op jit(solution)/shard_map/all_to_all | solution.py:460
  86.9 12.9 %collective-permute-start.14 = (bf16[128,1152]{1,0:T(8,128)(2,1)S(1)}, bf16[128,1152]{1,0:T(8,128)(2,1)S(1)}, u32[]{:S(2)}, u32[]{:S(2)}) collective-permute-start(bf16[128,1152]{1,0:T(8,128)(2,1)S(1)} %get-tuple-element.56), channel_id=1, source_target_pairs={{0,16},{4,20},{8,24},{12,28},{16,0},{20,4},{24,8},{28,12},{1,17},{... | collective-permute-start | bytes 884744 | tf_op jit(solution)/shard_map/ppermute | solution.py:339
  90.3 15.2 %collective-permute-start.9 = (bf16[256,1152]{1,0:T(8,128)(2,1)S(1)}, bf16[256,1152]{1,0:T(8,128)(2,1)S(1)}, u32[]{:S(2)}, u32[]{:S(2)}) collective-permute-start(bf16[256,1152]{1,0:T(8,128)(2,1)S(1)} %get-tuple-element.48), channel_id=1, source_target_pairs={{0,4},{4,0},{8,12},{12,8},{16,20},{20,16},{24,28},{28,24},{1,5},{5... | collective-permute-start | bytes 1769480 | tf_op jit(solution)/shard_map/ppermute | solution.py:339
  92.1 13.4 %collective-permute-start.12 = (bf16[128,1152]{1,0:T(8,128)(2,1)S(1)}, bf16[128,1152]{1,0:T(8,128)(2,1)S(1)}, u32[]{:S(2)}, u32[]{:S(2)}) collective-permute-start(bf16[128,1152]{1,0:T(8,128)(2,1)S(1)} %get-tuple-element.53), channel_id=1, source_target_pairs={{0,8},{4,12},{8,0},{12,4},{16,24},{20,28},{24,16},{28,20},{1,9},{5... | collective-permute-start | bytes 884744 | tf_op jit(solution)/shard_map/ppermute | solution.py:339
  92.7 12.8 %collective-permute-start.18 = (bf16[128,1152]{1,0:T(8,128)(2,1)S(1)}, bf16[128,1152]{1,0:T(8,128)(2,1)S(1)}, u32[]{:S(2)}, u32[]{:S(2)}) collective-permute-start(bf16[128,1152]{1,0:T(8,128)(2,1)S(1)} %get-tuple-element.61), channel_id=1, source_target_pairs={{0,16},{4,20},{8,24},{12,28},{16,0},{20,4},{24,8},{28,12},{1,17},{... | collective-permute-start | bytes 884744 | tf_op jit(solution)/shard_map/ppermute | solution.py:339
  115.8 14.1 %collective-permute-start.20 = (bf16[256,1152]{1,0:T(8,128)(2,1)S(1)}, bf16[256,1152]{1,0:T(8,128)(2,1)S(1)}, u32[]{:S(2)}, u32[]{:S(2)}) collective-permute-start(bf16[256,1152]{1,0:T(8,128)(2,1)S(1)} %get-tuple-element.62.refs_0_), channel_id=1, source_target_pairs={{0,8},{4,12},{8,0},{12,4},{16,24},{20,28},{24,16},{28,20},{1,9},{5... | collective-permute-start | bytes 1769480 | tf_op jit(solution)/shard_map/ppermute | solution.py:339
  116.2 14.4 %collective-permute-start.22 = (bf16[256,1152]{1,0:T(8,128)(2,1)S(1)}, bf16[256,1152]{1,0:T(8,128)(2,1)S(1)}, u32[]{:S(2)}, u32[]{:S(2)}) collective-permute-start(bf16[256,1152]{1,0:T(8,128)(2,1)S(1)} %get-tuple-element.62.refs_0_), channel_id=1, source_target_pairs={{0,16},{4,20},{8,24},{12,28},{16,0},{20,4},{24,8},{28,12},{1,17},{... | collective-permute-start | bytes 1769480 | tf_op jit(solution)/shard_map/ppermute | solution.py:339
  117.9 24.3 %collective-permute-start.19 = (bf16[256,1152]{1,0:T(8,128)(2,1)S(1)}, bf16[256,1152]{1,0:T(8,128)(2,1)S(1)}, u32[]{:S(2)}, u32[]{:S(2)}) collective-permute-start(bf16[256,1152]{1,0:T(8,128)(2,1)S(1)} %get-tuple-element.62.refs_0_), channel_id=1, source_target_pairs={{0,4},{4,0},{8,12},{12,8},{16,20},{20,16},{24,28},{28,24},{1,5},{5... | collective-permute-start | bytes 1769480 | tf_op jit(solution)/shard_map/ppermute | solution.py:339
  129.8 13.4 %collective-permute-start.21 = (bf16[256,1152]{1,0:T(8,128)(2,1)S(1)}, bf16[256,1152]{1,0:T(8,128)(2,1)}, u32[]{:S(2)}, u32[]{:S(2)}) collective-permute-start(bf16[256,1152]{1,0:T(8,128)(2,1)S(1)} %collective-permute-done.20.refs_2_), channel_id=1, source_target_pairs={{0,4},{4,0},{8,12},{12,8},{16,20},{20,16},{24,28},{28,24},{1,5},{5... | collective-permute-start | bytes 1769480 | tf_op jit(solution)/shard_map/ppermute | solution.py:339
  130.6 13.4 %collective-permute-start.23 = (bf16[256,1152]{1,0:T(8,128)(2,1)S(1)}, bf16[256,1152]{1,0:T(8,128)(2,1)}, u32[]{:S(2)}, u32[]{:S(2)}) collective-permute-start(bf16[256,1152]{1,0:T(8,128)(2,1)S(1)} %collective-permute-done.22.refs_4_), channel_id=1, source_target_pairs={{0,4},{4,0},{8,12},{12,8},{16,20},{20,16},{24,28},{28,24},{1,5},{5... | collective-permute-start | bytes 1769480 | tf_op jit(solution)/shard_map/ppermute | solution.py:339
  142.2 23.2 %collective-permute-start.29 = (bf16[256,1024]{1,0:T(8,128)(2,1)}, bf16[256,1024]{1,0:T(8,128)(2,1)S(1)}, u32[]{:S(2)}, u32[]{:S(2)}) collective-permute-start(bf16[256,1024]{1,0:T(8,128)(2,1)} %copy-done.6), channel_id=1, source_target_pairs={{0,8},{4,12},{8,0},{12,4},{16,24},{20,28},{24,16},{28,20},{1,9},{5... | collective-permute-start | bytes 1572872 | tf_op jit(solution)/shard_map/ppermute | solution.py:339
  143.2 25.5 %collective-permute-start.30 = (bf16[256,1024]{1,0:T(8,128)(2,1)}, bf16[256,1024]{1,0:T(8,128)(2,1)S(1)}, u32[]{:S(2)}, u32[]{:S(2)}) collective-permute-start(bf16[256,1024]{1,0:T(8,128)(2,1)} %copy-done.6), channel_id=1, source_target_pairs={{0,16},{4,20},{8,24},{12,28},{16,0},{20,4},{24,8},{28,12},{1,17},{... | collective-permute-start | bytes 1572872 | tf_op jit(solution)/shard_map/ppermute | solution.py:339
  144.0 24.7 %collective-permute-start.31 = (bf16[256,1024]{1,0:T(8,128)(2,1)}, bf16[256,1024]{1,0:T(8,128)(2,1)S(1)}, u32[]{:S(2)}, u32[]{:S(2)}) collective-permute-start(bf16[256,1024]{1,0:T(8,128)(2,1)} %copy-done.6), channel_id=1, source_target_pairs={{0,24},{4,28},{8,16},{12,20},{16,8},{20,12},{24,0},{28,4},{1,25},{... | collective-permute-start | bytes 1572872 | tf_op jit(solution)/shard_map/ppermute | solution.py:339
  180.4 19.4 %collective-permute-start.41 = (bf16[256,1024]{1,0:T(8,128)(2,1)S(1)}, bf16[256,1024]{1,0:T(8,128)(2,1)S(1)}, u32[]{:S(2)}, u32[]{:S(2)}) collective-permute-start(bf16[256,1024]{1,0:T(8,128)(2,1)S(1)} %copy-done.7), channel_id=1, source_target_pairs={{0,4},{4,0},{8,12},{12,8},{16,20},{20,16},{24,28},{28,24},{1,5},{5... | collective-permute-start | bytes 1572872 | tf_op jit(solution)/shard_map/ppermute | solution.py:339
  180.4 19.4 %collective-permute-start.42 = (bf16[256,1024]{1,0:T(8,128)(2,1)S(1)}, bf16[256,1024]{1,0:T(8,128)(2,1)S(1)}, u32[]{:S(2)}, u32[]{:S(2)}) collective-permute-start(bf16[256,1024]{1,0:T(8,128)(2,1)S(1)} %collective-permute-done.29.refs_2_), channel_id=1, source_target_pairs={{0,4},{4,0},{8,12},{12,8},{16,20},{20,16},{24,28},{28,24},{1,5},{5... | collective-permute-start | bytes 1572872 | tf_op jit(solution)/shard_map/ppermute | solution.py:339
  185.5 14.3 %collective-permute-start.43 = (bf16[256,1024]{1,0:T(8,128)(2,1)S(1)}, bf16[256,1024]{1,0:T(8,128)(2,1)S(1)}, u32[]{:S(2)}, u32[]{:S(2)}) collective-permute-start(bf16[256,1024]{1,0:T(8,128)(2,1)S(1)} %collective-permute-done.30.refs_4_), channel_id=1, source_target_pairs={{0,4},{4,0},{8,12},{12,8},{16,20},{20,16},{24,28},{28,24},{1,5},{5... | collective-permute-start | bytes 1572872 | tf_op jit(solution)/shard_map/ppermute | solution.py:339
  (35 other events, 364.0 us)
Sparse Core Ops, SparseCore 0:
  10.1 48.6 all-gather.1

commit v7 on v6

--- a/solution.py
+++ b/solution.py
@@ -99,6 +99,7 @@
         ],
         axis=0,
     )
+    q_groups, owns = [], []
     for g in range(groups):
         packs = [whole(q_refs[g * span + i]) for i in range(span)]
         digits = [pack[rows : rows + PAD].astype(F32)[:TOPK] for pack in packs]
@@ -106,32 +107,50 @@
         own = picked[0:1, :] == own_ids
         for t in range(1, TOPK):
             own = own | (picked[t : t + 1, :] == own_ids)
-        own = jnp.where(own, 1.0, 0.0)
-        rank = jnp.where(own > 0.5, mm(own.astype(BF16), earlier), -1.0)
-        hot = jnp.concatenate(
-            [jnp.where(rank[b : b + 1, :] == place, 1.0, 0.0) for b in range(block_count)], axis=0
-        ).astype(BF16)
-        hot_ref[g] = hot
-        q_group = joined([pack[:rows] for pack in packs], 0)
+        owns.append(jnp.where(own, 1.0, 0.0))
+        q_groups.append(joined([pack[:rows] for pack in packs], 0))
+    own_all = jnp.concatenate(owns, axis=0)
+    rank_all = jnp.where(own_all > 0.5, mm(own_all.astype(BF16), earlier), -1.0)
+    hots = []
+    for g in range(groups):
+        rank = rank_all[g * block_count : (g + 1) * block_count]
+        hots.append(
+            jnp.concatenate(
+                [
+                    jnp.where(rank[b : b + 1, :] == place, 1.0, 0.0).astype(BF16)
+                    for b in range(block_count)
+                ],
+                axis=0,
+            )
+        )
+        hot_ref[g] = hots[g]
+    all_marks = [mm(wide_marks, q_groups[g], NT) for g in range(groups)]
+    for g in range(groups):
+        qg_ref[:, g * cap : (g + 1) * cap, :] = (
+            mm(hots[g], q_groups[g]).astype(BF16).reshape(block_count, cap, width)
+        )
+    tails = []
+    for g in range(groups):
         tops, sums = [], []
-        marks = scale * mm(wide_marks, q_group, NT)
         for h in range(heads):
-            mark = jnp.where(own > 0.5, marks[h * block_count : (h + 1) * block_count], LOW)
+            mark = scale * all_marks[g][h * block_count : (h + 1) * block_count]
+            mark = jnp.where(owns[g] > 0.5, mark, LOW)
             top = jnp.max(mark, axis=0, keepdims=True).astype(BF16).astype(F32)
             tops.append(top)
-            sums.append(jnp.sum(own * jnp.exp(mark - top), axis=0, keepdims=True))
+            sums.append(jnp.sum(owns[g] * jnp.exp(mark - top), axis=0, keepdims=True))
         tops, sums = jnp.concatenate(tops, axis=0), jnp.concatenate(sums, axis=0)
         upper = sums.astype(BF16).astype(F32)
         spare = jnp.zeros((HD - 3 * heads, group_rows), F32)
-        tail = jnp.concatenate([tops, upper, sums - upper, spare], axis=0)
-        topg_ref[:, g * cap : (g + 1) * cap, :] = mm(hot, tail.astype(BF16), NT).reshape(
+        tails.append(jnp.concatenate([tops, upper, sums - upper, spare], axis=0))
+    for g in range(groups):
+        topg_ref[:, g * cap : (g + 1) * cap, :] = mm(hots[g], tails[g].astype(BF16), NT).reshape(
             block_count, cap, HD
         )
+    for g in range(groups):
         for i in range(span):
-            part_refs[g * span + i][:, width:] = tail[:, i * rows : (i + 1) * rows].T.astype(BF16)
-        qg_ref[:, g * cap : (g + 1) * cap, :] = (
-            mm(hot, q_group).astype(BF16).reshape(block_count, cap, width)
-        )
+            part_refs[g * span + i][:, width:] = (
+                tails[g][:, i * rows : (i + 1) * rows].T.astype(BF16)
+            )
 
     def one_block(b, carry):
         pairs = [slice(p * 2 * HD, (p + 1) * 2 * HD) for p in range(heads // 2)]
@@ -226,17 +245,35 @@
         out_ref[:, heads * HD :] = tailed([tops] + digits_of(sums, 2), out_ref.shape[0])
 
 
-def grad_kernel(w_ref, full_ref, ga_ref, w_buf, sems):
-    parts, step = w_buf.shape[0], w_buf.shape[1]
+def grad_kernel(lines, line_ref, w_ref, *refs):
+    own_ref, up_refs, down_refs = refs[0], refs[1:lines], refs[lines : 2 * lines - 1]
+    ga_ref, blocks_ref, full_ref, w_buf, sems = refs[2 * lines - 1 :]
+    width = own_ref.shape[1]
+    chunks, _, share = blocks_ref.shape
+    line = line_ref[0]
     copies = [
-        pltpu.make_async_copy(w_ref.at[pl.ds(i * step, step)], w_buf.at[i], sems.at[i])
-        for i in range(parts)
+        pltpu.make_async_copy(w_ref.at[pl.ds(i * width, width)], w_buf.at[i], sems.at[i])
+        for i in range(lines)
     ]
     start(copies)
+    full_ref[line] = own_ref[...]
+    for d in range(1, lines):
+
+        @pl.when(line >= d)
+        def _():
+            full_ref[line - d] = up_refs[d - 1][...]
+
+        @pl.when(line + d < lines)
+        def _():
+            full_ref[line + d] = down_refs[d - 1][...]
+
+    for j in range(chunks):
+        first = j * share
+        blocks_ref[j] = full_ref[first // width, :, first % width : first % width + share]
     total = None
-    for i in range(parts):
+    for i in range(lines):
         copies[i].wait()
-        term = mm(full_ref[i * step : (i + 1) * step], w_buf[i], TN)
+        term = mm(full_ref[i], w_buf[i])
         total = term if total is None else total + term
     ga_ref[...] = total.astype(BF16)
 
@@ -330,8 +367,8 @@
 def weight_kernel(counts, me_ref, cols_ref, *refs):
     attns, (out_ref,) = dealt(refs, counts)
     me = me_ref[0]
-    columns = joined([cols_ref[me ^ m] for m in range(len(counts))], 1)
-    out_ref[...] = mm(columns, joined([whole(pieces) for pieces in attns], 0))
+    columns = joined([cols_ref[me ^ m] for m in range(len(counts))], 0)
+    out_ref[...] = mm(columns, joined([whole(pieces) for pieces in attns], 0), TN)
 
 
 def swap(x, bits):
@@ -356,9 +393,11 @@
     return [[x], [near[0]], [near[1]], far]
 
 
-def with_cores(lists, own):
-    both = [lists[0], [swap(own, 1)]]
-    for pieces in lists[1:]:
+def with_cores(lists, *before):
+    both = []
+    for pieces in lists:
+        if before and pieces is lists[-1]:
+            pieces = [after(piece, *before) for piece in pieces]
         both += [pieces, [swap(piece, 1) for piece in pieces]]
     return both
 
@@ -366,7 +405,7 @@
 def from_core(parts, *before):
     received = [None] * (len(parts) // 2)
     for j in reversed(range(len(received))):
-        received[j] = after(swap(parts[2 * j + 1], 1), *before)
+        received[j] = swap(after(parts[2 * j + 1], *before), 1)
     return received
 
 
@@ -429,9 +468,19 @@
     return terms + [[x_top, x_low], [y_top, y_low]]
 
 
+def spread_line(x):
+    lines = lax.axis_size("head")
+    ups, downs = [x], [x]
+    for d in range(1, lines):
+        ups.append(lax.ppermute(ups[-1], "head", [(i, i + 1) for i in range(d - 1, lines - 1)]))
+        downs.append(lax.ppermute(downs[-1], "head", [(i, i - 1) for i in range(1, lines - d + 1)]))
+    return ups[1:], downs[1:]
+
+
 def body(queries, key_rows, value_rows, selected, out_grad, out_weight):
     chunks = lax.axis_size("ctx")
     chips = chunks // 2
+    lines = lax.axis_size("head")
     rows, width = queries.shape
     features = out_weight.shape[0]
     heads = width // HD
@@ -448,7 +497,6 @@
     values = value_rows.reshape(block_count, BLOCK, width)
     vmem = pl.BlockSpec(memory_space=pltpu.VMEM)
     smem = pl.BlockSpec(memory_space=pltpu.SMEM)
-    anywhere = pl.BlockSpec(memory_space=pl.ANY)
 
     def limit(mib):
         return pltpu.CompilerParams(vmem_limit_bytes=mib * MIB)
@@ -456,8 +504,7 @@
     def shaped(shape, kind=BF16):
         return jax.ShapeDtypeStruct(shape, kind)
 
-    grad_full = lax.all_gather(out_grad.T, "head", axis=0, tiled=True)
-    columns = lax.all_to_all(grad_full, "ctx", split_axis=0, concat_axis=0, tiled=True)
+    ups, downs = spread_line(out_grad)
     packed = pl.pallas_call(
         pack_kernel,
         out_shape=shaped((rows + PAD, width)),
@@ -466,8 +513,8 @@
         compiler_params=limit(8),
         name="pack",
     )(selected.T, queries)
-    query_chips = spread_chips(packed, rows // 2)
-    query_all = with_cores(query_chips, packed)
+    query_chips = spread_chips(packed, rows // 2, ups[0], downs[0])
+    query_all = with_cores(query_chips, ups[1], downs[1])
 
     outs = pl.pallas_call(
         functools.partial(forward_kernel, [len(pieces) for pieces in query_all], span, cap),
@@ -484,24 +531,28 @@
             pltpu.VMEM((block_count, slots, HD), F32),
             pltpu.VMEM((block_count, slots, width), BF16),
         ],
-        compiler_params=limit(40),
+        compiler_params=limit(30),
         name="forward",
     )(me, keys[:, BLOCK - 1], keys, values, *flat(query_all))
     q_slots, probs, logits, hot = outs[chunks:]
 
-    grad_attn = pl.pallas_call(
-        grad_kernel,
-        out_shape=shaped((rows, width)),
-        in_specs=[anywhere, vmem],
-        out_specs=vmem,
+    line = lax.axis_index("head").astype(jnp.int32).reshape(1)
+    grad_attn, blocks = pl.pallas_call(
+        functools.partial(grad_kernel, lines),
+        out_shape=[shaped((rows, width)), shaped((chunks, rows, features // chunks))],
+        in_specs=[smem, pl.BlockSpec(memory_space=pltpu.HBM)] + [vmem] * (2 * lines - 1),
+        out_specs=[vmem] * 2,
         scratch_shapes=[
-            pltpu.VMEM((features // width, width, width), BF16),
-            pltpu.SemaphoreType.DMA((features // width,)),
+            pltpu.VMEM((lines, rows, width), BF16),
+            pltpu.VMEM((lines, width, width), BF16),
+            pltpu.SemaphoreType.DMA((lines,)),
         ],
-        compiler_params=limit(24),
+        compiler_params=limit(28),
         name="grad",
-    )(out_weight, grad_full)
-    terms = merge_chips(outs[:chunks], from_core(outs[:chunks]), heads, grad_attn)
+    )(line, out_weight, out_grad, *ups, *downs)
+    columns = lax.all_to_all(blocks, "ctx", split_axis=0, concat_axis=0, tiled=True)
+    received = from_core(outs[:chunks], *ups[2:], *downs[2:])
+    terms = merge_chips(outs[:chunks], received, heads, grad_attn)
     attn_out, extended = pl.pallas_call(
         functools.partial(finish_kernel, [len(pieces) for pieces in terms]),
         out_shape=[shaped((rows, width)), shaped((rows, width + HD))],
@@ -510,8 +561,8 @@
         compiler_params=limit(24),
         name="finish",
     )(*flat(terms), grad_attn)
-    grad_chips = spread_chips(extended, rows // 2, columns)
-    grad_all = with_cores(grad_chips, extended)
+    grad_chips = spread_chips(extended, rows // 2)
+    grad_all = with_cores(grad_chips)
     arrived = flat(grad_chips[1:3])
     attns = [[attn_out]] + [[swap(after(attn_out, *arrived), 2 * j)] for j in range(1, chips)]
 
@@ -525,9 +576,9 @@
             pltpu.VMEM((block_count, slots, width + HD), BF16),
             pltpu.VMEM((block_count, slots, width), BF16),
         ],
-        compiler_params=limit(44),
+        compiler_params=limit(40),
         name="backward",
-    )(hot, q_slots, probs, logits, keys, values, *flat(grad_all))
+    )(hot, q_slots, probs, after(logits, columns), keys, values, *flat(grad_all))
     key_grad, value_grad = outs[chunks:]
     terms = collect_chips(outs[:chunks], from_core(outs[:chunks], *flat(attns[1:])))
     query_grad = pl.pallas_call(
@@ -539,7 +590,7 @@
         name="total",
     )(*flat(terms))
 
-    attns = with_cores(attns, attn_out)
+    attns = with_cores(attns)
     weight_grad = pl.pallas_call(
         functools.partial(weight_kernel, [len(pieces) for pieces in attns]),
         out_shape=shaped((features // chunks, width), F32),
@@ -547,7 +598,7 @@
         out_specs=vmem,
         compiler_params=limit(24),
         name="weight",
-    )(after(me, *flat(terms)), columns.reshape(chunks, features // chunks, rows), *flat(attns))
+    )(after(me, *flat(terms)), columns, *flat(attns))
     return (
         query_grad,
         key_grad.reshape(-1, width),

time: 212 us -> 237 us (1.12)
  local copies, waits for them, and re-layouts: 9.73 us -> 38.8 us
  between operations: 14.3 us -> 0.98 us
  starting transfers between devices: 37.2 us -> 45.9 us
    unnamed x26 -> x85, local copies, waits for them, and re-layouts: 7.2 us -> 38.7 us
    all_gather x1 -> x0, waiting for transfers between devices: 19.9 us -> none  [body(): grad_full = lax.all_gather(out_grad.T, 'head', axis=0, tiled=True)]
    ppermute x0 -> x6, starting transfers between devices: none -> 11.8 us  [the longest x3 7.98 us: spread_line(): lax.ppermute(ups[-1], 'head', [(i, i + 1) for i in range(d - 1, lines - 1)])]
    ppermute x0 -> x6, waiting for transfers between devices: none -> 11.3 us  [the longest x3 6.79 us: spread_line(): lax.ppermute(downs[-1], 'head', [(i, i - 1) for i in range(1, lines - d +...]
    ppermute x45, waiting for transfers between devices: 72.1 us -> 79.6 us  [swap(): return lax.ppermute(x, 'ctx', [(i, i ^ bits) for i in range(count)])]
    pallas_call x1, Pallas kernels: 19.6 us -> 14.5 us  [body(): pl.pallas_call(functools.partial(forward_kernel, [len(pieces) for pieces...]
    pallas_call x3, Pallas kernels: 5.82 us -> 9.35 us  [merged(): pl.pallas_call(functools.partial(merge_kernel, plan, heads), out_shape=[j...]
    ppermute x45, starting transfers between devices: 32.7 us -> 29.6 us  [swap(): return lax.ppermute(x, 'ctx', [(i, i ^ bits) for i in range(count)])]
  transfers between devices with their start and end apart: 47 -> 52, of which waited for: 16 -> 19; matrix products, arithmetic and copies ran while one was open for 2% -> 0% of each run, Pallas kernels for 25% -> 22%
where the time goes in v7:
time: 237 us; the launch traced here: 236 us
  waiting for transfers between devices  90.9 us (38%)
  Pallas kernels  58.4 us (25%)
  starting transfers between devices  45.9 us (19%)
  local copies, waits for them, and re-layouts  38.8 us (16%)
    ppermute x45, waiting for transfers between devices, swap(): return lax.ppermute(x, 'ctx', [(i, i ^ bits) for i in range(count)])  79.6 us
    unnamed x85, local copies, waits for them, and re-layouts  38.7 us
    ppermute x45, starting transfers between devices, swap(): return lax.ppermute(x, 'ctx', [(i, i ^ bits) for i in range(count)])  29.6 us
    pallas_call x1, Pallas kernels, body(): pl.pallas_call(functools.partial(backward_kernel, [len(pieces) for pieces...  17.9 us
    pallas_call x1, Pallas kernels, body(): pl.pallas_call(functools.partial(forward_kernel, [len(pieces) for pieces...  14.5 us
    pallas_call x3, Pallas kernels, merged(): pl.pallas_call(functools.partial(merge_kernel, plan, heads), out_shape=[j...  9.35 us
    ppermute x3, starting transfers between devices, spread_line(): lax.ppermute(ups[-1], 'head', [(i, i + 1) for i in range(d - 1, lines - 1)])  7.98 us
    ppermute x3, waiting for transfers between devices, spread_line(): lax.ppermute(downs[-1], 'head', [(i, i - 1) for i in range(1, lines - d +...  6.79 us
  transfers between devices with their start and end apart: 52, of which 19 were waited for; matrix products, arithmetic and copies ran while one was open for 0% of the time, Pallas kernels for 22%

profile of v7, /device:TPU:0, one launch (start us, length us, event | category | flops | bytes accessed | tf_op | source)
XLA Modules:
  0.0 235.7 jit_solution(2147695375462928300)
XLA Ops:
  0.6 5.1 %collective-permute-start.5 = (bf16[256,1024]{1,0:T(8,128)(2,1)}, bf16[256,1024]{1,0:T(8,128)(2,1)S(1)}, u32[]{:S(2)}, u32[]{:S(2)}) collective-permute-start(bf16[256,1024]{1,0:T(8,128)(2,1)} %refs_0_.1), channel_id=1, source_target_pairs={{0,1},{1,2},{2,3},{4,5},{5,6},{6,7},{8,9},{9,10},{10,11},{12,13},{... | collective-permute-start | bytes 1572872 | tf_op jit(solution)/shard_map/ppermute | solution.py:475
  12.7 4.5 %collective-permute-done.5.refs_1_ = bf16[256,1024]{1,0:T(8,128)(2,1)S(1)} collective-permute-done((bf16[256,1024]{1,0:T(8,128)(2,1)}, bf16[256,1024]{1,0:T(8,128)(2,1)S(1)}, u32[]{:S(2)}, u32[]{:S(2)}) %collective-permute-start.5) | collective-permute-done | bytes 524320 | tf_op jit(solution)/shard_map/ppermute | solution.py:475
  18.6 2.6 %collective-permute-done.6.refs_4_ = bf16[256,1024]{1,0:T(8,128)(2,1)S(1)} collective-permute-done((bf16[256,1024]{1,0:T(8,128)(2,1)}, bf16[256,1024]{1,0:T(8,128)(2,1)S(1)}, u32[]{:S(2)}, u32[]{:S(2)}) %collective-permute-start.6) | collective-permute-done | bytes 524320 | tf_op jit(solution)/shard_map/ppermute | solution.py:476
  28.1 2.9 %collective-permute-done.10.refs_7_ = bf16[144,1024]{1,0:T(8,128)(2,1)S(1)} collective-permute-done((bf16[144,1024]{1,0:T(8,128)(2,1)S(1)}, bf16[144,1024]{1,0:T(8,128)(2,1)S(1)}, u32[]{:S(2)}, u32[]{:S(2)}) %collective-permute-start.10) | collective-permute-done | bytes 294944 | tf_op jit(solution)/shard_map/ppermute | solution.py:376
  32.4 4.2 %collective-permute-done.9.refs_5_ = bf16[256,1024]{1,0:T(8,128)(2,1)} collective-permute-done((bf16[256,1024]{1,0:T(8,128)(2,1)S(1)}, bf16[256,1024]{1,0:T(8,128)(2,1)}, u32[]{:S(2)}, u32[]{:S(2)}) %collective-permute-start.9) | collective-permute-done | bytes 524320 | tf_op jit(solution)/shard_map/ppermute | solution.py:476
  50.4 14.5 %forward.1 = (bf16[256,1152]{1,0:T(8,128)(2,1)S(1)}, bf16[256,1152]{1,0:T(8,128)(2,1)}, bf16[256,1152]{1,0:T(8,128)(2,1)S(1)}, bf16[256,1152]{1,0:T(8,128)(2,1)}...) custom-call(s32[1]{0:T(128)} %bitcast.me_ref, ...), custom_call_target="tpu_custom_call" | custom-call | tf_op jit(solution)/shard_map/forward/pallas_call | solution.py:519
  64.9 2.0 copy-done.3
  71.2 2.6 %merge.4 = (bf16[128,1152]{1,0:T(8,128)(2,1)}, bf16[128,1152]{1,0:T(8,128)(2,1)}) custom-call(bf16[256,1152]{1,0:T(8,128)(2,1)S(1)} %get-tuple-element.72.refs_0_, bf16[256,1152]{1,0:T(8,128)(2,1)S(1)} %collective-permute-done.19.refs_1_), custom_call_target="tpu_custom_call" | custom-call | tf_op jit(solution)/shard_map/merge/pallas_call | solution.py:438
  76.8 3.4 %copy-done.1 = bf16[4096,1024]{1,0:T(8,128)(2,1)S(1)} copy-done((bf16[4096,1024]{1,0:T(8,128)(2,1)S(1)}, bf16[4096,1024]{1,0:T(8,128)(2,1)}, u32[]{:S(2)}) %copy-start.1) | copy-done | bytes 8388632
  83.3 5.0 %grad.1 = (bf16[256,1024]{1,0:T(8,128)(2,1)S(1)}, bf16[8,256,512]{2,1,0:T(8,128)(2,1)S(1)}) custom-call(s32[1]{0:T(128)} %bitcast.4.line_ref, bf16[4096,1024]{1,0:T(8,128)(2,1)S(1)} %copy-done.1, bf16[256,1024]{1,0:T(8,128)(2,1)S(1)} %copy-done.31, bf16[256,1024]{1,0:T(8,128)(2,1)S(1)} %copy-done.33, bf16[256,1024]{1,0:T(8,128)(2,1)} %collective-permute-done.8.refs_2_, ...), custom_call_target="tpu_custom_call" | custom-call | tf_op jit(solution)/shard_map/grad/pallas_call | solution.py:540
  90.5 4.5 %all-to-all-start = ((bf16[8,256,512]{2,1,0:T(8,128)(2,1)}), bf16[8,256,512]{2,1,0:T(8,128)(2,1)}, u32[]{:S(2)}, u32[]{:S(2)}) async-start(bf16[8,256,512]{2,1,0:T(8,128)(2,1)} %copy-done.6), calls=%async_computation | async-start | bytes 4194304 | tf_op jit(solution)/shard_map/all_to_all | solution.py:553
  95.0 3.1 %merge.3 = (bf16[128,1152]{1,0:T(8,128)(2,1)S(1)}, bf16[128,1152]{1,0:T(8,128)(2,1)S(1)}) custom-call(bf16[256,1152]{1,0:T(8,128)(2,1)S(1)} %get-tuple-element.65.refs_0_, bf16[256,1152]{1,0:T(8,128)(2,1)} %collective-permute-done.16.refs_1_, bf16[256,1152]{1,0:T(8,128)(2,1)S(1)} %get-tuple-element.68.refs_2_, bf16[256,1152]{1,0:T(8,128)(2,1)} %collective-permute-done.17.refs_3_), custom_call_target="tpu_custom_call" | custom-call | tf_op jit(solution)/shard_map/merge/pallas_call | solution.py:438
  101.4 3.7 %merge.5 = (bf16[128,1152]{1,0:T(8,128)(2,1)S(1)}, bf16[128,1152]{1,0:T(8,128)(2,1)S(1)}) custom-call(bf16[256,1152]{1,0:T(8,128)(2,1)S(1)} %get-tuple-element.65.refs_0_, bf16[256,1152]{1,0:T(8,128)(2,1)} %collective-permute-done.16.refs_1_, bf16[256,1152]{1,0:T(8,128)(2,1)S(1)} %get-tuple-element.68.refs_2_, ...), custom_call_target="tpu_custom_call" | custom-call | tf_op jit(solution)/shard_map/merge/pallas_call | solution.py:438
  106.0 21.2 %collective-permute-done.18.refs_2_ = bf16[128,1152]{1,0:T(8,128)(2,1)S(1)} collective-permute-done((bf16[128,1152]{1,0:T(8,128)(2,1)S(1)}, bf16[128,1152]{1,0:T(8,128)(2,1)S(1)}, u32[]{:S(2)}, u32[]{:S(2)}) %collective-permute-start.18) | collective-permute-done | bytes 294944 | tf_op jit(solution)/shard_map/ppermute | solution.py:376
  127.3 5.8 %collective-permute-done.22.refs_3_ = bf16[128,1152]{1,0:T(8,128)(2,1)S(1)} collective-permute-done((bf16[128,1152]{1,0:T(8,128)(2,1)S(1)}, bf16[128,1152]{1,0:T(8,128)(2,1)S(1)}, u32[]{:S(2)}, u32[]{:S(2)}) %collective-permute-start.22) | collective-permute-done | bytes 294944 | tf_op jit(solution)/shard_map/ppermute | solution.py:376
  133.1 4.4 %finish.1 = (bf16[256,1024]{1,0:T(8,128)(2,1)}, bf16[256,1152]{1,0:T(8,128)(2,1)S(1)}) custom-call(bf16[256,1152]{1,0:T(8,128)(2,1)S(1)} %copy-done.24, bf16[256,1152]{1,0:T(8,128)(2,1)} %collective-permute-done.15.refs_1_, bf16[128,1152]{1,0:T(8,128)(2,1)S(1)} %collective-permute-done.18.refs_2_, bf16[128,1152]{1,0:T(8,128)(2,1)S(1)} %collective-permute-done.22.refs_3_, ...), custom_call_target="tpu_custom_call" | custom-call | tf_op jit(solution)/shard_map/finish/pallas_call | solution.py:556
  139.6 12.9 %collective-permute-done.26.refs_2_ = bf16[256,1152]{1,0:T(8,128)(2,1)S(1)} collective-permute-done((bf16[256,1152]{1,0:T(8,128)(2,1)S(1)}, bf16[256,1152]{1,0:T(8,128)(2,1)S(1)}, u32[]{:S(2)}, u32[]{:S(2)}) %collective-permute-start.26) | collective-permute-done | bytes 589856 | tf_op jit(solution)/shard_map/ppermute | solution.py:376
  157.6 6.0 %collective-permute-done.30.refs_6_ = bf16[128,1152]{1,0:T(8,128)(2,1)} collective-permute-done((bf16[128,1152]{1,0:T(8,128)(2,1)S(1)}, bf16[128,1152]{1,0:T(8,128)(2,1)}, u32[]{:S(2)}, u32[]{:S(2)}) %collective-permute-start.30) | collective-permute-done | bytes 294944 | tf_op jit(solution)/shard_map/ppermute | solution.py:376
  177.3 17.9 %backward.1 = (bf16[256,1024]{1,0:T(8,128)(2,1)S(1)}, bf16[256,1024]{1,0:T(8,128)(2,1)S(1)}, bf16[256,1024]{1,0:T(8,128)(2,1)S(1)}, bf16[256,1024]{1,0:T(8,128)(...) custom-call(bf16[8,256,256]{2,1,0:T(8,128)(2,1)S(1)} %copy-done.14, ...), custom_call_target="tpu_custom_call" | custom-call | tf_op jit(solution)/shard_map/backward/pallas_call | solution.py:569
  199.3 6.8 %collective-permute-done.41 = bf16[128,1024]{1,0:T(8,128)(2,1)S(1)} collective-permute-done((bf16[128,1024]{1,0:T(8,128)(2,1)S(1)}, bf16[128,1024]{1,0:T(8,128)(2,1)S(1)}, u32[]{:S(2)}, u32[]{:S(2)}) %collective-permute-start.41) | collective-permute-done | bytes 262176 | tf_op jit(solution)/shard_map/ppermute | solution.py:376
  210.1 5.5 %collective-permute-done.39.refs_2_ = bf16[128,1024]{1,0:T(8,128)(2,1)S(1)} collective-permute-done((bf16[128,1024]{1,0:T(8,128)(2,1)S(1)}, bf16[128,1024]{1,0:T(8,128)(2,1)S(1)}, u32[]{:S(2)}, u32[]{:S(2)}) %collective-permute-start.39) | collective-permute-done | bytes 262176 | tf_op jit(solution)/shard_map/ppermute | solution.py:376
  215.6 4.1 %collective-permute-done.42.refs_3_ = bf16[128,1024]{1,0:T(8,128)(2,1)S(1)} collective-permute-done((bf16[128,1024]{1,0:T(8,128)(2,1)S(1)}, bf16[128,1024]{1,0:T(8,128)(2,1)S(1)}, u32[]{:S(2)}, u32[]{:S(2)}) %collective-permute-start.42) | collective-permute-done | bytes 262176 | tf_op jit(solution)/shard_map/ppermute | solution.py:376
  220.6 7.9 %collective-permute-done.46.refs_5_ = bf16[128,1024]{1,0:T(8,128)(2,1)S(1)} collective-permute-done((bf16[128,1024]{1,0:T(8,128)(2,1)S(1)}, bf16[128,1024]{1,0:T(8,128)(2,1)S(1)}, u32[]{:S(2)}, u32[]{:S(2)}) %collective-permute-start.46) | collective-permute-done | bytes 262176 | tf_op jit(solution)/shard_map/ppermute | solution.py:376
  229.9 5.8 %weight.1 = f32[512,1024]{1,0:T(8,128)} custom-call(s32[1]{0:T(128)} %bitcast.me_ref, bf16[8,256,512]{2,1,0:T(8,128)(2,1)} %all-to-all-done.cols_ref, bf16[256,1024]{1,0:T(8,128)(2,1)} %get-tuple-element.86.refs_0_, bf16[256,1024]{1,0:T(8,128)(2,1)S(1)} %collective-permute-done.47.refs_1_, bf16[256,1024]{1,0:T(8,128)(2,1)} %collective-permute-done.34.refs_2_, ...), custom_call_target="tpu_custom_call" | custom-call | tf_op jit(solution)/shard_map/weight/pallas_call | solution.py:594
  (183 shorter events, 78.1 us)
Async XLA Ops:
  0.6 16.5 %collective-permute-start.5 = (bf16[256,1024]{1,0:T(8,128)(2,1)}, bf16[256,1024]{1,0:T(8,128)(2,1)S(1)}, u32[]{:S(2)}, u32[]{:S(2)}) collective-permute-start(bf16[256,1024]{1,0:T(8,128)(2,1)} %refs_0_.1), channel_id=1, source_target_pairs={{0,1},{1,2},{2,3},{4,5},{5,6},{6,7},{8,9},{9,10},{10,11},{12,13},{... | collective-permute-start | bytes 1572872 | tf_op jit(solution)/shard_map/ppermute | solution.py:475
  5.7 15.5 %collective-permute-start.6 = (bf16[256,1024]{1,0:T(8,128)(2,1)}, bf16[256,1024]{1,0:T(8,128)(2,1)S(1)}, u32[]{:S(2)}, u32[]{:S(2)}) collective-permute-start(bf16[256,1024]{1,0:T(8,128)(2,1)} %refs_0_.1), channel_id=1, source_target_pairs={{1,0},{2,1},{3,2},{5,4},{6,5},{7,6},{9,8},{10,9},{11,10},{13,12},{... | collective-permute-start | bytes 1572872 | tf_op jit(solution)/shard_map/ppermute | solution.py:476
  10.4 14.5 %collective-permute-start.1 = (bf16[272,1024]{1,0:T(8,128)(2,1)S(1)}, bf16[272,1024]{1,0:T(8,128)(2,1)S(1)}, u32[]{:S(2)}, u32[]{:S(2)}) collective-permute-start(bf16[272,1024]{1,0:T(8,128)(2,1)S(1)} %pack.1.refs_0_), channel_id=1, source_target_pairs={{0,8},{4,12},{8,0},{12,4},{16,24},{20,28},{24,16},{28,20},{1,9},{5... | collective-permute-start | bytes 1671176 | tf_op jit(solution)/shard_map/ppermute | solution.py:376
  21.2 15.4 %collective-permute-start.9 = (bf16[256,1024]{1,0:T(8,128)(2,1)S(1)}, bf16[256,1024]{1,0:T(8,128)(2,1)}, u32[]{:S(2)}, u32[]{:S(2)}) collective-permute-start(bf16[256,1024]{1,0:T(8,128)(2,1)S(1)} %collective-permute-done.6.refs_4_), channel_id=1, source_target_pairs={{1,0},{2,1},{5,4},{6,5},{9,8},{10,9},{13,12},{14,13},{17,16},{18,1... | collective-permute-start | bytes 1572872 | tf_op jit(solution)/shard_map/ppermute | solution.py:476
  31.0 38.2 %collective-permute-start.13 = (bf16[256,1024]{1,0:T(8,128)(2,1)}, bf16[256,1024]{1,0:T(8,128)(2,1)}, u32[]{:S(2)}, u32[]{:S(2)}) collective-permute-start(bf16[256,1024]{1,0:T(8,128)(2,1)} %collective-permute-done.8.refs_2_), channel_id=1, source_target_pairs={{2,3},{6,7},{10,11},{14,15},{18,19},{22,23},{26,27},{30,31}} | collective-permute-start | bytes 1572872 | tf_op jit(solution)/shard_map/ppermute | solution.py:475
  36.6 32.6 %collective-permute-start.14 = (bf16[256,1024]{1,0:T(8,128)(2,1)}, bf16[256,1024]{1,0:T(8,128)(2,1)}, u32[]{:S(2)}, u32[]{:S(2)}) collective-permute-start(bf16[256,1024]{1,0:T(8,128)(2,1)} %collective-permute-done.9.refs_5_), channel_id=1, source_target_pairs={{1,0},{5,4},{9,8},{13,12},{17,16},{21,20},{25,24},{29,28}} | collective-permute-start | bytes 1572872 | tf_op jit(solution)/shard_map/ppermute | solution.py:476
  69.6 25.4 %collective-permute-start.16 = (bf16[256,1152]{1,0:T(8,128)(2,1)}, bf16[256,1152]{1,0:T(8,128)(2,1)}, u32[]{:S(2)}, u32[]{:S(2)}) collective-permute-start(bf16[256,1152]{1,0:T(8,128)(2,1)} %get-tuple-element.67), channel_id=1, source_target_pairs={{0,4},{4,0},{8,12},{12,8},{16,20},{20,16},{24,28},{28,24},{1,5},{5... | collective-permute-start | bytes 1769480 | tf_op jit(solution)/shard_map/ppermute | solution.py:376
  69.8 25.3 %collective-permute-start.17 = (bf16[256,1152]{1,0:T(8,128)(2,1)}, bf16[256,1152]{1,0:T(8,128)(2,1)}, u32[]{:S(2)}, u32[]{:S(2)}) collective-permute-start(bf16[256,1152]{1,0:T(8,128)(2,1)} %get-tuple-element.70), channel_id=1, source_target_pairs={{0,4},{4,0},{8,12},{12,8},{16,20},{20,16},{24,28},{28,24},{1,5},{5... | collective-permute-start | bytes 1769480 | tf_op jit(solution)/shard_map/ppermute | solution.py:376
  73.8 27.6 %collective-permute-start.20 = (bf16[128,1152]{1,0:T(8,128)(2,1)}, bf16[128,1152]{1,0:T(8,128)(2,1)}, u32[]{:S(2)}, u32[]{:S(2)}) collective-permute-start(bf16[128,1152]{1,0:T(8,128)(2,1)} %get-tuple-element.75), channel_id=1, source_target_pairs={{0,16},{4,20},{8,24},{12,28},{16,0},{20,4},{24,8},{28,12},{1,17},{... | collective-permute-start | bytes 884744 | tf_op jit(solution)/shard_map/ppermute | solution.py:376
  75.3 26.1 %collective-permute-start.21 = (bf16[128,1152]{1,0:T(8,128)(2,1)}, bf16[128,1152]{1,0:T(8,128)(2,1)}, u32[]{:S(2)}, u32[]{:S(2)}) collective-permute-start(bf16[128,1152]{1,0:T(8,128)(2,1)} %get-tuple-element.78), channel_id=1, source_target_pairs={{0,8},{4,12},{8,0},{12,4},{16,24},{20,28},{24,16},{28,20},{1,9},{5... | collective-permute-start | bytes 884744 | tf_op jit(solution)/shard_map/ppermute | solution.py:376
  76.8 29.2 %collective-permute-start.15 = (bf16[256,1152]{1,0:T(8,128)(2,1)}, bf16[256,1152]{1,0:T(8,128)(2,1)}, u32[]{:S(2)}, u32[]{:S(2)}) collective-permute-start(bf16[256,1152]{1,0:T(8,128)(2,1)} %get-tuple-element.64), channel_id=1, source_target_pairs={{0,4},{4,0},{8,12},{12,8},{16,20},{20,16},{24,28},{28,24},{1,5},{5... | collective-permute-start | bytes 1769480 | tf_op jit(solution)/shard_map/ppermute | solution.py:376
  90.5 78.2 %all-to-all-start = ((bf16[8,256,512]{2,1,0:T(8,128)(2,1)}), bf16[8,256,512]{2,1,0:T(8,128)(2,1)}, u32[]{:S(2)}, u32[]{:S(2)}) async-start(bf16[8,256,512]{2,1,0:T(8,128)(2,1)} %copy-done.6), calls=%async_computation | async-start | bytes 4194304 | tf_op jit(solution)/shard_map/all_to_all | solution.py:553
  98.1 29.1 %collective-permute-start.18 = (bf16[128,1152]{1,0:T(8,128)(2,1)S(1)}, bf16[128,1152]{1,0:T(8,128)(2,1)S(1)}, u32[]{:S(2)}, u32[]{:S(2)}) collective-permute-start(bf16[128,1152]{1,0:T(8,128)(2,1)S(1)} %get-tuple-element.71), channel_id=1, source_target_pairs={{0,8},{4,12},{8,0},{12,4},{16,24},{20,28},{24,16},{28,20},{1,9},{5... | collective-permute-start | bytes 884744 | tf_op jit(solution)/shard_map/ppermute | solution.py:376
  99.9 27.4 %collective-permute-start.24 = (bf16[128,1152]{1,0:T(8,128)(2,1)S(1)}, bf16[128,1152]{1,0:T(8,128)(2,1)S(1)}, u32[]{:S(2)}, u32[]{:S(2)}) collective-permute-start(bf16[128,1152]{1,0:T(8,128)(2,1)S(1)} %get-tuple-element.81), channel_id=1, source_target_pairs={{0,16},{4,20},{8,24},{12,28},{16,0},{20,4},{24,8},{28,12},{1,17},{... | collective-permute-start | bytes 884744 | tf_op jit(solution)/shard_map/ppermute | solution.py:376
  105.1 28.0 %collective-permute-start.22 = (bf16[128,1152]{1,0:T(8,128)(2,1)S(1)}, bf16[128,1152]{1,0:T(8,128)(2,1)S(1)}, u32[]{:S(2)}, u32[]{:S(2)}) collective-permute-start(bf16[128,1152]{1,0:T(8,128)(2,1)S(1)} %get-tuple-element.79), channel_id=1, source_target_pairs={{0,8},{4,12},{8,0},{12,4},{16,24},{20,28},{24,16},{28,20},{1,9},{5... | collective-permute-start | bytes 884744 | tf_op jit(solution)/shard_map/ppermute | solution.py:376
  105.7 27.4 %collective-permute-start.23 = (bf16[128,1152]{1,0:T(8,128)(2,1)S(1)}, bf16[128,1152]{1,0:T(8,128)(2,1)S(1)}, u32[]{:S(2)}, u32[]{:S(2)}) collective-permute-start(bf16[128,1152]{1,0:T(8,128)(2,1)S(1)} %get-tuple-element.80), channel_id=1, source_target_pairs={{0,16},{4,20},{8,24},{12,28},{16,0},{20,4},{24,8},{28,12},{1,17},{... | collective-permute-start | bytes 884744 | tf_op jit(solution)/shard_map/ppermute | solution.py:376
  137.6 14.9 %collective-permute-start.26 = (bf16[256,1152]{1,0:T(8,128)(2,1)S(1)}, bf16[256,1152]{1,0:T(8,128)(2,1)S(1)}, u32[]{:S(2)}, u32[]{:S(2)}) collective-permute-start(bf16[256,1152]{1,0:T(8,128)(2,1)S(1)} %get-tuple-element.82.refs_0_), channel_id=1, source_target_pairs={{0,8},{4,12},{8,0},{12,4},{16,24},{20,28},{24,16},{28,20},{1,9},{5... | collective-permute-start | bytes 1769480 | tf_op jit(solution)/shard_map/ppermute | solution.py:376
  139.0 15.0 %collective-permute-start.28 = (bf16[256,1152]{1,0:T(8,128)(2,1)S(1)}, bf16[256,1152]{1,0:T(8,128)(2,1)S(1)}, u32[]{:S(2)}, u32[]{:S(2)}) collective-permute-start(bf16[256,1152]{1,0:T(8,128)(2,1)S(1)} %get-tuple-element.82.refs_0_), channel_id=1, source_target_pairs={{0,16},{4,20},{8,24},{12,28},{16,0},{20,4},{24,8},{28,12},{1,17},{... | collective-permute-start | bytes 1769480 | tf_op jit(solution)/shard_map/ppermute | solution.py:376
  139.6 16.3 %collective-permute-start.25 = (bf16[256,1152]{1,0:T(8,128)(2,1)S(1)}, bf16[256,1152]{1,0:T(8,128)(2,1)S(1)}, u32[]{:S(2)}, u32[]{:S(2)}) collective-permute-start(bf16[256,1152]{1,0:T(8,128)(2,1)S(1)} %get-tuple-element.82.refs_0_), channel_id=1, source_target_pairs={{0,4},{4,0},{8,12},{12,8},{16,20},{20,16},{24,28},{28,24},{1,5},{5... | collective-permute-start | bytes 1769480 | tf_op jit(solution)/shard_map/ppermute | solution.py:376
  156.8 38.5 %collective-permute-start.34 = (bf16[256,1024]{1,0:T(8,128)(2,1)}, bf16[256,1024]{1,0:T(8,128)(2,1)}, u32[]{:S(2)}, u32[]{:S(2)}) collective-permute-start(bf16[256,1024]{1,0:T(8,128)(2,1)} %get-tuple-element.86.refs_0_), channel_id=1, source_target_pairs={{0,8},{4,12},{8,0},{12,4},{16,24},{20,28},{24,16},{28,20},{1,9},{5... | collective-permute-start | bytes 1572872 | tf_op jit(solution)/shard_map/ppermute | solution.py:376
  163.6 31.6 %collective-permute-start.35 = (bf16[256,1024]{1,0:T(8,128)(2,1)}, bf16[256,1024]{1,0:T(8,128)(2,1)}, u32[]{:S(2)}, u32[]{:S(2)}) collective-permute-start(bf16[256,1024]{1,0:T(8,128)(2,1)} %get-tuple-element.86.refs_0_), channel_id=1, source_target_pairs={{0,16},{4,20},{8,24},{12,28},{16,0},{20,4},{24,8},{28,12},{1,17},{... | collective-permute-start | bytes 1572872 | tf_op jit(solution)/shard_map/ppermute | solution.py:376
  164.6 30.6 %collective-permute-start.36 = (bf16[256,1024]{1,0:T(8,128)(2,1)}, bf16[256,1024]{1,0:T(8,128)(2,1)}, u32[]{:S(2)}, u32[]{:S(2)}) collective-permute-start(bf16[256,1024]{1,0:T(8,128)(2,1)} %get-tuple-element.86.refs_0_), channel_id=1, source_target_pairs={{0,24},{4,28},{8,16},{12,20},{16,8},{20,12},{24,0},{28,4},{1,25},{... | collective-permute-start | bytes 1572872 | tf_op jit(solution)/shard_map/ppermute | solution.py:376
  209.6 20.3 %collective-permute-start.47 = (bf16[256,1024]{1,0:T(8,128)(2,1)}, bf16[256,1024]{1,0:T(8,128)(2,1)S(1)}, u32[]{:S(2)}, u32[]{:S(2)}) collective-permute-start(bf16[256,1024]{1,0:T(8,128)(2,1)} %get-tuple-element.86.refs_0_), channel_id=1, source_target_pairs={{0,4},{4,0},{8,12},{12,8},{16,20},{20,16},{24,28},{28,24},{1,5},{5... | collective-permute-start | bytes 1572872 | tf_op jit(solution)/shard_map/ppermute | solution.py:376
  209.6 20.3 %collective-permute-start.48 = (bf16[256,1024]{1,0:T(8,128)(2,1)}, bf16[256,1024]{1,0:T(8,128)(2,1)S(1)}, u32[]{:S(2)}, u32[]{:S(2)}) collective-permute-start(bf16[256,1024]{1,0:T(8,128)(2,1)} %collective-permute-done.34.refs_2_), channel_id=1, source_target_pairs={{0,4},{4,0},{8,12},{12,8},{16,20},{20,16},{24,28},{28,24},{1,5},{5... | collective-permute-start | bytes 1572872 | tf_op jit(solution)/shard_map/ppermute | solution.py:376
  (70 other events, 484.5 us)

commit v8 on v7

--- a/solution.py
+++ b/solution.py
@@ -247,7 +247,7 @@
 
 def grad_kernel(lines, line_ref, w_ref, *refs):
     own_ref, up_refs, down_refs = refs[0], refs[1:lines], refs[lines : 2 * lines - 1]
-    ga_ref, blocks_ref, full_ref, w_buf, sems = refs[2 * lines - 1 :]
+    ga_ref, blocks_ref, full_ref, w_buf, sems, piece_sems = refs[2 * lines - 1 :]
     width = own_ref.shape[1]
     chunks, _, share = blocks_ref.shape
     line = line_ref[0]
@@ -256,17 +256,23 @@
         for i in range(lines)
     ]
     start(copies)
-    full_ref[line] = own_ref[...]
+
+    def placed(ref, i):
+        return pltpu.make_async_copy(ref, full_ref.at[i], piece_sems.at[i])
+
+    placed(own_ref, line).start()
     for d in range(1, lines):
 
         @pl.when(line >= d)
         def _():
-            full_ref[line - d] = up_refs[d - 1][...]
+            placed(up_refs[d - 1], line - d).start()
 
         @pl.when(line + d < lines)
         def _():
-            full_ref[line + d] = down_refs[d - 1][...]
-
+            placed(down_refs[d - 1], line + d).start()
+
+    for i in range(lines):
+        placed(own_ref, i).wait()
     for j in range(chunks):
         first = j * share
         blocks_ref[j] = full_ref[first // width, :, first % width : first % width + share]
@@ -429,7 +435,7 @@
     return terms + [[x_top, x_low], [y_top, y_low]]
 
 
-def merge_chips(parts, received, heads, *before):
+def merge_chips(parts, received, heads, between):
     chips = len(received)
     rows = parts[0].shape[0]
     half = rows // 2
@@ -451,7 +457,7 @@
         for j in range(1, chips):
             (both,) = merged([parts[2 * j], received[j]], [[(0, 0, rows), (1, 0, rows)]])
             terms.append([swap(both, 2 * j)])
-        return terms
+        return terms, between(received[0])
     top, low = (0, half), (half, half)
     x_far, y_far = merged(
         [parts[6], received[3]], [[(0, *top), (1, *top)], [(0, *low), (1, *low)]]
@@ -459,13 +465,14 @@
     x_far, y_far = swap(x_far, 2), swap(y_far, 4)
     ins = [parts[2], received[1], parts[4], received[2]]
     x_top, y_low = merged(ins, [[(0, *top), (1, *top)], [(2, *low), (3, *low)]])
+    done = between(x_top, y_low)
     x_top, y_low = swap(x_top, 2), swap(y_low, 4)
     x_low, y_top = merged(
-        ins + [after(y_far, *before), x_far],
+        ins + [after(y_far, done[0]), x_far],
         [[(0, *low), (1, *low), (4, *top)], [(2, *top), (3, *top), (5, *top)]],
     )
     x_low, y_top = swap(x_low, 2), swap(y_top, 4)
-    return terms + [[x_top, x_low], [y_top, y_low]]
+    return terms + [[x_top, x_low], [y_top, y_low]], done
 
 
 def spread_line(x):
@@ -514,7 +521,7 @@
         name="pack",
     )(selected.T, queries)
     query_chips = spread_chips(packed, rows // 2, ups[0], downs[0])
-    query_all = with_cores(query_chips, ups[1], downs[1])
+    query_all = with_cores(query_chips)
 
     outs = pl.pallas_call(
         functools.partial(forward_kernel, [len(pieces) for pieces in query_all], span, cap),
@@ -531,28 +538,33 @@
             pltpu.VMEM((block_count, slots, HD), F32),
             pltpu.VMEM((block_count, slots, width), BF16),
         ],
-        compiler_params=limit(30),
+        compiler_params=limit(40),
         name="forward",
     )(me, keys[:, BLOCK - 1], keys, values, *flat(query_all))
     q_slots, probs, logits, hot = outs[chunks:]
 
     line = lax.axis_index("head").astype(jnp.int32).reshape(1)
-    grad_attn, blocks = pl.pallas_call(
+    make_grad = pl.pallas_call(
         functools.partial(grad_kernel, lines),
         out_shape=[shaped((rows, width)), shaped((chunks, rows, features // chunks))],
-        in_specs=[smem, pl.BlockSpec(memory_space=pltpu.HBM)] + [vmem] * (2 * lines - 1),
+        in_specs=[smem] + [pl.BlockSpec(memory_space=pltpu.HBM)] * (2 * lines),
         out_specs=[vmem] * 2,
         scratch_shapes=[
             pltpu.VMEM((lines, rows, width), BF16),
             pltpu.VMEM((lines, width, width), BF16),
             pltpu.SemaphoreType.DMA((lines,)),
+            pltpu.SemaphoreType.DMA((lines,)),
         ],
         compiler_params=limit(28),
         name="grad",
-    )(line, out_weight, out_grad, *ups, *downs)
-    columns = lax.all_to_all(blocks, "ctx", split_axis=0, concat_axis=0, tiled=True)
-    received = from_core(outs[:chunks], *ups[2:], *downs[2:])
-    terms = merge_chips(outs[:chunks], received, heads, grad_attn)
+    )
+    received = from_core(outs[:chunks], ups[1], downs[1])
+    terms, (grad_attn, blocks) = merge_chips(
+        outs[:chunks],
+        received,
+        heads,
+        lambda *before: make_grad(after(line, *before), out_weight, out_grad, *ups, *downs),
+    )
     attn_out, extended = pl.pallas_call(
         functools.partial(finish_kernel, [len(pieces) for pieces in terms]),
         out_shape=[shaped((rows, width)), shaped((rows, width + HD))],
@@ -564,7 +576,10 @@
     grad_chips = spread_chips(extended, rows // 2)
     grad_all = with_cores(grad_chips)
     arrived = flat(grad_chips[1:3])
-    attns = [[attn_out]] + [[swap(after(attn_out, *arrived), 2 * j)] for j in range(1, chips)]
+    attns = spread_chips(after(attn_out, *arrived), rows // 2)
+    columns = lax.all_to_all(
+        after(blocks, *arrived), "ctx", split_axis=0, concat_axis=0, tiled=True
+    )
 
     outs = pl.pallas_call(
         functools.partial(backward_kernel, [len(pieces) for pieces in grad_all], span, cap),
@@ -576,11 +591,11 @@
             pltpu.VMEM((block_count, slots, width + HD), BF16),
             pltpu.VMEM((block_count, slots, width), BF16),
         ],
-        compiler_params=limit(40),
+        compiler_params=limit(44),
         name="backward",
-    )(hot, q_slots, probs, after(logits, columns), keys, values, *flat(grad_all))
+    )(hot, q_slots, probs, logits, keys, values, *flat(grad_all))
     key_grad, value_grad = outs[chunks:]
-    terms = collect_chips(outs[:chunks], from_core(outs[:chunks], *flat(attns[1:])))
+    terms = collect_chips(outs[:chunks], from_core(outs[:chunks], *flat(attns[1:3])))
     query_grad = pl.pallas_call(
         functools.partial(total_kernel, [len(pieces) for pieces in terms]),
         out_shape=shaped((rows, width), F32),

time: 237 us -> 243 us (1.025)
  waiting for transfers between devices: 90.9 us -> 101 us
  local copies, waits for them, and re-layouts: 38.8 us -> 35.3 us
    ppermute x3, waiting for transfers between devices: 6.79 us -> 14.9 us  [spread_line(): lax.ppermute(downs[-1], 'head', [(i, i - 1) for i in range(1, lines - d +...]
    ppermute x45 -> x47, waiting for transfers between devices: 79.6 us -> 83.2 us  [swap(): return lax.ppermute(x, 'ctx', [(i, i ^ bits) for i in range(count)])]
    unnamed x85 -> x101, local copies, waits for them, and re-layouts: 38.7 us -> 35.2 us
    ppermute x45 -> x47, starting transfers between devices: 29.6 us -> 29.9 us  [swap(): return lax.ppermute(x, 'ctx', [(i, i ^ bits) for i in range(count)])]
  transfers between devices with their start and end apart: 52 -> 54, of which waited for: 19 -> 20; matrix products, arithmetic and copies ran while one was open for 0% -> 1% of each run, Pallas kernels for 22% -> 20%
where the time goes in v8:
time: 243 us; the launch traced here: 242 us
  waiting for transfers between devices  101 us (42%)
  Pallas kernels  57.4 us (24%)
  starting transfers between devices  44.8 us (18%)
  local copies, waits for them, and re-layouts  35.3 us (15%)
    ppermute x47, waiting for transfers between devices, swap(): return lax.ppermute(x, 'ctx', [(i, i ^ bits) for i in range(count)])  83.2 us
    unnamed x101, local copies, waits for them, and re-layouts  35.2 us
    ppermute x47, starting transfers between devices, swap(): return lax.ppermute(x, 'ctx', [(i, i ^ bits) for i in range(count)])  29.9 us
    pallas_call x1, Pallas kernels, body(): pl.pallas_call(functools.partial(backward_kernel, [len(pieces) for pieces...  19 us
    pallas_call x1, Pallas kernels, body(): pl.pallas_call(functools.partial(forward_kernel, [len(pieces) for pieces...  16.4 us
    ppermute x3, waiting for transfers between devices, spread_line(): lax.ppermute(downs[-1], 'head', [(i, i - 1) for i in range(1, lines - d +...  14.9 us
    pallas_call x3, Pallas kernels, merged(): pl.pallas_call(functools.partial(merge_kernel, plan, heads), out_shape=[j...  8 us
    ppermute x3, starting transfers between devices, spread_line(): lax.ppermute(ups[-1], 'head', [(i, i + 1) for i in range(d - 1, lines - 1)])  7.22 us
  transfers between devices with their start and end apart: 54, of which 20 were waited for; matrix products, arithmetic and copies ran while one was open for 1% of the time, Pallas kernels for 20%

profile of v8, /device:TPU:0, one launch (start us, length us, event | category | flops | bytes accessed | tf_op | source)
XLA Modules:
  0.0 241.9 jit_solution(15077819535573295700)
XLA Ops:
  2.6 3.0 %collective-permute-start.1 = (bf16[272,1024]{1,0:T(8,128)(2,1)S(1)}, bf16[272,1024]{1,0:T(8,128)(2,1)S(1)}, u32[]{:S(2)}, u32[]{:S(2)}) collective-permute-start(bf16[272,1024]{1,0:T(8,128)(2,1)S(1)} %pack.1.refs_0_), channel_id=1, source_target_pairs={{0,8},{4,12},{8,0},{12,4},{16,24},{20,28},{24,16},{28,20},{1,9},{5... | collective-permute-start | bytes 1671176 | tf_op jit(solution)/shard_map/ppermute | solution.py:382
  7.1 4.3 %collective-permute-start.5 = (bf16[256,1024]{1,0:T(8,128)(2,1)}, bf16[256,1024]{1,0:T(8,128)(2,1)}, u32[]{:S(2)}, u32[]{:S(2)}) collective-permute-start(bf16[256,1024]{1,0:T(8,128)(2,1)} %refs_0_.1), channel_id=1, source_target_pairs={{0,1},{1,2},{2,3},{4,5},{5,6},{6,7},{8,9},{9,10},{10,11},{12,13},{... | collective-permute-start | bytes 1572872 | tf_op jit(solution)/shard_map/ppermute | solution.py:482
  13.6 4.6 %collective-permute-done.1.refs_2_ = bf16[272,1024]{1,0:T(8,128)(2,1)S(1)} collective-permute-done((bf16[272,1024]{1,0:T(8,128)(2,1)S(1)}, bf16[272,1024]{1,0:T(8,128)(2,1)S(1)}, u32[]{:S(2)}, u32[]{:S(2)}) %collective-permute-start.1) | collective-permute-done | bytes 557088 | tf_op jit(solution)/shard_map/ppermute | solution.py:382
  18.2 3.3 %collective-permute-done.5.refs_1_ = bf16[256,1024]{1,0:T(8,128)(2,1)} collective-permute-done((bf16[256,1024]{1,0:T(8,128)(2,1)}, bf16[256,1024]{1,0:T(8,128)(2,1)}, u32[]{:S(2)}, u32[]{:S(2)}) %collective-permute-start.5) | collective-permute-done | bytes 524320 | tf_op jit(solution)/shard_map/ppermute | solution.py:482
  21.5 4.9 %collective-permute-done.6.refs_4_ = bf16[256,1024]{1,0:T(8,128)(2,1)} collective-permute-done((bf16[256,1024]{1,0:T(8,128)(2,1)}, bf16[256,1024]{1,0:T(8,128)(2,1)}, u32[]{:S(2)}, u32[]{:S(2)}) %collective-permute-start.6) | collective-permute-done | bytes 524320 | tf_op jit(solution)/shard_map/ppermute | solution.py:483
  27.6 5.2 %collective-permute-done.7.refs_6_ = bf16[128,1024]{1,0:T(8,128)(2,1)S(1)} collective-permute-done((bf16[128,1024]{1,0:T(8,128)(2,1)S(1)}, bf16[128,1024]{1,0:T(8,128)(2,1)S(1)}, u32[]{:S(2)}, u32[]{:S(2)}) %collective-permute-start.7) | collective-permute-done | bytes 262176 | tf_op jit(solution)/shard_map/ppermute | solution.py:382
  47.1 16.4 %forward.1 = (bf16[256,1152]{1,0:T(8,128)(2,1)S(1)}, bf16[256,1152]{1,0:T(8,128)(2,1)}, bf16[256,1152]{1,0:T(8,128)(2,1)S(1)}, bf16[256,1152]{1,0:T(8,128)(2,1)S...) custom-call(s32[1]{0:T(128)} %bitcast.me_ref, ...), custom_call_target="tpu_custom_call" | custom-call | tf_op jit(solution)/shard_map/forward/pallas_call | solution.py:526
  76.1 10.0 %collective-permute-done.20.refs_6_ = bf16[256,1024]{1,0:T(8,128)(2,1)} collective-permute-done((bf16[256,1024]{1,0:T(8,128)(2,1)}, bf16[256,1024]{1,0:T(8,128)(2,1)}, u32[]{:S(2)}, u32[]{:S(2)}) %collective-permute-start.20) | collective-permute-done | bytes 524320 | tf_op jit(solution)/shard_map/ppermute | solution.py:483
  86.5 3.4 %copy-done.1 = bf16[4096,1024]{1,0:T(8,128)(2,1)S(1)} copy-done((bf16[4096,1024]{1,0:T(8,128)(2,1)S(1)}, bf16[4096,1024]{1,0:T(8,128)(2,1)}, u32[]{:S(2)}) %copy-start.1) | copy-done | bytes 8388632
  91.0 4.8 %grad.1 = (bf16[256,1024]{1,0:T(8,128)(2,1)S(1)}, bf16[8,256,512]{2,1,0:T(8,128)(2,1)S(1)}) custom-call(s32[1]{0:T(128)} %bitcast.4.line_ref, bf16[4096,1024]{1,0:T(8,128)(2,1)S(1)} %copy-done.1, bf16[256,1024]{1,0:T(8,128)(2,1)S(1)} %copy-done.16, bf16[256,1024]{1,0:T(8,128)(2,1)} %collective-permute-done.5.refs_1_, ...), custom_call_target="tpu_custom_call" | custom-call | tf_op jit(solution)/shard_map/grad/pallas_call | solution.py:566
  95.8 3.6 %merge.5 = (bf16[128,1152]{1,0:T(8,128)(2,1)S(1)}, bf16[128,1152]{1,0:T(8,128)(2,1)S(1)}) custom-call(bf16[256,1152]{1,0:T(8,128)(2,1)S(1)} %get-tuple-element.60.refs_0_, bf16[256,1152]{1,0:T(8,128)(2,1)S(1)} %collective-permute-done.14.refs_1_, bf16[256,1152]{1,0:T(8,128)(2,1)S(1)} %get-tuple-element.63.refs_2_, ...), custom_call_target="tpu_custom_call" | custom-call | tf_op jit(solution)/shard_map/merge/pallas_call | solution.py:444
  101.6 6.3 %collective-permute-done.22.refs_3_ = bf16[128,1152]{1,0:T(8,128)(2,1)S(1)} collective-permute-done((bf16[128,1152]{1,0:T(8,128)(2,1)S(1)}, bf16[128,1152]{1,0:T(8,128)(2,1)S(1)}, u32[]{:S(2)}, u32[]{:S(2)}) %collective-permute-start.22) | collective-permute-done | bytes 294944 | tf_op jit(solution)/shard_map/ppermute | solution.py:382
  108.2 4.2 %finish.1 = (bf16[256,1024]{1,0:T(8,128)(2,1)S(1)}, bf16[256,1152]{1,0:T(8,128)(2,1)S(1)}) custom-call(bf16[256,1152]{1,0:T(8,128)(2,1)S(1)} %copy-done.13, bf16[256,1152]{1,0:T(8,128)(2,1)} %collective-permute-done.13.refs_1_, bf16[128,1152]{1,0:T(8,128)(2,1)S(1)} %collective-permute-done.16.refs_2_, bf16[128,1152]{1,0:T(8,128)(2,1)S(1)} %collective-permute-done.22.refs_3_, ...), custom_call_target="tpu_custom_call" | custom-call | tf_op jit(solution)/shard_map/finish/pallas_call | solution.py:568
  115.5 10.6 %collective-permute-done.26.refs_2_ = bf16[256,1152]{1,0:T(8,128)(2,1)S(1)} collective-permute-done((bf16[256,1152]{1,0:T(8,128)(2,1)S(1)}, bf16[256,1152]{1,0:T(8,128)(2,1)S(1)}, u32[]{:S(2)}, u32[]{:S(2)}) %collective-permute-start.26) | collective-permute-done | bytes 589856 | tf_op jit(solution)/shard_map/ppermute | solution.py:382
  129.9 5.7 %collective-permute-done.30.refs_6_ = bf16[128,1152]{1,0:T(8,128)(2,1)S(1)} collective-permute-done((bf16[128,1152]{1,0:T(8,128)(2,1)S(1)}, bf16[128,1152]{1,0:T(8,128)(2,1)S(1)}, u32[]{:S(2)}, u32[]{:S(2)}) %collective-permute-start.30) | collective-permute-done | bytes 294944 | tf_op jit(solution)/shard_map/ppermute | solution.py:382
  139.7 19.0 %backward.1 = (bf16[256,1024]{1,0:T(8,128)(2,1)S(1)}, bf16[256,1024]{1,0:T(8,128)(2,1)S(1)}, bf16[256,1024]{1,0:T(8,128)(2,1)S(1)}, bf16[256,1024]{1,0:T(8,128)(...) custom-call(bf16[8,256,256]{2,1,0:T(8,128)(2,1)S(1)} %copy-done.11, ...), custom_call_target="tpu_custom_call" | custom-call | tf_op jit(solution)/shard_map/backward/pallas_call | solution.py:584
  163.8 3.8 %all-to-all-start = ((bf16[8,256,512]{2,1,0:T(8,128)(2,1)}), bf16[8,256,512]{2,1,0:T(8,128)(2,1)S(1)}, u32[]{:S(2)}, u32[]{:S(2)}) async-start(bf16[8,256,512]{2,1,0:T(8,128)(2,1)} %copy-done.4), calls=%async_computation | async-start | bytes 4194304 | tf_op jit(solution)/shard_map/all_to_all | solution.py:580
  173.6 25.6 %collective-permute-done.40 = bf16[128,1024]{1,0:T(8,128)(2,1)S(1)} collective-permute-done((bf16[128,1024]{1,0:T(8,128)(2,1)S(1)}, bf16[128,1024]{1,0:T(8,128)(2,1)S(1)}, u32[]{:S(2)}, u32[]{:S(2)}) %collective-permute-start.40) | collective-permute-done | bytes 262176 | tf_op jit(solution)/shard_map/ppermute | solution.py:382
  204.3 4.1 %collective-permute-done.50.refs_7_ = bf16[128,1024]{1,0:T(8,128)(2,1)S(1)} collective-permute-done((bf16[128,1024]{1,0:T(8,128)(2,1)S(1)}, bf16[128,1024]{1,0:T(8,128)(2,1)S(1)}, u32[]{:S(2)}, u32[]{:S(2)}) %collective-permute-start.50) | collective-permute-done | bytes 262176 | tf_op jit(solution)/shard_map/ppermute | solution.py:382
  208.9 5.1 %collective-permute-done.38.refs_2_ = bf16[128,1024]{1,0:T(8,128)(2,1)S(1)} collective-permute-done((bf16[128,1024]{1,0:T(8,128)(2,1)S(1)}, bf16[128,1024]{1,0:T(8,128)(2,1)S(1)}, u32[]{:S(2)}, u32[]{:S(2)}) %collective-permute-start.38) | collective-permute-done | bytes 262176 | tf_op jit(solution)/shard_map/ppermute | solution.py:382
  214.2 3.6 %collective-permute-done.41.refs_3_ = bf16[128,1024]{1,0:T(8,128)(2,1)S(1)} collective-permute-done((bf16[128,1024]{1,0:T(8,128)(2,1)S(1)}, bf16[128,1024]{1,0:T(8,128)(2,1)S(1)}, u32[]{:S(2)}, u32[]{:S(2)}) %collective-permute-start.41) | collective-permute-done | bytes 262176 | tf_op jit(solution)/shard_map/ppermute | solution.py:382
  218.4 3.4 %collective-permute-done.44.refs_4_ = bf16[128,1024]{1,0:T(8,128)(2,1)S(1)} collective-permute-done((bf16[128,1024]{1,0:T(8,128)(2,1)S(1)}, bf16[128,1024]{1,0:T(8,128)(2,1)S(1)}, u32[]{:S(2)}, u32[]{:S(2)}) %collective-permute-start.44) | collective-permute-done | bytes 262176 | tf_op jit(solution)/shard_map/ppermute | solution.py:382
  221.8 4.2 %collective-permute-done.45.refs_5_ = bf16[128,1024]{1,0:T(8,128)(2,1)S(1)} collective-permute-done((bf16[128,1024]{1,0:T(8,128)(2,1)S(1)}, bf16[128,1024]{1,0:T(8,128)(2,1)S(1)}, u32[]{:S(2)}, u32[]{:S(2)}) %collective-permute-start.45) | collective-permute-done | bytes 262176 | tf_op jit(solution)/shard_map/ppermute | solution.py:382
  238.2 3.7 %weight.1 = f32[512,1024]{1,0:T(8,128)} custom-call(s32[1]{0:T(128)} %bitcast.me_ref, bf16[8,256,512]{2,1,0:T(8,128)(2,1)S(1)} %all-to-all-done.cols_ref, bf16[256,1024]{1,0:T(8,128)(2,1)S(1)} %copy-done.19, bf16[256,1024]{1,0:T(8,128)(2,1)S(1)} %copy-done.25, bf16[256,1024]{1,0:T(8,128)(2,1)S(1)} %collective-permute-done.34.refs_2_, ...), custom_call_target="tpu_custom_call" | custom-call | tf_op jit(solution)/shard_map/weight/pallas_call | solution.py:609
  (205 shorter events, 78.0 us)
Async XLA Ops:
  2.6 15.6 %collective-permute-start.1 = (bf16[272,1024]{1,0:T(8,128)(2,1)S(1)}, bf16[272,1024]{1,0:T(8,128)(2,1)S(1)}, u32[]{:S(2)}, u32[]{:S(2)}) collective-permute-start(bf16[272,1024]{1,0:T(8,128)(2,1)S(1)} %pack.1.refs_0_), channel_id=1, source_target_pairs={{0,8},{4,12},{8,0},{12,4},{16,24},{20,28},{24,16},{28,20},{1,9},{5... | collective-permute-start | bytes 1671176 | tf_op jit(solution)/shard_map/ppermute | solution.py:382
  5.6 21.4 %collective-permute-start.3 = (bf16[272,1024]{1,0:T(8,128)(2,1)S(1)}, bf16[272,1024]{1,0:T(8,128)(2,1)S(1)}, u32[]{:S(2)}, u32[]{:S(2)}) collective-permute-start(bf16[272,1024]{1,0:T(8,128)(2,1)S(1)} %pack.1.refs_0_), channel_id=1, source_target_pairs={{0,16},{4,20},{8,24},{12,28},{16,0},{20,4},{24,8},{28,12},{1,17},{... | collective-permute-start | bytes 1671176 | tf_op jit(solution)/shard_map/ppermute | solution.py:382
  11.4 15.0 %collective-permute-start.6 = (bf16[256,1024]{1,0:T(8,128)(2,1)}, bf16[256,1024]{1,0:T(8,128)(2,1)}, u32[]{:S(2)}, u32[]{:S(2)}) collective-permute-start(bf16[256,1024]{1,0:T(8,128)(2,1)} %refs_0_.1), channel_id=1, source_target_pairs={{1,0},{2,1},{3,2},{5,4},{6,5},{7,6},{9,8},{10,9},{11,10},{13,12},{... | collective-permute-start | bytes 1572872 | tf_op jit(solution)/shard_map/ppermute | solution.py:483
  12.7 21.3 %collective-permute-start = (bf16[272,1024]{1,0:T(8,128)(2,1)S(1)}, bf16[272,1024]{1,0:T(8,128)(2,1)S(1)}, u32[]{:S(2)}, u32[]{:S(2)}) collective-permute-start(bf16[272,1024]{1,0:T(8,128)(2,1)S(1)} %pack.1.refs_0_), channel_id=1, source_target_pairs={{0,4},{4,0},{8,12},{12,8},{16,20},{20,16},{24,28},{28,24},{1,5},{5... | collective-permute-start | bytes 1671176 | tf_op jit(solution)/shard_map/ppermute | solution.py:382
  34.8 30.8 %collective-permute-start.11 = (bf16[256,1024]{1,0:T(8,128)(2,1)}, bf16[256,1024]{1,0:T(8,128)(2,1)}, u32[]{:S(2)}, u32[]{:S(2)}) collective-permute-start(bf16[256,1024]{1,0:T(8,128)(2,1)} %collective-permute-done.5.refs_1_), channel_id=1, source_target_pairs={{1,2},{2,3},{5,6},{6,7},{9,10},{10,11},{13,14},{14,15},{17,18},{18... | collective-permute-start | bytes 1572872 | tf_op jit(solution)/shard_map/ppermute | solution.py:482
  36.3 29.3 %collective-permute-start.12 = (bf16[256,1024]{1,0:T(8,128)(2,1)}, bf16[256,1024]{1,0:T(8,128)(2,1)}, u32[]{:S(2)}, u32[]{:S(2)}) collective-permute-start(bf16[256,1024]{1,0:T(8,128)(2,1)} %collective-permute-done.6.refs_4_), channel_id=1, source_target_pairs={{1,0},{2,1},{5,4},{6,5},{9,8},{10,9},{13,12},{14,13},{17,16},{18,1... | collective-permute-start | bytes 1572872 | tf_op jit(solution)/shard_map/ppermute | solution.py:483
  67.8 18.2 %collective-permute-start.20 = (bf16[256,1024]{1,0:T(8,128)(2,1)}, bf16[256,1024]{1,0:T(8,128)(2,1)}, u32[]{:S(2)}, u32[]{:S(2)}) collective-permute-start(bf16[256,1024]{1,0:T(8,128)(2,1)} %collective-permute-done.12.refs_5_), channel_id=1, source_target_pairs={{1,0},{5,4},{9,8},{13,12},{17,16},{21,20},{25,24},{29,28}} | collective-permute-start | bytes 1572872 | tf_op jit(solution)/shard_map/ppermute | solution.py:483
  71.7 24.1 %collective-permute-start.18 = (bf16[128,1152]{1,0:T(8,128)(2,1)}, bf16[128,1152]{1,0:T(8,128)(2,1)S(1)}, u32[]{:S(2)}, u32[]{:S(2)}) collective-permute-start(bf16[128,1152]{1,0:T(8,128)(2,1)} %get-tuple-element.70), channel_id=1, source_target_pairs={{0,16},{4,20},{8,24},{12,28},{16,0},{20,4},{24,8},{28,12},{1,17},{... | collective-permute-start | bytes 884744 | tf_op jit(solution)/shard_map/ppermute | solution.py:382
  72.2 23.6 %collective-permute-start.21 = (bf16[128,1152]{1,0:T(8,128)(2,1)}, bf16[128,1152]{1,0:T(8,128)(2,1)}, u32[]{:S(2)}, u32[]{:S(2)}) collective-permute-start(bf16[128,1152]{1,0:T(8,128)(2,1)} %get-tuple-element.75), channel_id=1, source_target_pairs={{0,8},{4,12},{8,0},{12,4},{16,24},{20,28},{24,16},{28,20},{1,9},{5... | collective-permute-start | bytes 884744 | tf_op jit(solution)/shard_map/ppermute | solution.py:382
  72.7 28.9 %collective-permute-start.13 = (bf16[256,1152]{1,0:T(8,128)(2,1)}, bf16[256,1152]{1,0:T(8,128)(2,1)}, u32[]{:S(2)}, u32[]{:S(2)}) collective-permute-start(bf16[256,1152]{1,0:T(8,128)(2,1)} %get-tuple-element.59), channel_id=1, source_target_pairs={{0,4},{4,0},{8,12},{12,8},{16,20},{20,16},{24,28},{28,24},{1,5},{5... | collective-permute-start | bytes 1769480 | tf_op jit(solution)/shard_map/ppermute | solution.py:382
  74.5 27.1 %collective-permute-start.16 = (bf16[128,1152]{1,0:T(8,128)(2,1)S(1)}, bf16[128,1152]{1,0:T(8,128)(2,1)S(1)}, u32[]{:S(2)}, u32[]{:S(2)}) collective-permute-start(bf16[128,1152]{1,0:T(8,128)(2,1)S(1)} %get-tuple-element.66), channel_id=1, source_target_pairs={{0,8},{4,12},{8,0},{12,4},{16,24},{20,28},{24,16},{28,20},{1,9},{5... | collective-permute-start | bytes 884744 | tf_op jit(solution)/shard_map/ppermute | solution.py:382
  86.0 15.6 %collective-permute-start.24 = (bf16[128,1152]{1,0:T(8,128)(2,1)S(1)}, bf16[128,1152]{1,0:T(8,128)(2,1)S(1)}, u32[]{:S(2)}, u32[]{:S(2)}) collective-permute-start(bf16[128,1152]{1,0:T(8,128)(2,1)S(1)} %get-tuple-element.71), channel_id=1, source_target_pairs={{0,16},{4,20},{8,24},{12,28},{16,0},{20,4},{24,8},{28,12},{1,17},{... | collective-permute-start | bytes 884744 | tf_op jit(solution)/shard_map/ppermute | solution.py:382
  129.2 33.5 %collective-permute-start.34 = (bf16[256,1024]{1,0:T(8,128)(2,1)S(1)}, bf16[256,1024]{1,0:T(8,128)(2,1)S(1)}, u32[]{:S(2)}, u32[]{:S(2)}) collective-permute-start(bf16[256,1024]{1,0:T(8,128)(2,1)S(1)} %get-tuple-element.82.refs_0_), channel_id=1, source_target_pairs={{0,8},{4,12},{8,0},{12,4},{16,24},{20,28},{24,16},{28,20},{1,9},{5... | collective-permute-start | bytes 1572872 | tf_op jit(solution)/shard_map/ppermute | solution.py:382
  135.6 27.1 %collective-permute-start.35 = (bf16[256,1024]{1,0:T(8,128)(2,1)S(1)}, bf16[256,1024]{1,0:T(8,128)(2,1)S(1)}, u32[]{:S(2)}, u32[]{:S(2)}) collective-permute-start(bf16[256,1024]{1,0:T(8,128)(2,1)S(1)} %get-tuple-element.82.refs_0_), channel_id=1, source_target_pairs={{0,16},{4,20},{8,24},{12,28},{16,0},{20,4},{24,8},{28,12},{1,17},{... | collective-permute-start | bytes 1572872 | tf_op jit(solution)/shard_map/ppermute | solution.py:382
  163.8 67.4 %all-to-all-start = ((bf16[8,256,512]{2,1,0:T(8,128)(2,1)}), bf16[8,256,512]{2,1,0:T(8,128)(2,1)S(1)}, u32[]{:S(2)}, u32[]{:S(2)}) async-start(bf16[8,256,512]{2,1,0:T(8,128)(2,1)} %copy-done.4), calls=%async_computation | async-start | bytes 4194304 | tf_op jit(solution)/shard_map/all_to_all | solution.py:580
  168.0 32.4 %collective-permute-start.42 = (bf16[256,1024]{1,0:T(8,128)(2,1)}, bf16[256,1024]{1,0:T(8,128)(2,1)S(1)}, u32[]{:S(2)}, u32[]{:S(2)}) collective-permute-start(bf16[256,1024]{1,0:T(8,128)(2,1)} %copy-done.48), channel_id=1, source_target_pairs={{0,4},{4,0},{8,12},{12,8},{16,20},{20,16},{24,28},{28,24},{1,5},{5... | collective-permute-start | bytes 1572872 | tf_op jit(solution)/shard_map/ppermute | solution.py:382
  169.7 29.4 %collective-permute-start.40 = (bf16[128,1024]{1,0:T(8,128)(2,1)S(1)}, bf16[128,1024]{1,0:T(8,128)(2,1)S(1)}, u32[]{:S(2)}, u32[]{:S(2)}) collective-permute-start(bf16[128,1024]{1,0:T(8,128)(2,1)S(1)} %get-tuple-element.101), channel_id=1, source_target_pairs={{0,16},{4,20},{8,24},{12,28},{16,0},{20,4},{24,8},{28,12},{1,17},{... | collective-permute-start | bytes 786440 | tf_op jit(solution)/shard_map/ppermute | solution.py:382
  171.4 37.0 %collective-permute-start.36 = (bf16[256,1024]{1,0:T(8,128)(2,1)}, bf16[256,1024]{1,0:T(8,128)(2,1)S(1)}, u32[]{:S(2)}, u32[]{:S(2)}) collective-permute-start(bf16[256,1024]{1,0:T(8,128)(2,1)} %copy-done.47), channel_id=1, source_target_pairs={{0,4},{4,0},{8,12},{12,8},{16,20},{20,16},{24,28},{28,24},{1,5},{5... | collective-permute-start | bytes 1572872 | tf_op jit(solution)/shard_map/ppermute | solution.py:382
  171.4 30.1 %collective-permute-start.43 = (bf16[128,1024]{1,0:T(8,128)(2,1)S(1)}, bf16[128,1024]{1,0:T(8,128)(2,1)S(1)}, u32[]{:S(2)}, u32[]{:S(2)}) collective-permute-start(bf16[128,1024]{1,0:T(8,128)(2,1)S(1)} %get-tuple-element.100), channel_id=1, source_target_pairs={{0,8},{4,12},{8,0},{12,4},{16,24},{20,28},{24,16},{28,20},{1,9},{5... | collective-permute-start | bytes 786440 | tf_op jit(solution)/shard_map/ppermute | solution.py:382
  173.0 31.3 %collective-permute-start.49 = (bf16[128,1024]{1,0:T(8,128)(2,1)S(1)}, bf16[128,1024]{1,0:T(8,128)(2,1)S(1)}, u32[]{:S(2)}, u32[]{:S(2)}) collective-permute-start(bf16[128,1024]{1,0:T(8,128)(2,1)S(1)} %slice.87), channel_id=1, source_target_pairs={{0,16},{4,20},{8,24},{12,28},{16,0},{20,4},{24,8},{28,12},{1,17},{... | collective-permute-start | bytes 786440 | tf_op jit(solution)/shard_map/ppermute | solution.py:382
  201.5 16.4 %collective-permute-start.41 = (bf16[128,1024]{1,0:T(8,128)(2,1)S(1)}, bf16[128,1024]{1,0:T(8,128)(2,1)S(1)}, u32[]{:S(2)}, u32[]{:S(2)}) collective-permute-start(bf16[128,1024]{1,0:T(8,128)(2,1)S(1)} %get-tuple-element.102), channel_id=1, source_target_pairs={{0,8},{4,12},{8,0},{12,4},{16,24},{20,28},{24,16},{28,20},{1,9},{5... | collective-permute-start | bytes 786440 | tf_op jit(solution)/shard_map/ppermute | solution.py:382
  204.3 23.0 %collective-permute-start.46 = (bf16[256,1024]{1,0:T(8,128)(2,1)S(1)}, bf16[256,1024]{1,0:T(8,128)(2,1)S(1)}, u32[]{:S(2)}, u32[]{:S(2)}) collective-permute-start(bf16[256,1024]{1,0:T(8,128)(2,1)S(1)} %copy-done.18), channel_id=1, source_target_pairs={{0,4},{4,0},{8,12},{12,8},{16,20},{20,16},{24,28},{28,24},{1,5},{5... | collective-permute-start | bytes 1572872 | tf_op jit(solution)/shard_map/ppermute | solution.py:382
  208.4 19.7 %collective-permute-start.47 = (bf16[256,1024]{1,0:T(8,128)(2,1)S(1)}, bf16[256,1024]{1,0:T(8,128)(2,1)S(1)}, u32[]{:S(2)}, u32[]{:S(2)}) collective-permute-start(bf16[256,1024]{1,0:T(8,128)(2,1)S(1)} %collective-permute-done.34.refs_2_), channel_id=1, source_target_pairs={{0,4},{4,0},{8,12},{12,8},{16,20},{20,16},{24,28},{28,24},{1,5},{5... | collective-permute-start | bytes 1572872 | tf_op jit(solution)/shard_map/ppermute | solution.py:382
  208.4 20.6 %collective-permute-start.48 = (bf16[256,1024]{1,0:T(8,128)(2,1)S(1)}, bf16[256,1024]{1,0:T(8,128)(2,1)S(1)}, u32[]{:S(2)}, u32[]{:S(2)}) collective-permute-start(bf16[256,1024]{1,0:T(8,128)(2,1)S(1)} %collective-permute-done.35.refs_4_), channel_id=1, source_target_pairs={{0,4},{4,0},{8,12},{12,8},{16,20},{20,16},{24,28},{28,24},{1,5},{5... | collective-permute-start | bytes 1572872 | tf_op jit(solution)/shard_map/ppermute | solution.py:382
  (80 other events, 645.2 us)

commit v9 on v8

--- a/solution.py
+++ b/solution.py
@@ -12,7 +12,8 @@
 TOPK = 4
 F32 = jnp.float32
 BF16 = jnp.bfloat16
-MIB = 1024 * 1024
+MOST = 58 * 1024 * 1024
+SOME = 20 * 1024 * 1024
 PAD = 16
 LOW = -(2.0**99)
 NN = (((1,), (0,)), ((), ()))
@@ -36,9 +37,29 @@
     return lists, refs[at:]
 
 
+def loads(lists, buf, sems):
+    copies, at = [], 0
+    for i, refs in enumerate(lists):
+        mine, row = [], 0
+        for ref in refs:
+            rows = ref.shape[0]
+            mine.append(
+                pltpu.make_async_copy(ref, buf.at[i, pl.ds(row, rows)], sems.at[at])
+            )
+            row += rows
+            at += 1
+        copies.append(mine)
+    return copies
+
+
 def start(copies):
     for copy in copies:
         copy.start()
+
+
+def wait(copies):
+    for copy in copies:
+        copy.wait()
 
 
 def whole(refs):
@@ -70,14 +91,29 @@
     out_ref[rows:] = jnp.concatenate(lines, axis=0).astype(BF16)
 
 
-def forward_kernel(counts, span, cap, me_ref, mark_ref, k_ref, v_ref, *refs):
+def forward_kernel(counts, span, cap, me_ref, mark_ref, k_any, v_any, *refs):
     chunks = len(counts)
     q_refs, refs = dealt(refs, counts)
-    part_refs, refs = refs[:chunks], refs[chunks:]
-    qg_ref, p_ref, logit_ref, hot_ref, topg_ref, out_ref = refs
+    part_any, refs = refs[:chunks], refs[chunks:]
+    qg_any, p_any, logit_ref, hot_any = refs[:4]
+    q_buf, part_refs, k_ref, v_ref, qg_ref, p_ref, hot_ref, topg_ref, out_ref = refs[4:13]
+    in_sems, kv_sems, out_sems = refs[13:]
+    q_copies = loads(q_refs, q_buf, in_sems)
+    kv_copies = [
+        pltpu.make_async_copy(k_any, k_ref, kv_sems.at[0]),
+        pltpu.make_async_copy(v_any, v_ref, kv_sems.at[1]),
+    ]
+    out_copies = [
+        pltpu.make_async_copy(qg_ref, qg_any, out_sems.at[chunks]),
+        pltpu.make_async_copy(hot_ref, hot_any, out_sems.at[chunks + 1]),
+        pltpu.make_async_copy(p_ref, p_any, out_sems.at[chunks + 2]),
+    ]
+    for copies in q_copies:
+        start(copies)
+    start(kv_copies)
     block_count, _, width = k_ref.shape
     heads = width // HD
-    rows = part_refs[0].shape[0]
+    rows = part_any[0].shape[0]
     group_rows = rows * span
     groups = chunks // span
     scale = HD ** (-0.5)
@@ -101,7 +137,9 @@
     )
     q_groups, owns = [], []
     for g in range(groups):
-        packs = [whole(q_refs[g * span + i]) for i in range(span)]
+        for i in range(span):
+            wait(q_copies[g * span + i])
+        packs = [q_buf[g * span + i] for i in range(span)]
         digits = [pack[rows : rows + PAD].astype(F32)[:TOPK] for pack in packs]
         picked = joined([16.0 * d[:, :rows] + d[:, rows : 2 * rows] for d in digits], 1)
         own = picked[0:1, :] == own_ids
@@ -148,9 +186,11 @@
         )
     for g in range(groups):
         for i in range(span):
-            part_refs[g * span + i][:, width:] = (
+            part_refs[g * span + i, :, width:] = (
                 tails[g][:, i * rows : (i + 1) * rows].T.astype(BF16)
             )
+    start(out_copies[:2])
+    wait(kv_copies)
 
     def one_block(b, carry):
         pairs = [slice(p * 2 * HD, (p + 1) * 2 * HD) for p in range(heads // 2)]
@@ -182,67 +222,82 @@
         return carry
 
     lax.fori_loop(0, block_count, one_block, 0)
+    start(out_copies[2:])
 
     for g in range(groups):
         slots = out_ref[:, g * cap : (g + 1) * cap, :].reshape(block_count * cap, width)
         part = mm(hot_ref[g], slots, TN).astype(BF16)
         for i in range(span):
-            part_refs[g * span + i][:, :width] = part[i * rows : (i + 1) * rows]
+            m = g * span + i
+            part_refs[m, :, :width] = part[i * rows : (i + 1) * rows]
+            copy = pltpu.make_async_copy(part_refs.at[m], part_any[m], out_sems.at[m])
+            copy.start()
+            out_copies.append(copy)
+    wait(out_copies)
+
+
+def shift(heads, *moves):
+    row = lax.broadcasted_iota(jnp.int32, (HD, HD), 0)
+    col = lax.broadcasted_iota(jnp.int32, (HD, HD), 1)
+    total = jnp.zeros((HD, HD), F32)
+    for source, target in moves:
+        inside = (row >= source * heads) & (row < (source + 1) * heads)
+        hit = inside & (col - target * heads == row - source * heads)
+        total = jnp.where(hit, 1.0, total)
+    return total.astype(BF16)
 
 
 def blend(terms, heads):
     width = heads * HD
-    tails = [joined([ref[rows, width:] for ref, rows in term], 0).astype(F32) for term in terms]
-    top = tails[0]
-    for tail in tails[1:]:
+    tails = [joined([ref[rows, width:] for ref, rows in term], 0) for term in terms]
+    wide = [tail.astype(F32) for tail in tails]
+    top = wide[0]
+    for tail in wide[1:]:
         top = jnp.maximum(top, tail)
-    tops, sums, columns = [], [], []
+    gather = shift(heads, (1, 0), (2, 0))
+    factors = [jnp.exp(tail - top) for tail in wide]
+    total = None
+    for tail, factor in zip(tails, factors):
+        share = factor * mm(tail, gather)
+        total = share if total is None else total + share
+    columns = []
     for h in range(heads):
         cols = slice(h * HD, (h + 1) * HD)
-        peak = top[:, h : h + 1]
-        total, column = None, None
-        for term, tail in zip(terms, tails):
-            factor = jnp.exp(tail[:, h : h + 1] - peak)
-            low = 2 * heads + h
-            share = factor * (tail[:, heads + h : heads + h + 1] + tail[:, low : low + 1])
-            part = factor * joined([ref[rows, cols] for ref, rows in term], 0).astype(F32)
-            total = share if total is None else total + share
+        column = None
+        for term, factor in zip(terms, factors):
+            values = joined([ref[rows, cols] for ref, rows in term], 0).astype(F32)
+            part = factor[:, h : h + 1] * values
             column = part if column is None else column + part
-        tops.append(peak)
-        sums.append(total)
         columns.append(column)
-    return tops, sums, columns
-
-
-def tailed(groups, rows):
-    lane = lax.broadcasted_iota(jnp.int32, (rows, HD), 1)
-    tail = jnp.zeros((rows, HD), F32)
-    at = 0
-    for group in groups:
-        for column in group:
-            tail = jnp.where(lane == at, column, tail)
-            at += 1
-    return tail.astype(BF16)
-
-
-def digits_of(columns, count):
-    groups = []
+    return top, total, columns
+
+
+def digits_of(tile, count):
+    digits = []
     for _ in range(count):
-        upper = [column.astype(BF16).astype(F32) for column in columns]
-        groups.append(upper)
-        columns = [column - part for column, part in zip(columns, upper)]
-    return groups
+        upper = tile.astype(BF16)
+        digits.append(upper)
+        tile = tile - upper.astype(F32)
+    return digits
+
+
+def packed_tail(digits, heads):
+    total = None
+    for i, digit in enumerate(digits):
+        part = mm(digit, shift(heads, (0, i)))
+        total = part if total is None else total + part
+    return total.astype(BF16)
 
 
 def merge_kernel(plan, heads, *refs):
     ins, outs = refs[: len(refs) - len(plan)], refs[len(refs) - len(plan) :]
     for terms, out_ref in zip(plan, outs):
-        tops, sums, columns = blend(
+        top, total, columns = blend(
             [[(ins[i], pl.ds(first, count))] for i, first, count in terms], heads
         )
         for h in range(heads):
             out_ref[:, h * HD : (h + 1) * HD] = columns[h].astype(BF16)
-        out_ref[:, heads * HD :] = tailed([tops] + digits_of(sums, 2), out_ref.shape[0])
+        out_ref[:, heads * HD :] = packed_tail([top.astype(BF16)] + digits_of(total, 2), heads)
 
 
 def grad_kernel(lines, line_ref, w_ref, *refs):
@@ -288,18 +343,22 @@
     terms, (ga_ref, attn_ref, ext_ref) = dealt(refs, counts)
     rows, width = ga_ref.shape
     heads = width // HD
-    tops, sums, columns = blend(
+    top, total, columns = blend(
         [[(ref, slice(None)) for ref in pieces] for pieces in terms], heads
     )
+    lane = lax.broadcasted_iota(jnp.int32, (rows, HD), 1)
+    total = jnp.where(lane < heads, total, 1.0)
+    inverse = 1.0 / total
+    dots = jnp.zeros((rows, HD), F32)
     ext_ref[:, :width] = ga_ref[...]
-    dots, levels = [], []
     for h in range(heads):
         cols = slice(h * HD, (h + 1) * HD)
-        total = columns[h] * (1.0 / sums[h])
-        attn_ref[:, cols] = total.astype(BF16)
-        dots.append(jnp.sum(total * ga_ref[:, cols].astype(F32), axis=1, keepdims=True))
-        levels.append(tops[h] + jnp.log(sums[h]))
-    ext_ref[:, width:] = tailed(digits_of(dots, 2) + digits_of(levels, 3), rows)
+        attn = columns[h] * inverse[:, h : h + 1]
+        attn_ref[:, cols] = attn.astype(BF16)
+        dot = jnp.sum(attn * ga_ref[:, cols].astype(F32), axis=1, keepdims=True)
+        dots = jnp.where(lane == h, dot, dots)
+    level = jnp.where(lane < heads, top + jnp.log(total), 0.0)
+    ext_ref[:, width:] = packed_tail(digits_of(dots, 2) + digits_of(level, 3), heads)
 
 
 def total_kernel(counts, *refs):
@@ -309,25 +368,52 @@
         out_ref[:, cols] = added(terms, cols)
 
 
-def backward_kernel(counts, span, cap, hot_ref, qg_ref, p_ref, logit_ref, k_ref, v_ref, *refs):
+def backward_kernel(counts, span, cap, logit_ref, hot_any, qg_any, p_any, k_any, v_any, *refs):
     chunks = len(counts)
     ga_refs, refs = dealt(refs, counts)
     part_refs, refs = refs[:chunks], refs[chunks:]
-    dk_ref, dv_ref, gag_ref, dq_ref = refs
+    dk_any, dv_any = refs[:2]
+    ga_buf, hot_ref, qg_ref, p_ref, k_ref, v_ref, gag_ref, dq_ref, dk_ref, dv_ref = refs[2:12]
+    in_sems, hot_sem, block_sems, out_sems, part_sems = refs[12:]
+    ga_copies = loads(ga_refs, ga_buf, in_sems)
+    hot_copy = pltpu.make_async_copy(hot_any, hot_ref, hot_sem.at[0])
+    hot_copy.start()
+    for copies in ga_copies:
+        start(copies)
+
+    def block_loads(b):
+        pairs = ((qg_any, qg_ref), (p_any, p_ref), (k_any, k_ref), (v_any, v_ref))
+        return [
+            pltpu.make_async_copy(far.at[b], near.at[b], block_sems.at[i, b])
+            for i, (far, near) in enumerate(pairs)
+        ]
+
+    def block_stores(b):
+        return [
+            pltpu.make_async_copy(dk_ref.at[b], dk_any.at[b], out_sems.at[0, b]),
+            pltpu.make_async_copy(dv_ref.at[b], dv_any.at[b], out_sems.at[1, b]),
+        ]
+
     block_count, _, width = k_ref.shape
     heads = width // HD
     rows = part_refs[0].shape[0]
     groups = chunks // span
     scale = HD ** (-0.5)
 
-    for g in range(groups):
-        ga_group = joined([whole(ga_refs[g * span + i]) for i in range(span)], 0)
+    for b in range(block_count):
+        start(block_loads(b))
+    hot_copy.wait()
+    for g in range(groups):
+        for i in range(span):
+            wait(ga_copies[g * span + i])
+        ga_group = joined([ga_buf[g * span + i] for i in range(span)], 0)
         gag_ref[:, g * cap : (g + 1) * cap, :] = (
             mm(hot_ref[g], ga_group).astype(BF16).reshape(block_count, cap, width + HD)
         )
     last = lax.broadcasted_iota(jnp.int32, (BLOCK, groups * cap), 0) == BLOCK - 1
 
     def one_block(b, carry):
+        wait(block_loads(b))
         pairs = [slice(p * 2 * HD, (p + 1) * 2 * HD) for p in range(heads // 2)]
         q = [qg_ref[b, :, cols] for cols in pairs]
         ga = [gag_ref[b, :, cols] for cols in pairs]
@@ -359,15 +445,27 @@
             dv_ref[b, :, cols] = jnp.concatenate([dv[:BLOCK, :HD], dv[BLOCK:, HD:]], axis=1)
             dk_ref[b, :, cols] = jnp.concatenate([dk[:BLOCK, :HD], dk[BLOCK:, HD:]], axis=1)
             dq_ref[b, :, cols] = dq
+        start(block_stores(b))
         return carry
 
     lax.fori_loop(0, block_count, one_block, 0)
+
+    part_copies = []
 
     for g in range(groups):
         slots = dq_ref[:, g * cap : (g + 1) * cap, :].reshape(block_count * cap, width)
         part = mm(hot_ref[g], slots, TN).astype(BF16)
         for i in range(span):
-            part_refs[g * span + i][...] = part[i * rows : (i + 1) * rows]
+            m = g * span + i
+            ga_buf[m, :, :width] = part[i * rows : (i + 1) * rows]
+            copy = pltpu.make_async_copy(
+                ga_buf.at[m, :, pl.ds(0, width)], part_refs[m], part_sems.at[m]
+            )
+            copy.start()
+            part_copies.append(copy)
+    for b in range(block_count):
+        wait(block_stores(b))
+    wait(part_copies)
 
 
 def weight_kernel(counts, me_ref, cols_ref, *refs):
@@ -448,7 +546,7 @@
             ],
             in_specs=[pl.BlockSpec(memory_space=pltpu.VMEM)] * len(ins),
             out_specs=[pl.BlockSpec(memory_space=pltpu.VMEM)] * len(plan),
-            compiler_params=pltpu.CompilerParams(vmem_limit_bytes=24 * MIB),
+            compiler_params=pltpu.CompilerParams(vmem_limit_bytes=SOME),
             name="merge",
         )(*ins)
 
@@ -504,9 +602,9 @@
     values = value_rows.reshape(block_count, BLOCK, width)
     vmem = pl.BlockSpec(memory_space=pltpu.VMEM)
     smem = pl.BlockSpec(memory_space=pltpu.SMEM)
-
-    def limit(mib):
-        return pltpu.CompilerParams(vmem_limit_bytes=mib * MIB)
+    anywhere = pl.BlockSpec(memory_space=pl.ANY)
+    params = pltpu.CompilerParams(vmem_limit_bytes=MOST)
+    small = pltpu.CompilerParams(vmem_limit_bytes=SOME)
 
     def shaped(shape, kind=BF16):
         return jax.ShapeDtypeStruct(shape, kind)
@@ -517,11 +615,11 @@
         out_shape=shaped((rows + PAD, width)),
         in_specs=[vmem] * 2,
         out_specs=vmem,
-        compiler_params=limit(8),
+        compiler_params=small,
         name="pack",
     )(selected.T, queries)
     query_chips = spread_chips(packed, rows // 2, ups[0], downs[0])
-    query_all = with_cores(query_chips)
+    query_all = with_cores(query_chips, ups[1], downs[1])
 
     outs = pl.pallas_call(
         functools.partial(forward_kernel, [len(pieces) for pieces in query_all], span, cap),
@@ -532,13 +630,23 @@
             shaped((block_count, heads, slots), F32),
             shaped((groups, block_count * cap, rows * span)),
         ],
-        in_specs=[smem] + [vmem] * (3 + len(flat(query_all))),
-        out_specs=[vmem] * (chunks + 4),
+        in_specs=[smem, vmem] + [anywhere] * (2 + len(flat(query_all))),
+        out_specs=[anywhere] * (chunks + 2) + [vmem, anywhere],
         scratch_shapes=[
+            pltpu.VMEM((chunks, rows + PAD, width), BF16),
+            pltpu.VMEM((chunks, rows, width + HD), BF16),
+            pltpu.VMEM((block_count, BLOCK, width), BF16),
+            pltpu.VMEM((block_count, BLOCK, width), BF16),
+            pltpu.VMEM((block_count, slots, width), BF16),
+            pltpu.VMEM((block_count, heads // 2, 2 * BLOCK, slots), BF16),
+            pltpu.VMEM((groups, block_count * cap, rows * span), BF16),
             pltpu.VMEM((block_count, slots, HD), F32),
             pltpu.VMEM((block_count, slots, width), BF16),
+            pltpu.SemaphoreType.DMA((len(flat(query_all)),)),
+            pltpu.SemaphoreType.DMA((2,)),
+            pltpu.SemaphoreType.DMA((chunks + 3,)),
         ],
-        compiler_params=limit(40),
+        compiler_params=params,
         name="forward",
     )(me, keys[:, BLOCK - 1], keys, values, *flat(query_all))
     q_slots, probs, logits, hot = outs[chunks:]
@@ -547,7 +655,7 @@
     make_grad = pl.pallas_call(
         functools.partial(grad_kernel, lines),
         out_shape=[shaped((rows, width)), shaped((chunks, rows, features // chunks))],
-        in_specs=[smem] + [pl.BlockSpec(memory_space=pltpu.HBM)] * (2 * lines),
+        in_specs=[smem] + [anywhere] * (2 * lines),
         out_specs=[vmem] * 2,
         scratch_shapes=[
             pltpu.VMEM((lines, rows, width), BF16),
@@ -555,10 +663,10 @@
             pltpu.SemaphoreType.DMA((lines,)),
             pltpu.SemaphoreType.DMA((lines,)),
         ],
-        compiler_params=limit(28),
+        compiler_params=small,
         name="grad",
     )
-    received = from_core(outs[:chunks], ups[1], downs[1])
+    received = from_core(outs[:chunks], *ups[2:], *downs[2:])
     terms, (grad_attn, blocks) = merge_chips(
         outs[:chunks],
         received,
@@ -570,7 +678,7 @@
         out_shape=[shaped((rows, width)), shaped((rows, width + HD))],
         in_specs=[vmem] * (len(flat(terms)) + 1),
         out_specs=[vmem] * 2,
-        compiler_params=limit(24),
+        compiler_params=small,
         name="finish",
     )(*flat(terms), grad_attn)
     grad_chips = spread_chips(extended, rows // 2)
@@ -585,23 +693,36 @@
         functools.partial(backward_kernel, [len(pieces) for pieces in grad_all], span, cap),
         out_shape=[shaped((rows, width))] * chunks
         + [shaped((block_count, BLOCK, width), F32)] * 2,
-        in_specs=[vmem] * (6 + len(flat(grad_all))),
-        out_specs=[vmem] * (chunks + 2),
+        in_specs=[vmem] + [anywhere] * (5 + len(flat(grad_all))),
+        out_specs=[anywhere] * (chunks + 2),
         scratch_shapes=[
+            pltpu.VMEM((chunks, rows, width + HD), BF16),
+            pltpu.VMEM((groups, block_count * cap, rows * span), BF16),
+            pltpu.VMEM((block_count, slots, width), BF16),
+            pltpu.VMEM((block_count, heads // 2, 2 * BLOCK, slots), BF16),
+            pltpu.VMEM((block_count, BLOCK, width), BF16),
+            pltpu.VMEM((block_count, BLOCK, width), BF16),
             pltpu.VMEM((block_count, slots, width + HD), BF16),
             pltpu.VMEM((block_count, slots, width), BF16),
+            pltpu.VMEM((block_count, BLOCK, width), F32),
+            pltpu.VMEM((block_count, BLOCK, width), F32),
+            pltpu.SemaphoreType.DMA((len(flat(grad_all)),)),
+            pltpu.SemaphoreType.DMA((1,)),
+            pltpu.SemaphoreType.DMA((4, block_count)),
+            pltpu.SemaphoreType.DMA((2, block_count)),
+            pltpu.SemaphoreType.DMA((chunks,)),
         ],
-        compiler_params=limit(44),
+        compiler_params=params,
         name="backward",
-    )(hot, q_slots, probs, logits, keys, values, *flat(grad_all))
+    )(logits, hot, q_slots, probs, keys, values, *flat(grad_all))
     key_grad, value_grad = outs[chunks:]
-    terms = collect_chips(outs[:chunks], from_core(outs[:chunks], *flat(attns[1:3])))
+    terms = collect_chips(outs[:chunks], from_core(outs[:chunks], columns, *flat(attns[1:3])))
     query_grad = pl.pallas_call(
         functools.partial(total_kernel, [len(pieces) for pieces in terms]),
         out_shape=shaped((rows, width), F32),
         in_specs=[vmem] * len(flat(terms)),
         out_specs=vmem,
-        compiler_params=limit(24),
+        compiler_params=small,
         name="total",
     )(*flat(terms))
 
@@ -611,7 +732,7 @@
         out_shape=shaped((features // chunks, width), F32),
         in_specs=[smem] + [vmem] * (1 + len(flat(attns))),
         out_specs=vmem,
-        compiler_params=limit(24),
+        compiler_params=small,
         name="weight",
     )(after(me, *flat(terms)), columns, *flat(attns))
     return (

time: 243 us -> 215 us (0.88)
  local copies, waits for them, and re-layouts: 35.3 us -> 13 us
  waiting for transfers between devices: 101 us -> 91.7 us
  starting transfers between devices: 44.8 us -> 48.2 us
    unnamed x101 -> x69, local copies, waits for them, and re-layouts: 35.2 us -> 9.97 us
    ppermute x3, waiting for transfers between devices: 14.9 us -> 7.02 us  [spread_line(): lax.ppermute(downs[-1], 'head', [(i, i - 1) for i in range(1, lines - d +...]
    ppermute x47, waiting for transfers between devices: 83.2 us -> 79.4 us  [swap(): return lax.ppermute(x, 'ctx', [(i, i ^ bits) for i in range(count)])]
    pallas_call x3, Pallas kernels: 8 us -> 4.46 us  [merged(): pl.pallas_call(functools.partial(merge_kernel, plan, heads), out_shape=[j...]
    ppermute x47, starting transfers between devices: 29.9 us -> 33.4 us  [swap(): return lax.ppermute(x, 'ctx', [(i, i ^ bits) for i in range(count)])]
    pallas_call x1, Pallas kernels: 19 us -> 21.6 us  [body(): pl.pallas_call(functools.partial(backward_kernel, [len(pieces) for pieces...]
  transfers between devices with their start and end apart: 54 -> 54, of which waited for: 20 -> 23; matrix products, arithmetic and copies ran while one was open for 1% -> 3% of each run, Pallas kernels for 20% -> 24%
where the time goes in v9:
time: 215 us
  waiting for transfers between devices  91.7 us (43%)
  Pallas kernels  58.8 us (27%)
  starting transfers between devices  48.2 us (22%)
  local copies, waits for them, and re-layouts  13 us (6%)
    ppermute x47, waiting for transfers between devices, swap(): return lax.ppermute(x, 'ctx', [(i, i ^ bits) for i in range(count)])  79.4 us
    ppermute x47, starting transfers between devices, swap(): return lax.ppermute(x, 'ctx', [(i, i ^ bits) for i in range(count)])  33.4 us
    pallas_call x1, Pallas kernels, body(): pl.pallas_call(functools.partial(backward_kernel, [len(pieces) for pieces...  21.6 us
    pallas_call x1, Pallas kernels, body(): pl.pallas_call(functools.partial(forward_kernel, [len(pieces) for pieces...  18.5 us
    unnamed x69, local copies, waits for them, and re-layouts  9.97 us
    ppermute x3, starting transfers between devices, spread_line(): lax.ppermute(ups[-1], 'head', [(i, i + 1) for i in range(d - 1, lines - 1)])  7.1 us
    ppermute x3, waiting for transfers between devices, spread_line(): lax.ppermute(downs[-1], 'head', [(i, i - 1) for i in range(1, lines - d +...  7.02 us
    ppermute x3, waiting for transfers between devices, spread_line(): lax.ppermute(ups[-1], 'head', [(i, i + 1) for i in range(d - 1, lines - 1)])  5.29 us
  transfers between devices with their start and end apart: 54, of which 23 were waited for; matrix products, arithmetic and copies ran while one was open for 3% of the time, Pallas kernels for 24%

profile of v9, /device:TPU:0, one launch (start us, length us, event | category | flops | bytes accessed | tf_op | source)
XLA Modules:
  0.0 214.6 jit_solution(5118859170201508052)
XLA Ops:
  0.6 5.0 %collective-permute-start.5 = (bf16[256,1024]{1,0:T(8,128)(2,1)}, bf16[256,1024]{1,0:T(8,128)(2,1)S(1)}, u32[]{:S(2)}, u32[]{:S(2)}) collective-permute-start(bf16[256,1024]{1,0:T(8,128)(2,1)} %refs_0_.1), channel_id=1, source_target_pairs={{0,1},{1,2},{2,3},{4,5},{5,6},{6,7},{8,9},{9,10},{10,11},{12,13},{... | collective-permute-start | bytes 1572872 | tf_op jit(solution)/shard_map/ppermute | solution.py:580
  8.7 1.6 collective-permute-start.3
  11.8 5.3 %collective-permute-done.5.refs_1_ = bf16[256,1024]{1,0:T(8,128)(2,1)S(1)} collective-permute-done((bf16[256,1024]{1,0:T(8,128)(2,1)}, bf16[256,1024]{1,0:T(8,128)(2,1)S(1)}, u32[]{:S(2)}, u32[]{:S(2)}) %collective-permute-start.5) | collective-permute-done | bytes 524320 | tf_op jit(solution)/shard_map/ppermute | solution.py:580
  17.7 3.4 %collective-permute-done.6.refs_4_ = bf16[256,1024]{1,0:T(8,128)(2,1)S(1)} collective-permute-done((bf16[256,1024]{1,0:T(8,128)(2,1)}, bf16[256,1024]{1,0:T(8,128)(2,1)S(1)}, u32[]{:S(2)}, u32[]{:S(2)}) %collective-permute-start.6) | collective-permute-done | bytes 524320 | tf_op jit(solution)/shard_map/ppermute | solution.py:581
  26.1 4.4 %collective-permute-done.10.refs_7_ = bf16[144,1024]{1,0:T(8,128)(2,1)S(1)} collective-permute-done((bf16[144,1024]{1,0:T(8,128)(2,1)S(1)}, bf16[144,1024]{1,0:T(8,128)(2,1)S(1)}, u32[]{:S(2)}, u32[]{:S(2)}) %collective-permute-start.10) | collective-permute-done | bytes 294944 | tf_op jit(solution)/shard_map/ppermute | solution.py:480
  32.0 3.7 %collective-permute-done.9.refs_5_ = bf16[256,1024]{1,0:T(8,128)(2,1)S(1)} collective-permute-done((bf16[256,1024]{1,0:T(8,128)(2,1)S(1)}, bf16[256,1024]{1,0:T(8,128)(2,1)S(1)}, u32[]{:S(2)}, u32[]{:S(2)}) %collective-permute-start.9) | collective-permute-done | bytes 524320 | tf_op jit(solution)/shard_map/ppermute | solution.py:581
  39.6 18.5 %forward.1 = (bf16[256,1152]{1,0:T(8,128)(2,1)}, bf16[256,1152]{1,0:T(8,128)(2,1)}, bf16[256,1152]{1,0:T(8,128)(2,1)}, bf16[256,1152]{1,0:T(8,128)(2,1)}, bf16[2...) custom-call(s32[1]{0:T(128)} %bitcast.me_ref, ...), custom_call_target="tpu_custom_call" | custom-call | tf_op jit(solution)/shard_map/forward/pallas_call | solution.py:624
  70.0 3.4 %copy-done = bf16[4096,1024]{1,0:T(8,128)(2,1)S(1)} copy-done((bf16[4096,1024]{1,0:T(8,128)(2,1)S(1)}, bf16[4096,1024]{1,0:T(8,128)(2,1)}, u32[]{:S(2)}) %copy-start) | copy-done | bytes 8388632
  73.4 4.7 %grad.1 = (bf16[256,1024]{1,0:T(8,128)(2,1)S(1)}, bf16[8,256,512]{2,1,0:T(8,128)(2,1)S(1)}) custom-call(s32[1]{0:T(128)} %bitcast.4.line_ref, bf16[4096,1024]{1,0:T(8,128)(2,1)S(1)} %copy-done, bf16[256,1024]{1,0:T(8,128)(2,1)S(1)} %copy-done.10, bf16[256,1024]{1,0:T(8,128)(2,1)S(1)} %collective-permute-done.5.refs_1_, bf16[256,1024]{1,0:T(8,128)(2,1)S(1)} %copy-done.14, ...), custom_call_target="tpu_custom_call" | custom-call | tf_op jit(solution)/shard_map/grad/pallas_call | solution.py:674
  78.2 2.3 %merge.5 = (bf16[128,1152]{1,0:T(8,128)(2,1)S(1)}, bf16[128,1152]{1,0:T(8,128)(2,1)S(1)}) custom-call(bf16[256,1152]{1,0:T(8,128)(2,1)S(1)} %copy-done.2, bf16[256,1152]{1,0:T(8,128)(2,1)S(1)} %collective-permute-done.16.refs_1_, bf16[256,1152]{1,0:T(8,128)(2,1)S(1)} %copy-done.4, bf16[256,1152]{1,0:T(8,128)(2,1)S(1)} %collective-permute-done.17.refs_3_, ...), custom_call_target="tpu_custom_call" | custom-call | tf_op jit(solution)/shard_map/merge/pallas_call | solution.py:542
  83.6 5.9 %collective-permute-done.22.refs_3_ = bf16[128,1152]{1,0:T(8,128)(2,1)S(1)} collective-permute-done((bf16[128,1152]{1,0:T(8,128)(2,1)S(1)}, bf16[128,1152]{1,0:T(8,128)(2,1)S(1)}, u32[]{:S(2)}, u32[]{:S(2)}) %collective-permute-start.22) | collective-permute-done | bytes 294944 | tf_op jit(solution)/shard_map/ppermute | solution.py:480
  90.7 3.3 %finish.1 = (bf16[256,1024]{1,0:T(8,128)(2,1)}, bf16[256,1152]{1,0:T(8,128)(2,1)S(1)}) custom-call(bf16[256,1152]{1,0:T(8,128)(2,1)S(1)} %copy-done.9, bf16[256,1152]{1,0:T(8,128)(2,1)S(1)} %collective-permute-done.15.refs_1_, bf16[128,1152]{1,0:T(8,128)(2,1)S(1)} %collective-permute-done.18.refs_2_, bf16[128,1152]{1,0:T(8,128)(2,1)S(1)} %collective-permute-done.22.refs_3_, ...), custom_call_target="tpu_custom_call" | custom-call | tf_op jit(solution)/shard_map/finish/pallas_call | solution.py:676
  96.1 12.1 %collective-permute-done.26.refs_2_ = bf16[256,1152]{1,0:T(8,128)(2,1)} collective-permute-done((bf16[256,1152]{1,0:T(8,128)(2,1)S(1)}, bf16[256,1152]{1,0:T(8,128)(2,1)}, u32[]{:S(2)}, u32[]{:S(2)}) %collective-permute-start.26) | collective-permute-done | bytes 589856 | tf_op jit(solution)/shard_map/ppermute | solution.py:480
  108.6 3.8 %all-to-all-start = ((bf16[8,256,512]{2,1,0:T(8,128)(2,1)}), bf16[8,256,512]{2,1,0:T(8,128)(2,1)S(1)}, u32[]{:S(2)}, u32[]{:S(2)}) async-start(bf16[8,256,512]{2,1,0:T(8,128)(2,1)} %copy-done.6), calls=%async_computation | async-start | bytes 4194304 | tf_op jit(solution)/shard_map/all_to_all | solution.py:688
  114.0 1.7 collective-permute-start.30
  118.9 25.3 %collective-permute-done.30.refs_6_ = bf16[128,1152]{1,0:T(8,128)(2,1)S(1)} collective-permute-done((bf16[128,1152]{1,0:T(8,128)(2,1)S(1)}, bf16[128,1152]{1,0:T(8,128)(2,1)S(1)}, u32[]{:S(2)}, u32[]{:S(2)}) %collective-permute-start.30) | collective-permute-done | bytes 294944 | tf_op jit(solution)/shard_map/ppermute | solution.py:480
  147.4 21.6 %backward.1 = (bf16[256,1024]{1,0:T(8,128)(2,1)}, bf16[256,1024]{1,0:T(8,128)(2,1)}, bf16[256,1024]{1,0:T(8,128)(2,1)}, bf16[256,1024]{1,0:T(8,128)(2,1)}, bf16[...) custom-call(f32[16,8,128]{2,1,0:T(8,128)} %get-tuple-element.57.logi, ...), custom_call_target="tpu_custom_call" | custom-call | tf_op jit(solution)/shard_map/backward/pallas_call | solution.py:692
  176.1 5.7 %collective-permute-done.40 = bf16[128,1024]{1,0:T(8,128)(2,1)S(1)} collective-permute-done((bf16[128,1024]{1,0:T(8,128)(2,1)S(1)}, bf16[128,1024]{1,0:T(8,128)(2,1)S(1)}, u32[]{:S(2)}, u32[]{:S(2)}) %collective-permute-start.40) | collective-permute-done | bytes 262176 | tf_op jit(solution)/shard_map/ppermute | solution.py:480
  186.6 4.4 %collective-permute-done.50.refs_7_ = bf16[128,1024]{1,0:T(8,128)(2,1)S(1)} collective-permute-done((bf16[128,1024]{1,0:T(8,128)(2,1)S(1)}, bf16[128,1024]{1,0:T(8,128)(2,1)S(1)}, u32[]{:S(2)}, u32[]{:S(2)}) %collective-permute-start.50) | collective-permute-done | bytes 262176 | tf_op jit(solution)/shard_map/ppermute | solution.py:480
  191.6 5.1 %collective-permute-done.38.refs_2_ = bf16[128,1024]{1,0:T(8,128)(2,1)S(1)} collective-permute-done((bf16[128,1024]{1,0:T(8,128)(2,1)S(1)}, bf16[128,1024]{1,0:T(8,128)(2,1)S(1)}, u32[]{:S(2)}, u32[]{:S(2)}) %collective-permute-start.38) | collective-permute-done | bytes 262176 | tf_op jit(solution)/shard_map/ppermute | solution.py:480
  198.2 1.6 collective-permute-done.41.refs_3_
  201.2 4.3 %collective-permute-done.44.refs_4_ = bf16[128,1024]{1,0:T(8,128)(2,1)S(1)} collective-permute-done((bf16[128,1024]{1,0:T(8,128)(2,1)S(1)}, bf16[128,1024]{1,0:T(8,128)(2,1)S(1)}, u32[]{:S(2)}, u32[]{:S(2)}) %collective-permute-start.44) | collective-permute-done | bytes 262176 | tf_op jit(solution)/shard_map/ppermute | solution.py:480
  205.6 2.8 %collective-permute-done.45.refs_5_ = bf16[128,1024]{1,0:T(8,128)(2,1)S(1)} collective-permute-done((bf16[128,1024]{1,0:T(8,128)(2,1)S(1)}, bf16[128,1024]{1,0:T(8,128)(2,1)S(1)}, u32[]{:S(2)}, u32[]{:S(2)}) %collective-permute-start.45) | collective-permute-done | bytes 262176 | tf_op jit(solution)/shard_map/ppermute | solution.py:480
  209.9 4.7 %weight.1 = f32[512,1024]{1,0:T(8,128)} custom-call(s32[1]{0:T(128)} %bitcast.me_ref, bf16[8,256,512]{2,1,0:T(8,128)(2,1)S(1)} %all-to-all-done.cols_ref, bf16[256,1024]{1,0:T(8,128)(2,1)} %get-tuple-element.88.refs_0_, bf16[256,1024]{1,0:T(8,128)(2,1)S(1)} %collective-permute-done.46.refs_1_, bf16[256,1024]{1,0:T(8,128)(2,1)S(1)} %collective-permute-done.34.refs_2_, ...), custom_call_target="tpu_custom_call" | custom-call | tf_op jit(solution)/shard_map/weight/pallas_call | solution.py:730
  (173 shorter events, 58.8 us)
Async XLA Ops:
  0.6 16.4 %collective-permute-start.5 = (bf16[256,1024]{1,0:T(8,128)(2,1)}, bf16[256,1024]{1,0:T(8,128)(2,1)S(1)}, u32[]{:S(2)}, u32[]{:S(2)}) collective-permute-start(bf16[256,1024]{1,0:T(8,128)(2,1)} %refs_0_.1), channel_id=1, source_target_pairs={{0,1},{1,2},{2,3},{4,5},{5,6},{6,7},{8,9},{9,10},{10,11},{12,13},{... | collective-permute-start | bytes 1572872 | tf_op jit(solution)/shard_map/ppermute | solution.py:580
  5.6 15.5 %collective-permute-start.6 = (bf16[256,1024]{1,0:T(8,128)(2,1)}, bf16[256,1024]{1,0:T(8,128)(2,1)S(1)}, u32[]{:S(2)}, u32[]{:S(2)}) collective-permute-start(bf16[256,1024]{1,0:T(8,128)(2,1)} %refs_0_.1), channel_id=1, source_target_pairs={{1,0},{2,1},{3,2},{5,4},{6,5},{7,6},{9,8},{10,9},{11,10},{13,12},{... | collective-permute-start | bytes 1572872 | tf_op jit(solution)/shard_map/ppermute | solution.py:581
  8.7 14.2 %collective-permute-start.3 = (bf16[272,1024]{1,0:T(8,128)(2,1)S(1)}, bf16[272,1024]{1,0:T(8,128)(2,1)S(1)}, u32[]{:S(2)}, u32[]{:S(2)}) collective-permute-start(bf16[272,1024]{1,0:T(8,128)(2,1)S(1)} %pack.1.refs_0_), channel_id=1, source_target_pairs={{0,16},{4,20},{8,24},{12,28},{16,0},{20,4},{24,8},{28,12},{1,17},{... | collective-permute-start | bytes 1671176 | tf_op jit(solution)/shard_map/ppermute | solution.py:480
  10.3 14.2 %collective-permute-start.1 = (bf16[272,1024]{1,0:T(8,128)(2,1)S(1)}, bf16[272,1024]{1,0:T(8,128)(2,1)S(1)}, u32[]{:S(2)}, u32[]{:S(2)}) collective-permute-start(bf16[272,1024]{1,0:T(8,128)(2,1)S(1)} %pack.1.refs_0_), channel_id=1, source_target_pairs={{0,8},{4,12},{8,0},{12,4},{16,24},{20,28},{24,16},{28,20},{1,9},{5... | collective-permute-start | bytes 1671176 | tf_op jit(solution)/shard_map/ppermute | solution.py:480
  21.1 14.5 %collective-permute-start.9 = (bf16[256,1024]{1,0:T(8,128)(2,1)S(1)}, bf16[256,1024]{1,0:T(8,128)(2,1)S(1)}, u32[]{:S(2)}, u32[]{:S(2)}) collective-permute-start(bf16[256,1024]{1,0:T(8,128)(2,1)S(1)} %collective-permute-done.6.refs_4_), channel_id=1, source_target_pairs={{1,0},{2,1},{5,4},{6,5},{9,8},{10,9},{13,12},{14,13},{17,16},{18,1... | collective-permute-start | bytes 1572872 | tf_op jit(solution)/shard_map/ppermute | solution.py:581
  30.5 27.6 %collective-permute-start.13 = (bf16[256,1024]{1,0:T(8,128)(2,1)S(1)}, bf16[256,1024]{1,0:T(8,128)(2,1)}, u32[]{:S(2)}, u32[]{:S(2)}) collective-permute-start(bf16[256,1024]{1,0:T(8,128)(2,1)S(1)} %collective-permute-done.8.refs_2_), channel_id=1, source_target_pairs={{2,3},{6,7},{10,11},{14,15},{18,19},{22,23},{26,27},{30,31}} | collective-permute-start | bytes 1572872 | tf_op jit(solution)/shard_map/ppermute | solution.py:580
  35.6 22.5 %collective-permute-start.14 = (bf16[256,1024]{1,0:T(8,128)(2,1)S(1)}, bf16[256,1024]{1,0:T(8,128)(2,1)}, u32[]{:S(2)}, u32[]{:S(2)}) collective-permute-start(bf16[256,1024]{1,0:T(8,128)(2,1)S(1)} %collective-permute-done.9.refs_5_), channel_id=1, source_target_pairs={{1,0},{5,4},{9,8},{13,12},{17,16},{21,20},{25,24},{29,28}} | collective-permute-start | bytes 1572872 | tf_op jit(solution)/shard_map/ppermute | solution.py:581
  63.0 15.1 %collective-permute-start.20 = (bf16[128,1152]{1,0:T(8,128)(2,1)}, bf16[128,1152]{1,0:T(8,128)(2,1)S(1)}, u32[]{:S(2)}, u32[]{:S(2)}) collective-permute-start(bf16[128,1152]{1,0:T(8,128)(2,1)} %get-tuple-element.74), channel_id=1, source_target_pairs={{0,16},{4,20},{8,24},{12,28},{16,0},{20,4},{24,8},{28,12},{1,17},{... | collective-permute-start | bytes 884744 | tf_op jit(solution)/shard_map/ppermute | solution.py:480
  66.0 17.6 %collective-permute-start.15 = (bf16[256,1152]{1,0:T(8,128)(2,1)}, bf16[256,1152]{1,0:T(8,128)(2,1)S(1)}, u32[]{:S(2)}, u32[]{:S(2)}) collective-permute-start(bf16[256,1152]{1,0:T(8,128)(2,1)} %get-tuple-element.63), channel_id=1, source_target_pairs={{0,4},{4,0},{8,12},{12,8},{16,20},{20,16},{24,28},{28,24},{1,5},{5... | collective-permute-start | bytes 1769480 | tf_op jit(solution)/shard_map/ppermute | solution.py:480
  68.9 14.7 %collective-permute-start.18 = (bf16[128,1152]{1,0:T(8,128)(2,1)S(1)}, bf16[128,1152]{1,0:T(8,128)(2,1)S(1)}, u32[]{:S(2)}, u32[]{:S(2)}) collective-permute-start(bf16[128,1152]{1,0:T(8,128)(2,1)S(1)} %get-tuple-element.70), channel_id=1, source_target_pairs={{0,8},{4,12},{8,0},{12,4},{16,24},{20,28},{24,16},{28,20},{1,9},{5... | collective-permute-start | bytes 884744 | tf_op jit(solution)/shard_map/ppermute | solution.py:480
  69.5 14.1 %collective-permute-start.24 = (bf16[128,1152]{1,0:T(8,128)(2,1)S(1)}, bf16[128,1152]{1,0:T(8,128)(2,1)S(1)}, u32[]{:S(2)}, u32[]{:S(2)}) collective-permute-start(bf16[128,1152]{1,0:T(8,128)(2,1)S(1)} %get-tuple-element.75), channel_id=1, source_target_pairs={{0,16},{4,20},{8,24},{12,28},{16,0},{20,4},{24,8},{28,12},{1,17},{... | collective-permute-start | bytes 884744 | tf_op jit(solution)/shard_map/ppermute | solution.py:480
  94.0 14.1 %collective-permute-start.26 = (bf16[256,1152]{1,0:T(8,128)(2,1)S(1)}, bf16[256,1152]{1,0:T(8,128)(2,1)}, u32[]{:S(2)}, u32[]{:S(2)}) collective-permute-start(bf16[256,1152]{1,0:T(8,128)(2,1)S(1)} %get-tuple-element.82.refs_0_), channel_id=1, source_target_pairs={{0,8},{4,12},{8,0},{12,4},{16,24},{20,28},{24,16},{28,20},{1,9},{5... | collective-permute-start | bytes 1769480 | tf_op jit(solution)/shard_map/ppermute | solution.py:480
  108.6 60.5 %all-to-all-start = ((bf16[8,256,512]{2,1,0:T(8,128)(2,1)}), bf16[8,256,512]{2,1,0:T(8,128)(2,1)S(1)}, u32[]{:S(2)}, u32[]{:S(2)}) async-start(bf16[8,256,512]{2,1,0:T(8,128)(2,1)} %copy-done.6), calls=%async_computation | async-start | bytes 4194304 | tf_op jit(solution)/shard_map/all_to_all | solution.py:688
  112.6 32.1 %collective-permute-start.27 = (bf16[256,1152]{1,0:T(8,128)(2,1)}, bf16[256,1152]{1,0:T(8,128)(2,1)S(1)}, u32[]{:S(2)}, u32[]{:S(2)}) collective-permute-start(bf16[256,1152]{1,0:T(8,128)(2,1)} %collective-permute-done.26.refs_2_), channel_id=1, source_target_pairs={{0,4},{4,0},{8,12},{12,8},{16,20},{20,16},{24,28},{28,24},{1,5},{5... | collective-permute-start | bytes 1769480 | tf_op jit(solution)/shard_map/ppermute | solution.py:480
  114.0 30.1 %collective-permute-start.30 = (bf16[128,1152]{1,0:T(8,128)(2,1)S(1)}, bf16[128,1152]{1,0:T(8,128)(2,1)S(1)}, u32[]{:S(2)}, u32[]{:S(2)}) collective-permute-start(bf16[128,1152]{1,0:T(8,128)(2,1)S(1)} %slice.79), channel_id=1, source_target_pairs={{0,16},{4,20},{8,24},{12,28},{16,0},{20,4},{24,8},{28,12},{1,17},{... | collective-permute-start | bytes 884744 | tf_op jit(solution)/shard_map/ppermute | solution.py:480
  116.7 28.0 %collective-permute-start.31 = (bf16[128,1152]{1,0:T(8,128)(2,1)S(1)}, bf16[128,1152]{1,0:T(8,128)(2,1)S(1)}, u32[]{:S(2)}, u32[]{:S(2)}) collective-permute-start(bf16[128,1152]{1,0:T(8,128)(2,1)S(1)} %slice.80), channel_id=1, source_target_pairs={{0,8},{4,12},{8,0},{12,4},{16,24},{20,28},{24,16},{28,20},{1,9},{5... | collective-permute-start | bytes 884744 | tf_op jit(solution)/shard_map/ppermute | solution.py:480
  118.2 27.0 %collective-permute-start.29 = (bf16[256,1152]{1,0:T(8,128)(2,1)}, bf16[256,1152]{1,0:T(8,128)(2,1)S(1)}, u32[]{:S(2)}, u32[]{:S(2)}) collective-permute-start(bf16[256,1152]{1,0:T(8,128)(2,1)} %collective-permute-done.28.refs_4_), channel_id=1, source_target_pairs={{0,4},{4,0},{8,12},{12,8},{16,20},{20,16},{24,28},{28,24},{1,5},{5... | collective-permute-start | bytes 1769480 | tf_op jit(solution)/shard_map/ppermute | solution.py:480
  118.3 50.8 %collective-permute-start.34 = (bf16[256,1024]{1,0:T(8,128)(2,1)}, bf16[256,1024]{1,0:T(8,128)(2,1)S(1)}, u32[]{:S(2)}, u32[]{:S(2)}) collective-permute-start(bf16[256,1024]{1,0:T(8,128)(2,1)} %get-tuple-element.88.refs_0_), channel_id=1, source_target_pairs={{0,8},{4,12},{8,0},{12,4},{16,24},{20,28},{24,16},{28,20},{1,9},{5... | collective-permute-start | bytes 1572872 | tf_op jit(solution)/shard_map/ppermute | solution.py:480
  144.2 24.9 %collective-permute-start.35 = (bf16[256,1024]{1,0:T(8,128)(2,1)}, bf16[256,1024]{1,0:T(8,128)(2,1)S(1)}, u32[]{:S(2)}, u32[]{:S(2)}) collective-permute-start(bf16[256,1024]{1,0:T(8,128)(2,1)} %get-tuple-element.88.refs_0_), channel_id=1, source_target_pairs={{0,16},{4,20},{8,24},{12,28},{16,0},{20,4},{24,8},{28,12},{1,17},{... | collective-permute-start | bytes 1572872 | tf_op jit(solution)/shard_map/ppermute | solution.py:480
  174.1 16.9 %collective-permute-start.36 = (bf16[256,1024]{1,0:T(8,128)(2,1)}, bf16[256,1024]{1,0:T(8,128)(2,1)S(1)}, u32[]{:S(2)}, u32[]{:S(2)}) collective-permute-start(bf16[256,1024]{1,0:T(8,128)(2,1)} %get-tuple-element.89), channel_id=1, source_target_pairs={{0,4},{4,0},{8,12},{12,8},{16,20},{20,16},{24,28},{28,24},{1,5},{5... | collective-permute-start | bytes 1572872 | tf_op jit(solution)/shard_map/ppermute | solution.py:480
  184.1 15.6 %collective-permute-start.41 = (bf16[128,1024]{1,0:T(8,128)(2,1)S(1)}, bf16[128,1024]{1,0:T(8,128)(2,1)S(1)}, u32[]{:S(2)}, u32[]{:S(2)}) collective-permute-start(bf16[128,1024]{1,0:T(8,128)(2,1)S(1)} %get-tuple-element.106), channel_id=1, source_target_pairs={{0,8},{4,12},{8,0},{12,4},{16,24},{20,28},{24,16},{28,20},{1,9},{5... | collective-permute-start | bytes 786440 | tf_op jit(solution)/shard_map/ppermute | solution.py:480
  186.6 23.1 %collective-permute-start.46 = (bf16[256,1024]{1,0:T(8,128)(2,1)}, bf16[256,1024]{1,0:T(8,128)(2,1)S(1)}, u32[]{:S(2)}, u32[]{:S(2)}) collective-permute-start(bf16[256,1024]{1,0:T(8,128)(2,1)} %get-tuple-element.88.refs_0_), channel_id=1, source_target_pairs={{0,4},{4,0},{8,12},{12,8},{16,20},{20,16},{24,28},{28,24},{1,5},{5... | collective-permute-start | bytes 1572872 | tf_op jit(solution)/shard_map/ppermute | solution.py:480
  191.0 18.7 %collective-permute-start.47 = (bf16[256,1024]{1,0:T(8,128)(2,1)S(1)}, bf16[256,1024]{1,0:T(8,128)(2,1)S(1)}, u32[]{:S(2)}, u32[]{:S(2)}) collective-permute-start(bf16[256,1024]{1,0:T(8,128)(2,1)S(1)} %collective-permute-done.34.refs_2_), channel_id=1, source_target_pairs={{0,4},{4,0},{8,12},{12,8},{16,20},{20,16},{24,28},{28,24},{1,5},{5... | collective-permute-start | bytes 1572872 | tf_op jit(solution)/shard_map/ppermute | solution.py:480
  191.1 18.7 %collective-permute-start.48 = (bf16[256,1024]{1,0:T(8,128)(2,1)S(1)}, bf16[256,1024]{1,0:T(8,128)(2,1)S(1)}, u32[]{:S(2)}, u32[]{:S(2)}) collective-permute-start(bf16[256,1024]{1,0:T(8,128)(2,1)S(1)} %collective-permute-done.35.refs_4_), channel_id=1, source_target_pairs={{0,4},{4,0},{8,12},{12,8},{16,20},{20,16},{24,28},{28,24},{1,5},{5... | collective-permute-start | bytes 1572872 | tf_op jit(solution)/shard_map/ppermute | solution.py:480
  (64 other events, 609.7 us)

commit v10 on v9

--- a/solution.py
+++ b/solution.py
@@ -15,6 +15,7 @@
 MOST = 58 * 1024 * 1024
 SOME = 20 * 1024 * 1024
 PAD = 16
+TOGETHER = 2
 LOW = -(2.0**99)
 NN = (((1,), (0,)), ((), ()))
 NT = (((1,), (1,)), ((), ()))
@@ -192,36 +193,47 @@
     start(out_copies[:2])
     wait(kv_copies)
 
-    def one_block(b, carry):
-        pairs = [slice(p * 2 * HD, (p + 1) * 2 * HD) for p in range(heads // 2)]
-        logits = [mm(diagonal(k_ref[b, :, cols]), qg_ref[b, :, cols], NT) for cols in pairs]
-        wide = [diagonal(v_ref[b, :, cols]) for cols in pairs]
-        tops = topg_ref[b].T[:heads]
-        marks = scale * jnp.concatenate(
-            [logits[h // 2][(h % 2 + 1) * BLOCK - 1 : (h % 2 + 1) * BLOCK] for h in range(heads)],
-            axis=0,
-        )
-        gates = jnp.exp(marks - tops)
-        probs, gated = [], []
-        for p in range(heads // 2):
-            for i in range(2):
-                part = logits[p][i * BLOCK : (i + 1) * BLOCK]
-                weight = jnp.exp2(rate * (part - jnp.max(part, axis=0, keepdims=True)))
-                inverse = 1.0 / jnp.sum(weight, axis=0, keepdims=True)
-                gate = gates[2 * p + i : 2 * p + i + 1, :]
-                probs.append((weight * inverse).astype(BF16))
-                gated.append((weight * (inverse * gate)).astype(BF16))
-        outs = [
-            mm(jnp.concatenate(gated[2 * p : 2 * p + 2], axis=0), wide[p], TN).astype(BF16)
-            for p in range(heads // 2)
+    pairs = [slice(p * 2 * HD, (p + 1) * 2 * HD) for p in range(heads // 2)]
+
+    def some_blocks(step, carry):
+        blocks = [step * TOGETHER + u for u in range(TOGETHER)]
+        logits = [
+            [mm(diagonal(k_ref[b, :, cols]), qg_ref[b, :, cols], NT) for cols in pairs]
+            for b in blocks
         ]
-        logit_ref[b] = marks
-        for p in range(heads // 2):
-            p_ref[b, p] = jnp.concatenate(probs[2 * p : 2 * p + 2], axis=0)
-            out_ref[b, :, pairs[p]] = outs[p]
+        probs, gated, kept = [], [], []
+        for b, scores in zip(blocks, logits):
+            tops = topg_ref[b].T[:heads]
+            marks = scale * jnp.concatenate(
+                [scores[h // 2][(h % 2 + 1) * BLOCK - 1 : (h % 2 + 1) * BLOCK] for h in range(heads)],
+                axis=0,
+            )
+            gates = jnp.exp(marks - tops)
+            kept.append(marks)
+            for p in range(heads // 2):
+                low, high = [], []
+                for i in range(2):
+                    part = scores[p][i * BLOCK : (i + 1) * BLOCK]
+                    weight = jnp.exp2(rate * (part - jnp.max(part, axis=0, keepdims=True)))
+                    inverse = 1.0 / jnp.sum(weight, axis=0, keepdims=True)
+                    gate = gates[2 * p + i : 2 * p + i + 1, :]
+                    low.append((weight * inverse).astype(BF16))
+                    high.append((weight * (inverse * gate)).astype(BF16))
+                probs.append(jnp.concatenate(low, axis=0))
+                gated.append(jnp.concatenate(high, axis=0))
+        outs = []
+        for u, b in enumerate(blocks):
+            for p, cols in enumerate(pairs):
+                both = gated[u * len(pairs) + p]
+                outs.append(mm(both, diagonal(v_ref[b, :, cols]), TN).astype(BF16))
+        for u, b in enumerate(blocks):
+            logit_ref[b] = kept[u]
+            for p, cols in enumerate(pairs):
+                p_ref[b, p] = probs[u * len(pairs) + p]
+                out_ref[b, :, cols] = outs[u * len(pairs) + p]
         return carry
 
-    lax.fori_loop(0, block_count, one_block, 0)
+    lax.fori_loop(0, block_count // TOGETHER, some_blocks, 0)
     start(out_copies[2:])
 
     for g in range(groups):
@@ -412,43 +424,51 @@
         )
     last = lax.broadcasted_iota(jnp.int32, (BLOCK, groups * cap), 0) == BLOCK - 1
 
-    def one_block(b, carry):
-        wait(block_loads(b))
-        pairs = [slice(p * 2 * HD, (p + 1) * 2 * HD) for p in range(heads // 2)]
-        q = [qg_ref[b, :, cols] for cols in pairs]
-        ga = [gag_ref[b, :, cols] for cols in pairs]
-        grads = [mm(diagonal(v_ref[b, :, cols]), ga[p], NT) for p, cols in enumerate(pairs)]
-        wide = [diagonal(k_ref[b, :, cols]) for cols in pairs]
-        probs = [p_ref[b, p].astype(F32) for p in range(heads // 2)]
-        tail = gag_ref[b, :, width:].astype(F32).T
-        tail = [tail[i * heads : (i + 1) * heads] for i in range(5)]
-        dots = tail[0] + tail[1]
-        gates = jnp.exp(jnp.minimum(logit_ref[b] - (tail[2] + tail[3] + tail[4]), 0.0))
-        gated, score = [], []
-        for p in range(heads // 2):
-            for i in range(2):
-                at = slice(i * BLOCK, (i + 1) * BLOCK)
-                h = 2 * p + i
-                gate = gates[h : h + 1, :]
-                grad = grads[p][at]
-                delta = jnp.sum(probs[p][at] * grad, axis=0, keepdims=True)
-                weight = probs[p][at] * gate
-                extra = jnp.where(last, scale * gate * (delta - dots[h : h + 1, :]), 0.0)
-                score.append((weight * (scale * (grad - delta)) + extra).astype(BF16))
-                gated.append(weight.astype(BF16))
-        for p, cols in enumerate(pairs):
-            both = jnp.concatenate(gated[2 * p : 2 * p + 2], axis=0)
-            scores = jnp.concatenate(score[2 * p : 2 * p + 2], axis=0)
-            dv = mm(both, ga[p])
-            dk = mm(scores, q[p])
-            dq = mm(scores, wide[p], TN).astype(BF16)
-            dv_ref[b, :, cols] = jnp.concatenate([dv[:BLOCK, :HD], dv[BLOCK:, HD:]], axis=1)
-            dk_ref[b, :, cols] = jnp.concatenate([dk[:BLOCK, :HD], dk[BLOCK:, HD:]], axis=1)
-            dq_ref[b, :, cols] = dq
-        start(block_stores(b))
+    pairs = [slice(p * 2 * HD, (p + 1) * 2 * HD) for p in range(heads // 2)]
+
+    def some_blocks(step, carry):
+        blocks = [step * TOGETHER + u for u in range(TOGETHER)]
+        for b in blocks:
+            wait(block_loads(b))
+        grads = [
+            [mm(diagonal(v_ref[b, :, cols]), gag_ref[b, :, cols], NT) for cols in pairs]
+            for b in blocks
+        ]
+        gated, scores = [], []
+        for b, grad_pairs in zip(blocks, grads):
+            tail = gag_ref[b, :, width:].astype(F32).T
+            tail = [tail[i * heads : (i + 1) * heads] for i in range(5)]
+            dots = tail[0] + tail[1]
+            gates = jnp.exp(jnp.minimum(logit_ref[b] - (tail[2] + tail[3] + tail[4]), 0.0))
+            for p in range(heads // 2):
+                both = p_ref[b, p].astype(F32)
+                low, high = [], []
+                for i in range(2):
+                    at = slice(i * BLOCK, (i + 1) * BLOCK)
+                    h = 2 * p + i
+                    gate = gates[h : h + 1, :]
+                    grad, probs = grad_pairs[p][at], both[at]
+                    delta = jnp.sum(probs * grad, axis=0, keepdims=True)
+                    weight = probs * gate
+                    extra = jnp.where(last, scale * gate * (delta - dots[h : h + 1, :]), 0.0)
+                    low.append((weight * (scale * (grad - delta)) + extra).astype(BF16))
+                    high.append(weight.astype(BF16))
+                scores.append(jnp.concatenate(low, axis=0))
+                gated.append(jnp.concatenate(high, axis=0))
+        for u, b in enumerate(blocks):
+            for p, cols in enumerate(pairs):
+                score, weight = scores[u * len(pairs) + p], gated[u * len(pairs) + p]
+                dv = mm(weight, gag_ref[b, :, cols])
+                dk = mm(score, qg_ref[b, :, cols])
+                dq = mm(score, diagonal(k_ref[b, :, cols]), TN).astype(BF16)
+                dv_ref[b, :, cols] = jnp.concatenate([dv[:BLOCK, :HD], dv[BLOCK:, HD:]], axis=1)
+                dk_ref[b, :, cols] = jnp.concatenate([dk[:BLOCK, :HD], dk[BLOCK:, HD:]], axis=1)
+                dq_ref[b, :, cols] = dq
+        for b in blocks:
+            start(block_stores(b))
         return carry
 
-    lax.fori_loop(0, block_count, one_block, 0)
+    lax.fori_loop(0, block_count // TOGETHER, some_blocks, 0)
 
     part_copies = []
 
@@ -488,13 +508,21 @@
     return [x for pieces in lists for x in pieces]
 
 
+def spread_near(x):
+    chips = lax.axis_size("ctx") // 2
+    return [[x]] + [[swap(x, 2 * j)] for j in range(1, chips if chips != 4 else 3)]
+
+
+def spread_far(near, half, *before):
+    if len(near) != 3:
+        return near
+    (x_way,), (y_way,) = near[1:]
+    far = [swap(after(x_way[:half], *before), 4), swap(after(y_way[half:], *before), 2)]
+    return near + [far]
+
+
 def spread_chips(x, half, *before):
-    chips = lax.axis_size("ctx") // 2
-    near = [swap(x, 2 * j) for j in range(1, chips)] if chips != 4 else [swap(x, 2), swap(x, 4)]
-    if chips != 4:
-        return [[x]] + [[piece] for piece in near]
-    far = [swap(after(near[0][:half], *before), 4), swap(after(near[1][half:], *before), 2)]
-    return [[x], [near[0]], [near[1]], far]
+    return spread_far(spread_near(x), half, *before)
 
 
 def with_cores(lists, *before):
@@ -516,8 +544,9 @@
 def collect_chips(parts, received):
     chips = len(received)
 
-    def both(j, rows, extra=None):
-        total = parts[2 * j][rows].astype(F32) + received[j][rows].astype(F32)
+    def both(j, rows, extra=None, earlier=None):
+        mine = parts[2 * j] if earlier is None else after(parts[2 * j], earlier)
+        total = mine[rows].astype(F32) + received[j][rows].astype(F32)
         if extra is not None:
             total = total + extra.astype(F32)
         return total.astype(BF16)
@@ -528,8 +557,9 @@
     half = parts[0].shape[0] // 2
     top, low = slice(0, half), slice(half, None)
     x_far, y_far = swap(both(3, top), 2), swap(both(3, low), 4)
-    x_top, y_low = swap(both(1, top), 2), swap(both(2, low), 4)
-    x_low, y_top = swap(both(1, low, y_far), 2), swap(both(2, top, x_far), 4)
+    x_sum, y_sum = both(1, top), both(2, low)
+    x_top, y_low = swap(x_sum, 2), swap(y_sum, 4)
+    x_low, y_top = swap(both(1, low, y_far, x_sum), 2), swap(both(2, top, x_far, y_sum), 4)
     return terms + [[x_top, x_low], [y_top, y_low]]
 
 
@@ -663,7 +693,7 @@
             pltpu.SemaphoreType.DMA((lines,)),
             pltpu.SemaphoreType.DMA((lines,)),
         ],
-        compiler_params=small,
+        compiler_params=params,
         name="grad",
     )
     received = from_core(outs[:chunks], *ups[2:], *downs[2:])
@@ -684,9 +714,9 @@
     grad_chips = spread_chips(extended, rows // 2)
     grad_all = with_cores(grad_chips)
     arrived = flat(grad_chips[1:3])
-    attns = spread_chips(after(attn_out, *arrived), rows // 2)
+    attns = spread_near(after(attn_out, *arrived))
     columns = lax.all_to_all(
-        after(blocks, *arrived), "ctx", split_axis=0, concat_axis=0, tiled=True
+        after(blocks, *flat(grad_chips)), "ctx", split_axis=0, concat_axis=0, tiled=True
     )
 
     outs = pl.pallas_call(
@@ -726,7 +756,7 @@
         name="total",
     )(*flat(terms))
 
-    attns = with_cores(attns)
+    attns = with_cores(spread_far(attns, rows // 2, terms[2][0], terms[-1][-1]))
     weight_grad = pl.pallas_call(
         functools.partial(weight_kernel, [len(pieces) for pieces in attns]),
         out_shape=shaped((features // chunks, width), F32),

time: 215 us -> 196 us (0.912)
  waiting for transfers between devices: 91.7 us -> 79.5 us
  Pallas kernels: 58.8 us -> 54.2 us
  local copies, waits for them, and re-layouts: 13 us -> 10.1 us
    ppermute x47, waiting for transfers between devices: 79.4 us -> 67.2 us  [swap(): return lax.ppermute(x, 'ctx', [(i, i ^ bits) for i in range(count)])]
    pallas_call x1, Pallas kernels: 18.5 us -> 15.1 us  [body(): pl.pallas_call(functools.partial(forward_kernel, [len(pieces) for pieces...]
    pallas_call x1, Pallas kernels: 4.72 us -> 7.73 us  [body(): make_grad(after(line, *before), out_weight, out_grad, *ups, *downs)]
    unnamed x69 -> x53, local copies, waits for them, and re-layouts: 9.97 us -> 7.01 us
    pallas_call x1, Pallas kernels: 21.6 us -> 19.2 us  [body(): pl.pallas_call(functools.partial(backward_kernel, [len(pieces) for pieces...]
    pallas_call x3, Pallas kernels: 4.46 us -> 2.28 us  [merged(): pl.pallas_call(functools.partial(merge_kernel, plan, heads), out_shape=[j...]
  transfers between devices with their start and end apart: 54 -> 54, of which waited for: 23 -> 23; matrix products, arithmetic and copies ran while one was open for 3% -> 3% of each run, Pallas kernels for 24% -> 23%
where the time goes in v10:
time: 196 us
  waiting for transfers between devices  79.5 us (41%)
  Pallas kernels  54.2 us (28%)
  starting transfers between devices  48.2 us (25%)
  local copies, waits for them, and re-layouts  10.1 us (5%)
  other arithmetic  2.55 us (1%)
    ppermute x47, waiting for transfers between devices, swap(): return lax.ppermute(x, 'ctx', [(i, i ^ bits) for i in range(count)])  67.2 us
    ppermute x47, starting transfers between devices, swap(): return lax.ppermute(x, 'ctx', [(i, i ^ bits) for i in range(count)])  32.6 us
    pallas_call x1, Pallas kernels, body(): pl.pallas_call(functools.partial(backward_kernel, [len(pieces) for pieces...  19.2 us
    pallas_call x1, Pallas kernels, body(): pl.pallas_call(functools.partial(forward_kernel, [len(pieces) for pieces...  15.1 us
    ppermute x3, starting transfers between devices, spread_line(): lax.ppermute(ups[-1], 'head', [(i, i + 1) for i in range(d - 1, lines - 1)])  7.89 us
    pallas_call x1, Pallas kernels, body(): make_grad(after(line, *before), out_weight, out_grad, *ups, *downs)  7.73 us
    ppermute x3, waiting for transfers between devices, spread_line(): lax.ppermute(downs[-1], 'head', [(i, i - 1) for i in range(1, lines - d +...  7.01 us
    unnamed x53, local copies, waits for them, and re-layouts  7.01 us
  transfers between devices with their start and end apart: 54, of which 23 were waited for; matrix products, arithmetic and copies ran while one was open for 3% of the time, Pallas kernels for 23%

profile of v10, /device:TPU:0, one launch (start us, length us, event | category | flops | bytes accessed | tf_op | source)
XLA Modules:
  0.0 195.5 jit_solution(10108987693847935140)
XLA Ops:
  0.6 5.0 %collective-permute-start.5 = (bf16[256,1024]{1,0:T(8,128)(2,1)}, bf16[256,1024]{1,0:T(8,128)(2,1)S(1)}, u32[]{:S(2)}, u32[]{:S(2)}) collective-permute-start(bf16[256,1024]{1,0:T(8,128)(2,1)} %refs_0_.1), channel_id=1, source_target_pairs={{0,1},{1,2},{2,3},{4,5},{5,6},{6,7},{8,9},{9,10},{10,11},{12,13},{... | collective-permute-start | bytes 1572872 | tf_op jit(solution)/shard_map/ppermute | solution.py:610
  8.7 1.6 collective-permute-start.3
  11.8 5.3 %collective-permute-done.5.refs_1_ = bf16[256,1024]{1,0:T(8,128)(2,1)S(1)} collective-permute-done((bf16[256,1024]{1,0:T(8,128)(2,1)}, bf16[256,1024]{1,0:T(8,128)(2,1)S(1)}, u32[]{:S(2)}, u32[]{:S(2)}) %collective-permute-start.5) | collective-permute-done | bytes 524320 | tf_op jit(solution)/shard_map/ppermute | solution.py:610
  18.5 2.6 %collective-permute-done.6.refs_4_ = bf16[256,1024]{1,0:T(8,128)(2,1)S(1)} collective-permute-done((bf16[256,1024]{1,0:T(8,128)(2,1)}, bf16[256,1024]{1,0:T(8,128)(2,1)S(1)}, u32[]{:S(2)}, u32[]{:S(2)}) %collective-permute-start.6) | collective-permute-done | bytes 524320 | tf_op jit(solution)/shard_map/ppermute | solution.py:611
  24.5 1.6 collective-permute-start.7
  26.1 4.5 %collective-permute-done.10.refs_7_ = bf16[144,1024]{1,0:T(8,128)(2,1)} collective-permute-done((bf16[144,1024]{1,0:T(8,128)(2,1)S(1)}, bf16[144,1024]{1,0:T(8,128)(2,1)}, u32[]{:S(2)}, u32[]{:S(2)}) %collective-permute-start.10) | collective-permute-done | bytes 294944 | tf_op jit(solution)/shard_map/ppermute | solution.py:500
  32.1 4.4 %collective-permute-done.9.refs_5_ = bf16[256,1024]{1,0:T(8,128)(2,1)} collective-permute-done((bf16[256,1024]{1,0:T(8,128)(2,1)S(1)}, bf16[256,1024]{1,0:T(8,128)(2,1)}, u32[]{:S(2)}, u32[]{:S(2)}) %collective-permute-start.9) | collective-permute-done | bytes 524320 | tf_op jit(solution)/shard_map/ppermute | solution.py:611
  40.9 15.1 %forward.1 = (bf16[256,1152]{1,0:T(8,128)(2,1)}, bf16[256,1152]{1,0:T(8,128)(2,1)}, bf16[256,1152]{1,0:T(8,128)(2,1)}, bf16[256,1152]{1,0:T(8,128)(2,1)}, bf16[2...) custom-call(s32[1]{0:T(128)} %bitcast.me_ref, ...), custom_call_target="tpu_custom_call" | custom-call | tf_op jit(solution)/shard_map/forward/pallas_call | solution.py:654
  67.1 7.7 %grad.1 = (bf16[256,1024]{1,0:T(8,128)(2,1)}, bf16[8,256,512]{2,1,0:T(8,128)(2,1)}) custom-call(s32[1]{0:T(128)} %bitcast.4.line_ref, bf16[4096,1024]{1,0:T(8,128)(2,1)} %w_ref.1, bf16[256,1024]{1,0:T(8,128)(2,1)} %refs_0_.1, bf16[256,1024]{1,0:T(8,128)(2,1)} %copy-done.19, bf16[256,1024]{1,0:T(8,128)(2,1)} %collective-permute-done.8.refs_2_, ...), custom_call_target="tpu_custom_call" | custom-call | tf_op jit(solution)/shard_map/grad/pallas_call | solution.py:704
  78.9 5.8 %collective-permute-done.22.refs_3_ = bf16[128,1152]{1,0:T(8,128)(2,1)S(1)} collective-permute-done((bf16[128,1152]{1,0:T(8,128)(2,1)S(1)}, bf16[128,1152]{1,0:T(8,128)(2,1)S(1)}, u32[]{:S(2)}, u32[]{:S(2)}) %collective-permute-start.22) | collective-permute-done | bytes 294944 | tf_op jit(solution)/shard_map/ppermute | solution.py:500
  86.0 3.7 %finish.1 = (bf16[256,1024]{1,0:T(8,128)(2,1)}, bf16[256,1152]{1,0:T(8,128)(2,1)}) custom-call(bf16[256,1152]{1,0:T(8,128)(2,1)S(1)} %copy-done.6, bf16[256,1152]{1,0:T(8,128)(2,1)S(1)} %collective-permute-done.15.refs_1_, bf16[128,1152]{1,0:T(8,128)(2,1)S(1)} %collective-permute-done.18.refs_2_, bf16[128,1152]{1,0:T(8,128)(2,1)S(1)} %collective-permute-done.22.refs_3_, ...), custom_call_target="tpu_custom_call" | custom-call | tf_op jit(solution)/shard_map/finish/pallas_call | solution.py:706
  91.7 12.3 %collective-permute-done.26.refs_2_ = bf16[256,1152]{1,0:T(8,128)(2,1)} collective-permute-done((bf16[256,1152]{1,0:T(8,128)(2,1)}, bf16[256,1152]{1,0:T(8,128)(2,1)}, u32[]{:S(2)}, u32[]{:S(2)}) %collective-permute-start.26) | collective-permute-done | bytes 589856 | tf_op jit(solution)/shard_map/ppermute | solution.py:500
  108.2 3.6 %collective-permute-done.30.refs_6_ = bf16[128,1152]{1,0:T(8,128)(2,1)S(1)} collective-permute-done((bf16[128,1152]{1,0:T(8,128)(2,1)S(1)}, bf16[128,1152]{1,0:T(8,128)(2,1)S(1)}, u32[]{:S(2)}, u32[]{:S(2)}) %collective-permute-start.30) | collective-permute-done | bytes 294944 | tf_op jit(solution)/shard_map/ppermute | solution.py:500
  111.8 2.6 %collective-permute-done.31.refs_7_ = bf16[128,1152]{1,0:T(8,128)(2,1)} collective-permute-done((bf16[128,1152]{1,0:T(8,128)(2,1)S(1)}, bf16[128,1152]{1,0:T(8,128)(2,1)}, u32[]{:S(2)}, u32[]{:S(2)}) %collective-permute-start.31) | collective-permute-done | bytes 294944 | tf_op jit(solution)/shard_map/ppermute | solution.py:500
  114.4 3.8 %all-to-all-start = ((bf16[8,256,512]{2,1,0:T(8,128)(2,1)}), bf16[8,256,512]{2,1,0:T(8,128)(2,1)S(1)}, u32[]{:S(2)}, u32[]{:S(2)}) async-start(bf16[8,256,512]{2,1,0:T(8,128)(2,1)} %get-tuple-element.90), calls=%async_computation | async-start | bytes 4194304 | tf_op jit(solution)/shard_map/all_to_all | solution.py:718
  119.0 1.7 collective-permute-start.34
  125.1 19.2 %backward.1 = (bf16[256,1024]{1,0:T(8,128)(2,1)}, bf16[256,1024]{1,0:T(8,128)(2,1)}, bf16[256,1024]{1,0:T(8,128)(2,1)}, bf16[256,1024]{1,0:T(8,128)(2,1)}, bf16[...) custom-call(f32[16,8,128]{2,1,0:T(8,128)} %get-tuple-element.61.logi, ...), custom_call_target="tpu_custom_call" | custom-call | tf_op jit(solution)/shard_map/backward/pallas_call | solution.py:722
  144.3 10.6 %collective-permute-done.34.refs_2_ = bf16[256,1024]{1,0:T(8,128)(2,1)S(1)} collective-permute-done((bf16[256,1024]{1,0:T(8,128)(2,1)}, bf16[256,1024]{1,0:T(8,128)(2,1)S(1)}, u32[]{:S(2)}, u32[]{:S(2)}) %collective-permute-start.34) | collective-permute-done | bytes 524320 | tf_op jit(solution)/shard_map/ppermute | solution.py:500
  163.8 3.9 %collective-permute-done.40 = bf16[128,1024]{1,0:T(8,128)(2,1)S(1)} collective-permute-done((bf16[128,1024]{1,0:T(8,128)(2,1)S(1)}, bf16[128,1024]{1,0:T(8,128)(2,1)S(1)}, u32[]{:S(2)}, u32[]{:S(2)}) %collective-permute-start.40) | collective-permute-done | bytes 262176 | tf_op jit(solution)/shard_map/ppermute | solution.py:500
  169.2 6.7 %collective-permute-done.43 = bf16[128,1024]{1,0:T(8,128)(2,1)S(1)} collective-permute-done((bf16[128,1024]{1,0:T(8,128)(2,1)S(1)}, bf16[128,1024]{1,0:T(8,128)(2,1)S(1)}, u32[]{:S(2)}, u32[]{:S(2)}) %collective-permute-start.43) | collective-permute-done | bytes 262176 | tf_op jit(solution)/shard_map/ppermute | solution.py:500
  177.3 3.0 %collective-permute-done.41.refs_3_ = bf16[128,1024]{1,0:T(8,128)(2,1)S(1)} collective-permute-done((bf16[128,1024]{1,0:T(8,128)(2,1)S(1)}, bf16[128,1024]{1,0:T(8,128)(2,1)S(1)}, u32[]{:S(2)}, u32[]{:S(2)}) %collective-permute-start.41) | collective-permute-done | bytes 262176 | tf_op jit(solution)/shard_map/ppermute | solution.py:500
  180.9 2.0 %collective-permute-done.44.refs_4_ = bf16[128,1024]{1,0:T(8,128)(2,1)S(1)} collective-permute-done((bf16[128,1024]{1,0:T(8,128)(2,1)S(1)}, bf16[128,1024]{1,0:T(8,128)(2,1)S(1)}, u32[]{:S(2)}, u32[]{:S(2)}) %collective-permute-start.44) | collective-permute-done | bytes 262176 | tf_op jit(solution)/shard_map/ppermute | solution.py:500
  183.4 4.6 %collective-permute-done.49.refs_6_ = bf16[128,1024]{1,0:T(8,128)(2,1)S(1)} collective-permute-done((bf16[128,1024]{1,0:T(8,128)(2,1)S(1)}, bf16[128,1024]{1,0:T(8,128)(2,1)S(1)}, u32[]{:S(2)}, u32[]{:S(2)}) %collective-permute-start.49) | collective-permute-done | bytes 262176 | tf_op jit(solution)/shard_map/ppermute | solution.py:500
  190.8 4.7 %weight.1 = f32[512,1024]{1,0:T(8,128)} custom-call(s32[1]{0:T(128)} %bitcast.me_ref, bf16[8,256,512]{2,1,0:T(8,128)(2,1)S(1)} %all-to-all-done.cols_ref, bf16[256,1024]{1,0:T(8,128)(2,1)} %get-tuple-element.92.refs_0_, bf16[256,1024]{1,0:T(8,128)(2,1)S(1)} %collective-permute-done.46.refs_1_, bf16[256,1024]{1,0:T(8,128)(2,1)S(1)} %collective-permute-done.34.refs_2_, ...), custom_call_target="tpu_custom_call" | custom-call | tf_op jit(solution)/shard_map/weight/pallas_call | solution.py:760
  (159 shorter events, 58.3 us)
Async XLA Ops:
  0.6 16.4 %collective-permute-start.5 = (bf16[256,1024]{1,0:T(8,128)(2,1)}, bf16[256,1024]{1,0:T(8,128)(2,1)S(1)}, u32[]{:S(2)}, u32[]{:S(2)}) collective-permute-start(bf16[256,1024]{1,0:T(8,128)(2,1)} %refs_0_.1), channel_id=1, source_target_pairs={{0,1},{1,2},{2,3},{4,5},{5,6},{6,7},{8,9},{9,10},{10,11},{12,13},{... | collective-permute-start | bytes 1572872 | tf_op jit(solution)/shard_map/ppermute | solution.py:610
  5.6 15.5 %collective-permute-start.6 = (bf16[256,1024]{1,0:T(8,128)(2,1)}, bf16[256,1024]{1,0:T(8,128)(2,1)S(1)}, u32[]{:S(2)}, u32[]{:S(2)}) collective-permute-start(bf16[256,1024]{1,0:T(8,128)(2,1)} %refs_0_.1), channel_id=1, source_target_pairs={{1,0},{2,1},{3,2},{5,4},{6,5},{7,6},{9,8},{10,9},{11,10},{13,12},{... | collective-permute-start | bytes 1572872 | tf_op jit(solution)/shard_map/ppermute | solution.py:611
  8.7 14.2 %collective-permute-start.3 = (bf16[272,1024]{1,0:T(8,128)(2,1)S(1)}, bf16[272,1024]{1,0:T(8,128)(2,1)S(1)}, u32[]{:S(2)}, u32[]{:S(2)}) collective-permute-start(bf16[272,1024]{1,0:T(8,128)(2,1)S(1)} %pack.1.refs_0_), channel_id=1, source_target_pairs={{0,16},{4,20},{8,24},{12,28},{16,0},{20,4},{24,8},{28,12},{1,17},{... | collective-permute-start | bytes 1671176 | tf_op jit(solution)/shard_map/ppermute | solution.py:500
  10.3 14.2 %collective-permute-start.1 = (bf16[272,1024]{1,0:T(8,128)(2,1)S(1)}, bf16[272,1024]{1,0:T(8,128)(2,1)S(1)}, u32[]{:S(2)}, u32[]{:S(2)}) collective-permute-start(bf16[272,1024]{1,0:T(8,128)(2,1)S(1)} %pack.1.refs_0_), channel_id=1, source_target_pairs={{0,8},{4,12},{8,0},{12,4},{16,24},{20,28},{24,16},{28,20},{1,9},{5... | collective-permute-start | bytes 1671176 | tf_op jit(solution)/shard_map/ppermute | solution.py:500
  17.1 13.5 %collective-permute-start.8 = (bf16[256,1024]{1,0:T(8,128)(2,1)S(1)}, bf16[256,1024]{1,0:T(8,128)(2,1)}, u32[]{:S(2)}, u32[]{:S(2)}) collective-permute-start(bf16[256,1024]{1,0:T(8,128)(2,1)S(1)} %collective-permute-done.5.refs_1_), channel_id=1, source_target_pairs={{1,2},{2,3},{5,6},{6,7},{9,10},{10,11},{13,14},{14,15},{17,18},{18... | collective-permute-start | bytes 1572872 | tf_op jit(solution)/shard_map/ppermute | solution.py:610
  21.1 15.4 %collective-permute-start.9 = (bf16[256,1024]{1,0:T(8,128)(2,1)S(1)}, bf16[256,1024]{1,0:T(8,128)(2,1)}, u32[]{:S(2)}, u32[]{:S(2)}) collective-permute-start(bf16[256,1024]{1,0:T(8,128)(2,1)S(1)} %collective-permute-done.6.refs_4_), channel_id=1, source_target_pairs={{1,0},{2,1},{5,4},{6,5},{9,8},{10,9},{13,12},{14,13},{17,16},{18,1... | collective-permute-start | bytes 1572872 | tf_op jit(solution)/shard_map/ppermute | solution.py:611
  24.4 13.5 %collective-permute-start.2 = (bf16[272,1024]{1,0:T(8,128)(2,1)S(1)}, bf16[272,1024]{1,0:T(8,128)(2,1)S(1)}, u32[]{:S(2)}, u32[]{:S(2)}) collective-permute-start(bf16[272,1024]{1,0:T(8,128)(2,1)S(1)} %collective-permute-done.1.refs_2_), channel_id=1, source_target_pairs={{0,4},{4,0},{8,12},{12,8},{16,20},{20,16},{24,28},{28,24},{1,5},{5... | collective-permute-start | bytes 1671176 | tf_op jit(solution)/shard_map/ppermute | solution.py:500
  24.5 13.3 %collective-permute-start.7 = (bf16[128,1024]{1,0:T(8,128)(2,1)S(1)}, bf16[128,1024]{1,0:T(8,128)(2,1)}, u32[]{:S(2)}, u32[]{:S(2)}) collective-permute-start(bf16[128,1024]{1,0:T(8,128)(2,1)S(1)} %slice.77), channel_id=1, source_target_pairs={{0,16},{4,20},{8,24},{12,28},{16,0},{20,4},{24,8},{28,12},{1,17},{... | collective-permute-start | bytes 786440 | tf_op jit(solution)/shard_map/ppermute | solution.py:500
  30.6 25.5 %collective-permute-start.13 = (bf16[256,1024]{1,0:T(8,128)(2,1)}, bf16[256,1024]{1,0:T(8,128)(2,1)}, u32[]{:S(2)}, u32[]{:S(2)}) collective-permute-start(bf16[256,1024]{1,0:T(8,128)(2,1)} %collective-permute-done.8.refs_2_), channel_id=1, source_target_pairs={{2,3},{6,7},{10,11},{14,15},{18,19},{22,23},{26,27},{30,31}} | collective-permute-start | bytes 1572872 | tf_op jit(solution)/shard_map/ppermute | solution.py:610
  36.5 19.6 %collective-permute-start.14 = (bf16[256,1024]{1,0:T(8,128)(2,1)}, bf16[256,1024]{1,0:T(8,128)(2,1)}, u32[]{:S(2)}, u32[]{:S(2)}) collective-permute-start(bf16[256,1024]{1,0:T(8,128)(2,1)} %collective-permute-done.9.refs_5_), channel_id=1, source_target_pairs={{1,0},{5,4},{9,8},{13,12},{17,16},{21,20},{25,24},{29,28}} | collective-permute-start | bytes 1572872 | tf_op jit(solution)/shard_map/ppermute | solution.py:611
  60.1 14.8 %collective-permute-start.20 = (bf16[128,1152]{1,0:T(8,128)(2,1)S(1)}, bf16[128,1152]{1,0:T(8,128)(2,1)S(1)}, u32[]{:S(2)}, u32[]{:S(2)}) collective-permute-start(bf16[128,1152]{1,0:T(8,128)(2,1)S(1)} %get-tuple-element.78), channel_id=1, source_target_pairs={{0,16},{4,20},{8,24},{12,28},{16,0},{20,4},{24,8},{28,12},{1,17},{... | collective-permute-start | bytes 884744 | tf_op jit(solution)/shard_map/ppermute | solution.py:500
  63.2 15.7 %collective-permute-start.15 = (bf16[256,1152]{1,0:T(8,128)(2,1)}, bf16[256,1152]{1,0:T(8,128)(2,1)S(1)}, u32[]{:S(2)}, u32[]{:S(2)}) collective-permute-start(bf16[256,1152]{1,0:T(8,128)(2,1)} %get-tuple-element.67), channel_id=1, source_target_pairs={{0,4},{4,0},{8,12},{12,8},{16,20},{20,16},{24,28},{28,24},{1,5},{5... | collective-permute-start | bytes 1769480 | tf_op jit(solution)/shard_map/ppermute | solution.py:500
  89.7 14.3 %collective-permute-start.26 = (bf16[256,1152]{1,0:T(8,128)(2,1)}, bf16[256,1152]{1,0:T(8,128)(2,1)}, u32[]{:S(2)}, u32[]{:S(2)}) collective-permute-start(bf16[256,1152]{1,0:T(8,128)(2,1)} %get-tuple-element.86.refs_0_), channel_id=1, source_target_pairs={{0,8},{4,12},{8,0},{12,4},{16,24},{20,28},{24,16},{28,20},{1,9},{5... | collective-permute-start | bytes 1769480 | tf_op jit(solution)/shard_map/ppermute | solution.py:500
  90.2 16.4 %collective-permute-start.28 = (bf16[256,1152]{1,0:T(8,128)(2,1)}, bf16[256,1152]{1,0:T(8,128)(2,1)}, u32[]{:S(2)}, u32[]{:S(2)}) collective-permute-start(bf16[256,1152]{1,0:T(8,128)(2,1)} %get-tuple-element.86.refs_0_), channel_id=1, source_target_pairs={{0,16},{4,20},{8,24},{12,28},{16,0},{20,4},{24,8},{28,12},{1,17},{... | collective-permute-start | bytes 1769480 | tf_op jit(solution)/shard_map/ppermute | solution.py:500
  114.4 40.5 %all-to-all-start = ((bf16[8,256,512]{2,1,0:T(8,128)(2,1)}), bf16[8,256,512]{2,1,0:T(8,128)(2,1)S(1)}, u32[]{:S(2)}, u32[]{:S(2)}) async-start(bf16[8,256,512]{2,1,0:T(8,128)(2,1)} %get-tuple-element.90), calls=%async_computation | async-start | bytes 4194304 | tf_op jit(solution)/shard_map/all_to_all | solution.py:718
  119.0 36.0 %collective-permute-start.34 = (bf16[256,1024]{1,0:T(8,128)(2,1)}, bf16[256,1024]{1,0:T(8,128)(2,1)S(1)}, u32[]{:S(2)}, u32[]{:S(2)}) collective-permute-start(bf16[256,1024]{1,0:T(8,128)(2,1)} %get-tuple-element.92.refs_0_), channel_id=1, source_target_pairs={{0,8},{4,12},{8,0},{12,4},{16,24},{20,28},{24,16},{28,20},{1,9},{5... | collective-permute-start | bytes 1572872 | tf_op jit(solution)/shard_map/ppermute | solution.py:500
  120.7 34.3 %collective-permute-start.35 = (bf16[256,1024]{1,0:T(8,128)(2,1)}, bf16[256,1024]{1,0:T(8,128)(2,1)S(1)}, u32[]{:S(2)}, u32[]{:S(2)}) collective-permute-start(bf16[256,1024]{1,0:T(8,128)(2,1)} %get-tuple-element.92.refs_0_), channel_id=1, source_target_pairs={{0,16},{4,20},{8,24},{12,28},{16,0},{20,4},{24,8},{28,12},{1,17},{... | collective-permute-start | bytes 1572872 | tf_op jit(solution)/shard_map/ppermute | solution.py:500
  155.7 21.6 %collective-permute-start.36 = (bf16[256,1024]{1,0:T(8,128)(2,1)}, bf16[256,1024]{1,0:T(8,128)(2,1)S(1)}, u32[]{:S(2)}, u32[]{:S(2)}) collective-permute-start(bf16[256,1024]{1,0:T(8,128)(2,1)} %get-tuple-element.93), channel_id=1, source_target_pairs={{0,4},{4,0},{8,12},{12,8},{16,20},{20,16},{24,28},{28,24},{1,5},{5... | collective-permute-start | bytes 1572872 | tf_op jit(solution)/shard_map/ppermute | solution.py:500
  161.0 15.7 %collective-permute-start.38 = (bf16[128,1024]{1,0:T(8,128)(2,1)S(1)}, bf16[128,1024]{1,0:T(8,128)(2,1)S(1)}, u32[]{:S(2)}, u32[]{:S(2)}) collective-permute-start(bf16[128,1024]{1,0:T(8,128)(2,1)S(1)} %add_convert_fusion.5), channel_id=1, source_target_pairs={{0,8},{4,12},{8,0},{12,4},{16,24},{20,28},{24,16},{28,20},{1,9},{5... | collective-permute-start | bytes 786440 | tf_op jit(solution)/shard_map/ppermute | solution.py:500
  161.6 14.3 %collective-permute-start.43 = (bf16[128,1024]{1,0:T(8,128)(2,1)S(1)}, bf16[128,1024]{1,0:T(8,128)(2,1)S(1)}, u32[]{:S(2)}, u32[]{:S(2)}) collective-permute-start(bf16[128,1024]{1,0:T(8,128)(2,1)S(1)} %get-tuple-element.110), channel_id=1, source_target_pairs={{0,8},{4,12},{8,0},{12,4},{16,24},{20,28},{24,16},{28,20},{1,9},{5... | collective-permute-start | bytes 786440 | tf_op jit(solution)/shard_map/ppermute | solution.py:500
  163.2 13.6 %collective-permute-start.45 = (bf16[128,1024]{1,0:T(8,128)(2,1)S(1)}, bf16[128,1024]{1,0:T(8,128)(2,1)S(1)}, u32[]{:S(2)}, u32[]{:S(2)}) collective-permute-start(bf16[128,1024]{1,0:T(8,128)(2,1)S(1)} %add_convert_fusion.2), channel_id=1, source_target_pairs={{0,16},{4,20},{8,24},{12,28},{16,0},{20,4},{24,8},{28,12},{1,17},{... | collective-permute-start | bytes 786440 | tf_op jit(solution)/shard_map/ppermute | solution.py:500
  176.7 13.9 %collective-permute-start.46 = (bf16[256,1024]{1,0:T(8,128)(2,1)}, bf16[256,1024]{1,0:T(8,128)(2,1)S(1)}, u32[]{:S(2)}, u32[]{:S(2)}) collective-permute-start(bf16[256,1024]{1,0:T(8,128)(2,1)} %get-tuple-element.92.refs_0_), channel_id=1, source_target_pairs={{0,4},{4,0},{8,12},{12,8},{16,20},{20,16},{24,28},{28,24},{1,5},{5... | collective-permute-start | bytes 1572872 | tf_op jit(solution)/shard_map/ppermute | solution.py:500
  176.8 13.8 %collective-permute-start.47 = (bf16[256,1024]{1,0:T(8,128)(2,1)S(1)}, bf16[256,1024]{1,0:T(8,128)(2,1)S(1)}, u32[]{:S(2)}, u32[]{:S(2)}) collective-permute-start(bf16[256,1024]{1,0:T(8,128)(2,1)S(1)} %collective-permute-done.34.refs_2_), channel_id=1, source_target_pairs={{0,4},{4,0},{8,12},{12,8},{16,20},{20,16},{24,28},{28,24},{1,5},{5... | collective-permute-start | bytes 1572872 | tf_op jit(solution)/shard_map/ppermute | solution.py:500
  177.3 13.3 %collective-permute-start.48 = (bf16[256,1024]{1,0:T(8,128)(2,1)S(1)}, bf16[256,1024]{1,0:T(8,128)(2,1)S(1)}, u32[]{:S(2)}, u32[]{:S(2)}) collective-permute-start(bf16[256,1024]{1,0:T(8,128)(2,1)S(1)} %collective-permute-done.35.refs_4_), channel_id=1, source_target_pairs={{0,4},{4,0},{8,12},{12,8},{16,20},{20,16},{24,28},{28,24},{1,5},{5... | collective-permute-start | bytes 1572872 | tf_op jit(solution)/shard_map/ppermute | solution.py:500
  (56 other events, 428.0 us)

commit v11 on v10

--- a/solution.py
+++ b/solution.py
@@ -15,7 +15,7 @@
 MOST = 58 * 1024 * 1024
 SOME = 20 * 1024 * 1024
 PAD = 16
-TOGETHER = 2
+TOGETHER = 4
 LOW = -(2.0**99)
 NN = (((1,), (0,)), ((), ()))
 NT = (((1,), (1,)), ((), ()))
@@ -352,8 +352,9 @@
 
 
 def finish_kernel(counts, *refs):
-    terms, (ga_ref, attn_ref, ext_ref) = dealt(refs, counts)
+    terms, (ga_ref, attn_ref, *ext_refs) = dealt(refs, counts)
     rows, width = ga_ref.shape
+    half = rows // len(ext_refs)
     heads = width // HD
     top, total, columns = blend(
         [[(ref, slice(None)) for ref in pieces] for pieces in terms], heads
@@ -362,7 +363,8 @@
     total = jnp.where(lane < heads, total, 1.0)
     inverse = 1.0 / total
     dots = jnp.zeros((rows, HD), F32)
-    ext_ref[:, :width] = ga_ref[...]
+    for i, ext_ref in enumerate(ext_refs):
+        ext_ref[:, :width] = ga_ref[i * half : (i + 1) * half]
     for h in range(heads):
         cols = slice(h * HD, (h + 1) * HD)
         attn = columns[h] * inverse[:, h : h + 1]
@@ -370,7 +372,9 @@
         dot = jnp.sum(attn * ga_ref[:, cols].astype(F32), axis=1, keepdims=True)
         dots = jnp.where(lane == h, dot, dots)
     level = jnp.where(lane < heads, top + jnp.log(total), 0.0)
-    ext_ref[:, width:] = packed_tail(digits_of(dots, 2) + digits_of(level, 3), heads)
+    tail = packed_tail(digits_of(dots, 2) + digits_of(level, 3), heads)
+    for i, ext_ref in enumerate(ext_refs):
+        ext_ref[:, width:] = tail[i * half : (i + 1) * half]
 
 
 def total_kernel(counts, *refs):
@@ -525,6 +529,15 @@
     return spread_far(spread_near(x), half, *before)
 
 
+def spread_halves(top, low):
+    chips = lax.axis_size("ctx") // 2
+    if chips != 4:
+        return [[swap(x, 2 * j) if j else x for x in (top, low)] for j in range(chips)]
+    x_top, y_low = swap(top, 2), swap(low, 4)
+    x_low, y_top = swap(low, 2), swap(top, 4)
+    return [[top, low], [x_top, x_low], [y_top, y_low], [swap(x_top, 4), swap(y_low, 2)]]
+
+
 def with_cores(lists, *before):
     both = []
     for pieces in lists:
@@ -593,12 +606,12 @@
     x_far, y_far = swap(x_far, 2), swap(y_far, 4)
     ins = [parts[2], received[1], parts[4], received[2]]
     x_top, y_low = merged(ins, [[(0, *top), (1, *top)], [(2, *low), (3, *low)]])
-    done = between(x_top, y_low)
     x_top, y_low = swap(x_top, 2), swap(y_low, 4)
     x_low, y_top = merged(
-        ins + [after(y_far, done[0]), x_far],
+        ins + [y_far, x_far],
         [[(0, *low), (1, *low), (4, *top)], [(2, *top), (3, *top), (5, *top)]],
     )
+    done = between(x_low, y_top)
     x_low, y_top = swap(x_low, 2), swap(y_top, 4)
     return terms + [[x_top, x_low], [y_top, y_low]], done
 
@@ -648,8 +661,8 @@
         compiler_params=small,
         name="pack",
     )(selected.T, queries)
-    query_chips = spread_chips(packed, rows // 2, ups[0], downs[0])
-    query_all = with_cores(query_chips, ups[1], downs[1])
+    query_chips = spread_chips(packed, rows // 2)
+    query_all = with_cores(query_chips, ups[0], downs[0])
 
     outs = pl.pallas_call(
         functools.partial(forward_kernel, [len(pieces) for pieces in query_all], span, cap),
@@ -696,27 +709,27 @@
         compiler_params=params,
         name="grad",
     )
-    received = from_core(outs[:chunks], *ups[2:], *downs[2:])
+    received = from_core(outs[:chunks], ups[1], downs[1])
     terms, (grad_attn, blocks) = merge_chips(
         outs[:chunks],
         received,
         heads,
         lambda *before: make_grad(after(line, *before), out_weight, out_grad, *ups, *downs),
     )
-    attn_out, extended = pl.pallas_call(
+    attn_out, *extended = pl.pallas_call(
         functools.partial(finish_kernel, [len(pieces) for pieces in terms]),
-        out_shape=[shaped((rows, width)), shaped((rows, width + HD))],
+        out_shape=[shaped((rows, width))] + [shaped((rows // 2, width + HD))] * 2,
         in_specs=[vmem] * (len(flat(terms)) + 1),
-        out_specs=[vmem] * 2,
+        out_specs=[vmem] * 3,
         compiler_params=small,
         name="finish",
     )(*flat(terms), grad_attn)
-    grad_chips = spread_chips(extended, rows // 2)
+    grad_chips = spread_halves(*extended)
     grad_all = with_cores(grad_chips)
-    arrived = flat(grad_chips[1:3])
+    arrived = [grad_chips[1][-1], grad_chips[2][0]]
     attns = spread_near(after(attn_out, *arrived))
     columns = lax.all_to_all(
-        after(blocks, *flat(grad_chips)), "ctx", split_axis=0, concat_axis=0, tiled=True
+        after(blocks, *arrived), "ctx", split_axis=0, concat_axis=0, tiled=True
     )
 
     outs = pl.pallas_call(
@@ -746,7 +759,8 @@
         name="backward",
     )(logits, hot, q_slots, probs, keys, values, *flat(grad_all))
     key_grad, value_grad = outs[chunks:]
-    terms = collect_chips(outs[:chunks], from_core(outs[:chunks], columns, *flat(attns[1:3])))
+    received = from_core(outs[:chunks], columns, *flat(attns[1:3]))
+    terms = collect_chips(outs[:chunks], received)
     query_grad = pl.pallas_call(
         functools.partial(total_kernel, [len(pieces) for pieces in terms]),
         out_shape=shaped((rows, width), F32),

time: 196 us -> 202 us (1.031)
  starting transfers between devices: 48.2 us -> 51.1 us
  Pallas kernels: 54.2 us -> 51.6 us
  waiting for transfers between devices: 79.5 us -> 81.9 us
    ppermute x47 -> x52, waiting for transfers between devices: 67.2 us -> 75.7 us  [swap(): return lax.ppermute(x, 'ctx', [(i, i ^ bits) for i in range(count)])]
    ppermute x3, waiting for transfers between devices: 5.29 us -> 0.01 us  [spread_line(): lax.ppermute(ups[-1], 'head', [(i, i + 1) for i in range(d - 1, lines - 1)])]
    ppermute x47 -> x52, starting transfers between devices: 32.6 us -> 36.8 us  [swap(): return lax.ppermute(x, 'ctx', [(i, i ^ bits) for i in range(count)])]
    unnamed x53 -> x73, local copies, waits for them, and re-layouts: 7.01 us -> 10.1 us
  transfers between devices with their start and end apart: 54 -> 59, of which waited for: 23 -> 21; matrix products, arithmetic and copies ran while one was open for 3% -> 2% of each run, Pallas kernels for 23% -> 22%
where the time goes in v11:
time: 202 us; the launch traced here: 200 us
  waiting for transfers between devices  81.9 us (41%)
  Pallas kernels  51.6 us (26%)
  starting transfers between devices  51.1 us (25%)
  local copies, waits for them, and re-layouts  11.2 us (6%)
  other arithmetic  2.55 us (1%)
    ppermute x52, waiting for transfers between devices, swap(): return lax.ppermute(x, 'ctx', [(i, i ^ bits) for i in range(count)])  75.7 us
    ppermute x52, starting transfers between devices, swap(): return lax.ppermute(x, 'ctx', [(i, i ^ bits) for i in range(count)])  36.8 us
    pallas_call x1, Pallas kernels, body(): pl.pallas_call(functools.partial(backward_kernel, [len(pieces) for pieces...  18.7 us
    pallas_call x1, Pallas kernels, body(): pl.pallas_call(functools.partial(forward_kernel, [len(pieces) for pieces...  13.5 us
    unnamed x73, local copies, waits for them, and re-layouts  10.1 us
    pallas_call x1, Pallas kernels, body(): make_grad(after(line, *before), out_weight, out_grad, *ups, *downs)  7.66 us
    ppermute x3, starting transfers between devices, spread_line(): lax.ppermute(ups[-1], 'head', [(i, i + 1) for i in range(d - 1, lines - 1)])  6.44 us
    ppermute x3, waiting for transfers between devices, spread_line(): lax.ppermute(downs[-1], 'head', [(i, i - 1) for i in range(1, lines - d +...  6.17 us
  transfers between devices with their start and end apart: 59, of which 21 were waited for; matrix products, arithmetic and copies ran while one was open for 2% of the time, Pallas kernels for 22%

profile of v11, /device:TPU:0, one launch (start us, length us, event | category | flops | bytes accessed | tf_op | source)
XLA Modules:
  0.0 199.6 jit_solution(5812654695711666481)
XLA Ops:
  2.4 3.0 %collective-permute-start.1 = (bf16[272,1024]{1,0:T(8,128)(2,1)S(1)}, bf16[272,1024]{1,0:T(8,128)(2,1)S(1)}, u32[]{:S(2)}, u32[]{:S(2)}) collective-permute-start(bf16[272,1024]{1,0:T(8,128)(2,1)S(1)} %pack.1.refs_0_), channel_id=1, source_target_pairs={{0,8},{4,12},{8,0},{12,4},{16,24},{20,28},{24,16},{28,20},{1,9},{5... | collective-permute-start | bytes 1671176 | tf_op jit(solution)/shard_map/ppermute | solution.py:504
  5.4 1.5 collective-permute-start.3
  6.9 4.3 %collective-permute-start.6 = (bf16[256,1024]{1,0:T(8,128)(2,1)}, bf16[256,1024]{1,0:T(8,128)(2,1)}, u32[]{:S(2)}, u32[]{:S(2)}) collective-permute-start(bf16[256,1024]{1,0:T(8,128)(2,1)} %refs_0_.1), channel_id=1, source_target_pairs={{0,1},{1,2},{2,3},{4,5},{5,6},{6,7},{8,9},{9,10},{10,11},{12,13},{... | collective-permute-start | bytes 1572872 | tf_op jit(solution)/shard_map/ppermute | solution.py:623
  12.6 5.4 %collective-permute-done.1.refs_2_ = bf16[272,1024]{1,0:T(8,128)(2,1)S(1)} collective-permute-done((bf16[272,1024]{1,0:T(8,128)(2,1)S(1)}, bf16[272,1024]{1,0:T(8,128)(2,1)S(1)}, u32[]{:S(2)}, u32[]{:S(2)}) %collective-permute-start.1) | collective-permute-done | bytes 557088 | tf_op jit(solution)/shard_map/ppermute | solution.py:504
  18.1 1.8 collective-permute-start.5
  19.9 1.6 collective-permute-start.8
  21.5 4.8 %collective-permute-done.7.refs_4_ = bf16[256,1024]{1,0:T(8,128)(2,1)} collective-permute-done((bf16[256,1024]{1,0:T(8,128)(2,1)}, bf16[256,1024]{1,0:T(8,128)(2,1)}, u32[]{:S(2)}, u32[]{:S(2)}) %collective-permute-start.7) | collective-permute-done | bytes 524320 | tf_op jit(solution)/shard_map/ppermute | solution.py:624
  33.4 13.5 %forward.1 = (bf16[256,1152]{1,0:T(8,128)(2,1)}, bf16[256,1152]{1,0:T(8,128)(2,1)}, bf16[256,1152]{1,0:T(8,128)(2,1)}, bf16[256,1152]{1,0:T(8,128)(2,1)}, bf16[2...) custom-call(s32[1]{0:T(128)} %bitcast.me_ref, ...), custom_call_target="tpu_custom_call" | custom-call | tf_op jit(solution)/shard_map/forward/pallas_call | solution.py:667
  56.9 4.1 %collective-permute-done.18.refs_4_ = bf16[128,1152]{1,0:T(8,128)(2,1)S(1)} collective-permute-done((bf16[128,1152]{1,0:T(8,128)(2,1)S(1)}, bf16[128,1152]{1,0:T(8,128)(2,1)S(1)}, u32[]{:S(2)}, u32[]{:S(2)}) %collective-permute-start.18) | collective-permute-done | bytes 294944 | tf_op jit(solution)/shard_map/ppermute | solution.py:504
  67.3 1.5 collective-permute-start.21
  68.8 7.7 %grad.1 = (bf16[256,1024]{1,0:T(8,128)(2,1)}, bf16[8,256,512]{2,1,0:T(8,128)(2,1)}) custom-call(s32[1]{0:T(128)} %bitcast.4.line_ref, bf16[4096,1024]{1,0:T(8,128)(2,1)} %w_ref.1, bf16[256,1024]{1,0:T(8,128)(2,1)} %refs_0_.1, bf16[256,1024]{1,0:T(8,128)(2,1)} %collective-permute-done.6.refs_1_, bf16[256,1024]{1,0:T(8,128)(2,1)} %collective-permute-done.11.refs_2_, ...), custom_call_target="tpu_custom_call" | custom-call | tf_op jit(solution)/shard_map/grad/pallas_call | solution.py:717
  77.7 3.4 %finish.1 = (bf16[256,1024]{1,0:T(8,128)(2,1)}, bf16[128,1152]{1,0:T(8,128)(2,1)S(1)}, bf16[128,1152]{1,0:T(8,128)(2,1)S(1)}) custom-call(bf16[256,1152]{1,0:T(8,128)(2,1)S(1)} %copy-done.4, bf16[256,1152]{1,0:T(8,128)(2,1)S(1)} %collective-permute-done.13.refs_1_, bf16[128,1152]{1,0:T(8,128)(2,1)S(1)} %collective-permute-done.16.refs_2_, ...), custom_call_target="tpu_custom_call" | custom-call | tf_op jit(solution)/shard_map/finish/pallas_call | solution.py:719
  81.1 1.5 collective-permute-start.31
  83.4 6.0 %collective-permute-done.31.refs_8_ = bf16[128,1152]{1,0:T(8,128)(2,1)S(1)} collective-permute-done((bf16[128,1152]{1,0:T(8,128)(2,1)S(1)}, bf16[128,1152]{1,0:T(8,128)(2,1)S(1)}, u32[]{:S(2)}, u32[]{:S(2)}) %collective-permute-start.31) | collective-permute-done | bytes 294944 | tf_op jit(solution)/shard_map/ppermute | solution.py:504
  90.7 3.8 %all-to-all-start = ((bf16[8,256,512]{2,1,0:T(8,128)(2,1)}), bf16[8,256,512]{2,1,0:T(8,128)(2,1)S(1)}, u32[]{:S(2)}, u32[]{:S(2)}) async-start(bf16[8,256,512]{2,1,0:T(8,128)(2,1)} %get-tuple-element.86), calls=%async_computation | async-start | bytes 4194304 | tf_op jit(solution)/shard_map/all_to_all | solution.py:731
  94.5 1.7 collective-permute-start.27
  98.2 28.1 %collective-permute-done.27.refs_4_ = bf16[128,1152]{1,0:T(8,128)(2,1)S(1)} collective-permute-done((bf16[128,1152]{1,0:T(8,128)(2,1)S(1)}, bf16[128,1152]{1,0:T(8,128)(2,1)S(1)}, u32[]{:S(2)}, u32[]{:S(2)}) %collective-permute-start.27) | collective-permute-done | bytes 294944 | tf_op jit(solution)/shard_map/ppermute | solution.py:504
  129.0 7.3 %collective-permute-done.35.refs_12_ = bf16[128,1152]{1,0:T(8,128)(2,1)S(1)} collective-permute-done((bf16[128,1152]{1,0:T(8,128)(2,1)S(1)}, bf16[128,1152]{1,0:T(8,128)(2,1)S(1)}, u32[]{:S(2)}, u32[]{:S(2)}) %collective-permute-start.35) | collective-permute-done | bytes 294944 | tf_op jit(solution)/shard_map/ppermute | solution.py:504
  140.8 18.7 %backward.1 = (bf16[256,1024]{1,0:T(8,128)(2,1)}, bf16[256,1024]{1,0:T(8,128)(2,1)}, bf16[256,1024]{1,0:T(8,128)(2,1)}, bf16[256,1024]{1,0:T(8,128)(2,1)}, bf16[...) custom-call(f32[16,8,128]{2,1,0:T(8,128)} %get-tuple-element.57.logi, ...), custom_call_target="tpu_custom_call" | custom-call | tf_op jit(solution)/shard_map/backward/pallas_call | solution.py:735
  168.3 3.9 %collective-permute-done.45 = bf16[128,1024]{1,0:T(8,128)(2,1)S(1)} collective-permute-done((bf16[128,1024]{1,0:T(8,128)(2,1)S(1)}, bf16[128,1024]{1,0:T(8,128)(2,1)S(1)}, u32[]{:S(2)}, u32[]{:S(2)}) %collective-permute-start.45) | collective-permute-done | bytes 262176 | tf_op jit(solution)/shard_map/ppermute | solution.py:504
  173.4 6.6 %collective-permute-done.48 = bf16[128,1024]{1,0:T(8,128)(2,1)S(1)} collective-permute-done((bf16[128,1024]{1,0:T(8,128)(2,1)S(1)}, bf16[128,1024]{1,0:T(8,128)(2,1)S(1)}, u32[]{:S(2)}, u32[]{:S(2)}) %collective-permute-start.48) | collective-permute-done | bytes 262176 | tf_op jit(solution)/shard_map/ppermute | solution.py:504
  181.9 2.6 %collective-permute-done.46.refs_3_ = bf16[128,1024]{1,0:T(8,128)(2,1)S(1)} collective-permute-done((bf16[128,1024]{1,0:T(8,128)(2,1)S(1)}, bf16[128,1024]{1,0:T(8,128)(2,1)S(1)}, u32[]{:S(2)}, u32[]{:S(2)}) %collective-permute-start.46) | collective-permute-done | bytes 262176 | tf_op jit(solution)/shard_map/ppermute | solution.py:504
  188.3 3.8 %collective-permute-done.54.refs_6_ = bf16[128,1024]{1,0:T(8,128)(2,1)S(1)} collective-permute-done((bf16[128,1024]{1,0:T(8,128)(2,1)S(1)}, bf16[128,1024]{1,0:T(8,128)(2,1)S(1)}, u32[]{:S(2)}, u32[]{:S(2)}) %collective-permute-start.54) | collective-permute-done | bytes 262176 | tf_op jit(solution)/shard_map/ppermute | solution.py:504
  194.9 4.7 %weight.1 = f32[512,1024]{1,0:T(8,128)} custom-call(s32[1]{0:T(128)} %bitcast.me_ref, bf16[8,256,512]{2,1,0:T(8,128)(2,1)S(1)} %all-to-all-done.cols_ref, bf16[256,1024]{1,0:T(8,128)(2,1)} %get-tuple-element.88.refs_0_, bf16[256,1024]{1,0:T(8,128)(2,1)S(1)} %collective-permute-done.51.refs_1_, bf16[256,1024]{1,0:T(8,128)(2,1)S(1)} %collective-permute-done.39.refs_2_, ...), custom_call_target="tpu_custom_call" | custom-call | tf_op jit(solution)/shard_map/weight/pallas_call | solution.py:774
  (187 shorter events, 57.2 us)
Async XLA Ops:
  2.4 15.6 %collective-permute-start.1 = (bf16[272,1024]{1,0:T(8,128)(2,1)S(1)}, bf16[272,1024]{1,0:T(8,128)(2,1)S(1)}, u32[]{:S(2)}, u32[]{:S(2)}) collective-permute-start(bf16[272,1024]{1,0:T(8,128)(2,1)S(1)} %pack.1.refs_0_), channel_id=1, source_target_pairs={{0,8},{4,12},{8,0},{12,4},{16,24},{20,28},{24,16},{28,20},{1,9},{5... | collective-permute-start | bytes 1671176 | tf_op jit(solution)/shard_map/ppermute | solution.py:504
  5.4 14.5 %collective-permute-start.3 = (bf16[272,1024]{1,0:T(8,128)(2,1)S(1)}, bf16[272,1024]{1,0:T(8,128)(2,1)S(1)}, u32[]{:S(2)}, u32[]{:S(2)}) collective-permute-start(bf16[272,1024]{1,0:T(8,128)(2,1)S(1)} %pack.1.refs_0_), channel_id=1, source_target_pairs={{0,16},{4,20},{8,24},{12,28},{16,0},{20,4},{24,8},{28,12},{1,17},{... | collective-permute-start | bytes 1671176 | tf_op jit(solution)/shard_map/ppermute | solution.py:504
  6.9 14.6 %collective-permute-start.6 = (bf16[256,1024]{1,0:T(8,128)(2,1)}, bf16[256,1024]{1,0:T(8,128)(2,1)}, u32[]{:S(2)}, u32[]{:S(2)}) collective-permute-start(bf16[256,1024]{1,0:T(8,128)(2,1)} %refs_0_.1), channel_id=1, source_target_pairs={{0,1},{1,2},{2,3},{4,5},{5,6},{6,7},{8,9},{9,10},{10,11},{12,13},{... | collective-permute-start | bytes 1572872 | tf_op jit(solution)/shard_map/ppermute | solution.py:623
  11.2 15.0 %collective-permute-start.7 = (bf16[256,1024]{1,0:T(8,128)(2,1)}, bf16[256,1024]{1,0:T(8,128)(2,1)}, u32[]{:S(2)}, u32[]{:S(2)}) collective-permute-start(bf16[256,1024]{1,0:T(8,128)(2,1)} %refs_0_.1), channel_id=1, source_target_pairs={{1,0},{2,1},{3,2},{5,4},{6,5},{7,6},{9,8},{10,9},{11,10},{13,12},{... | collective-permute-start | bytes 1572872 | tf_op jit(solution)/shard_map/ppermute | solution.py:624
  12.5 14.3 %collective-permute-start = (bf16[272,1024]{1,0:T(8,128)(2,1)S(1)}, bf16[272,1024]{1,0:T(8,128)(2,1)S(1)}, u32[]{:S(2)}, u32[]{:S(2)}) collective-permute-start(bf16[272,1024]{1,0:T(8,128)(2,1)S(1)} %pack.1.refs_0_), channel_id=1, source_target_pairs={{0,4},{4,0},{8,12},{12,8},{16,20},{20,16},{24,28},{28,24},{1,5},{5... | collective-permute-start | bytes 1671176 | tf_op jit(solution)/shard_map/ppermute | solution.py:504
  26.8 20.1 %collective-permute-start.11 = (bf16[256,1024]{1,0:T(8,128)(2,1)}, bf16[256,1024]{1,0:T(8,128)(2,1)}, u32[]{:S(2)}, u32[]{:S(2)}) collective-permute-start(bf16[256,1024]{1,0:T(8,128)(2,1)} %collective-permute-done.6.refs_1_), channel_id=1, source_target_pairs={{1,2},{2,3},{5,6},{6,7},{9,10},{10,11},{13,14},{14,15},{17,18},{18... | collective-permute-start | bytes 1572872 | tf_op jit(solution)/shard_map/ppermute | solution.py:623
  28.3 18.6 %collective-permute-start.12 = (bf16[256,1024]{1,0:T(8,128)(2,1)}, bf16[256,1024]{1,0:T(8,128)(2,1)}, u32[]{:S(2)}, u32[]{:S(2)}) collective-permute-start(bf16[256,1024]{1,0:T(8,128)(2,1)} %collective-permute-done.7.refs_4_), channel_id=1, source_target_pairs={{1,0},{2,1},{5,4},{6,5},{9,8},{10,9},{13,12},{14,13},{17,16},{18,1... | collective-permute-start | bytes 1572872 | tf_op jit(solution)/shard_map/ppermute | solution.py:624
  47.6 16.8 %collective-permute-start.23 = (bf16[256,1024]{1,0:T(8,128)(2,1)}, bf16[256,1024]{1,0:T(8,128)(2,1)S(1)}, u32[]{:S(2)}, u32[]{:S(2)}) collective-permute-start(bf16[256,1024]{1,0:T(8,128)(2,1)} %collective-permute-done.11.refs_2_), channel_id=1, source_target_pairs={{2,3},{6,7},{10,11},{14,15},{18,19},{22,23},{26,27},{30,31}} | collective-permute-start | bytes 1572872 | tf_op jit(solution)/shard_map/ppermute | solution.py:623
  48.3 18.1 %collective-permute-start.24 = (bf16[256,1024]{1,0:T(8,128)(2,1)}, bf16[256,1024]{1,0:T(8,128)(2,1)S(1)}, u32[]{:S(2)}, u32[]{:S(2)}) collective-permute-start(bf16[256,1024]{1,0:T(8,128)(2,1)} %collective-permute-done.12.refs_5_), channel_id=1, source_target_pairs={{1,0},{5,4},{9,8},{13,12},{17,16},{21,20},{25,24},{29,28}} | collective-permute-start | bytes 1572872 | tf_op jit(solution)/shard_map/ppermute | solution.py:624
  54.1 22.4 %collective-permute-start.13 = (bf16[256,1152]{1,0:T(8,128)(2,1)}, bf16[256,1152]{1,0:T(8,128)(2,1)S(1)}, u32[]{:S(2)}, u32[]{:S(2)}) collective-permute-start(bf16[256,1152]{1,0:T(8,128)(2,1)} %get-tuple-element.63), channel_id=1, source_target_pairs={{0,4},{4,0},{8,12},{12,8},{16,20},{20,16},{24,28},{28,24},{1,5},{5... | collective-permute-start | bytes 1769480 | tf_op jit(solution)/shard_map/ppermute | solution.py:504
  61.0 15.5 %collective-permute-start.16 = (bf16[128,1152]{1,0:T(8,128)(2,1)S(1)}, bf16[128,1152]{1,0:T(8,128)(2,1)S(1)}, u32[]{:S(2)}, u32[]{:S(2)}) collective-permute-start(bf16[128,1152]{1,0:T(8,128)(2,1)S(1)} %get-tuple-element.70), channel_id=1, source_target_pairs={{0,8},{4,12},{8,0},{12,4},{16,24},{20,28},{24,16},{28,20},{1,9},{5... | collective-permute-start | bytes 884744 | tf_op jit(solution)/shard_map/ppermute | solution.py:504
  62.0 14.5 %collective-permute-start.22 = (bf16[128,1152]{1,0:T(8,128)(2,1)S(1)}, bf16[128,1152]{1,0:T(8,128)(2,1)S(1)}, u32[]{:S(2)}, u32[]{:S(2)}) collective-permute-start(bf16[128,1152]{1,0:T(8,128)(2,1)S(1)} %get-tuple-element.78), channel_id=1, source_target_pairs={{0,16},{4,20},{8,24},{12,28},{16,0},{20,4},{24,8},{28,12},{1,17},{... | collective-permute-start | bytes 884744 | tf_op jit(solution)/shard_map/ppermute | solution.py:504
  90.7 68.9 %all-to-all-start = ((bf16[8,256,512]{2,1,0:T(8,128)(2,1)}), bf16[8,256,512]{2,1,0:T(8,128)(2,1)S(1)}, u32[]{:S(2)}, u32[]{:S(2)}) async-start(bf16[8,256,512]{2,1,0:T(8,128)(2,1)} %get-tuple-element.86), calls=%async_computation | async-start | bytes 4194304 | tf_op jit(solution)/shard_map/all_to_all | solution.py:731
  94.5 31.8 %collective-permute-start.27 = (bf16[128,1152]{1,0:T(8,128)(2,1)S(1)}, bf16[128,1152]{1,0:T(8,128)(2,1)S(1)}, u32[]{:S(2)}, u32[]{:S(2)}) collective-permute-start(bf16[128,1152]{1,0:T(8,128)(2,1)S(1)} %get-tuple-element.81.refs_0_), channel_id=1, source_target_pairs={{0,8},{4,12},{8,0},{12,4},{16,24},{20,28},{24,16},{28,20},{1,9},{5... | collective-permute-start | bytes 884744 | tf_op jit(solution)/shard_map/ppermute | solution.py:504
  96.2 31.6 %collective-permute-start.25 = (bf16[128,1152]{1,0:T(8,128)(2,1)S(1)}, bf16[128,1152]{1,0:T(8,128)(2,1)S(1)}, u32[]{:S(2)}, u32[]{:S(2)}) collective-permute-start(bf16[128,1152]{1,0:T(8,128)(2,1)S(1)} %get-tuple-element.81.refs_0_), channel_id=1, source_target_pairs={{0,4},{4,0},{8,12},{12,8},{16,20},{20,16},{24,28},{28,24},{1,5},{5... | collective-permute-start | bytes 884744 | tf_op jit(solution)/shard_map/ppermute | solution.py:504
  96.2 31.6 %collective-permute-start.32 = (bf16[128,1152]{1,0:T(8,128)(2,1)S(1)}, bf16[128,1152]{1,0:T(8,128)(2,1)S(1)}, u32[]{:S(2)}, u32[]{:S(2)}) collective-permute-start(bf16[128,1152]{1,0:T(8,128)(2,1)S(1)} %get-tuple-element.82.refs_1_), channel_id=1, source_target_pairs={{0,16},{4,20},{8,24},{12,28},{16,0},{20,4},{24,8},{28,12},{1,17},{... | collective-permute-start | bytes 884744 | tf_op jit(solution)/shard_map/ppermute | solution.py:504
  97.7 30.7 %collective-permute-start.26 = (bf16[128,1152]{1,0:T(8,128)(2,1)S(1)}, bf16[128,1152]{1,0:T(8,128)(2,1)S(1)}, u32[]{:S(2)}, u32[]{:S(2)}) collective-permute-start(bf16[128,1152]{1,0:T(8,128)(2,1)S(1)} %get-tuple-element.82.refs_1_), channel_id=1, source_target_pairs={{0,4},{4,0},{8,12},{12,8},{16,20},{20,16},{24,28},{28,24},{1,5},{5... | collective-permute-start | bytes 884744 | tf_op jit(solution)/shard_map/ppermute | solution.py:504
  98.0 30.7 %collective-permute-start.33 = (bf16[128,1152]{1,0:T(8,128)(2,1)S(1)}, bf16[128,1152]{1,0:T(8,128)(2,1)S(1)}, u32[]{:S(2)}, u32[]{:S(2)}) collective-permute-start(bf16[128,1152]{1,0:T(8,128)(2,1)S(1)} %collective-permute-done.31.refs_8_), channel_id=1, source_target_pairs={{0,4},{4,0},{8,12},{12,8},{16,20},{20,16},{24,28},{28,24},{1,5},{5... | collective-permute-start | bytes 884744 | tf_op jit(solution)/shard_map/ppermute | solution.py:504
  128.6 30.9 %collective-permute-start.40 = (bf16[256,1024]{1,0:T(8,128)(2,1)}, bf16[256,1024]{1,0:T(8,128)(2,1)S(1)}, u32[]{:S(2)}, u32[]{:S(2)}) collective-permute-start(bf16[256,1024]{1,0:T(8,128)(2,1)} %get-tuple-element.88.refs_0_), channel_id=1, source_target_pairs={{0,16},{4,20},{8,24},{12,28},{16,0},{20,4},{24,8},{28,12},{1,17},{... | collective-permute-start | bytes 1572872 | tf_op jit(solution)/shard_map/ppermute | solution.py:504
  136.2 23.3 %collective-permute-start.39 = (bf16[256,1024]{1,0:T(8,128)(2,1)}, bf16[256,1024]{1,0:T(8,128)(2,1)S(1)}, u32[]{:S(2)}, u32[]{:S(2)}) collective-permute-start(bf16[256,1024]{1,0:T(8,128)(2,1)} %get-tuple-element.88.refs_0_), channel_id=1, source_target_pairs={{0,8},{4,12},{8,0},{12,4},{16,24},{20,28},{24,16},{28,20},{1,9},{5... | collective-permute-start | bytes 1572872 | tf_op jit(solution)/shard_map/ppermute | solution.py:504
  160.3 21.6 %collective-permute-start.41 = (bf16[256,1024]{1,0:T(8,128)(2,1)}, bf16[256,1024]{1,0:T(8,128)(2,1)S(1)}, u32[]{:S(2)}, u32[]{:S(2)}) collective-permute-start(bf16[256,1024]{1,0:T(8,128)(2,1)} %get-tuple-element.89), channel_id=1, source_target_pairs={{0,4},{4,0},{8,12},{12,8},{16,20},{20,16},{24,28},{28,24},{1,5},{5... | collective-permute-start | bytes 1572872 | tf_op jit(solution)/shard_map/ppermute | solution.py:504
  165.1 16.1 %collective-permute-start.43 = (bf16[128,1024]{1,0:T(8,128)(2,1)S(1)}, bf16[128,1024]{1,0:T(8,128)(2,1)S(1)}, u32[]{:S(2)}, u32[]{:S(2)}) collective-permute-start(bf16[128,1024]{1,0:T(8,128)(2,1)S(1)} %add_convert_fusion.5), channel_id=1, source_target_pairs={{0,8},{4,12},{8,0},{12,4},{16,24},{20,28},{24,16},{28,20},{1,9},{5... | collective-permute-start | bytes 786440 | tf_op jit(solution)/shard_map/ppermute | solution.py:504
  167.3 14.1 %collective-permute-start.50 = (bf16[128,1024]{1,0:T(8,128)(2,1)S(1)}, bf16[128,1024]{1,0:T(8,128)(2,1)S(1)}, u32[]{:S(2)}, u32[]{:S(2)}) collective-permute-start(bf16[128,1024]{1,0:T(8,128)(2,1)S(1)} %add_convert_fusion.2), channel_id=1, source_target_pairs={{0,16},{4,20},{8,24},{12,28},{16,0},{20,4},{24,8},{28,12},{1,17},{... | collective-permute-start | bytes 786440 | tf_op jit(solution)/shard_map/ppermute | solution.py:504
  181.2 13.4 %collective-permute-start.51 = (bf16[256,1024]{1,0:T(8,128)(2,1)}, bf16[256,1024]{1,0:T(8,128)(2,1)S(1)}, u32[]{:S(2)}, u32[]{:S(2)}) collective-permute-start(bf16[256,1024]{1,0:T(8,128)(2,1)} %get-tuple-element.88.refs_0_), channel_id=1, source_target_pairs={{0,4},{4,0},{8,12},{12,8},{16,20},{20,16},{24,28},{28,24},{1,5},{5... | collective-permute-start | bytes 1572872 | tf_op jit(solution)/shard_map/ppermute | solution.py:504
  (71 other events, 544.8 us)

commit v12 on v11

--- a/solution.py
+++ b/solution.py
@@ -457,17 +457,17 @@
                     extra = jnp.where(last, scale * gate * (delta - dots[h : h + 1, :]), 0.0)
                     low.append((weight * (scale * (grad - delta)) + extra).astype(BF16))
                     high.append(weight.astype(BF16))
-                scores.append(jnp.concatenate(low, axis=0))
-                gated.append(jnp.concatenate(high, axis=0))
+                scores.append(low)
+                gated.append(high)
         for u, b in enumerate(blocks):
             for p, cols in enumerate(pairs):
                 score, weight = scores[u * len(pairs) + p], gated[u * len(pairs) + p]
-                dv = mm(weight, gag_ref[b, :, cols])
-                dk = mm(score, qg_ref[b, :, cols])
-                dq = mm(score, diagonal(k_ref[b, :, cols]), TN).astype(BF16)
-                dv_ref[b, :, cols] = jnp.concatenate([dv[:BLOCK, :HD], dv[BLOCK:, HD:]], axis=1)
-                dk_ref[b, :, cols] = jnp.concatenate([dk[:BLOCK, :HD], dk[BLOCK:, HD:]], axis=1)
-                dq_ref[b, :, cols] = dq
+                for i in range(2):
+                    head = slice((2 * p + i) * HD, (2 * p + i + 1) * HD)
+                    dv_ref[b, :, head] = mm(weight[i], gag_ref[b, :, head])
+                    dk_ref[b, :, head] = mm(score[i], qg_ref[b, :, head])
+                both = jnp.concatenate(score, axis=0)
+                dq_ref[b, :, cols] = mm(both, diagonal(k_ref[b, :, cols]), TN).astype(BF16)
         for b in blocks:
             start(block_stores(b))
         return carry
@@ -492,11 +492,14 @@
     wait(part_copies)
 
 
-def weight_kernel(counts, me_ref, cols_ref, *refs):
-    attns, (out_ref,) = dealt(refs, counts)
+def weight_kernel(counts, first, me_ref, cols_ref, *refs):
+    attns, (*before, out_ref) = dealt(refs, counts)
     me = me_ref[0]
-    columns = joined([cols_ref[me ^ m] for m in range(len(counts))], 0)
-    out_ref[...] = mm(columns, joined([whole(pieces) for pieces in attns], 0), TN)
+    columns = joined([cols_ref[me ^ (first + m)] for m in range(len(counts))], 0)
+    total = mm(columns, joined([whole(pieces) for pieces in attns], 0), TN)
+    for ref in before:
+        total = total + ref[...]
+    out_ref[...] = total
 
 
 def swap(x, bits):
@@ -566,14 +569,16 @@
 
     terms = [[parts[0]], [received[0]]]
     if chips != 4:
-        return terms + [[swap(both(j, slice(None)), 2 * j)] for j in range(1, chips)]
+        return terms + [[swap(both(j, slice(None)), 2 * j)] for j in range(1, chips)], []
     half = parts[0].shape[0] // 2
     top, low = slice(0, half), slice(half, None)
-    x_far, y_far = swap(both(3, top), 2), swap(both(3, low), 4)
-    x_sum, y_sum = both(1, top), both(2, low)
+    x_sum, y_sum = both(3, top), both(3, low)
+    x_far, y_far = swap(x_sum, 2), swap(y_sum, 4)
+    x_sum, y_sum = both(1, top, None, x_sum), both(2, low, None, y_sum)
     x_top, y_low = swap(x_sum, 2), swap(y_sum, 4)
-    x_low, y_top = swap(both(1, low, y_far, x_sum), 2), swap(both(2, top, x_far, y_sum), 4)
-    return terms + [[x_top, x_low], [y_top, y_low]]
+    x_sum, y_sum = both(1, low, y_far, x_sum), both(2, top, x_far, y_sum)
+    x_low, y_top = swap(x_sum, 2), swap(y_sum, 4)
+    return terms + [[x_top, x_low], [y_top, y_low]], [x_sum, y_sum]
 
 
 def merge_chips(parts, received, heads, between):
@@ -726,7 +731,7 @@
     )(*flat(terms), grad_attn)
     grad_chips = spread_halves(*extended)
     grad_all = with_cores(grad_chips)
-    arrived = [grad_chips[1][-1], grad_chips[2][0]]
+    arrived = flat(grad_chips[1:])
     attns = spread_near(after(attn_out, *arrived))
     columns = lax.all_to_all(
         after(blocks, *arrived), "ctx", split_axis=0, concat_axis=0, tiled=True
@@ -760,7 +765,20 @@
     )(logits, hot, q_slots, probs, keys, values, *flat(grad_all))
     key_grad, value_grad = outs[chunks:]
     received = from_core(outs[:chunks], columns, *flat(attns[1:3]))
-    terms = collect_chips(outs[:chunks], received)
+    terms, last_sums = collect_chips(outs[:chunks], received)
+    attns = with_cores(spread_far(attns, rows // 2, *last_sums))
+
+    def weight_part(chosen, first, when, *before):
+        return pl.pallas_call(
+            functools.partial(weight_kernel, [len(pieces) for pieces in chosen], first),
+            out_shape=shaped((features // chunks, width), F32),
+            in_specs=[smem] + [vmem] * (1 + len(flat(chosen)) + len(before)),
+            out_specs=vmem,
+            compiler_params=small,
+            name="weight",
+        )(when, columns, *flat(chosen), *before)
+
+    weight_near = weight_part(attns[:-2], 0, after(me, terms[2][0]))
     query_grad = pl.pallas_call(
         functools.partial(total_kernel, [len(pieces) for pieces in terms]),
         out_shape=shaped((rows, width), F32),
@@ -768,17 +786,8 @@
         out_specs=vmem,
         compiler_params=small,
         name="total",
-    )(*flat(terms))
-
-    attns = with_cores(spread_far(attns, rows // 2, terms[2][0], terms[-1][-1]))
-    weight_grad = pl.pallas_call(
-        functools.partial(weight_kernel, [len(pieces) for pieces in attns]),
-        out_shape=shaped((features // chunks, width), F32),
-        in_specs=[smem] + [vmem] * (1 + len(flat(attns))),
-        out_specs=vmem,
-        compiler_params=small,
-        name="weight",
-    )(after(me, *flat(terms)), columns, *flat(attns))
+    )(after(terms[0][0], weight_near), *flat(terms[1:]))
+    weight_grad = weight_part(attns[-2:], chunks - 2, after(me, query_grad), weight_near)
     return (
         query_grad,
         key_grad.reshape(-1, width),

time: 202 us -> 184 us (0.911)
  waiting for transfers between devices: 81.9 us -> 64.8 us
    ppermute x52, waiting for transfers between devices: 75.7 us -> 58.3 us  [swap(): return lax.ppermute(x, 'ctx', [(i, i ^ bits) for i in range(count)])]
    unnamed x73 -> x75, local copies, waits for them, and re-layouts: 10.1 us -> 11.1 us
    pallas_call x1 -> x2, Pallas kernels: 4.71 us -> 4.92 us  [weight_part(): pl.pallas_call(functools.partial(weight_kernel, [len(pieces) for pieces i...]
  transfers between devices with their start and end apart: 59 -> 59, of which waited for: 21 -> 23; matrix products, arithmetic and copies ran while one was open for 2% -> 2% of each run, Pallas kernels for 22% -> 25%
where the time goes in v12:
time: 184 us; the launch traced here: 182 us
  waiting for transfers between devices  64.8 us (35%)
  Pallas kernels  51.9 us (28%)
  starting transfers between devices  50.4 us (27%)
  local copies, waits for them, and re-layouts  12.2 us (7%)
    ppermute x52, waiting for transfers between devices, swap(): return lax.ppermute(x, 'ctx', [(i, i ^ bits) for i in range(count)])  58.3 us
    ppermute x52, starting transfers between devices, swap(): return lax.ppermute(x, 'ctx', [(i, i ^ bits) for i in range(count)])  36.1 us
    pallas_call x1, Pallas kernels, body(): pl.pallas_call(functools.partial(backward_kernel, [len(pieces) for pieces...  18.7 us
    pallas_call x1, Pallas kernels, body(): pl.pallas_call(functools.partial(forward_kernel, [len(pieces) for pieces...  13.5 us
    unnamed x75, local copies, waits for them, and re-layouts  11.1 us
    pallas_call x1, Pallas kernels, body(): make_grad(after(line, *before), out_weight, out_grad, *ups, *downs)  7.68 us
    ppermute x3, waiting for transfers between devices, spread_line(): lax.ppermute(downs[-1], 'head', [(i, i - 1) for i in range(1, lines - d +...  6.54 us
    ppermute x3, starting transfers between devices, spread_line(): lax.ppermute(ups[-1], 'head', [(i, i + 1) for i in range(d - 1, lines - 1)])  6.44 us
  transfers between devices with their start and end apart: 59, of which 23 were waited for; matrix products, arithmetic and copies ran while one was open for 2% of the time, Pallas kernels for 25%

profile of v12, /device:TPU:0, one launch (start us, length us, event | category | flops | bytes accessed | tf_op | source)
XLA Modules:
  0.0 182.0 jit_solution(16610234135857278927)
XLA Ops:
  2.4 3.0 %collective-permute-start.1 = (bf16[272,1024]{1,0:T(8,128)(2,1)S(1)}, bf16[272,1024]{1,0:T(8,128)(2,1)S(1)}, u32[]{:S(2)}, u32[]{:S(2)}) collective-permute-start(bf16[272,1024]{1,0:T(8,128)(2,1)S(1)} %pack.1.refs_0_), channel_id=1, source_target_pairs={{0,8},{4,12},{8,0},{12,4},{16,24},{20,28},{24,16},{28,20},{1,9},{5... | collective-permute-start | bytes 1671176 | tf_op jit(solution)/shard_map/ppermute | solution.py:507
  6.9 4.3 %collective-permute-start.6 = (bf16[256,1024]{1,0:T(8,128)(2,1)}, bf16[256,1024]{1,0:T(8,128)(2,1)}, u32[]{:S(2)}, u32[]{:S(2)}) collective-permute-start(bf16[256,1024]{1,0:T(8,128)(2,1)} %refs_0_.1), channel_id=1, source_target_pairs={{0,1},{1,2},{2,3},{4,5},{5,6},{6,7},{8,9},{9,10},{10,11},{12,13},{... | collective-permute-start | bytes 1572872 | tf_op jit(solution)/shard_map/ppermute | solution.py:628
  12.6 5.4 %collective-permute-done.1.refs_2_ = bf16[272,1024]{1,0:T(8,128)(2,1)S(1)} collective-permute-done((bf16[272,1024]{1,0:T(8,128)(2,1)S(1)}, bf16[272,1024]{1,0:T(8,128)(2,1)S(1)}, u32[]{:S(2)}, u32[]{:S(2)}) %collective-permute-start.1) | collective-permute-done | bytes 557088 | tf_op jit(solution)/shard_map/ppermute | solution.py:507
  18.1 1.8 %collective-permute-start.5 = (bf16[128,1024]{1,0:T(8,128)(2,1)S(1)}, bf16[128,1024]{1,0:T(8,128)(2,1)S(1)}, u32[]{:S(2)}, u32[]{:S(2)}) collective-permute-start(bf16[128,1024]{1,0:T(8,128)(2,1)S(1)} %slice.69), channel_id=1, source_target_pairs={{0,16},{4,20},{8,24},{12,28},{16,0},{20,4},{24,8},{28,12},{1,17},{... | collective-permute-start | bytes 786440 | tf_op jit(solution)/shard_map/ppermute | solution.py:507
  19.9 1.6 collective-permute-start.8
  21.5 4.8 %collective-permute-done.7.refs_4_ = bf16[256,1024]{1,0:T(8,128)(2,1)} collective-permute-done((bf16[256,1024]{1,0:T(8,128)(2,1)}, bf16[256,1024]{1,0:T(8,128)(2,1)}, u32[]{:S(2)}, u32[]{:S(2)}) %collective-permute-start.7) | collective-permute-done | bytes 524320 | tf_op jit(solution)/shard_map/ppermute | solution.py:629
  33.0 13.5 %forward.1 = (bf16[256,1152]{1,0:T(8,128)(2,1)}, bf16[256,1152]{1,0:T(8,128)(2,1)}, bf16[256,1152]{1,0:T(8,128)(2,1)}, bf16[256,1152]{1,0:T(8,128)(2,1)}, bf16[2...) custom-call(s32[1]{0:T(128)} %bitcast.me_ref, ...), custom_call_target="tpu_custom_call" | custom-call | tf_op jit(solution)/shard_map/forward/pallas_call | solution.py:672
  56.8 3.8 %collective-permute-done.18.refs_4_ = bf16[128,1152]{1,0:T(8,128)(2,1)S(1)} collective-permute-done((bf16[128,1152]{1,0:T(8,128)(2,1)S(1)}, bf16[128,1152]{1,0:T(8,128)(2,1)S(1)}, u32[]{:S(2)}, u32[]{:S(2)}) %collective-permute-start.18) | collective-permute-done | bytes 294944 | tf_op jit(solution)/shard_map/ppermute | solution.py:507
  64.6 1.8 collective-permute-done.24.refs_6_
  68.7 7.7 %grad.1 = (bf16[256,1024]{1,0:T(8,128)(2,1)}, bf16[8,256,512]{2,1,0:T(8,128)(2,1)}) custom-call(s32[1]{0:T(128)} %bitcast.4.line_ref, bf16[4096,1024]{1,0:T(8,128)(2,1)} %w_ref.1, bf16[256,1024]{1,0:T(8,128)(2,1)} %refs_0_.1, bf16[256,1024]{1,0:T(8,128)(2,1)} %collective-permute-done.6.refs_1_, bf16[256,1024]{1,0:T(8,128)(2,1)} %collective-permute-done.11.refs_2_, ...), custom_call_target="tpu_custom_call" | custom-call | tf_op jit(solution)/shard_map/grad/pallas_call | solution.py:722
  77.5 3.4 %finish.1 = (bf16[256,1024]{1,0:T(8,128)(2,1)}, bf16[128,1152]{1,0:T(8,128)(2,1)S(1)}, bf16[128,1152]{1,0:T(8,128)(2,1)S(1)}) custom-call(bf16[256,1152]{1,0:T(8,128)(2,1)S(1)} %copy-done.4, bf16[256,1152]{1,0:T(8,128)(2,1)S(1)} %collective-permute-done.13.refs_1_, bf16[128,1152]{1,0:T(8,128)(2,1)S(1)} %collective-permute-done.16.refs_2_, ...), custom_call_target="tpu_custom_call" | custom-call | tf_op jit(solution)/shard_map/finish/pallas_call | solution.py:724
  84.9 5.9 %collective-permute-done.27.refs_4_ = bf16[128,1152]{1,0:T(8,128)(2,1)S(1)} collective-permute-done((bf16[128,1152]{1,0:T(8,128)(2,1)S(1)}, bf16[128,1152]{1,0:T(8,128)(2,1)S(1)}, u32[]{:S(2)}, u32[]{:S(2)}) %collective-permute-start.27) | collective-permute-done | bytes 294944 | tf_op jit(solution)/shard_map/ppermute | solution.py:507
  93.0 5.6 %collective-permute-done.31.refs_8_ = bf16[128,1152]{1,0:T(8,128)(2,1)S(1)} collective-permute-done((bf16[128,1152]{1,0:T(8,128)(2,1)S(1)}, bf16[128,1152]{1,0:T(8,128)(2,1)S(1)}, u32[]{:S(2)}, u32[]{:S(2)}) %collective-permute-start.31) | collective-permute-done | bytes 294944 | tf_op jit(solution)/shard_map/ppermute | solution.py:507
  98.6 4.3 %collective-permute-done.35.refs_12_ = bf16[128,1152]{1,0:T(8,128)(2,1)S(1)} collective-permute-done((bf16[128,1152]{1,0:T(8,128)(2,1)S(1)}, bf16[128,1152]{1,0:T(8,128)(2,1)S(1)}, u32[]{:S(2)}, u32[]{:S(2)}) %collective-permute-start.35) | collective-permute-done | bytes 294944 | tf_op jit(solution)/shard_map/ppermute | solution.py:507
  104.4 3.8 %all-to-all-start = ((bf16[8,256,512]{2,1,0:T(8,128)(2,1)}), bf16[8,256,512]{2,1,0:T(8,128)(2,1)S(1)}, u32[]{:S(2)}, u32[]{:S(2)}) async-start(bf16[8,256,512]{2,1,0:T(8,128)(2,1)} %get-tuple-element.92), calls=%async_computation | async-start | bytes 4194304 | tf_op jit(solution)/shard_map/all_to_all | solution.py:736
  109.9 1.7 collective-permute-start.40
  116.4 18.7 %backward.1 = (bf16[256,1024]{1,0:T(8,128)(2,1)}, bf16[256,1024]{1,0:T(8,128)(2,1)}, bf16[256,1024]{1,0:T(8,128)(2,1)}, bf16[256,1024]{1,0:T(8,128)(2,1)}, bf16[...) custom-call(f32[16,8,128]{2,1,0:T(8,128)} %get-tuple-element.61.logi, ...), custom_call_target="tpu_custom_call" | custom-call | tf_op jit(solution)/shard_map/backward/pallas_call | solution.py:740
  135.1 9.7 %collective-permute-done.40.refs_4_ = bf16[256,1024]{1,0:T(8,128)(2,1)S(1)} collective-permute-done((bf16[256,1024]{1,0:T(8,128)(2,1)}, bf16[256,1024]{1,0:T(8,128)(2,1)S(1)}, u32[]{:S(2)}, u32[]{:S(2)}) %collective-permute-start.40) | collective-permute-done | bytes 524320 | tf_op jit(solution)/shard_map/ppermute | solution.py:507
  148.5 1.6 collective-permute-start.48
  150.8 6.3 %collective-permute-done.48 = bf16[128,1024]{1,0:T(8,128)(2,1)S(1)} collective-permute-done((bf16[128,1024]{1,0:T(8,128)(2,1)S(1)}, bf16[128,1024]{1,0:T(8,128)(2,1)S(1)}, u32[]{:S(2)}, u32[]{:S(2)}) %collective-permute-start.48) | collective-permute-done | bytes 262176 | tf_op jit(solution)/shard_map/ppermute | solution.py:507
  163.4 4.3 %collective-permute-done.43.refs_2_ = bf16[128,1024]{1,0:T(8,128)(2,1)S(1)} collective-permute-done((bf16[128,1024]{1,0:T(8,128)(2,1)S(1)}, bf16[128,1024]{1,0:T(8,128)(2,1)S(1)}, u32[]{:S(2)}, u32[]{:S(2)}) %collective-permute-start.43) | collective-permute-done | bytes 262176 | tf_op jit(solution)/shard_map/ppermute | solution.py:507
  168.5 4.8 %collective-permute-done.55.refs_1_ = bf16[128,1024]{1,0:T(8,128)(2,1)S(1)} collective-permute-done((bf16[128,1024]{1,0:T(8,128)(2,1)S(1)}, bf16[128,1024]{1,0:T(8,128)(2,1)S(1)}, u32[]{:S(2)}, u32[]{:S(2)}) %collective-permute-start.55) | collective-permute-done | bytes 262176 | tf_op jit(solution)/shard_map/ppermute | solution.py:507
  173.4 2.9 %weight.2.refs_4_ = f32[512,1024]{1,0:T(8,128)S(1)} custom-call(s32[1]{0:T(128)} %bitcast.me_ref, bf16[8,256,512]{2,1,0:T(8,128)(2,1)S(1)} %all-to-all-done.cols_ref, bf16[256,1024]{1,0:T(8,128)(2,1)} %get-tuple-element.94.refs_0_, bf16[256,1024]{1,0:T(8,128)(2,1)S(1)} %collective-permute-done.44.refs_1_, ...), custom_call_target="tpu_custom_call" | custom-call | tf_op jit(solution)/shard_map/weight/pallas_call | solution.py:772
  180.0 2.1 %weight.3 = f32[512,1024]{1,0:T(8,128)} custom-call(s32[1]{0:T(128)} %bitcast.me_ref, bf16[8,256,512]{2,1,0:T(8,128)(2,1)S(1)} %all-to-all-done.cols_ref, bf16[128,1024]{1,0:T(8,128)(2,1)S(1)} %collective-permute-done.54.refs_0_, bf16[128,1024]{1,0:T(8,128)(2,1)S(1)} %collective-permute-done.55.refs_1_, ...), custom_call_target="tpu_custom_call" | custom-call | tf_op jit(solution)/shard_map/weight/pallas_call | solution.py:772
  (190 shorter events, 58.2 us)
Async XLA Ops:
  2.4 15.6 %collective-permute-start.1 = (bf16[272,1024]{1,0:T(8,128)(2,1)S(1)}, bf16[272,1024]{1,0:T(8,128)(2,1)S(1)}, u32[]{:S(2)}, u32[]{:S(2)}) collective-permute-start(bf16[272,1024]{1,0:T(8,128)(2,1)S(1)} %pack.1.refs_0_), channel_id=1, source_target_pairs={{0,8},{4,12},{8,0},{12,4},{16,24},{20,28},{24,16},{28,20},{1,9},{5... | collective-permute-start | bytes 1671176 | tf_op jit(solution)/shard_map/ppermute | solution.py:507
  5.4 14.5 %collective-permute-start.3 = (bf16[272,1024]{1,0:T(8,128)(2,1)S(1)}, bf16[272,1024]{1,0:T(8,128)(2,1)S(1)}, u32[]{:S(2)}, u32[]{:S(2)}) collective-permute-start(bf16[272,1024]{1,0:T(8,128)(2,1)S(1)} %pack.1.refs_0_), channel_id=1, source_target_pairs={{0,16},{4,20},{8,24},{12,28},{16,0},{20,4},{24,8},{28,12},{1,17},{... | collective-permute-start | bytes 1671176 | tf_op jit(solution)/shard_map/ppermute | solution.py:507
  6.9 14.6 %collective-permute-start.6 = (bf16[256,1024]{1,0:T(8,128)(2,1)}, bf16[256,1024]{1,0:T(8,128)(2,1)}, u32[]{:S(2)}, u32[]{:S(2)}) collective-permute-start(bf16[256,1024]{1,0:T(8,128)(2,1)} %refs_0_.1), channel_id=1, source_target_pairs={{0,1},{1,2},{2,3},{4,5},{5,6},{6,7},{8,9},{9,10},{10,11},{12,13},{... | collective-permute-start | bytes 1572872 | tf_op jit(solution)/shard_map/ppermute | solution.py:628
  11.2 15.0 %collective-permute-start.7 = (bf16[256,1024]{1,0:T(8,128)(2,1)}, bf16[256,1024]{1,0:T(8,128)(2,1)}, u32[]{:S(2)}, u32[]{:S(2)}) collective-permute-start(bf16[256,1024]{1,0:T(8,128)(2,1)} %refs_0_.1), channel_id=1, source_target_pairs={{1,0},{2,1},{3,2},{5,4},{6,5},{7,6},{9,8},{10,9},{11,10},{13,12},{... | collective-permute-start | bytes 1572872 | tf_op jit(solution)/shard_map/ppermute | solution.py:629
  12.5 14.3 %collective-permute-start = (bf16[272,1024]{1,0:T(8,128)(2,1)S(1)}, bf16[272,1024]{1,0:T(8,128)(2,1)S(1)}, u32[]{:S(2)}, u32[]{:S(2)}) collective-permute-start(bf16[272,1024]{1,0:T(8,128)(2,1)S(1)} %pack.1.refs_0_), channel_id=1, source_target_pairs={{0,4},{4,0},{8,12},{12,8},{16,20},{20,16},{24,28},{28,24},{1,5},{5... | collective-permute-start | bytes 1671176 | tf_op jit(solution)/shard_map/ppermute | solution.py:507
  26.8 19.7 %collective-permute-start.11 = (bf16[256,1024]{1,0:T(8,128)(2,1)}, bf16[256,1024]{1,0:T(8,128)(2,1)}, u32[]{:S(2)}, u32[]{:S(2)}) collective-permute-start(bf16[256,1024]{1,0:T(8,128)(2,1)} %collective-permute-done.6.refs_1_), channel_id=1, source_target_pairs={{1,2},{2,3},{5,6},{6,7},{9,10},{10,11},{13,14},{14,15},{17,18},{18... | collective-permute-start | bytes 1572872 | tf_op jit(solution)/shard_map/ppermute | solution.py:628
  28.3 18.3 %collective-permute-start.12 = (bf16[256,1024]{1,0:T(8,128)(2,1)}, bf16[256,1024]{1,0:T(8,128)(2,1)}, u32[]{:S(2)}, u32[]{:S(2)}) collective-permute-start(bf16[256,1024]{1,0:T(8,128)(2,1)} %collective-permute-done.7.refs_4_), channel_id=1, source_target_pairs={{1,0},{2,1},{5,4},{6,5},{9,8},{10,9},{13,12},{14,13},{17,16},{18,1... | collective-permute-start | bytes 1572872 | tf_op jit(solution)/shard_map/ppermute | solution.py:629
  47.6 16.4 %collective-permute-start.23 = (bf16[256,1024]{1,0:T(8,128)(2,1)}, bf16[256,1024]{1,0:T(8,128)(2,1)S(1)}, u32[]{:S(2)}, u32[]{:S(2)}) collective-permute-start(bf16[256,1024]{1,0:T(8,128)(2,1)} %collective-permute-done.11.refs_2_), channel_id=1, source_target_pairs={{2,3},{6,7},{10,11},{14,15},{18,19},{22,23},{26,27},{30,31}} | collective-permute-start | bytes 1572872 | tf_op jit(solution)/shard_map/ppermute | solution.py:628
  48.3 18.1 %collective-permute-start.24 = (bf16[256,1024]{1,0:T(8,128)(2,1)}, bf16[256,1024]{1,0:T(8,128)(2,1)S(1)}, u32[]{:S(2)}, u32[]{:S(2)}) collective-permute-start(bf16[256,1024]{1,0:T(8,128)(2,1)} %collective-permute-done.12.refs_5_), channel_id=1, source_target_pairs={{1,0},{5,4},{9,8},{13,12},{17,16},{21,20},{25,24},{29,28}} | collective-permute-start | bytes 1572872 | tf_op jit(solution)/shard_map/ppermute | solution.py:629
  54.0 22.4 %collective-permute-start.13 = (bf16[256,1152]{1,0:T(8,128)(2,1)}, bf16[256,1152]{1,0:T(8,128)(2,1)S(1)}, u32[]{:S(2)}, u32[]{:S(2)}) collective-permute-start(bf16[256,1152]{1,0:T(8,128)(2,1)} %get-tuple-element.67), channel_id=1, source_target_pairs={{0,4},{4,0},{8,12},{12,8},{16,20},{20,16},{24,28},{28,24},{1,5},{5... | collective-permute-start | bytes 1769480 | tf_op jit(solution)/shard_map/ppermute | solution.py:507
  60.6 15.8 %collective-permute-start.16 = (bf16[128,1152]{1,0:T(8,128)(2,1)S(1)}, bf16[128,1152]{1,0:T(8,128)(2,1)S(1)}, u32[]{:S(2)}, u32[]{:S(2)}) collective-permute-start(bf16[128,1152]{1,0:T(8,128)(2,1)S(1)} %get-tuple-element.74), channel_id=1, source_target_pairs={{0,8},{4,12},{8,0},{12,4},{16,24},{20,28},{24,16},{28,20},{1,9},{5... | collective-permute-start | bytes 884744 | tf_op jit(solution)/shard_map/ppermute | solution.py:507
  61.6 14.8 %collective-permute-start.22 = (bf16[128,1152]{1,0:T(8,128)(2,1)S(1)}, bf16[128,1152]{1,0:T(8,128)(2,1)S(1)}, u32[]{:S(2)}, u32[]{:S(2)}) collective-permute-start(bf16[128,1152]{1,0:T(8,128)(2,1)S(1)} %get-tuple-element.82), channel_id=1, source_target_pairs={{0,16},{4,20},{8,24},{12,28},{16,0},{20,4},{24,8},{28,12},{1,17},{... | collective-permute-start | bytes 884744 | tf_op jit(solution)/shard_map/ppermute | solution.py:507
  64.0 12.4 %collective-permute-start.20 = (bf16[128,1152]{1,0:T(8,128)(2,1)S(1)}, bf16[128,1152]{1,0:T(8,128)(2,1)S(1)}, u32[]{:S(2)}, u32[]{:S(2)}) collective-permute-start(bf16[128,1152]{1,0:T(8,128)(2,1)S(1)} %get-tuple-element.80), channel_id=1, source_target_pairs={{0,8},{4,12},{8,0},{12,4},{16,24},{20,28},{24,16},{28,20},{1,9},{5... | collective-permute-start | bytes 884744 | tf_op jit(solution)/shard_map/ppermute | solution.py:507
  83.1 15.5 %collective-permute-start.31 = (bf16[128,1152]{1,0:T(8,128)(2,1)S(1)}, bf16[128,1152]{1,0:T(8,128)(2,1)S(1)}, u32[]{:S(2)}, u32[]{:S(2)}) collective-permute-start(bf16[128,1152]{1,0:T(8,128)(2,1)S(1)} %get-tuple-element.85.refs_0_), channel_id=1, source_target_pairs={{0,16},{4,20},{8,24},{12,28},{16,0},{20,4},{24,8},{28,12},{1,17},{... | collective-permute-start | bytes 884744 | tf_op jit(solution)/shard_map/ppermute | solution.py:507
  84.4 14.2 %collective-permute-start.28 = (bf16[128,1152]{1,0:T(8,128)(2,1)S(1)}, bf16[128,1152]{1,0:T(8,128)(2,1)S(1)}, u32[]{:S(2)}, u32[]{:S(2)}) collective-permute-start(bf16[128,1152]{1,0:T(8,128)(2,1)S(1)} %get-tuple-element.86.refs_1_), channel_id=1, source_target_pairs={{0,8},{4,12},{8,0},{12,4},{16,24},{20,28},{24,16},{28,20},{1,9},{5... | collective-permute-start | bytes 884744 | tf_op jit(solution)/shard_map/ppermute | solution.py:507
  104.4 40.5 %all-to-all-start = ((bf16[8,256,512]{2,1,0:T(8,128)(2,1)}), bf16[8,256,512]{2,1,0:T(8,128)(2,1)S(1)}, u32[]{:S(2)}, u32[]{:S(2)}) async-start(bf16[8,256,512]{2,1,0:T(8,128)(2,1)} %get-tuple-element.92), calls=%async_computation | async-start | bytes 4194304 | tf_op jit(solution)/shard_map/all_to_all | solution.py:736
  109.9 35.0 %collective-permute-start.40 = (bf16[256,1024]{1,0:T(8,128)(2,1)}, bf16[256,1024]{1,0:T(8,128)(2,1)S(1)}, u32[]{:S(2)}, u32[]{:S(2)}) collective-permute-start(bf16[256,1024]{1,0:T(8,128)(2,1)} %get-tuple-element.94.refs_0_), channel_id=1, source_target_pairs={{0,16},{4,20},{8,24},{12,28},{16,0},{20,4},{24,8},{28,12},{1,17},{... | collective-permute-start | bytes 1572872 | tf_op jit(solution)/shard_map/ppermute | solution.py:507
  111.5 33.4 %collective-permute-start.39 = (bf16[256,1024]{1,0:T(8,128)(2,1)}, bf16[256,1024]{1,0:T(8,128)(2,1)S(1)}, u32[]{:S(2)}, u32[]{:S(2)}) collective-permute-start(bf16[256,1024]{1,0:T(8,128)(2,1)} %get-tuple-element.94.refs_0_), channel_id=1, source_target_pairs={{0,8},{4,12},{8,0},{12,4},{16,24},{20,28},{24,16},{28,20},{1,9},{5... | collective-permute-start | bytes 1572872 | tf_op jit(solution)/shard_map/ppermute | solution.py:507
  145.6 13.7 %collective-permute-start.44 = (bf16[256,1024]{1,0:T(8,128)(2,1)}, bf16[256,1024]{1,0:T(8,128)(2,1)S(1)}, u32[]{:S(2)}, u32[]{:S(2)}) collective-permute-start(bf16[256,1024]{1,0:T(8,128)(2,1)} %get-tuple-element.94.refs_0_), channel_id=1, source_target_pairs={{0,4},{4,0},{8,12},{12,8},{16,20},{20,16},{24,28},{28,24},{1,5},{5... | collective-permute-start | bytes 1572872 | tf_op jit(solution)/shard_map/ppermute | solution.py:507
  146.0 14.6 %collective-permute-start.46 = (bf16[256,1024]{1,0:T(8,128)(2,1)S(1)}, bf16[256,1024]{1,0:T(8,128)(2,1)S(1)}, u32[]{:S(2)}, u32[]{:S(2)}) collective-permute-start(bf16[256,1024]{1,0:T(8,128)(2,1)S(1)} %collective-permute-done.40.refs_4_), channel_id=1, source_target_pairs={{0,4},{4,0},{8,12},{12,8},{16,20},{20,16},{24,28},{28,24},{1,5},{5... | collective-permute-start | bytes 1572872 | tf_op jit(solution)/shard_map/ppermute | solution.py:507
  147.1 14.3 %collective-permute-start.45 = (bf16[256,1024]{1,0:T(8,128)(2,1)S(1)}, bf16[256,1024]{1,0:T(8,128)(2,1)S(1)}, u32[]{:S(2)}, u32[]{:S(2)}) collective-permute-start(bf16[256,1024]{1,0:T(8,128)(2,1)S(1)} %collective-permute-done.39.refs_2_), channel_id=1, source_target_pairs={{0,4},{4,0},{8,12},{12,8},{16,20},{20,16},{24,28},{28,24},{1,5},{5... | collective-permute-start | bytes 1572872 | tf_op jit(solution)/shard_map/ppermute | solution.py:507
  160.6 12.7 %collective-permute-start.55 = (bf16[128,1024]{1,0:T(8,128)(2,1)S(1)}, bf16[128,1024]{1,0:T(8,128)(2,1)S(1)}, u32[]{:S(2)}, u32[]{:S(2)}) collective-permute-start(bf16[128,1024]{1,0:T(8,128)(2,1)S(1)} %slice.78), channel_id=1, source_target_pairs={{0,8},{4,12},{8,0},{12,4},{16,24},{20,28},{24,16},{28,20},{1,9},{5... | collective-permute-start | bytes 786440 | tf_op jit(solution)/shard_map/ppermute | solution.py:507
  161.4 14.8 %collective-permute-start.53 = (bf16[128,1024]{1,0:T(8,128)(2,1)S(1)}, bf16[128,1024]{1,0:T(8,128)(2,1)S(1)}, u32[]{:S(2)}, u32[]{:S(2)}) collective-permute-start(bf16[128,1024]{1,0:T(8,128)(2,1)S(1)} %add_convert_fusion.1), channel_id=1, source_target_pairs={{0,16},{4,20},{8,24},{12,28},{16,0},{20,4},{24,8},{28,12},{1,17},{... | collective-permute-start | bytes 786440 | tf_op jit(solution)/shard_map/ppermute | solution.py:507
  162.8 14.5 %collective-permute-start.49 = (bf16[128,1024]{1,0:T(8,128)(2,1)S(1)}, bf16[128,1024]{1,0:T(8,128)(2,1)S(1)}, u32[]{:S(2)}, u32[]{:S(2)}) collective-permute-start(bf16[128,1024]{1,0:T(8,128)(2,1)S(1)} %add_convert_fusion.2), channel_id=1, source_target_pairs={{0,8},{4,12},{8,0},{12,4},{16,24},{20,28},{24,16},{28,20},{1,9},{5... | collective-permute-start | bytes 786440 | tf_op jit(solution)/shard_map/ppermute | solution.py:507
  (72 other events, 465.7 us)

commit v13 on v12

--- a/solution.py
+++ b/solution.py
@@ -625,8 +625,16 @@
     lines = lax.axis_size("head")
     ups, downs = [x], [x]
     for d in range(1, lines):
-        ups.append(lax.ppermute(ups[-1], "head", [(i, i + 1) for i in range(d - 1, lines - 1)]))
-        downs.append(lax.ppermute(downs[-1], "head", [(i, i - 1) for i in range(1, lines - d + 1)]))
+        up = [(i, i + 1) for i in range(d - 1, lines - 1)]
+        down = [(i, i - 1) for i in range(1, lines - d + 1)]
+        if d == lines - 1 and lines > 2:
+            last = jnp.where(lax.axis_index("head") == lines - 2, ups[-1], downs[-1])
+            last = lax.ppermute(last, "head", up + down)
+            ups.append(last)
+            downs.append(last)
+        else:
+            ups.append(lax.ppermute(ups[-1], "head", up))
+            downs.append(lax.ppermute(downs[-1], "head", down))
     return ups[1:], downs[1:]
 
 
@@ -732,7 +740,7 @@
     grad_chips = spread_halves(*extended)
     grad_all = with_cores(grad_chips)
     arrived = flat(grad_chips[1:])
-    attns = spread_near(after(attn_out, *arrived))
+    attns = spread_near(after(attn_out, *flat(grad_chips[1:3])))
     columns = lax.all_to_all(
         after(blocks, *arrived), "ctx", split_axis=0, concat_axis=0, tiled=True
     )
@@ -766,7 +774,8 @@
     key_grad, value_grad = outs[chunks:]
     received = from_core(outs[:chunks], columns, *flat(attns[1:3]))
     terms, last_sums = collect_chips(outs[:chunks], received)
-    attns = with_cores(spread_far(attns, rows // 2, *last_sums))
+    near = [[after(x, *last_sums) for x in pieces] for pieces in attns]
+    attns = with_cores(spread_far(near, rows // 2, terms[2][0], terms[-1][-1]))
 
     def weight_part(chosen, first, when, *before):
         return pl.pallas_call(

time: 184 us -> 185 us (level)
  local copies, waits for them, and re-layouts: 12.2 us -> 8.53 us
  waiting for transfers between devices: 64.8 us -> 67.9 us
    ppermute x52, waiting for transfers between devices: 58.3 us -> 62.3 us  [swap(): return lax.ppermute(x, 'ctx', [(i, i ^ bits) for i in range(count)])]
    unnamed x75 -> x71, local copies, waits for them, and re-layouts: 11.1 us -> 7.43 us
    ppermute x52, starting transfers between devices: 36.1 us -> 38.4 us  [swap(): return lax.ppermute(x, 'ctx', [(i, i ^ bits) for i in range(count)])]
    ppermute x6 -> x5, starting transfers between devices: 10.5 us -> 9.01 us  [the longest x2 4.98 us: spread_line(): ups.append(lax.ppermute(ups[-1], 'head', up))]
    ppermute x6 -> x5, waiting for transfers between devices: 6.54 us -> 5.61 us  [the longest x2 4.77 us: spread_line(): downs.append(lax.ppermute(downs[-1], 'head', down))]
  transfers between devices with their start and end apart: 59 -> 58, of which waited for: 23 -> 26; matrix products, arithmetic and copies ran while one was open for 2% -> 2% of each run, Pallas kernels for 25% -> 25%
where the time goes in v13:
time: 185 us; the launch traced here: 183 us
  waiting for transfers between devices  67.9 us (37%)
  Pallas kernels  51.9 us (28%)
  starting transfers between devices  51.2 us (28%)
  local copies, waits for them, and re-layouts  8.53 us (5%)
  other arithmetic  2.61 us (1%)
    ppermute x52, waiting for transfers between devices, swap(): return lax.ppermute(x, 'ctx', [(i, i ^ bits) for i in range(count)])  62.3 us
    ppermute x52, starting transfers between devices, swap(): return lax.ppermute(x, 'ctx', [(i, i ^ bits) for i in range(count)])  38.4 us
    pallas_call x1, Pallas kernels, body(): pl.pallas_call(functools.partial(backward_kernel, [len(pieces) for pieces...  18.7 us
    pallas_call x1, Pallas kernels, body(): pl.pallas_call(functools.partial(forward_kernel, [len(pieces) for pieces...  13.5 us
    pallas_call x1, Pallas kernels, body(): make_grad(after(line, *before), out_weight, out_grad, *ups, *downs)  7.67 us
    unnamed x71, local copies, waits for them, and re-layouts  7.43 us
    ppermute x2, starting transfers between devices, spread_line(): ups.append(lax.ppermute(ups[-1], 'head', up))  4.98 us
    pallas_call x2, Pallas kernels, weight_part(): pl.pallas_call(functools.partial(weight_kernel, [len(pieces) for pieces i...  4.91 us
  transfers between devices with their start and end apart: 58, of which 26 were waited for; matrix products, arithmetic and copies ran while one was open for 2% of the time, Pallas kernels for 25%

profile of v13, /device:TPU:0, one launch (start us, length us, event | category | flops | bytes accessed | tf_op | source)
XLA Modules:
  0.0 183.2 jit_solution(12057884605281158559)
XLA Ops:
  2.4 3.0 %collective-permute-start.1 = (bf16[272,1024]{1,0:T(8,128)(2,1)S(1)}, bf16[272,1024]{1,0:T(8,128)(2,1)S(1)}, u32[]{:S(2)}, u32[]{:S(2)}) collective-permute-start(bf16[272,1024]{1,0:T(8,128)(2,1)S(1)} %pack.1.refs_0_), channel_id=1, source_target_pairs={{0,8},{4,12},{8,0},{12,4},{16,24},{20,28},{24,16},{28,20},{1,9},{5... | collective-permute-start | bytes 1671176 | tf_op jit(solution)/shard_map/ppermute | solution.py:507
  6.9 4.3 %collective-permute-start.6 = (bf16[256,1024]{1,0:T(8,128)(2,1)}, bf16[256,1024]{1,0:T(8,128)(2,1)}, u32[]{:S(2)}, u32[]{:S(2)}) collective-permute-start(bf16[256,1024]{1,0:T(8,128)(2,1)} %refs_0_.1), channel_id=1, source_target_pairs={{0,1},{1,2},{2,3},{4,5},{5,6},{6,7},{8,9},{9,10},{10,11},{12,13},{... | collective-permute-start | bytes 1572872 | tf_op jit(solution)/shard_map/ppermute | solution.py:636
  12.6 5.4 %collective-permute-done.1.refs_2_ = bf16[272,1024]{1,0:T(8,128)(2,1)S(1)} collective-permute-done((bf16[272,1024]{1,0:T(8,128)(2,1)S(1)}, bf16[272,1024]{1,0:T(8,128)(2,1)S(1)}, u32[]{:S(2)}, u32[]{:S(2)}) %collective-permute-start.1) | collective-permute-done | bytes 557088 | tf_op jit(solution)/shard_map/ppermute | solution.py:507
  18.1 1.8 %collective-permute-start.5 = (bf16[128,1024]{1,0:T(8,128)(2,1)S(1)}, bf16[128,1024]{1,0:T(8,128)(2,1)S(1)}, u32[]{:S(2)}, u32[]{:S(2)}) collective-permute-start(bf16[128,1024]{1,0:T(8,128)(2,1)S(1)} %slice.69), channel_id=1, source_target_pairs={{0,16},{4,20},{8,24},{12,28},{16,0},{20,4},{24,8},{28,12},{1,17},{... | collective-permute-start | bytes 786440 | tf_op jit(solution)/shard_map/ppermute | solution.py:507
  21.5 4.8 %collective-permute-done.7.refs_4_ = bf16[256,1024]{1,0:T(8,128)(2,1)} collective-permute-done((bf16[256,1024]{1,0:T(8,128)(2,1)}, bf16[256,1024]{1,0:T(8,128)(2,1)}, u32[]{:S(2)}, u32[]{:S(2)}) %collective-permute-start.7) | collective-permute-done | bytes 524320 | tf_op jit(solution)/shard_map/ppermute | solution.py:637
  31.8 13.5 %forward.1 = (bf16[256,1152]{1,0:T(8,128)(2,1)}, bf16[256,1152]{1,0:T(8,128)(2,1)}, bf16[256,1152]{1,0:T(8,128)(2,1)}, bf16[256,1152]{1,0:T(8,128)(2,1)}, bf16[2...) custom-call(s32[1]{0:T(128)} %bitcast.me_ref, ...), custom_call_target="tpu_custom_call" | custom-call | tf_op jit(solution)/shard_map/forward/pallas_call | solution.py:680
  53.7 5.1 %collective-permute-done.18.refs_4_ = bf16[128,1152]{1,0:T(8,128)(2,1)S(1)} collective-permute-done((bf16[128,1152]{1,0:T(8,128)(2,1)S(1)}, bf16[128,1152]{1,0:T(8,128)(2,1)S(1)}, u32[]{:S(2)}, u32[]{:S(2)}) %collective-permute-start.18) | collective-permute-done | bytes 294944 | tf_op jit(solution)/shard_map/ppermute | solution.py:507
  61.7 1.6 collective-permute-start.20
  65.6 7.7 %grad.1 = (bf16[256,1024]{1,0:T(8,128)(2,1)}, bf16[8,256,512]{2,1,0:T(8,128)(2,1)}) custom-call(s32[1]{0:T(128)} %bitcast.4.line_ref, bf16[4096,1024]{1,0:T(8,128)(2,1)} %w_ref.1, bf16[256,1024]{1,0:T(8,128)(2,1)} %refs_0_.1, bf16[256,1024]{1,0:T(8,128)(2,1)} %collective-permute-done.6.refs_1_, bf16[256,1024]{1,0:T(8,128)(2,1)} %copy-done.12, ...), custom_call_target="tpu_custom_call" | custom-call | tf_op jit(solution)/shard_map/grad/pallas_call | solution.py:730
  74.6 3.4 %finish.1 = (bf16[256,1024]{1,0:T(8,128)(2,1)}, bf16[128,1152]{1,0:T(8,128)(2,1)S(1)}, bf16[128,1152]{1,0:T(8,128)(2,1)S(1)}) custom-call(bf16[256,1152]{1,0:T(8,128)(2,1)S(1)} %copy-done.4, bf16[256,1152]{1,0:T(8,128)(2,1)S(1)} %collective-permute-done.13.refs_1_, bf16[128,1152]{1,0:T(8,128)(2,1)S(1)} %collective-permute-done.16.refs_2_, ...), custom_call_target="tpu_custom_call" | custom-call | tf_op jit(solution)/shard_map/finish/pallas_call | solution.py:732
  82.0 5.9 %collective-permute-done.26.refs_4_ = bf16[128,1152]{1,0:T(8,128)(2,1)S(1)} collective-permute-done((bf16[128,1152]{1,0:T(8,128)(2,1)S(1)}, bf16[128,1152]{1,0:T(8,128)(2,1)S(1)}, u32[]{:S(2)}, u32[]{:S(2)}) %collective-permute-start.26) | collective-permute-done | bytes 294944 | tf_op jit(solution)/shard_map/ppermute | solution.py:507
  90.6 5.1 %collective-permute-done.30.refs_8_ = bf16[128,1152]{1,0:T(8,128)(2,1)S(1)} collective-permute-done((bf16[128,1152]{1,0:T(8,128)(2,1)S(1)}, bf16[128,1152]{1,0:T(8,128)(2,1)S(1)}, u32[]{:S(2)}, u32[]{:S(2)}) %collective-permute-start.30) | collective-permute-done | bytes 294944 | tf_op jit(solution)/shard_map/ppermute | solution.py:507
  95.7 4.5 %collective-permute-done.34.refs_12_ = bf16[128,1152]{1,0:T(8,128)(2,1)S(1)} collective-permute-done((bf16[128,1152]{1,0:T(8,128)(2,1)S(1)}, bf16[128,1152]{1,0:T(8,128)(2,1)S(1)}, u32[]{:S(2)}, u32[]{:S(2)}) %collective-permute-start.34) | collective-permute-done | bytes 294944 | tf_op jit(solution)/shard_map/ppermute | solution.py:507
  101.6 3.8 %all-to-all-start = ((bf16[8,256,512]{2,1,0:T(8,128)(2,1)}), bf16[8,256,512]{2,1,0:T(8,128)(2,1)S(1)}, u32[]{:S(2)}, u32[]{:S(2)}) async-start(bf16[8,256,512]{2,1,0:T(8,128)(2,1)} %get-tuple-element.95), calls=%async_computation | async-start | bytes 4194304 | tf_op jit(solution)/shard_map/all_to_all | solution.py:744
  107.1 1.7 collective-permute-start.39
  113.6 18.7 %backward.1 = (bf16[256,1024]{1,0:T(8,128)(2,1)}, bf16[256,1024]{1,0:T(8,128)(2,1)}, bf16[256,1024]{1,0:T(8,128)(2,1)}, bf16[256,1024]{1,0:T(8,128)(2,1)}, bf16[...) custom-call(f32[16,8,128]{2,1,0:T(8,128)} %get-tuple-element.64.logi, ...), custom_call_target="tpu_custom_call" | custom-call | tf_op jit(solution)/shard_map/backward/pallas_call | solution.py:748
  132.4 9.7 %collective-permute-done.39.refs_4_ = bf16[256,1024]{1,0:T(8,128)(2,1)S(1)} collective-permute-done((bf16[256,1024]{1,0:T(8,128)(2,1)}, bf16[256,1024]{1,0:T(8,128)(2,1)S(1)}, u32[]{:S(2)}, u32[]{:S(2)}) %collective-permute-start.39) | collective-permute-done | bytes 524320 | tf_op jit(solution)/shard_map/ppermute | solution.py:507
  150.9 5.3 %collective-permute-done.43 = bf16[128,1024]{1,0:T(8,128)(2,1)S(1)} collective-permute-done((bf16[128,1024]{1,0:T(8,128)(2,1)S(1)}, bf16[128,1024]{1,0:T(8,128)(2,1)S(1)}, u32[]{:S(2)}, u32[]{:S(2)}) %collective-permute-start.43) | collective-permute-done | bytes 262176 | tf_op jit(solution)/shard_map/ppermute | solution.py:507
  156.5 3.1 %collective-permute-done.42.refs_2_ = bf16[128,1024]{1,0:T(8,128)(2,1)S(1)} collective-permute-done((bf16[128,1024]{1,0:T(8,128)(2,1)S(1)}, bf16[128,1024]{1,0:T(8,128)(2,1)S(1)}, u32[]{:S(2)}, u32[]{:S(2)}) %collective-permute-start.42) | collective-permute-done | bytes 262176 | tf_op jit(solution)/shard_map/ppermute | solution.py:507
  163.5 4.5 %collective-permute-done.53.refs_0_ = bf16[128,1024]{1,0:T(8,128)(2,1)S(1)} collective-permute-done((bf16[128,1024]{1,0:T(8,128)(2,1)S(1)}, bf16[128,1024]{1,0:T(8,128)(2,1)S(1)}, u32[]{:S(2)}, u32[]{:S(2)}) %collective-permute-start.53) | collective-permute-done | bytes 262176 | tf_op jit(solution)/shard_map/ppermute | solution.py:507
  167.9 2.8 %collective-permute-done.54.refs_1_ = bf16[128,1024]{1,0:T(8,128)(2,1)S(1)} collective-permute-done((bf16[128,1024]{1,0:T(8,128)(2,1)S(1)}, bf16[128,1024]{1,0:T(8,128)(2,1)S(1)}, u32[]{:S(2)}, u32[]{:S(2)}) %collective-permute-start.54) | collective-permute-done | bytes 262176 | tf_op jit(solution)/shard_map/ppermute | solution.py:507
  173.2 2.9 %weight.2.refs_4_ = f32[512,1024]{1,0:T(8,128)S(1)} custom-call(s32[1]{0:T(128)} %bitcast.me_ref, bf16[8,256,512]{2,1,0:T(8,128)(2,1)S(1)} %all-to-all-done.cols_ref, bf16[256,1024]{1,0:T(8,128)(2,1)} %get-tuple-element.109.refs_0_, bf16[256,1024]{1,0:T(8,128)(2,1)S(1)} %collective-permute-done.46.refs_1_, ...), custom_call_target="tpu_custom_call" | custom-call | tf_op jit(solution)/shard_map/weight/pallas_call | solution.py:781
  176.1 2.5 %collective-permute-done.50.refs_3_ = bf16[128,1024]{1,0:T(8,128)(2,1)S(1)} collective-permute-done((bf16[128,1024]{1,0:T(8,128)(2,1)S(1)}, bf16[128,1024]{1,0:T(8,128)(2,1)S(1)}, u32[]{:S(2)}, u32[]{:S(2)}) %collective-permute-start.50) | collective-permute-done | bytes 262176 | tf_op jit(solution)/shard_map/ppermute | solution.py:507
  181.2 2.1 %weight.3 = f32[512,1024]{1,0:T(8,128)} custom-call(s32[1]{0:T(128)} %bitcast.me_ref, bf16[8,256,512]{2,1,0:T(8,128)(2,1)S(1)} %all-to-all-done.cols_ref, bf16[128,1024]{1,0:T(8,128)(2,1)S(1)} %collective-permute-done.53.refs_0_, bf16[128,1024]{1,0:T(8,128)(2,1)S(1)} %collective-permute-done.54.refs_1_, ...), custom_call_target="tpu_custom_call" | custom-call | tf_op jit(solution)/shard_map/weight/pallas_call | solution.py:781
  (185 shorter events, 59.0 us)
Async XLA Ops:
  2.4 15.6 %collective-permute-start.1 = (bf16[272,1024]{1,0:T(8,128)(2,1)S(1)}, bf16[272,1024]{1,0:T(8,128)(2,1)S(1)}, u32[]{:S(2)}, u32[]{:S(2)}) collective-permute-start(bf16[272,1024]{1,0:T(8,128)(2,1)S(1)} %pack.1.refs_0_), channel_id=1, source_target_pairs={{0,8},{4,12},{8,0},{12,4},{16,24},{20,28},{24,16},{28,20},{1,9},{5... | collective-permute-start | bytes 1671176 | tf_op jit(solution)/shard_map/ppermute | solution.py:507
  5.4 14.5 %collective-permute-start.3 = (bf16[272,1024]{1,0:T(8,128)(2,1)S(1)}, bf16[272,1024]{1,0:T(8,128)(2,1)S(1)}, u32[]{:S(2)}, u32[]{:S(2)}) collective-permute-start(bf16[272,1024]{1,0:T(8,128)(2,1)S(1)} %pack.1.refs_0_), channel_id=1, source_target_pairs={{0,16},{4,20},{8,24},{12,28},{16,0},{20,4},{24,8},{28,12},{1,17},{... | collective-permute-start | bytes 1671176 | tf_op jit(solution)/shard_map/ppermute | solution.py:507
  6.9 14.6 %collective-permute-start.6 = (bf16[256,1024]{1,0:T(8,128)(2,1)}, bf16[256,1024]{1,0:T(8,128)(2,1)}, u32[]{:S(2)}, u32[]{:S(2)}) collective-permute-start(bf16[256,1024]{1,0:T(8,128)(2,1)} %refs_0_.1), channel_id=1, source_target_pairs={{0,1},{1,2},{2,3},{4,5},{5,6},{6,7},{8,9},{9,10},{10,11},{12,13},{... | collective-permute-start | bytes 1572872 | tf_op jit(solution)/shard_map/ppermute | solution.py:636
  11.2 15.0 %collective-permute-start.7 = (bf16[256,1024]{1,0:T(8,128)(2,1)}, bf16[256,1024]{1,0:T(8,128)(2,1)}, u32[]{:S(2)}, u32[]{:S(2)}) collective-permute-start(bf16[256,1024]{1,0:T(8,128)(2,1)} %refs_0_.1), channel_id=1, source_target_pairs={{1,0},{2,1},{3,2},{5,4},{6,5},{7,6},{9,8},{10,9},{11,10},{13,12},{... | collective-permute-start | bytes 1572872 | tf_op jit(solution)/shard_map/ppermute | solution.py:637
  12.5 14.3 %collective-permute-start = (bf16[272,1024]{1,0:T(8,128)(2,1)S(1)}, bf16[272,1024]{1,0:T(8,128)(2,1)S(1)}, u32[]{:S(2)}, u32[]{:S(2)}) collective-permute-start(bf16[272,1024]{1,0:T(8,128)(2,1)S(1)} %pack.1.refs_0_), channel_id=1, source_target_pairs={{0,4},{4,0},{8,12},{12,8},{16,20},{20,16},{24,28},{28,24},{1,5},{5... | collective-permute-start | bytes 1671176 | tf_op jit(solution)/shard_map/ppermute | solution.py:507
  26.8 18.5 %collective-permute-start.11 = (bf16[256,1024]{1,0:T(8,128)(2,1)}, bf16[256,1024]{1,0:T(8,128)(2,1)S(1)}, u32[]{:S(2)}, u32[]{:S(2)}) collective-permute-start(bf16[256,1024]{1,0:T(8,128)(2,1)} %collective-permute-done.6.refs_1_), channel_id=1, source_target_pairs={{1,2},{2,3},{5,6},{6,7},{9,10},{10,11},{13,14},{14,15},{17,18},{18... | collective-permute-start | bytes 1572872 | tf_op jit(solution)/shard_map/ppermute | solution.py:636
  27.8 17.5 %collective-permute-start.12 = (bf16[256,1024]{1,0:T(8,128)(2,1)}, bf16[256,1024]{1,0:T(8,128)(2,1)S(1)}, u32[]{:S(2)}, u32[]{:S(2)}) collective-permute-start(bf16[256,1024]{1,0:T(8,128)(2,1)} %collective-permute-done.7.refs_4_), channel_id=1, source_target_pairs={{1,0},{2,1},{5,4},{6,5},{9,8},{10,9},{13,12},{14,13},{17,16},{18,1... | collective-permute-start | bytes 1572872 | tf_op jit(solution)/shard_map/ppermute | solution.py:637
  46.4 17.7 %collective-permute-start.23 = (bf16[256,1024]{1,0:T(8,128)(2,1)S(1)}, bf16[256,1024]{1,0:T(8,128)(2,1)S(1)}, u32[]{:S(2)}, u32[]{:S(2)}) collective-permute-start(bf16[256,1024]{1,0:T(8,128)(2,1)S(1)} %broadcast_select_fusion), channel_id=1, source_target_pairs={{2,3},{1,0},{6,7},{5,4},{10,11},{9,8},{14,15},{13,12},{18,19},{17,... | collective-permute-start | bytes 1572872 | tf_op jit(solution)/shard_map/ppermute | solution.py:632
  52.4 20.9 %collective-permute-start.13 = (bf16[256,1152]{1,0:T(8,128)(2,1)}, bf16[256,1152]{1,0:T(8,128)(2,1)S(1)}, u32[]{:S(2)}, u32[]{:S(2)}) collective-permute-start(bf16[256,1152]{1,0:T(8,128)(2,1)} %get-tuple-element.70), channel_id=1, source_target_pairs={{0,4},{4,0},{8,12},{12,8},{16,20},{20,16},{24,28},{28,24},{1,5},{5... | collective-permute-start | bytes 1769480 | tf_op jit(solution)/shard_map/ppermute | solution.py:507
  53.1 20.2 %collective-permute-start.16 = (bf16[128,1152]{1,0:T(8,128)(2,1)S(1)}, bf16[128,1152]{1,0:T(8,128)(2,1)S(1)}, u32[]{:S(2)}, u32[]{:S(2)}) collective-permute-start(bf16[128,1152]{1,0:T(8,128)(2,1)S(1)} %get-tuple-element.77), channel_id=1, source_target_pairs={{0,8},{4,12},{8,0},{12,4},{16,24},{20,28},{24,16},{28,20},{1,9},{5... | collective-permute-start | bytes 884744 | tf_op jit(solution)/shard_map/ppermute | solution.py:507
  58.8 14.5 %collective-permute-start.22 = (bf16[128,1152]{1,0:T(8,128)(2,1)S(1)}, bf16[128,1152]{1,0:T(8,128)(2,1)S(1)}, u32[]{:S(2)}, u32[]{:S(2)}) collective-permute-start(bf16[128,1152]{1,0:T(8,128)(2,1)S(1)} %get-tuple-element.85), channel_id=1, source_target_pairs={{0,16},{4,20},{8,24},{12,28},{16,0},{20,4},{24,8},{28,12},{1,17},{... | collective-permute-start | bytes 884744 | tf_op jit(solution)/shard_map/ppermute | solution.py:507
  61.7 11.6 %collective-permute-start.20 = (bf16[128,1152]{1,0:T(8,128)(2,1)S(1)}, bf16[128,1152]{1,0:T(8,128)(2,1)S(1)}, u32[]{:S(2)}, u32[]{:S(2)}) collective-permute-start(bf16[128,1152]{1,0:T(8,128)(2,1)S(1)} %get-tuple-element.83), channel_id=1, source_target_pairs={{0,8},{4,12},{8,0},{12,4},{16,24},{20,28},{24,16},{28,20},{1,9},{5... | collective-permute-start | bytes 884744 | tf_op jit(solution)/shard_map/ppermute | solution.py:507
  80.6 15.1 %collective-permute-start.30 = (bf16[128,1152]{1,0:T(8,128)(2,1)S(1)}, bf16[128,1152]{1,0:T(8,128)(2,1)S(1)}, u32[]{:S(2)}, u32[]{:S(2)}) collective-permute-start(bf16[128,1152]{1,0:T(8,128)(2,1)S(1)} %get-tuple-element.88.refs_0_), channel_id=1, source_target_pairs={{0,16},{4,20},{8,24},{12,28},{16,0},{20,4},{24,8},{28,12},{1,17},{... | collective-permute-start | bytes 884744 | tf_op jit(solution)/shard_map/ppermute | solution.py:507
  81.5 14.2 %collective-permute-start.27 = (bf16[128,1152]{1,0:T(8,128)(2,1)S(1)}, bf16[128,1152]{1,0:T(8,128)(2,1)S(1)}, u32[]{:S(2)}, u32[]{:S(2)}) collective-permute-start(bf16[128,1152]{1,0:T(8,128)(2,1)S(1)} %get-tuple-element.89.refs_1_), channel_id=1, source_target_pairs={{0,8},{4,12},{8,0},{12,4},{16,24},{20,28},{24,16},{28,20},{1,9},{5... | collective-permute-start | bytes 884744 | tf_op jit(solution)/shard_map/ppermute | solution.py:507
  87.9 12.3 %collective-permute-start.34 = (bf16[128,1152]{1,0:T(8,128)(2,1)S(1)}, bf16[128,1152]{1,0:T(8,128)(2,1)S(1)}, u32[]{:S(2)}, u32[]{:S(2)}) collective-permute-start(bf16[128,1152]{1,0:T(8,128)(2,1)S(1)} %collective-permute-done.26.refs_4_), channel_id=1, source_target_pairs={{0,16},{4,20},{8,24},{12,28},{16,0},{20,4},{24,8},{28,12},{1,17},{... | collective-permute-start | bytes 884744 | tf_op jit(solution)/shard_map/ppermute | solution.py:507
  89.5 10.7 %collective-permute-start.35 = (bf16[128,1152]{1,0:T(8,128)(2,1)}, bf16[128,1152]{1,0:T(8,128)(2,1)S(1)}, u32[]{:S(2)}, u32[]{:S(2)}) collective-permute-start(bf16[128,1152]{1,0:T(8,128)(2,1)} %collective-permute-done.31.refs_9_), channel_id=1, source_target_pairs={{0,8},{4,12},{8,0},{12,4},{16,24},{20,28},{24,16},{28,20},{1,9},{5... | collective-permute-start | bytes 884744 | tf_op jit(solution)/shard_map/ppermute | solution.py:507
  101.6 40.5 %all-to-all-start = ((bf16[8,256,512]{2,1,0:T(8,128)(2,1)}), bf16[8,256,512]{2,1,0:T(8,128)(2,1)S(1)}, u32[]{:S(2)}, u32[]{:S(2)}) async-start(bf16[8,256,512]{2,1,0:T(8,128)(2,1)} %get-tuple-element.95), calls=%async_computation | async-start | bytes 4194304 | tf_op jit(solution)/shard_map/all_to_all | solution.py:744
  107.1 35.0 %collective-permute-start.39 = (bf16[256,1024]{1,0:T(8,128)(2,1)}, bf16[256,1024]{1,0:T(8,128)(2,1)S(1)}, u32[]{:S(2)}, u32[]{:S(2)}) collective-permute-start(bf16[256,1024]{1,0:T(8,128)(2,1)} %get-tuple-element.109.refs_0_), channel_id=1, source_target_pairs={{0,16},{4,20},{8,24},{12,28},{16,0},{20,4},{24,8},{28,12},{1,17},{... | collective-permute-start | bytes 1572872 | tf_op jit(solution)/shard_map/ppermute | solution.py:507
  108.8 33.4 %collective-permute-start.38 = (bf16[256,1024]{1,0:T(8,128)(2,1)}, bf16[256,1024]{1,0:T(8,128)(2,1)S(1)}, u32[]{:S(2)}, u32[]{:S(2)}) collective-permute-start(bf16[256,1024]{1,0:T(8,128)(2,1)} %get-tuple-element.109.refs_0_), channel_id=1, source_target_pairs={{0,8},{4,12},{8,0},{12,4},{16,24},{20,28},{24,16},{28,20},{1,9},{5... | collective-permute-start | bytes 1572872 | tf_op jit(solution)/shard_map/ppermute | solution.py:507
  145.6 10.8 %collective-permute-start.45 = (bf16[128,1024]{1,0:T(8,128)(2,1)S(1)}, bf16[128,1024]{1,0:T(8,128)(2,1)S(1)}, u32[]{:S(2)}, u32[]{:S(2)}) collective-permute-start(bf16[128,1024]{1,0:T(8,128)(2,1)S(1)} %get-tuple-element.121), channel_id=1, source_target_pairs={{0,8},{4,12},{8,0},{12,4},{16,24},{20,28},{24,16},{28,20},{1,9},{5... | collective-permute-start | bytes 786440 | tf_op jit(solution)/shard_map/ppermute | solution.py:507
  148.7 10.9 %collective-permute-start.42 = (bf16[128,1024]{1,0:T(8,128)(2,1)S(1)}, bf16[128,1024]{1,0:T(8,128)(2,1)S(1)}, u32[]{:S(2)}, u32[]{:S(2)}) collective-permute-start(bf16[128,1024]{1,0:T(8,128)(2,1)S(1)} %add_convert_fusion.4), channel_id=1, source_target_pairs={{0,8},{4,12},{8,0},{12,4},{16,24},{20,28},{24,16},{28,20},{1,9},{5... | collective-permute-start | bytes 786440 | tf_op jit(solution)/shard_map/ppermute | solution.py:507
  161.4 10.8 %collective-permute-start.46 = (bf16[256,1024]{1,0:T(8,128)(2,1)}, bf16[256,1024]{1,0:T(8,128)(2,1)S(1)}, u32[]{:S(2)}, u32[]{:S(2)}) collective-permute-start(bf16[256,1024]{1,0:T(8,128)(2,1)} %get-tuple-element.109.refs_0_), channel_id=1, source_target_pairs={{0,4},{4,0},{8,12},{12,8},{16,20},{20,16},{24,28},{28,24},{1,5},{5... | collective-permute-start | bytes 1572872 | tf_op jit(solution)/shard_map/ppermute | solution.py:507
  161.4 11.4 %collective-permute-start.47 = (bf16[256,1024]{1,0:T(8,128)(2,1)S(1)}, bf16[256,1024]{1,0:T(8,128)(2,1)S(1)}, u32[]{:S(2)}, u32[]{:S(2)}) collective-permute-start(bf16[256,1024]{1,0:T(8,128)(2,1)S(1)} %collective-permute-done.38.refs_2_), channel_id=1, source_target_pairs={{0,4},{4,0},{8,12},{12,8},{16,20},{20,16},{24,28},{28,24},{1,5},{5... | collective-permute-start | bytes 1572872 | tf_op jit(solution)/shard_map/ppermute | solution.py:507
  161.9 10.8 %collective-permute-start.48 = (bf16[256,1024]{1,0:T(8,128)(2,1)S(1)}, bf16[256,1024]{1,0:T(8,128)(2,1)S(1)}, u32[]{:S(2)}, u32[]{:S(2)}) collective-permute-start(bf16[256,1024]{1,0:T(8,128)(2,1)S(1)} %collective-permute-done.39.refs_4_), channel_id=1, source_target_pairs={{0,4},{4,0},{8,12},{12,8},{16,20},{20,16},{24,28},{28,24},{1,5},{5... | collective-permute-start | bytes 1572872 | tf_op jit(solution)/shard_map/ppermute | solution.py:507
  (69 other events, 469.2 us)

commit v14 on v13

--- a/solution.py
+++ b/solution.py
@@ -739,10 +739,9 @@
     )(*flat(terms), grad_attn)
     grad_chips = spread_halves(*extended)
     grad_all = with_cores(grad_chips)
-    arrived = flat(grad_chips[1:])
     attns = spread_near(after(attn_out, *flat(grad_chips[1:3])))
     columns = lax.all_to_all(
-        after(blocks, *arrived), "ctx", split_axis=0, concat_axis=0, tiled=True
+        after(blocks, *flat(attns[1:3]), *flat(grad_chips[3:])), "ctx", split_axis=0, concat_axis=0, tiled=True
     )
 
     outs = pl.pallas_call(
@@ -772,10 +771,10 @@
         name="backward",
     )(logits, hot, q_slots, probs, keys, values, *flat(grad_all))
     key_grad, value_grad = outs[chunks:]
-    received = from_core(outs[:chunks], columns, *flat(attns[1:3]))
+    received = from_core(outs[:chunks], columns)
     terms, last_sums = collect_chips(outs[:chunks], received)
     near = [[after(x, *last_sums) for x in pieces] for pieces in attns]
-    attns = with_cores(spread_far(near, rows // 2, terms[2][0], terms[-1][-1]))
+    attns = with_cores(spread_far(near, rows // 2, terms[2][-1], terms[-1][0]))
 
     def weight_part(chosen, first, when, *before):
         return pl.pallas_call(

time: 185 us -> 188 us (1.016)
  waiting for transfers between devices: 67.9 us -> 76.4 us
  starting transfers between devices: 51.2 us -> 49.2 us
    ppermute x52, waiting for transfers between devices: 62.3 us -> 68.8 us  [swap(): return lax.ppermute(x, 'ctx', [(i, i ^ bits) for i in range(count)])]
    all_to_all x1, waiting for transfers between devices: 0.01 us -> 2.05 us  [body(): lax.all_to_all(after(blocks, *flat(attns[1:3]), *flat(grad_chips[3:])), '...]
    ppermute x52, starting transfers between devices: 38.4 us -> 36.3 us  [swap(): return lax.ppermute(x, 'ctx', [(i, i ^ bits) for i in range(count)])]
    unnamed x71 -> x77, local copies, waits for them, and re-layouts: 7.43 us -> 6.74 us
  transfers between devices with their start and end apart: 58 -> 58, of which waited for: 26 -> 28; matrix products, arithmetic and copies ran while one was open for 2% -> 2% of each run, Pallas kernels for 25% -> 24%
where the time goes in v14:
time: 188 us
  waiting for transfers between devices  76.4 us (41%)
  Pallas kernels  50.3 us (27%)
  starting transfers between devices  49.2 us (26%)
  local copies, waits for them, and re-layouts  7.83 us (4%)
  other arithmetic  2.61 us (1%)
    ppermute x52, waiting for transfers between devices, swap(): return lax.ppermute(x, 'ctx', [(i, i ^ bits) for i in range(count)])  68.8 us
    ppermute x52, starting transfers between devices, swap(): return lax.ppermute(x, 'ctx', [(i, i ^ bits) for i in range(count)])  36.3 us
    pallas_call x1, Pallas kernels, body(): pl.pallas_call(functools.partial(backward_kernel, [len(pieces) for pieces...  18.7 us
    pallas_call x1, Pallas kernels, body(): pl.pallas_call(functools.partial(forward_kernel, [len(pieces) for pieces...  13.5 us
    pallas_call x1, Pallas kernels, body(): make_grad(after(line, *before), out_weight, out_grad, *ups, *downs)  7.66 us
    unnamed x77, local copies, waits for them, and re-layouts  6.74 us
    ppermute x2, starting transfers between devices, spread_line(): ups.append(lax.ppermute(ups[-1], 'head', up))  4.98 us
    ppermute x2, waiting for transfers between devices, spread_line(): downs.append(lax.ppermute(downs[-1], 'head', down))  4.77 us
  transfers between devices with their start and end apart: 58, of which 28 were waited for; matrix products, arithmetic and copies ran while one was open for 2% of the time, Pallas kernels for 24%

profile of v14, /device:TPU:0, one launch (start us, length us, event | category | flops | bytes accessed | tf_op | source)
XLA Modules:
  0.0 187.5 jit_solution(17272206178254788708)
XLA Ops:
  2.4 3.0 %collective-permute-start.1 = (bf16[272,1024]{1,0:T(8,128)(2,1)S(1)}, bf16[272,1024]{1,0:T(8,128)(2,1)S(1)}, u32[]{:S(2)}, u32[]{:S(2)}) collective-permute-start(bf16[272,1024]{1,0:T(8,128)(2,1)S(1)} %pack.1.refs_0_), channel_id=1, source_target_pairs={{0,8},{4,12},{8,0},{12,4},{16,24},{20,28},{24,16},{28,20},{1,9},{5... | collective-permute-start | bytes 1671176 | tf_op jit(solution)/shard_map/ppermute | solution.py:507
  6.9 4.3 %collective-permute-start.6 = (bf16[256,1024]{1,0:T(8,128)(2,1)}, bf16[256,1024]{1,0:T(8,128)(2,1)}, u32[]{:S(2)}, u32[]{:S(2)}) collective-permute-start(bf16[256,1024]{1,0:T(8,128)(2,1)} %refs_0_.1), channel_id=1, source_target_pairs={{0,1},{1,2},{2,3},{4,5},{5,6},{6,7},{8,9},{9,10},{10,11},{12,13},{... | collective-permute-start | bytes 1572872 | tf_op jit(solution)/shard_map/ppermute | solution.py:636
  12.6 5.4 %collective-permute-done.1.refs_2_ = bf16[272,1024]{1,0:T(8,128)(2,1)S(1)} collective-permute-done((bf16[272,1024]{1,0:T(8,128)(2,1)S(1)}, bf16[272,1024]{1,0:T(8,128)(2,1)S(1)}, u32[]{:S(2)}, u32[]{:S(2)}) %collective-permute-start.1) | collective-permute-done | bytes 557088 | tf_op jit(solution)/shard_map/ppermute | solution.py:507
  18.1 1.8 collective-permute-start.5
  21.5 4.8 %collective-permute-done.7.refs_4_ = bf16[256,1024]{1,0:T(8,128)(2,1)} collective-permute-done((bf16[256,1024]{1,0:T(8,128)(2,1)}, bf16[256,1024]{1,0:T(8,128)(2,1)}, u32[]{:S(2)}, u32[]{:S(2)}) %collective-permute-start.7) | collective-permute-done | bytes 524320 | tf_op jit(solution)/shard_map/ppermute | solution.py:637
  31.8 13.5 %forward.1 = (bf16[256,1152]{1,0:T(8,128)(2,1)}, bf16[256,1152]{1,0:T(8,128)(2,1)}, bf16[256,1152]{1,0:T(8,128)(2,1)}, bf16[256,1152]{1,0:T(8,128)(2,1)}, bf16[2...) custom-call(s32[1]{0:T(128)} %bitcast.me_ref, ...), custom_call_target="tpu_custom_call" | custom-call | tf_op jit(solution)/shard_map/forward/pallas_call | solution.py:680
  53.7 5.0 %collective-permute-done.18.refs_4_ = bf16[128,1152]{1,0:T(8,128)(2,1)S(1)} collective-permute-done((bf16[128,1152]{1,0:T(8,128)(2,1)S(1)}, bf16[128,1152]{1,0:T(8,128)(2,1)S(1)}, u32[]{:S(2)}, u32[]{:S(2)}) %collective-permute-start.18) | collective-permute-done | bytes 294944 | tf_op jit(solution)/shard_map/ppermute | solution.py:507
  61.7 1.6 collective-permute-start.20
  65.5 7.7 %grad.1 = (bf16[256,1024]{1,0:T(8,128)(2,1)}, bf16[8,256,512]{2,1,0:T(8,128)(2,1)}) custom-call(s32[1]{0:T(128)} %bitcast.4.line_ref, bf16[4096,1024]{1,0:T(8,128)(2,1)} %w_ref.1, bf16[256,1024]{1,0:T(8,128)(2,1)} %refs_0_.1, bf16[256,1024]{1,0:T(8,128)(2,1)} %collective-permute-done.6.refs_1_, bf16[256,1024]{1,0:T(8,128)(2,1)} %copy-done.14, ...), custom_call_target="tpu_custom_call" | custom-call | tf_op jit(solution)/shard_map/grad/pallas_call | solution.py:730
  74.4 2.8 %finish.1 = (bf16[256,1024]{1,0:T(8,128)(2,1)S(1)}, bf16[128,1152]{1,0:T(8,128)(2,1)S(1)}, bf16[128,1152]{1,0:T(8,128)(2,1)S(1)}) custom-call(bf16[256,1152]{1,0:T(8,128)(2,1)S(1)} %copy-done.4, bf16[256,1152]{1,0:T(8,128)(2,1)S(1)} %collective-permute-done.13.refs_1_, bf16[128,1152]{1,0:T(8,128)(2,1)S(1)} %collective-permute-done.16.refs_2_, ...), custom_call_target="tpu_custom_call" | custom-call | tf_op jit(solution)/shard_map/finish/pallas_call | solution.py:732
  81.4 5.9 %collective-permute-done.26.refs_4_ = bf16[128,1152]{1,0:T(8,128)(2,1)S(1)} collective-permute-done((bf16[128,1152]{1,0:T(8,128)(2,1)S(1)}, bf16[128,1152]{1,0:T(8,128)(2,1)S(1)}, u32[]{:S(2)}, u32[]{:S(2)}) %collective-permute-start.26) | collective-permute-done | bytes 294944 | tf_op jit(solution)/shard_map/ppermute | solution.py:507
  87.3 4.7 %collective-permute-done.27.refs_5_ = bf16[128,1152]{1,0:T(8,128)(2,1)S(1)} collective-permute-done((bf16[128,1152]{1,0:T(8,128)(2,1)S(1)}, bf16[128,1152]{1,0:T(8,128)(2,1)S(1)}, u32[]{:S(2)}, u32[]{:S(2)}) %collective-permute-start.27) | collective-permute-done | bytes 294944 | tf_op jit(solution)/shard_map/ppermute | solution.py:507
  97.6 15.3 %collective-permute-done.34.refs_12_ = bf16[128,1152]{1,0:T(8,128)(2,1)S(1)} collective-permute-done((bf16[128,1152]{1,0:T(8,128)(2,1)S(1)}, bf16[128,1152]{1,0:T(8,128)(2,1)S(1)}, u32[]{:S(2)}, u32[]{:S(2)}) %collective-permute-start.34) | collective-permute-done | bytes 294944 | tf_op jit(solution)/shard_map/ppermute | solution.py:507
  113.7 3.8 %all-to-all-start = ((bf16[8,256,512]{2,1,0:T(8,128)(2,1)}), bf16[8,256,512]{2,1,0:T(8,128)(2,1)S(1)}, u32[]{:S(2)}, u32[]{:S(2)}) async-start(bf16[8,256,512]{2,1,0:T(8,128)(2,1)} %get-tuple-element.97), calls=%async_computation | async-start | bytes 4194304 | tf_op jit(solution)/shard_map/all_to_all | solution.py:743
  123.1 18.7 %backward.1 = (bf16[256,1024]{1,0:T(8,128)(2,1)}, bf16[256,1024]{1,0:T(8,128)(2,1)}, bf16[256,1024]{1,0:T(8,128)(2,1)}, bf16[256,1024]{1,0:T(8,128)(2,1)}, bf16[...) custom-call(f32[16,8,128]{2,1,0:T(8,128)} %get-tuple-element.64.logi, ...), custom_call_target="tpu_custom_call" | custom-call | tf_op jit(solution)/shard_map/backward/pallas_call | solution.py:747
  141.9 2.0 %all-to-all-done.cols_ref = bf16[8,256,512]{2,1,0:T(8,128)(2,1)S(1)} async-done(((bf16[8,256,512]{2,1,0:T(8,128)(2,1)}), bf16[8,256,512]{2,1,0:T(8,128)(2,1)S(1)}, u32[]{:S(2)}, u32[]{:S(2)}) %all-to-all-start) | async-done | bytes 2097184 | tf_op jit(solution)/shard_map/all_to_all | solution.py:743
  149.6 6.3 %collective-permute-done.43 = bf16[128,1024]{1,0:T(8,128)(2,1)S(1)} collective-permute-done((bf16[128,1024]{1,0:T(8,128)(2,1)S(1)}, bf16[128,1024]{1,0:T(8,128)(2,1)S(1)}, u32[]{:S(2)}, u32[]{:S(2)}) %collective-permute-start.43) | collective-permute-done | bytes 262176 | tf_op jit(solution)/shard_map/ppermute | solution.py:507
  156.3 1.6 collective-permute-start.50
  159.3 6.1 %collective-permute-done.50.refs_3_ = bf16[128,1024]{1,0:T(8,128)(2,1)S(1)} collective-permute-done((bf16[128,1024]{1,0:T(8,128)(2,1)S(1)}, bf16[128,1024]{1,0:T(8,128)(2,1)S(1)}, u32[]{:S(2)}, u32[]{:S(2)}) %collective-permute-start.50) | collective-permute-done | bytes 262176 | tf_op jit(solution)/shard_map/ppermute | solution.py:507
  166.2 4.4 %collective-permute-done.42.refs_2_ = bf16[128,1024]{1,0:T(8,128)(2,1)S(1)} collective-permute-done((bf16[128,1024]{1,0:T(8,128)(2,1)S(1)}, bf16[128,1024]{1,0:T(8,128)(2,1)S(1)}, u32[]{:S(2)}, u32[]{:S(2)}) %collective-permute-start.42) | collective-permute-done | bytes 262176 | tf_op jit(solution)/shard_map/ppermute | solution.py:507
  174.2 5.7 %collective-permute-done.53.refs_0_ = bf16[128,1024]{1,0:T(8,128)(2,1)S(1)} collective-permute-done((bf16[128,1024]{1,0:T(8,128)(2,1)S(1)}, bf16[128,1024]{1,0:T(8,128)(2,1)S(1)}, u32[]{:S(2)}, u32[]{:S(2)}) %collective-permute-start.53) | collective-permute-done | bytes 262176 | tf_op jit(solution)/shard_map/ppermute | solution.py:507
  180.4 1.8 weight.2.refs_4_
  182.2 1.9 %collective-permute-done.52.refs_5_ = bf16[128,1024]{1,0:T(8,128)(2,1)S(1)} collective-permute-done((bf16[128,1024]{1,0:T(8,128)(2,1)S(1)}, bf16[128,1024]{1,0:T(8,128)(2,1)S(1)}, u32[]{:S(2)}, u32[]{:S(2)}) %collective-permute-start.52) | collective-permute-done | bytes 262176 | tf_op jit(solution)/shard_map/ppermute | solution.py:507
  185.4 2.1 %weight.3 = f32[512,1024]{1,0:T(8,128)} custom-call(s32[1]{0:T(128)} %bitcast.me_ref, bf16[8,256,512]{2,1,0:T(8,128)(2,1)S(1)} %all-to-all-done.cols_ref, bf16[128,1024]{1,0:T(8,128)(2,1)S(1)} %collective-permute-done.53.refs_0_, bf16[128,1024]{1,0:T(8,128)(2,1)S(1)} %collective-permute-done.54.refs_1_, ...), custom_call_target="tpu_custom_call" | custom-call | tf_op jit(solution)/shard_map/weight/pallas_call | solution.py:780
  (191 shorter events, 56.0 us)
Async XLA Ops:
  2.4 15.6 %collective-permute-start.1 = (bf16[272,1024]{1,0:T(8,128)(2,1)S(1)}, bf16[272,1024]{1,0:T(8,128)(2,1)S(1)}, u32[]{:S(2)}, u32[]{:S(2)}) collective-permute-start(bf16[272,1024]{1,0:T(8,128)(2,1)S(1)} %pack.1.refs_0_), channel_id=1, source_target_pairs={{0,8},{4,12},{8,0},{12,4},{16,24},{20,28},{24,16},{28,20},{1,9},{5... | collective-permute-start | bytes 1671176 | tf_op jit(solution)/shard_map/ppermute | solution.py:507
  5.4 14.5 %collective-permute-start.3 = (bf16[272,1024]{1,0:T(8,128)(2,1)S(1)}, bf16[272,1024]{1,0:T(8,128)(2,1)S(1)}, u32[]{:S(2)}, u32[]{:S(2)}) collective-permute-start(bf16[272,1024]{1,0:T(8,128)(2,1)S(1)} %pack.1.refs_0_), channel_id=1, source_target_pairs={{0,16},{4,20},{8,24},{12,28},{16,0},{20,4},{24,8},{28,12},{1,17},{... | collective-permute-start | bytes 1671176 | tf_op jit(solution)/shard_map/ppermute | solution.py:507
  6.9 14.6 %collective-permute-start.6 = (bf16[256,1024]{1,0:T(8,128)(2,1)}, bf16[256,1024]{1,0:T(8,128)(2,1)}, u32[]{:S(2)}, u32[]{:S(2)}) collective-permute-start(bf16[256,1024]{1,0:T(8,128)(2,1)} %refs_0_.1), channel_id=1, source_target_pairs={{0,1},{1,2},{2,3},{4,5},{5,6},{6,7},{8,9},{9,10},{10,11},{12,13},{... | collective-permute-start | bytes 1572872 | tf_op jit(solution)/shard_map/ppermute | solution.py:636
  11.2 15.0 %collective-permute-start.7 = (bf16[256,1024]{1,0:T(8,128)(2,1)}, bf16[256,1024]{1,0:T(8,128)(2,1)}, u32[]{:S(2)}, u32[]{:S(2)}) collective-permute-start(bf16[256,1024]{1,0:T(8,128)(2,1)} %refs_0_.1), channel_id=1, source_target_pairs={{1,0},{2,1},{3,2},{5,4},{6,5},{7,6},{9,8},{10,9},{11,10},{13,12},{... | collective-permute-start | bytes 1572872 | tf_op jit(solution)/shard_map/ppermute | solution.py:637
  12.5 14.3 %collective-permute-start = (bf16[272,1024]{1,0:T(8,128)(2,1)S(1)}, bf16[272,1024]{1,0:T(8,128)(2,1)S(1)}, u32[]{:S(2)}, u32[]{:S(2)}) collective-permute-start(bf16[272,1024]{1,0:T(8,128)(2,1)S(1)} %pack.1.refs_0_), channel_id=1, source_target_pairs={{0,4},{4,0},{8,12},{12,8},{16,20},{20,16},{24,28},{28,24},{1,5},{5... | collective-permute-start | bytes 1671176 | tf_op jit(solution)/shard_map/ppermute | solution.py:507
  26.8 18.5 %collective-permute-start.11 = (bf16[256,1024]{1,0:T(8,128)(2,1)}, bf16[256,1024]{1,0:T(8,128)(2,1)S(1)}, u32[]{:S(2)}, u32[]{:S(2)}) collective-permute-start(bf16[256,1024]{1,0:T(8,128)(2,1)} %collective-permute-done.6.refs_1_), channel_id=1, source_target_pairs={{1,2},{2,3},{5,6},{6,7},{9,10},{10,11},{13,14},{14,15},{17,18},{18... | collective-permute-start | bytes 1572872 | tf_op jit(solution)/shard_map/ppermute | solution.py:636
  27.8 17.5 %collective-permute-start.12 = (bf16[256,1024]{1,0:T(8,128)(2,1)}, bf16[256,1024]{1,0:T(8,128)(2,1)S(1)}, u32[]{:S(2)}, u32[]{:S(2)}) collective-permute-start(bf16[256,1024]{1,0:T(8,128)(2,1)} %collective-permute-done.7.refs_4_), channel_id=1, source_target_pairs={{1,0},{2,1},{5,4},{6,5},{9,8},{10,9},{13,12},{14,13},{17,16},{18,1... | collective-permute-start | bytes 1572872 | tf_op jit(solution)/shard_map/ppermute | solution.py:637
  46.3 17.7 %collective-permute-start.23 = (bf16[256,1024]{1,0:T(8,128)(2,1)S(1)}, bf16[256,1024]{1,0:T(8,128)(2,1)S(1)}, u32[]{:S(2)}, u32[]{:S(2)}) collective-permute-start(bf16[256,1024]{1,0:T(8,128)(2,1)S(1)} %broadcast_select_fusion), channel_id=1, source_target_pairs={{2,3},{1,0},{6,7},{5,4},{10,11},{9,8},{14,15},{13,12},{18,19},{17,... | collective-permute-start | bytes 1572872 | tf_op jit(solution)/shard_map/ppermute | solution.py:632
  52.4 20.8 %collective-permute-start.13 = (bf16[256,1152]{1,0:T(8,128)(2,1)}, bf16[256,1152]{1,0:T(8,128)(2,1)S(1)}, u32[]{:S(2)}, u32[]{:S(2)}) collective-permute-start(bf16[256,1152]{1,0:T(8,128)(2,1)} %get-tuple-element.70), channel_id=1, source_target_pairs={{0,4},{4,0},{8,12},{12,8},{16,20},{20,16},{24,28},{28,24},{1,5},{5... | collective-permute-start | bytes 1769480 | tf_op jit(solution)/shard_map/ppermute | solution.py:507
  53.1 20.1 %collective-permute-start.16 = (bf16[128,1152]{1,0:T(8,128)(2,1)S(1)}, bf16[128,1152]{1,0:T(8,128)(2,1)S(1)}, u32[]{:S(2)}, u32[]{:S(2)}) collective-permute-start(bf16[128,1152]{1,0:T(8,128)(2,1)S(1)} %get-tuple-element.77), channel_id=1, source_target_pairs={{0,8},{4,12},{8,0},{12,4},{16,24},{20,28},{24,16},{28,20},{1,9},{5... | collective-permute-start | bytes 884744 | tf_op jit(solution)/shard_map/ppermute | solution.py:507
  58.7 14.5 %collective-permute-start.22 = (bf16[128,1152]{1,0:T(8,128)(2,1)S(1)}, bf16[128,1152]{1,0:T(8,128)(2,1)S(1)}, u32[]{:S(2)}, u32[]{:S(2)}) collective-permute-start(bf16[128,1152]{1,0:T(8,128)(2,1)S(1)} %get-tuple-element.85), channel_id=1, source_target_pairs={{0,16},{4,20},{8,24},{12,28},{16,0},{20,4},{24,8},{28,12},{1,17},{... | collective-permute-start | bytes 884744 | tf_op jit(solution)/shard_map/ppermute | solution.py:507
  78.9 13.2 %collective-permute-start.27 = (bf16[128,1152]{1,0:T(8,128)(2,1)S(1)}, bf16[128,1152]{1,0:T(8,128)(2,1)S(1)}, u32[]{:S(2)}, u32[]{:S(2)}) collective-permute-start(bf16[128,1152]{1,0:T(8,128)(2,1)S(1)} %get-tuple-element.89.refs_1_), channel_id=1, source_target_pairs={{0,8},{4,12},{8,0},{12,4},{16,24},{20,28},{24,16},{28,20},{1,9},{5... | collective-permute-start | bytes 884744 | tf_op jit(solution)/shard_map/ppermute | solution.py:507
  79.4 12.6 %collective-permute-start.30 = (bf16[128,1152]{1,0:T(8,128)(2,1)S(1)}, bf16[128,1152]{1,0:T(8,128)(2,1)S(1)}, u32[]{:S(2)}, u32[]{:S(2)}) collective-permute-start(bf16[128,1152]{1,0:T(8,128)(2,1)S(1)} %get-tuple-element.88.refs_0_), channel_id=1, source_target_pairs={{0,16},{4,20},{8,24},{12,28},{16,0},{20,4},{24,8},{28,12},{1,17},{... | collective-permute-start | bytes 884744 | tf_op jit(solution)/shard_map/ppermute | solution.py:507
  80.7 12.8 %collective-permute-start.31 = (bf16[128,1152]{1,0:T(8,128)(2,1)S(1)}, bf16[128,1152]{1,0:T(8,128)(2,1)S(1)}, u32[]{:S(2)}, u32[]{:S(2)}) collective-permute-start(bf16[128,1152]{1,0:T(8,128)(2,1)S(1)} %get-tuple-element.89.refs_1_), channel_id=1, source_target_pairs={{0,16},{4,20},{8,24},{12,28},{16,0},{20,4},{24,8},{28,12},{1,17},{... | collective-permute-start | bytes 884744 | tf_op jit(solution)/shard_map/ppermute | solution.py:507
  93.5 19.4 %collective-permute-start.38 = (bf16[256,1024]{1,0:T(8,128)(2,1)S(1)}, bf16[256,1024]{1,0:T(8,128)(2,1)S(1)}, u32[]{:S(2)}, u32[]{:S(2)}) collective-permute-start(bf16[256,1024]{1,0:T(8,128)(2,1)S(1)} %get-tuple-element.109.refs_0_), channel_id=1, source_target_pairs={{0,8},{4,12},{8,0},{12,4},{16,24},{20,28},{24,16},{28,20},{1,9},{5... | collective-permute-start | bytes 1572872 | tf_op jit(solution)/shard_map/ppermute | solution.py:507
  95.0 17.9 %collective-permute-start.39 = (bf16[256,1024]{1,0:T(8,128)(2,1)S(1)}, bf16[256,1024]{1,0:T(8,128)(2,1)S(1)}, u32[]{:S(2)}, u32[]{:S(2)}) collective-permute-start(bf16[256,1024]{1,0:T(8,128)(2,1)S(1)} %get-tuple-element.109.refs_0_), channel_id=1, source_target_pairs={{0,16},{4,20},{8,24},{12,28},{16,0},{20,4},{24,8},{28,12},{1,17},{... | collective-permute-start | bytes 1572872 | tf_op jit(solution)/shard_map/ppermute | solution.py:507
  96.3 16.6 %collective-permute-start.34 = (bf16[128,1152]{1,0:T(8,128)(2,1)S(1)}, bf16[128,1152]{1,0:T(8,128)(2,1)S(1)}, u32[]{:S(2)}, u32[]{:S(2)}) collective-permute-start(bf16[128,1152]{1,0:T(8,128)(2,1)S(1)} %collective-permute-done.26.refs_4_), channel_id=1, source_target_pairs={{0,16},{4,20},{8,24},{12,28},{16,0},{20,4},{24,8},{28,12},{1,17},{... | collective-permute-start | bytes 884744 | tf_op jit(solution)/shard_map/ppermute | solution.py:507
  97.1 15.8 %collective-permute-start.35 = (bf16[128,1152]{1,0:T(8,128)(2,1)S(1)}, bf16[128,1152]{1,0:T(8,128)(2,1)S(1)}, u32[]{:S(2)}, u32[]{:S(2)}) collective-permute-start(bf16[128,1152]{1,0:T(8,128)(2,1)S(1)} %collective-permute-done.31.refs_9_), channel_id=1, source_target_pairs={{0,8},{4,12},{8,0},{12,4},{16,24},{20,28},{24,16},{28,20},{1,9},{5... | collective-permute-start | bytes 884744 | tf_op jit(solution)/shard_map/ppermute | solution.py:507
  113.7 30.2 %all-to-all-start = ((bf16[8,256,512]{2,1,0:T(8,128)(2,1)}), bf16[8,256,512]{2,1,0:T(8,128)(2,1)S(1)}, u32[]{:S(2)}, u32[]{:S(2)}) async-start(bf16[8,256,512]{2,1,0:T(8,128)(2,1)} %get-tuple-element.97), calls=%async_computation | async-start | bytes 4194304 | tf_op jit(solution)/shard_map/all_to_all | solution.py:743
  156.2 15.3 %collective-permute-start.46 = (bf16[256,1024]{1,0:T(8,128)(2,1)S(1)}, bf16[256,1024]{1,0:T(8,128)(2,1)S(1)}, u32[]{:S(2)}, u32[]{:S(2)}) collective-permute-start(bf16[256,1024]{1,0:T(8,128)(2,1)S(1)} %copy-done.9), channel_id=1, source_target_pairs={{0,4},{4,0},{8,12},{12,8},{16,20},{20,16},{24,28},{28,24},{1,5},{5... | collective-permute-start | bytes 1572872 | tf_op jit(solution)/shard_map/ppermute | solution.py:507
  158.4 14.3 %collective-permute-start.47 = (bf16[256,1024]{1,0:T(8,128)(2,1)S(1)}, bf16[256,1024]{1,0:T(8,128)(2,1)S(1)}, u32[]{:S(2)}, u32[]{:S(2)}) collective-permute-start(bf16[256,1024]{1,0:T(8,128)(2,1)S(1)} %collective-permute-done.38.refs_2_), channel_id=1, source_target_pairs={{0,4},{4,0},{8,12},{12,8},{16,20},{20,16},{24,28},{28,24},{1,5},{5... | collective-permute-start | bytes 1572872 | tf_op jit(solution)/shard_map/ppermute | solution.py:507
  158.4 12.2 %collective-permute-start.42 = (bf16[128,1024]{1,0:T(8,128)(2,1)S(1)}, bf16[128,1024]{1,0:T(8,128)(2,1)S(1)}, u32[]{:S(2)}, u32[]{:S(2)}) collective-permute-start(bf16[128,1024]{1,0:T(8,128)(2,1)S(1)} %add_convert_fusion.4), channel_id=1, source_target_pairs={{0,8},{4,12},{8,0},{12,4},{16,24},{20,28},{24,16},{28,20},{1,9},{5... | collective-permute-start | bytes 786440 | tf_op jit(solution)/shard_map/ppermute | solution.py:507
  165.4 14.9 %collective-permute-start.48 = (bf16[256,1024]{1,0:T(8,128)(2,1)S(1)}, bf16[256,1024]{1,0:T(8,128)(2,1)S(1)}, u32[]{:S(2)}, u32[]{:S(2)}) collective-permute-start(bf16[256,1024]{1,0:T(8,128)(2,1)S(1)} %collective-permute-done.39.refs_4_), channel_id=1, source_target_pairs={{0,4},{4,0},{8,12},{12,8},{16,20},{20,16},{24,28},{28,24},{1,5},{5... | collective-permute-start | bytes 1572872 | tf_op jit(solution)/shard_map/ppermute | solution.py:507
  166.2 15.9 %collective-permute-start.49 = (bf16[256,1024]{1,0:T(8,128)(2,1)S(1)}, bf16[256,1024]{1,0:T(8,128)(2,1)S(1)}, u32[]{:S(2)}, u32[]{:S(2)}) collective-permute-start(bf16[256,1024]{1,0:T(8,128)(2,1)S(1)} %copy-done.37), channel_id=1, source_target_pairs={{0,4},{4,0},{8,12},{12,8},{16,20},{20,16},{24,28},{28,24},{1,5},{5... | collective-permute-start | bytes 1572872 | tf_op jit(solution)/shard_map/ppermute | solution.py:507
  (72 other events, 587.5 us)

commit v15 on v13

--- a/solution.py
+++ b/solution.py
@@ -492,14 +492,11 @@
     wait(part_copies)
 
 
-def weight_kernel(counts, first, me_ref, cols_ref, *refs):
-    attns, (*before, out_ref) = dealt(refs, counts)
+def weight_kernel(counts, me_ref, cols_ref, *refs):
+    attns, (out_ref,) = dealt(refs, counts)
     me = me_ref[0]
-    columns = joined([cols_ref[me ^ (first + m)] for m in range(len(counts))], 0)
-    total = mm(columns, joined([whole(pieces) for pieces in attns], 0), TN)
-    for ref in before:
-        total = total + ref[...]
-    out_ref[...] = total
+    columns = joined([cols_ref[me ^ m] for m in range(len(counts))], 0)
+    out_ref[...] = mm(columns, joined([whole(pieces) for pieces in attns], 0), TN)
 
 
 def swap(x, bits):
@@ -576,7 +573,7 @@
     x_far, y_far = swap(x_sum, 2), swap(y_sum, 4)
     x_sum, y_sum = both(1, top, None, x_sum), both(2, low, None, y_sum)
     x_top, y_low = swap(x_sum, 2), swap(y_sum, 4)
-    x_sum, y_sum = both(1, low, y_far, x_sum), both(2, top, x_far, y_sum)
+    x_sum, y_sum = both(1, low, y_far, x_top), both(2, top, x_far, y_low)
     x_low, y_top = swap(x_sum, 2), swap(y_sum, 4)
     return terms + [[x_top, x_low], [y_top, y_low]], [x_sum, y_sum]
 
@@ -598,8 +595,8 @@
             name="merge",
         )(*ins)
 
-    terms = [[parts[0]], [received[0]]]
     if chips != 4:
+        terms = [[parts[0]], [swap(parts[1], 1)]]
         for j in range(1, chips):
             (both,) = merged([parts[2 * j], received[j]], [[(0, 0, rows), (1, 0, rows)]])
             terms.append([swap(both, 2 * j)])
@@ -611,6 +608,7 @@
     x_far, y_far = swap(x_far, 2), swap(y_far, 4)
     ins = [parts[2], received[1], parts[4], received[2]]
     x_top, y_low = merged(ins, [[(0, *top), (1, *top)], [(2, *low), (3, *low)]])
+    terms = [[parts[0]], [swap(after(parts[1], x_top), 1)]]
     x_top, y_low = swap(x_top, 2), swap(y_low, 4)
     x_low, y_top = merged(
         ins + [y_far, x_far],
@@ -740,7 +738,8 @@
     grad_chips = spread_halves(*extended)
     grad_all = with_cores(grad_chips)
     arrived = flat(grad_chips[1:])
-    attns = spread_near(after(attn_out, *flat(grad_chips[1:3])))
+    near = after(attn_out, *flat(grad_chips[1:3]))
+    attns = [[attn_out]] + [[swap(near, 2 * j)] for j in range(1, chips)]
     columns = lax.all_to_all(
         after(blocks, *arrived), "ctx", split_axis=0, concat_axis=0, tiled=True
     )
@@ -772,22 +771,17 @@
         name="backward",
     )(logits, hot, q_slots, probs, keys, values, *flat(grad_all))
     key_grad, value_grad = outs[chunks:]
-    received = from_core(outs[:chunks], columns, *flat(attns[1:3]))
+    received = from_core(outs[:chunks], columns, *flat(attns[1:]))
     terms, last_sums = collect_chips(outs[:chunks], received)
-    near = [[after(x, *last_sums) for x in pieces] for pieces in attns]
-    attns = with_cores(spread_far(near, rows // 2, terms[2][0], terms[-1][-1]))
-
-    def weight_part(chosen, first, when, *before):
-        return pl.pallas_call(
-            functools.partial(weight_kernel, [len(pieces) for pieces in chosen], first),
-            out_shape=shaped((features // chunks, width), F32),
-            in_specs=[smem] + [vmem] * (1 + len(flat(chosen)) + len(before)),
-            out_specs=vmem,
-            compiler_params=small,
-            name="weight",
-        )(when, columns, *flat(chosen), *before)
-
-    weight_near = weight_part(attns[:-2], 0, after(me, terms[2][0]))
+    attns = with_cores([[after(x, *last_sums) for x in pieces] for pieces in attns])
+    weight_grad = pl.pallas_call(
+        functools.partial(weight_kernel, [len(pieces) for pieces in attns]),
+        out_shape=shaped((features // chunks, width), F32),
+        in_specs=[smem] + [vmem] * (1 + len(flat(attns))),
+        out_specs=vmem,
+        compiler_params=small,
+        name="weight",
+    )(me, columns, *flat(attns))
     query_grad = pl.pallas_call(
         functools.partial(total_kernel, [len(pieces) for pieces in terms]),
         out_shape=shaped((rows, width), F32),
@@ -795,8 +789,7 @@
         out_specs=vmem,
         compiler_params=small,
         name="total",
-    )(after(terms[0][0], weight_near), *flat(terms[1:]))
-    weight_grad = weight_part(attns[-2:], chunks - 2, after(me, query_grad), weight_near)
+    )(after(terms[0][0], weight_grad), *flat(terms[1:]))
     return (
         query_grad,
         key_grad.reshape(-1, width),

time: 185 us -> 189 us (1.022)
  waiting for transfers between devices: 67.9 us -> 74.7 us
  starting transfers between devices: 51.2 us -> 48.3 us
    ppermute x52 -> x50, waiting for transfers between devices: 62.3 us -> 69.2 us  [swap(): return lax.ppermute(x, 'ctx', [(i, i ^ bits) for i in range(count)])]
    ppermute x52 -> x50, starting transfers between devices: 38.4 us -> 35.5 us  [swap(): return lax.ppermute(x, 'ctx', [(i, i ^ bits) for i in range(count)])]
    unnamed x71 -> x77, local copies, waits for them, and re-layouts: 7.43 us -> 7.97 us
    pallas_call x2 -> x1, Pallas kernels: 4.91 us -> 4.72 us  [body(): pl.pallas_call(functools.partial(weight_kernel, [len(pieces) for pieces i...]
  transfers between devices with their start and end apart: 58 -> 56, of which waited for: 26 -> 27; matrix products, arithmetic and copies ran while one was open for 2% -> 3% of each run, Pallas kernels for 25% -> 25%
where the time goes in v15:
time: 189 us; the launch traced here: 188 us
  waiting for transfers between devices  74.7 us (40%)
  Pallas kernels  51.2 us (27%)
  starting transfers between devices  48.3 us (26%)
  local copies, waits for them, and re-layouts  9.02 us (5%)
  other arithmetic  3.73 us (2%)
    ppermute x50, waiting for transfers between devices, swap(): return lax.ppermute(x, 'ctx', [(i, i ^ bits) for i in range(count)])  69.2 us
    ppermute x50, starting transfers between devices, swap(): return lax.ppermute(x, 'ctx', [(i, i ^ bits) for i in range(count)])  35.5 us
    pallas_call x1, Pallas kernels, body(): pl.pallas_call(functools.partial(backward_kernel, [len(pieces) for pieces...  18.7 us
    pallas_call x1, Pallas kernels, body(): pl.pallas_call(functools.partial(forward_kernel, [len(pieces) for pieces...  13.6 us
    unnamed x77, local copies, waits for them, and re-layouts  7.97 us
    pallas_call x1, Pallas kernels, body(): make_grad(after(line, *before), out_weight, out_grad, *ups, *downs)  7.66 us
    ppermute x2, starting transfers between devices, spread_line(): ups.append(lax.ppermute(ups[-1], 'head', up))  4.97 us
    ppermute x2, waiting for transfers between devices, spread_line(): downs.append(lax.ppermute(downs[-1], 'head', down))  4.76 us
  transfers between devices with their start and end apart: 56, of which 27 were waited for; matrix products, arithmetic and copies ran while one was open for 3% of the time, Pallas kernels for 25%

profile of v15, /device:TPU:0, one launch (start us, length us, event | category | flops | bytes accessed | tf_op | source)
XLA Modules:
  0.0 188.1 jit_solution(16457250126426472731)
XLA Ops:
  2.4 3.0 %collective-permute-start.1 = (bf16[272,1024]{1,0:T(8,128)(2,1)S(1)}, bf16[272,1024]{1,0:T(8,128)(2,1)S(1)}, u32[]{:S(2)}, u32[]{:S(2)}) collective-permute-start(bf16[272,1024]{1,0:T(8,128)(2,1)S(1)} %pack.1.refs_0_), channel_id=1, source_target_pairs={{0,8},{4,12},{8,0},{12,4},{16,24},{20,28},{24,16},{28,20},{1,9},{5... | collective-permute-start | bytes 1671176 | tf_op jit(solution)/shard_map/ppermute | solution.py:504
  6.9 4.3 %collective-permute-start.6 = (bf16[256,1024]{1,0:T(8,128)(2,1)}, bf16[256,1024]{1,0:T(8,128)(2,1)}, u32[]{:S(2)}, u32[]{:S(2)}) collective-permute-start(bf16[256,1024]{1,0:T(8,128)(2,1)} %refs_0_.1), channel_id=1, source_target_pairs={{0,1},{1,2},{2,3},{4,5},{5,6},{6,7},{8,9},{9,10},{10,11},{12,13},{... | collective-permute-start | bytes 1572872 | tf_op jit(solution)/shard_map/ppermute | solution.py:634
  12.6 5.4 %collective-permute-done.1.refs_2_ = bf16[272,1024]{1,0:T(8,128)(2,1)S(1)} collective-permute-done((bf16[272,1024]{1,0:T(8,128)(2,1)S(1)}, bf16[272,1024]{1,0:T(8,128)(2,1)S(1)}, u32[]{:S(2)}, u32[]{:S(2)}) %collective-permute-start.1) | collective-permute-done | bytes 557088 | tf_op jit(solution)/shard_map/ppermute | solution.py:504
  18.1 1.8 collective-permute-start.5
  21.5 4.8 %collective-permute-done.7.refs_4_ = bf16[256,1024]{1,0:T(8,128)(2,1)} collective-permute-done((bf16[256,1024]{1,0:T(8,128)(2,1)}, bf16[256,1024]{1,0:T(8,128)(2,1)}, u32[]{:S(2)}, u32[]{:S(2)}) %collective-permute-start.7) | collective-permute-done | bytes 524320 | tf_op jit(solution)/shard_map/ppermute | solution.py:635
  31.8 13.6 %forward.1 = (bf16[256,1152]{1,0:T(8,128)(2,1)}, bf16[256,1152]{1,0:T(8,128)(2,1)}, bf16[256,1152]{1,0:T(8,128)(2,1)}, bf16[256,1152]{1,0:T(8,128)(2,1)}, bf16[2...) custom-call(s32[1]{0:T(128)} %bitcast.me_ref, ...), custom_call_target="tpu_custom_call" | custom-call | tf_op jit(solution)/shard_map/forward/pallas_call | solution.py:678
  55.3 4.9 %collective-permute-done.18.refs_4_ = bf16[128,1152]{1,0:T(8,128)(2,1)S(1)} collective-permute-done((bf16[128,1152]{1,0:T(8,128)(2,1)S(1)}, bf16[128,1152]{1,0:T(8,128)(2,1)S(1)}, u32[]{:S(2)}, u32[]{:S(2)}) %collective-permute-start.18) | collective-permute-done | bytes 294944 | tf_op jit(solution)/shard_map/ppermute | solution.py:504
  67.1 7.7 %grad.1 = (bf16[256,1024]{1,0:T(8,128)(2,1)}, bf16[8,256,512]{2,1,0:T(8,128)(2,1)}) custom-call(s32[1]{0:T(128)} %bitcast.4.line_ref, bf16[4096,1024]{1,0:T(8,128)(2,1)} %w_ref.1, bf16[256,1024]{1,0:T(8,128)(2,1)} %refs_0_.1, bf16[256,1024]{1,0:T(8,128)(2,1)} %collective-permute-done.6.refs_1_, bf16[256,1024]{1,0:T(8,128)(2,1)} %copy-done.14, ...), custom_call_target="tpu_custom_call" | custom-call | tf_op jit(solution)/shard_map/grad/pallas_call | solution.py:728
  76.0 2.8 %finish.1 = (bf16[256,1024]{1,0:T(8,128)(2,1)S(1)}, bf16[128,1152]{1,0:T(8,128)(2,1)S(1)}, bf16[128,1152]{1,0:T(8,128)(2,1)S(1)}) custom-call(bf16[256,1152]{1,0:T(8,128)(2,1)S(1)} %copy-done.4, bf16[256,1152]{1,0:T(8,128)(2,1)S(1)} %collective-permute-done.15.refs_1_, bf16[128,1152]{1,0:T(8,128)(2,1)S(1)} %collective-permute-done.16.refs_2_, ...), custom_call_target="tpu_custom_call" | custom-call | tf_op jit(solution)/shard_map/finish/pallas_call | solution.py:730
  78.9 1.6 collective-permute-start.26
  83.0 5.9 %collective-permute-done.26.refs_4_ = bf16[128,1152]{1,0:T(8,128)(2,1)S(1)} collective-permute-done((bf16[128,1152]{1,0:T(8,128)(2,1)S(1)}, bf16[128,1152]{1,0:T(8,128)(2,1)S(1)}, u32[]{:S(2)}, u32[]{:S(2)}) %collective-permute-start.26) | collective-permute-done | bytes 294944 | tf_op jit(solution)/shard_map/ppermute | solution.py:504
  91.2 5.5 %collective-permute-done.30.refs_8_ = bf16[128,1152]{1,0:T(8,128)(2,1)S(1)} collective-permute-done((bf16[128,1152]{1,0:T(8,128)(2,1)S(1)}, bf16[128,1152]{1,0:T(8,128)(2,1)S(1)}, u32[]{:S(2)}, u32[]{:S(2)}) %collective-permute-start.30) | collective-permute-done | bytes 294944 | tf_op jit(solution)/shard_map/ppermute | solution.py:504
  96.8 4.4 %collective-permute-done.34.refs_12_ = bf16[128,1152]{1,0:T(8,128)(2,1)S(1)} collective-permute-done((bf16[128,1152]{1,0:T(8,128)(2,1)S(1)}, bf16[128,1152]{1,0:T(8,128)(2,1)S(1)}, u32[]{:S(2)}, u32[]{:S(2)}) %collective-permute-start.34) | collective-permute-done | bytes 294944 | tf_op jit(solution)/shard_map/ppermute | solution.py:504
  102.0 3.8 %all-to-all-start = ((bf16[8,256,512]{2,1,0:T(8,128)(2,1)}), bf16[8,256,512]{2,1,0:T(8,128)(2,1)S(1)}, u32[]{:S(2)}, u32[]{:S(2)}) async-start(bf16[8,256,512]{2,1,0:T(8,128)(2,1)} %get-tuple-element.89), calls=%async_computation | async-start | bytes 4194304 | tf_op jit(solution)/shard_map/all_to_all | solution.py:743
  108.2 2.7 %collective-permute-start.40 = (bf16[256,1024]{1,0:T(8,128)(2,1)S(1)}, bf16[256,1024]{1,0:T(8,128)(2,1)S(1)}, u32[]{:S(2)}, u32[]{:S(2)}) collective-permute-start(bf16[256,1024]{1,0:T(8,128)(2,1)S(1)} %get-tuple-element.105.refs_0_), channel_id=1, source_target_pairs={{0,24},{4,28},{8,16},{12,20},{16,8},{20,12},{24,0},{28,4},{1,25},{... | collective-permute-start | bytes 1572872 | tf_op jit(solution)/shard_map/ppermute | solution.py:504
  115.0 18.7 %backward.1 = (bf16[256,1024]{1,0:T(8,128)(2,1)}, bf16[256,1024]{1,0:T(8,128)(2,1)}, bf16[256,1024]{1,0:T(8,128)(2,1)}, bf16[256,1024]{1,0:T(8,128)(2,1)}, bf16[...) custom-call(f32[16,8,128]{2,1,0:T(8,128)} %get-tuple-element.61.logi, ...), custom_call_target="tpu_custom_call" | custom-call | tf_op jit(solution)/shard_map/backward/pallas_call | solution.py:747
  133.8 10.2 %collective-permute-done.40.refs_6_ = bf16[256,1024]{1,0:T(8,128)(2,1)S(1)} collective-permute-done((bf16[256,1024]{1,0:T(8,128)(2,1)S(1)}, bf16[256,1024]{1,0:T(8,128)(2,1)S(1)}, u32[]{:S(2)}, u32[]{:S(2)}) %collective-permute-start.40) | collective-permute-done | bytes 524320 | tf_op jit(solution)/shard_map/ppermute | solution.py:504
  143.9 9.8 %collective-permute-done.39.refs_4_ = bf16[256,1024]{1,0:T(8,128)(2,1)S(1)} collective-permute-done((bf16[256,1024]{1,0:T(8,128)(2,1)S(1)}, bf16[256,1024]{1,0:T(8,128)(2,1)S(1)}, u32[]{:S(2)}, u32[]{:S(2)}) %collective-permute-start.39) | collective-permute-done | bytes 524320 | tf_op jit(solution)/shard_map/ppermute | solution.py:504
  161.1 1.7 collective-permute-start.44
  163.3 4.9 %collective-permute-done.43.refs_2_ = bf16[128,1024]{1,0:T(8,128)(2,1)S(1)} collective-permute-done((bf16[128,1024]{1,0:T(8,128)(2,1)S(1)}, bf16[128,1024]{1,0:T(8,128)(2,1)S(1)}, u32[]{:S(2)}, u32[]{:S(2)}) %collective-permute-start.43) | collective-permute-done | bytes 262176 | tf_op jit(solution)/shard_map/ppermute | solution.py:504
  168.3 1.7 collective-permute-done.46.refs_5_
  169.9 4.5 %collective-permute-done.44 = bf16[128,1024]{1,0:T(8,128)(2,1)S(1)} collective-permute-done((bf16[128,1024]{1,0:T(8,128)(2,1)S(1)}, bf16[128,1024]{1,0:T(8,128)(2,1)S(1)}, u32[]{:S(2)}, u32[]{:S(2)}) %collective-permute-start.44) | collective-permute-done | bytes 262176 | tf_op jit(solution)/shard_map/ppermute | solution.py:504
  178.9 4.7 %weight.1 = f32[512,1024]{1,0:T(8,128)} custom-call(s32[1]{0:T(128)} %bitcast.me_ref, bf16[8,256,512]{2,1,0:T(8,128)(2,1)S(1)} %all-to-all-done.cols_ref, bf16[256,1024]{1,0:T(8,128)(2,1)S(1)} %get-tuple-element.105.refs_0_, bf16[256,1024]{1,0:T(8,128)(2,1)S(1)} %collective-permute-done.48.refs_1_, bf16[256,1024]{1,0:T(8,128)(2,1)} %collective-permute-done.38.refs_2_, ...), custom_call_target="tpu_custom_call" | custom-call | tf_op jit(solution)/shard_map/weight/pallas_call | solution.py:777
  185.0 1.7 collective-permute-done.54.refs_4_
  (184 shorter events, 56.8 us)
Async XLA Ops:
  2.4 15.6 %collective-permute-start.1 = (bf16[272,1024]{1,0:T(8,128)(2,1)S(1)}, bf16[272,1024]{1,0:T(8,128)(2,1)S(1)}, u32[]{:S(2)}, u32[]{:S(2)}) collective-permute-start(bf16[272,1024]{1,0:T(8,128)(2,1)S(1)} %pack.1.refs_0_), channel_id=1, source_target_pairs={{0,8},{4,12},{8,0},{12,4},{16,24},{20,28},{24,16},{28,20},{1,9},{5... | collective-permute-start | bytes 1671176 | tf_op jit(solution)/shard_map/ppermute | solution.py:504
  5.4 14.5 %collective-permute-start.3 = (bf16[272,1024]{1,0:T(8,128)(2,1)S(1)}, bf16[272,1024]{1,0:T(8,128)(2,1)S(1)}, u32[]{:S(2)}, u32[]{:S(2)}) collective-permute-start(bf16[272,1024]{1,0:T(8,128)(2,1)S(1)} %pack.1.refs_0_), channel_id=1, source_target_pairs={{0,16},{4,20},{8,24},{12,28},{16,0},{20,4},{24,8},{28,12},{1,17},{... | collective-permute-start | bytes 1671176 | tf_op jit(solution)/shard_map/ppermute | solution.py:504
  6.9 14.6 %collective-permute-start.6 = (bf16[256,1024]{1,0:T(8,128)(2,1)}, bf16[256,1024]{1,0:T(8,128)(2,1)}, u32[]{:S(2)}, u32[]{:S(2)}) collective-permute-start(bf16[256,1024]{1,0:T(8,128)(2,1)} %refs_0_.1), channel_id=1, source_target_pairs={{0,1},{1,2},{2,3},{4,5},{5,6},{6,7},{8,9},{9,10},{10,11},{12,13},{... | collective-permute-start | bytes 1572872 | tf_op jit(solution)/shard_map/ppermute | solution.py:634
  11.2 15.0 %collective-permute-start.7 = (bf16[256,1024]{1,0:T(8,128)(2,1)}, bf16[256,1024]{1,0:T(8,128)(2,1)}, u32[]{:S(2)}, u32[]{:S(2)}) collective-permute-start(bf16[256,1024]{1,0:T(8,128)(2,1)} %refs_0_.1), channel_id=1, source_target_pairs={{1,0},{2,1},{3,2},{5,4},{6,5},{7,6},{9,8},{10,9},{11,10},{13,12},{... | collective-permute-start | bytes 1572872 | tf_op jit(solution)/shard_map/ppermute | solution.py:635
  12.5 14.3 %collective-permute-start = (bf16[272,1024]{1,0:T(8,128)(2,1)S(1)}, bf16[272,1024]{1,0:T(8,128)(2,1)S(1)}, u32[]{:S(2)}, u32[]{:S(2)}) collective-permute-start(bf16[272,1024]{1,0:T(8,128)(2,1)S(1)} %pack.1.refs_0_), channel_id=1, source_target_pairs={{0,4},{4,0},{8,12},{12,8},{16,20},{20,16},{24,28},{28,24},{1,5},{5... | collective-permute-start | bytes 1671176 | tf_op jit(solution)/shard_map/ppermute | solution.py:504
  21.5 10.0 %collective-permute-start.4 = (bf16[272,1024]{1,0:T(8,128)(2,1)S(1)}, bf16[272,1024]{1,0:T(8,128)(2,1)}, u32[]{:S(2)}, u32[]{:S(2)}) collective-permute-start(bf16[272,1024]{1,0:T(8,128)(2,1)S(1)} %collective-permute-done.3.refs_4_), channel_id=1, source_target_pairs={{0,4},{4,0},{8,12},{12,8},{16,20},{20,16},{24,28},{28,24},{1,5},{5... | collective-permute-start | bytes 1671176 | tf_op jit(solution)/shard_map/ppermute | solution.py:504
  26.8 18.6 %collective-permute-start.11 = (bf16[256,1024]{1,0:T(8,128)(2,1)}, bf16[256,1024]{1,0:T(8,128)(2,1)S(1)}, u32[]{:S(2)}, u32[]{:S(2)}) collective-permute-start(bf16[256,1024]{1,0:T(8,128)(2,1)} %collective-permute-done.6.refs_1_), channel_id=1, source_target_pairs={{1,2},{2,3},{5,6},{6,7},{9,10},{10,11},{13,14},{14,15},{17,18},{18... | collective-permute-start | bytes 1572872 | tf_op jit(solution)/shard_map/ppermute | solution.py:634
  27.8 17.6 %collective-permute-start.12 = (bf16[256,1024]{1,0:T(8,128)(2,1)}, bf16[256,1024]{1,0:T(8,128)(2,1)S(1)}, u32[]{:S(2)}, u32[]{:S(2)}) collective-permute-start(bf16[256,1024]{1,0:T(8,128)(2,1)} %collective-permute-done.7.refs_4_), channel_id=1, source_target_pairs={{1,0},{2,1},{5,4},{6,5},{9,8},{10,9},{13,12},{14,13},{17,16},{18,1... | collective-permute-start | bytes 1572872 | tf_op jit(solution)/shard_map/ppermute | solution.py:635
  47.8 17.8 %collective-permute-start.23 = (bf16[256,1024]{1,0:T(8,128)(2,1)S(1)}, bf16[256,1024]{1,0:T(8,128)(2,1)S(1)}, u32[]{:S(2)}, u32[]{:S(2)}) collective-permute-start(bf16[256,1024]{1,0:T(8,128)(2,1)S(1)} %broadcast_select_fusion), channel_id=1, source_target_pairs={{2,3},{1,0},{6,7},{5,4},{10,11},{9,8},{14,15},{13,12},{18,19},{17,... | collective-permute-start | bytes 1572872 | tf_op jit(solution)/shard_map/ppermute | solution.py:630
  54.7 20.3 %collective-permute-start.15 = (bf16[256,1152]{1,0:T(8,128)(2,1)}, bf16[256,1152]{1,0:T(8,128)(2,1)S(1)}, u32[]{:S(2)}, u32[]{:S(2)}) collective-permute-start(bf16[256,1152]{1,0:T(8,128)(2,1)} %get-tuple-element.74), channel_id=1, source_target_pairs={{0,4},{4,0},{8,12},{12,8},{16,20},{20,16},{24,28},{28,24},{1,5},{5... | collective-permute-start | bytes 1769480 | tf_op jit(solution)/shard_map/ppermute | solution.py:504
  54.7 20.0 %collective-permute-start.16 = (bf16[128,1152]{1,0:T(8,128)(2,1)S(1)}, bf16[128,1152]{1,0:T(8,128)(2,1)S(1)}, u32[]{:S(2)}, u32[]{:S(2)}) collective-permute-start(bf16[128,1152]{1,0:T(8,128)(2,1)S(1)} %get-tuple-element.73), channel_id=1, source_target_pairs={{0,8},{4,12},{8,0},{12,4},{16,24},{20,28},{24,16},{28,20},{1,9},{5... | collective-permute-start | bytes 884744 | tf_op jit(solution)/shard_map/ppermute | solution.py:504
  60.3 14.5 %collective-permute-start.22 = (bf16[128,1152]{1,0:T(8,128)(2,1)S(1)}, bf16[128,1152]{1,0:T(8,128)(2,1)S(1)}, u32[]{:S(2)}, u32[]{:S(2)}) collective-permute-start(bf16[128,1152]{1,0:T(8,128)(2,1)S(1)} %get-tuple-element.82), channel_id=1, source_target_pairs={{0,16},{4,20},{8,24},{12,28},{16,0},{20,4},{24,8},{28,12},{1,17},{... | collective-permute-start | bytes 884744 | tf_op jit(solution)/shard_map/ppermute | solution.py:504
  63.3 11.5 %collective-permute-start.20 = (bf16[128,1152]{1,0:T(8,128)(2,1)S(1)}, bf16[128,1152]{1,0:T(8,128)(2,1)S(1)}, u32[]{:S(2)}, u32[]{:S(2)}) collective-permute-start(bf16[128,1152]{1,0:T(8,128)(2,1)S(1)} %get-tuple-element.80), channel_id=1, source_target_pairs={{0,8},{4,12},{8,0},{12,4},{16,24},{20,28},{24,16},{28,20},{1,9},{5... | collective-permute-start | bytes 884744 | tf_op jit(solution)/shard_map/ppermute | solution.py:504
  78.9 10.0 %collective-permute-start.26 = (bf16[128,1152]{1,0:T(8,128)(2,1)S(1)}, bf16[128,1152]{1,0:T(8,128)(2,1)S(1)}, u32[]{:S(2)}, u32[]{:S(2)}) collective-permute-start(bf16[128,1152]{1,0:T(8,128)(2,1)S(1)} %get-tuple-element.85.refs_0_), channel_id=1, source_target_pairs={{0,8},{4,12},{8,0},{12,4},{16,24},{20,28},{24,16},{28,20},{1,9},{5... | collective-permute-start | bytes 884744 | tf_op jit(solution)/shard_map/ppermute | solution.py:504
  81.3 15.5 %collective-permute-start.30 = (bf16[128,1152]{1,0:T(8,128)(2,1)S(1)}, bf16[128,1152]{1,0:T(8,128)(2,1)S(1)}, u32[]{:S(2)}, u32[]{:S(2)}) collective-permute-start(bf16[128,1152]{1,0:T(8,128)(2,1)S(1)} %get-tuple-element.85.refs_0_), channel_id=1, source_target_pairs={{0,16},{4,20},{8,24},{12,28},{16,0},{20,4},{24,8},{28,12},{1,17},{... | collective-permute-start | bytes 884744 | tf_op jit(solution)/shard_map/ppermute | solution.py:504
  82.5 14.2 %collective-permute-start.27 = (bf16[128,1152]{1,0:T(8,128)(2,1)S(1)}, bf16[128,1152]{1,0:T(8,128)(2,1)S(1)}, u32[]{:S(2)}, u32[]{:S(2)}) collective-permute-start(bf16[128,1152]{1,0:T(8,128)(2,1)S(1)} %get-tuple-element.86.refs_1_), channel_id=1, source_target_pairs={{0,8},{4,12},{8,0},{12,4},{16,24},{20,28},{24,16},{28,20},{1,9},{5... | collective-permute-start | bytes 884744 | tf_op jit(solution)/shard_map/ppermute | solution.py:504
  88.9 12.3 %collective-permute-start.34 = (bf16[128,1152]{1,0:T(8,128)(2,1)S(1)}, bf16[128,1152]{1,0:T(8,128)(2,1)S(1)}, u32[]{:S(2)}, u32[]{:S(2)}) collective-permute-start(bf16[128,1152]{1,0:T(8,128)(2,1)S(1)} %collective-permute-done.26.refs_4_), channel_id=1, source_target_pairs={{0,16},{4,20},{8,24},{12,28},{16,0},{20,4},{24,8},{28,12},{1,17},{... | collective-permute-start | bytes 884744 | tf_op jit(solution)/shard_map/ppermute | solution.py:504
  90.4 10.7 %collective-permute-start.35 = (bf16[128,1152]{1,0:T(8,128)(2,1)S(1)}, bf16[128,1152]{1,0:T(8,128)(2,1)S(1)}, u32[]{:S(2)}, u32[]{:S(2)}) collective-permute-start(bf16[128,1152]{1,0:T(8,128)(2,1)S(1)} %collective-permute-done.31.refs_9_), channel_id=1, source_target_pairs={{0,8},{4,12},{8,0},{12,4},{16,24},{20,28},{24,16},{28,20},{1,9},{5... | collective-permute-start | bytes 884744 | tf_op jit(solution)/shard_map/ppermute | solution.py:504
  102.0 52.5 %all-to-all-start = ((bf16[8,256,512]{2,1,0:T(8,128)(2,1)}), bf16[8,256,512]{2,1,0:T(8,128)(2,1)S(1)}, u32[]{:S(2)}, u32[]{:S(2)}) async-start(bf16[8,256,512]{2,1,0:T(8,128)(2,1)} %get-tuple-element.89), calls=%async_computation | async-start | bytes 4194304 | tf_op jit(solution)/shard_map/all_to_all | solution.py:743
  108.2 35.7 %collective-permute-start.40 = (bf16[256,1024]{1,0:T(8,128)(2,1)S(1)}, bf16[256,1024]{1,0:T(8,128)(2,1)S(1)}, u32[]{:S(2)}, u32[]{:S(2)}) collective-permute-start(bf16[256,1024]{1,0:T(8,128)(2,1)S(1)} %get-tuple-element.105.refs_0_), channel_id=1, source_target_pairs={{0,24},{4,28},{8,16},{12,20},{16,8},{20,12},{24,0},{28,4},{1,25},{... | collective-permute-start | bytes 1572872 | tf_op jit(solution)/shard_map/ppermute | solution.py:504
  110.9 42.8 %collective-permute-start.39 = (bf16[256,1024]{1,0:T(8,128)(2,1)S(1)}, bf16[256,1024]{1,0:T(8,128)(2,1)S(1)}, u32[]{:S(2)}, u32[]{:S(2)}) collective-permute-start(bf16[256,1024]{1,0:T(8,128)(2,1)S(1)} %get-tuple-element.105.refs_0_), channel_id=1, source_target_pairs={{0,16},{4,20},{8,24},{12,28},{16,0},{20,4},{24,8},{28,12},{1,17},{... | collective-permute-start | bytes 1572872 | tf_op jit(solution)/shard_map/ppermute | solution.py:504
  111.5 43.0 %collective-permute-start.38 = (bf16[256,1024]{1,0:T(8,128)(2,1)S(1)}, bf16[256,1024]{1,0:T(8,128)(2,1)}, u32[]{:S(2)}, u32[]{:S(2)}) collective-permute-start(bf16[256,1024]{1,0:T(8,128)(2,1)S(1)} %get-tuple-element.105.refs_0_), channel_id=1, source_target_pairs={{0,8},{4,12},{8,0},{12,4},{16,24},{20,28},{24,16},{28,20},{1,9},{5... | collective-permute-start | bytes 1572872 | tf_op jit(solution)/shard_map/ppermute | solution.py:504
  161.1 13.3 %collective-permute-start.44 = (bf16[128,1024]{1,0:T(8,128)(2,1)S(1)}, bf16[128,1024]{1,0:T(8,128)(2,1)S(1)}, u32[]{:S(2)}, u32[]{:S(2)}) collective-permute-start(bf16[128,1024]{1,0:T(8,128)(2,1)S(1)} %get-tuple-element.115), channel_id=1, source_target_pairs={{0,16},{4,20},{8,24},{12,28},{16,0},{20,4},{24,8},{28,12},{1,17},{... | collective-permute-start | bytes 786440 | tf_op jit(solution)/shard_map/ppermute | solution.py:504
  162.8 11.8 %collective-permute-start.47 = (bf16[128,1024]{1,0:T(8,128)(2,1)S(1)}, bf16[128,1024]{1,0:T(8,128)(2,1)S(1)}, u32[]{:S(2)}, u32[]{:S(2)}) collective-permute-start(bf16[128,1024]{1,0:T(8,128)(2,1)S(1)} %get-tuple-element.114), channel_id=1, source_target_pairs={{0,8},{4,12},{8,0},{12,4},{16,24},{20,28},{24,16},{28,20},{1,9},{5... | collective-permute-start | bytes 786440 | tf_op jit(solution)/shard_map/ppermute | solution.py:504
  (70 other events, 471.2 us)

commit v16 on v13

--- a/solution.py
+++ b/solution.py
@@ -575,10 +575,11 @@
     x_sum, y_sum = both(3, top), both(3, low)
     x_far, y_far = swap(x_sum, 2), swap(y_sum, 4)
     x_sum, y_sum = both(1, top, None, x_sum), both(2, low, None, y_sum)
+    near_sums = [x_sum, y_sum]
     x_top, y_low = swap(x_sum, 2), swap(y_sum, 4)
     x_sum, y_sum = both(1, low, y_far, x_sum), both(2, top, x_far, y_sum)
     x_low, y_top = swap(x_sum, 2), swap(y_sum, 4)
-    return terms + [[x_top, x_low], [y_top, y_low]], [x_sum, y_sum]
+    return terms + [[x_top, x_low], [y_top, y_low]], near_sums
 
 
 def merge_chips(parts, received, heads, between):
@@ -740,7 +741,6 @@
     grad_chips = spread_halves(*extended)
     grad_all = with_cores(grad_chips)
     arrived = flat(grad_chips[1:])
-    attns = spread_near(after(attn_out, *flat(grad_chips[1:3])))
     columns = lax.all_to_all(
         after(blocks, *arrived), "ctx", split_axis=0, concat_axis=0, tiled=True
     )
@@ -772,10 +772,9 @@
         name="backward",
     )(logits, hot, q_slots, probs, keys, values, *flat(grad_all))
     key_grad, value_grad = outs[chunks:]
-    received = from_core(outs[:chunks], columns, *flat(attns[1:3]))
-    terms, last_sums = collect_chips(outs[:chunks], received)
-    near = [[after(x, *last_sums) for x in pieces] for pieces in attns]
-    attns = with_cores(spread_far(near, rows // 2, terms[2][0], terms[-1][-1]))
+    received = from_core(outs[:chunks], columns)
+    terms, near_sums = collect_chips(outs[:chunks], received)
+    attns = with_cores(spread_chips(after(attn_out, *near_sums), rows // 2))
 
     def weight_part(chosen, first, when, *before):
         return pl.pallas_call(
@@ -787,7 +786,7 @@
             name="weight",
         )(when, columns, *flat(chosen), *before)
 
-    weight_near = weight_part(attns[:-2], 0, after(me, terms[2][0]))
+    weight_near = weight_part(attns[:-2], 0, me)
     query_grad = pl.pallas_call(
         functools.partial(total_kernel, [len(pieces) for pieces in terms]),
         out_shape=shaped((rows, width), F32),
@@ -795,8 +794,8 @@
         out_specs=vmem,
         compiler_params=small,
         name="total",
-    )(after(terms[0][0], weight_near), *flat(terms[1:]))
-    weight_grad = weight_part(attns[-2:], chunks - 2, after(me, query_grad), weight_near)
+    )(*flat(terms))
+    weight_grad = weight_part(attns[-2:], chunks - 2, me, weight_near)
     return (
         query_grad,
         key_grad.reshape(-1, width),

time: 185 us -> 188 us (1.016)
  waiting for transfers between devices: 67.9 us -> 75.7 us
  starting transfers between devices: 51.2 us -> 47.6 us
    ppermute x52, waiting for transfers between devices: 62.3 us -> 68.1 us  [swap(): return lax.ppermute(x, 'ctx', [(i, i ^ bits) for i in range(count)])]
    ppermute x52, starting transfers between devices: 38.4 us -> 34.8 us  [swap(): return lax.ppermute(x, 'ctx', [(i, i ^ bits) for i in range(count)])]
    all_to_all x1, waiting for transfers between devices: 0.01 us -> 1.98 us  [body(): lax.all_to_all(after(blocks, *arrived), 'ctx', split_axis=0, concat_axis=...]
    unnamed x71 -> x69, local copies, waits for them, and re-layouts: 7.43 us -> 7.43 us
  transfers between devices with their start and end apart: 58 -> 58, of which waited for: 26 -> 27; matrix products, arithmetic and copies ran while one was open for 2% -> 2% of each run, Pallas kernels for 25% -> 24%
where the time goes in v16:
time: 188 us; the launch traced here: 186 us
  waiting for transfers between devices  75.7 us (40%)
  Pallas kernels  50.3 us (27%)
  starting transfers between devices  47.6 us (25%)
  local copies, waits for them, and re-layouts  8.53 us (5%)
  other arithmetic  2.61 us (1%)
    ppermute x52, waiting for transfers between devices, swap(): return lax.ppermute(x, 'ctx', [(i, i ^ bits) for i in range(count)])  68.1 us
    ppermute x52, starting transfers between devices, swap(): return lax.ppermute(x, 'ctx', [(i, i ^ bits) for i in range(count)])  34.8 us
    pallas_call x1, Pallas kernels, body(): pl.pallas_call(functools.partial(backward_kernel, [len(pieces) for pieces...  18.7 us
    pallas_call x1, Pallas kernels, body(): pl.pallas_call(functools.partial(forward_kernel, [len(pieces) for pieces...  13.5 us
    pallas_call x1, Pallas kernels, body(): make_grad(after(line, *before), out_weight, out_grad, *ups, *downs)  7.68 us
    unnamed x69, local copies, waits for them, and re-layouts  7.43 us
    ppermute x2, starting transfers between devices, spread_line(): ups.append(lax.ppermute(ups[-1], 'head', up))  4.98 us
    ppermute x2, waiting for transfers between devices, spread_line(): downs.append(lax.ppermute(downs[-1], 'head', down))  4.77 us
  transfers between devices with their start and end apart: 58, of which 27 were waited for; matrix products, arithmetic and copies ran while one was open for 2% of the time, Pallas kernels for 24%

profile of v16, /device:TPU:0, one launch (start us, length us, event | category | flops | bytes accessed | tf_op | source)
XLA Modules:
  0.0 185.9 jit_solution(7326870036575755831)
XLA Ops:
  2.4 3.0 %collective-permute-start.1 = (bf16[272,1024]{1,0:T(8,128)(2,1)S(1)}, bf16[272,1024]{1,0:T(8,128)(2,1)S(1)}, u32[]{:S(2)}, u32[]{:S(2)}) collective-permute-start(bf16[272,1024]{1,0:T(8,128)(2,1)S(1)} %pack.1.refs_0_), channel_id=1, source_target_pairs={{0,8},{4,12},{8,0},{12,4},{16,24},{20,28},{24,16},{28,20},{1,9},{5... | collective-permute-start | bytes 1671176 | tf_op jit(solution)/shard_map/ppermute | solution.py:507
  6.9 4.3 %collective-permute-start.6 = (bf16[256,1024]{1,0:T(8,128)(2,1)}, bf16[256,1024]{1,0:T(8,128)(2,1)}, u32[]{:S(2)}, u32[]{:S(2)}) collective-permute-start(bf16[256,1024]{1,0:T(8,128)(2,1)} %refs_0_.1), channel_id=1, source_target_pairs={{0,1},{1,2},{2,3},{4,5},{5,6},{6,7},{8,9},{9,10},{10,11},{12,13},{... | collective-permute-start | bytes 1572872 | tf_op jit(solution)/shard_map/ppermute | solution.py:637
  12.6 5.4 %collective-permute-done.1.refs_2_ = bf16[272,1024]{1,0:T(8,128)(2,1)S(1)} collective-permute-done((bf16[272,1024]{1,0:T(8,128)(2,1)S(1)}, bf16[272,1024]{1,0:T(8,128)(2,1)S(1)}, u32[]{:S(2)}, u32[]{:S(2)}) %collective-permute-start.1) | collective-permute-done | bytes 557088 | tf_op jit(solution)/shard_map/ppermute | solution.py:507
  18.1 1.8 collective-permute-start.5
  21.5 4.8 %collective-permute-done.7.refs_4_ = bf16[256,1024]{1,0:T(8,128)(2,1)} collective-permute-done((bf16[256,1024]{1,0:T(8,128)(2,1)}, bf16[256,1024]{1,0:T(8,128)(2,1)}, u32[]{:S(2)}, u32[]{:S(2)}) %collective-permute-start.7) | collective-permute-done | bytes 524320 | tf_op jit(solution)/shard_map/ppermute | solution.py:638
  31.8 13.5 %forward.1 = (bf16[256,1152]{1,0:T(8,128)(2,1)}, bf16[256,1152]{1,0:T(8,128)(2,1)}, bf16[256,1152]{1,0:T(8,128)(2,1)}, bf16[256,1152]{1,0:T(8,128)(2,1)}, bf16[2...) custom-call(s32[1]{0:T(128)} %bitcast.me_ref, ...), custom_call_target="tpu_custom_call" | custom-call | tf_op jit(solution)/shard_map/forward/pallas_call | solution.py:681
  53.7 5.1 %collective-permute-done.18.refs_4_ = bf16[128,1152]{1,0:T(8,128)(2,1)S(1)} collective-permute-done((bf16[128,1152]{1,0:T(8,128)(2,1)S(1)}, bf16[128,1152]{1,0:T(8,128)(2,1)S(1)}, u32[]{:S(2)}, u32[]{:S(2)}) %collective-permute-start.18) | collective-permute-done | bytes 294944 | tf_op jit(solution)/shard_map/ppermute | solution.py:507
  65.6 7.7 %grad.1 = (bf16[256,1024]{1,0:T(8,128)(2,1)}, bf16[8,256,512]{2,1,0:T(8,128)(2,1)}) custom-call(s32[1]{0:T(128)} %bitcast.4.line_ref, bf16[4096,1024]{1,0:T(8,128)(2,1)} %w_ref.1, bf16[256,1024]{1,0:T(8,128)(2,1)} %refs_0_.1, bf16[256,1024]{1,0:T(8,128)(2,1)} %collective-permute-done.6.refs_1_, bf16[256,1024]{1,0:T(8,128)(2,1)} %copy-done.12, ...), custom_call_target="tpu_custom_call" | custom-call | tf_op jit(solution)/shard_map/grad/pallas_call | solution.py:731
  74.6 2.8 %finish.1 = (bf16[256,1024]{1,0:T(8,128)(2,1)S(1)}, bf16[128,1152]{1,0:T(8,128)(2,1)S(1)}, bf16[128,1152]{1,0:T(8,128)(2,1)S(1)}) custom-call(bf16[256,1152]{1,0:T(8,128)(2,1)S(1)} %copy-done.4, bf16[256,1152]{1,0:T(8,128)(2,1)S(1)} %collective-permute-done.13.refs_1_, bf16[128,1152]{1,0:T(8,128)(2,1)S(1)} %collective-permute-done.16.refs_2_, ...), custom_call_target="tpu_custom_call" | custom-call | tf_op jit(solution)/shard_map/finish/pallas_call | solution.py:733
  81.6 5.9 %collective-permute-done.26.refs_4_ = bf16[128,1152]{1,0:T(8,128)(2,1)S(1)} collective-permute-done((bf16[128,1152]{1,0:T(8,128)(2,1)S(1)}, bf16[128,1152]{1,0:T(8,128)(2,1)S(1)}, u32[]{:S(2)}, u32[]{:S(2)}) %collective-permute-start.26) | collective-permute-done | bytes 294944 | tf_op jit(solution)/shard_map/ppermute | solution.py:507
  90.1 5.2 %collective-permute-done.30.refs_8_ = bf16[128,1152]{1,0:T(8,128)(2,1)} collective-permute-done((bf16[128,1152]{1,0:T(8,128)(2,1)S(1)}, bf16[128,1152]{1,0:T(8,128)(2,1)}, u32[]{:S(2)}, u32[]{:S(2)}) %collective-permute-start.30) | collective-permute-done | bytes 294944 | tf_op jit(solution)/shard_map/ppermute | solution.py:507
  95.4 4.4 %collective-permute-done.34.refs_12_ = bf16[128,1152]{1,0:T(8,128)(2,1)S(1)} collective-permute-done((bf16[128,1152]{1,0:T(8,128)(2,1)S(1)}, bf16[128,1152]{1,0:T(8,128)(2,1)S(1)}, u32[]{:S(2)}, u32[]{:S(2)}) %collective-permute-start.34) | collective-permute-done | bytes 294944 | tf_op jit(solution)/shard_map/ppermute | solution.py:507
  101.2 3.8 %all-to-all-start = ((bf16[8,256,512]{2,1,0:T(8,128)(2,1)}), bf16[8,256,512]{2,1,0:T(8,128)(2,1)S(1)}, u32[]{:S(2)}, u32[]{:S(2)}) async-start(bf16[8,256,512]{2,1,0:T(8,128)(2,1)} %get-tuple-element.85), calls=%async_computation | async-start | bytes 4194304 | tf_op jit(solution)/shard_map/all_to_all | solution.py:744
  110.7 18.7 %backward.1 = (bf16[256,1024]{1,0:T(8,128)(2,1)}, bf16[256,1024]{1,0:T(8,128)(2,1)}, bf16[256,1024]{1,0:T(8,128)(2,1)}, bf16[256,1024]{1,0:T(8,128)(2,1)}, bf16[...) custom-call(f32[16,8,128]{2,1,0:T(8,128)} %get-tuple-element.56.logi, ...), custom_call_target="tpu_custom_call" | custom-call | tf_op jit(solution)/shard_map/backward/pallas_call | solution.py:748
  129.4 2.0 %all-to-all-done.cols_ref = bf16[8,256,512]{2,1,0:T(8,128)(2,1)S(1)} async-done(((bf16[8,256,512]{2,1,0:T(8,128)(2,1)}), bf16[8,256,512]{2,1,0:T(8,128)(2,1)S(1)}, u32[]{:S(2)}, u32[]{:S(2)}) %all-to-all-start) | async-done | bytes 2097184 | tf_op jit(solution)/shard_map/all_to_all | solution.py:744
  140.0 3.9 %collective-permute-done.42 = bf16[128,1024]{1,0:T(8,128)(2,1)S(1)} collective-permute-done((bf16[128,1024]{1,0:T(8,128)(2,1)S(1)}, bf16[128,1024]{1,0:T(8,128)(2,1)S(1)}, u32[]{:S(2)}, u32[]{:S(2)}) %collective-permute-start.42) | collective-permute-done | bytes 262176 | tf_op jit(solution)/shard_map/ppermute | solution.py:507
  144.6 12.4 %collective-permute-done.45 = bf16[128,1024]{1,0:T(8,128)(2,1)S(1)} collective-permute-done((bf16[128,1024]{1,0:T(8,128)(2,1)S(1)}, bf16[128,1024]{1,0:T(8,128)(2,1)S(1)}, u32[]{:S(2)}, u32[]{:S(2)}) %collective-permute-start.45) | collective-permute-done | bytes 262176 | tf_op jit(solution)/shard_map/ppermute | solution.py:507
  157.7 1.6 collective-permute-start.43
  160.8 5.4 %collective-permute-done.41.refs_2_ = bf16[128,1024]{1,0:T(8,128)(2,1)S(1)} collective-permute-done((bf16[128,1024]{1,0:T(8,128)(2,1)S(1)}, bf16[128,1024]{1,0:T(8,128)(2,1)S(1)}, u32[]{:S(2)}, u32[]{:S(2)}) %collective-permute-start.41) | collective-permute-done | bytes 262176 | tf_op jit(solution)/shard_map/ppermute | solution.py:507
  166.3 5.6 %collective-permute-done.43.refs_3_ = bf16[128,1024]{1,0:T(8,128)(2,1)S(1)} collective-permute-done((bf16[128,1024]{1,0:T(8,128)(2,1)S(1)}, bf16[128,1024]{1,0:T(8,128)(2,1)S(1)}, u32[]{:S(2)}, u32[]{:S(2)}) %collective-permute-start.43) | collective-permute-done | bytes 262176 | tf_op jit(solution)/shard_map/ppermute | solution.py:507
  172.4 2.7 %collective-permute-done.51.refs_1_ = bf16[128,1024]{1,0:T(8,128)(2,1)S(1)} collective-permute-done((bf16[128,1024]{1,0:T(8,128)(2,1)S(1)}, bf16[128,1024]{1,0:T(8,128)(2,1)S(1)}, u32[]{:S(2)}, u32[]{:S(2)}) %collective-permute-start.51) | collective-permute-done | bytes 262176 | tf_op jit(solution)/shard_map/ppermute | solution.py:507
  175.1 5.5 %collective-permute-done.49.refs_0_ = bf16[128,1024]{1,0:T(8,128)(2,1)S(1)} collective-permute-done((bf16[128,1024]{1,0:T(8,128)(2,1)S(1)}, bf16[128,1024]{1,0:T(8,128)(2,1)S(1)}, u32[]{:S(2)}, u32[]{:S(2)}) %collective-permute-start.49) | collective-permute-done | bytes 262176 | tf_op jit(solution)/shard_map/ppermute | solution.py:507
  182.0 1.8 weight.2.refs_4_
  183.8 2.1 %weight.3 = f32[512,1024]{1,0:T(8,128)} custom-call(s32[1]{0:T(128)} %bitcast.me_ref, bf16[8,256,512]{2,1,0:T(8,128)(2,1)S(1)} %all-to-all-done.cols_ref, bf16[128,1024]{1,0:T(8,128)(2,1)S(1)} %collective-permute-done.49.refs_0_, bf16[128,1024]{1,0:T(8,128)(2,1)S(1)} %collective-permute-done.51.refs_1_, ...), custom_call_target="tpu_custom_call" | custom-call | tf_op jit(solution)/shard_map/weight/pallas_call | solution.py:780
  (183 shorter events, 55.2 us)
Async XLA Ops:
  2.4 15.6 %collective-permute-start.1 = (bf16[272,1024]{1,0:T(8,128)(2,1)S(1)}, bf16[272,1024]{1,0:T(8,128)(2,1)S(1)}, u32[]{:S(2)}, u32[]{:S(2)}) collective-permute-start(bf16[272,1024]{1,0:T(8,128)(2,1)S(1)} %pack.1.refs_0_), channel_id=1, source_target_pairs={{0,8},{4,12},{8,0},{12,4},{16,24},{20,28},{24,16},{28,20},{1,9},{5... | collective-permute-start | bytes 1671176 | tf_op jit(solution)/shard_map/ppermute | solution.py:507
  5.4 14.5 %collective-permute-start.3 = (bf16[272,1024]{1,0:T(8,128)(2,1)S(1)}, bf16[272,1024]{1,0:T(8,128)(2,1)S(1)}, u32[]{:S(2)}, u32[]{:S(2)}) collective-permute-start(bf16[272,1024]{1,0:T(8,128)(2,1)S(1)} %pack.1.refs_0_), channel_id=1, source_target_pairs={{0,16},{4,20},{8,24},{12,28},{16,0},{20,4},{24,8},{28,12},{1,17},{... | collective-permute-start | bytes 1671176 | tf_op jit(solution)/shard_map/ppermute | solution.py:507
  6.9 14.6 %collective-permute-start.6 = (bf16[256,1024]{1,0:T(8,128)(2,1)}, bf16[256,1024]{1,0:T(8,128)(2,1)}, u32[]{:S(2)}, u32[]{:S(2)}) collective-permute-start(bf16[256,1024]{1,0:T(8,128)(2,1)} %refs_0_.1), channel_id=1, source_target_pairs={{0,1},{1,2},{2,3},{4,5},{5,6},{6,7},{8,9},{9,10},{10,11},{12,13},{... | collective-permute-start | bytes 1572872 | tf_op jit(solution)/shard_map/ppermute | solution.py:637
  11.2 15.0 %collective-permute-start.7 = (bf16[256,1024]{1,0:T(8,128)(2,1)}, bf16[256,1024]{1,0:T(8,128)(2,1)}, u32[]{:S(2)}, u32[]{:S(2)}) collective-permute-start(bf16[256,1024]{1,0:T(8,128)(2,1)} %refs_0_.1), channel_id=1, source_target_pairs={{1,0},{2,1},{3,2},{5,4},{6,5},{7,6},{9,8},{10,9},{11,10},{13,12},{... | collective-permute-start | bytes 1572872 | tf_op jit(solution)/shard_map/ppermute | solution.py:638
  12.5 14.3 %collective-permute-start = (bf16[272,1024]{1,0:T(8,128)(2,1)S(1)}, bf16[272,1024]{1,0:T(8,128)(2,1)S(1)}, u32[]{:S(2)}, u32[]{:S(2)}) collective-permute-start(bf16[272,1024]{1,0:T(8,128)(2,1)S(1)} %pack.1.refs_0_), channel_id=1, source_target_pairs={{0,4},{4,0},{8,12},{12,8},{16,20},{20,16},{24,28},{28,24},{1,5},{5... | collective-permute-start | bytes 1671176 | tf_op jit(solution)/shard_map/ppermute | solution.py:507
  26.8 18.5 %collective-permute-start.11 = (bf16[256,1024]{1,0:T(8,128)(2,1)}, bf16[256,1024]{1,0:T(8,128)(2,1)S(1)}, u32[]{:S(2)}, u32[]{:S(2)}) collective-permute-start(bf16[256,1024]{1,0:T(8,128)(2,1)} %collective-permute-done.6.refs_1_), channel_id=1, source_target_pairs={{1,2},{2,3},{5,6},{6,7},{9,10},{10,11},{13,14},{14,15},{17,18},{18... | collective-permute-start | bytes 1572872 | tf_op jit(solution)/shard_map/ppermute | solution.py:637
  27.8 17.5 %collective-permute-start.12 = (bf16[256,1024]{1,0:T(8,128)(2,1)}, bf16[256,1024]{1,0:T(8,128)(2,1)S(1)}, u32[]{:S(2)}, u32[]{:S(2)}) collective-permute-start(bf16[256,1024]{1,0:T(8,128)(2,1)} %collective-permute-done.7.refs_4_), channel_id=1, source_target_pairs={{1,0},{2,1},{5,4},{6,5},{9,8},{10,9},{13,12},{14,13},{17,16},{18,1... | collective-permute-start | bytes 1572872 | tf_op jit(solution)/shard_map/ppermute | solution.py:638
  46.3 17.8 %collective-permute-start.23 = (bf16[256,1024]{1,0:T(8,128)(2,1)S(1)}, bf16[256,1024]{1,0:T(8,128)(2,1)S(1)}, u32[]{:S(2)}, u32[]{:S(2)}) collective-permute-start(bf16[256,1024]{1,0:T(8,128)(2,1)S(1)} %broadcast_select_fusion), channel_id=1, source_target_pairs={{2,3},{1,0},{6,7},{5,4},{10,11},{9,8},{14,15},{13,12},{18,19},{17,... | collective-permute-start | bytes 1572872 | tf_op jit(solution)/shard_map/ppermute | solution.py:633
  52.4 20.9 %collective-permute-start.13 = (bf16[256,1152]{1,0:T(8,128)(2,1)}, bf16[256,1152]{1,0:T(8,128)(2,1)S(1)}, u32[]{:S(2)}, u32[]{:S(2)}) collective-permute-start(bf16[256,1152]{1,0:T(8,128)(2,1)} %get-tuple-element.62), channel_id=1, source_target_pairs={{0,4},{4,0},{8,12},{12,8},{16,20},{20,16},{24,28},{28,24},{1,5},{5... | collective-permute-start | bytes 1769480 | tf_op jit(solution)/shard_map/ppermute | solution.py:507
  53.1 20.2 %collective-permute-start.16 = (bf16[128,1152]{1,0:T(8,128)(2,1)S(1)}, bf16[128,1152]{1,0:T(8,128)(2,1)S(1)}, u32[]{:S(2)}, u32[]{:S(2)}) collective-permute-start(bf16[128,1152]{1,0:T(8,128)(2,1)S(1)} %get-tuple-element.69), channel_id=1, source_target_pairs={{0,8},{4,12},{8,0},{12,4},{16,24},{20,28},{24,16},{28,20},{1,9},{5... | collective-permute-start | bytes 884744 | tf_op jit(solution)/shard_map/ppermute | solution.py:507
  58.8 14.5 %collective-permute-start.22 = (bf16[128,1152]{1,0:T(8,128)(2,1)S(1)}, bf16[128,1152]{1,0:T(8,128)(2,1)S(1)}, u32[]{:S(2)}, u32[]{:S(2)}) collective-permute-start(bf16[128,1152]{1,0:T(8,128)(2,1)S(1)} %get-tuple-element.77), channel_id=1, source_target_pairs={{0,16},{4,20},{8,24},{12,28},{16,0},{20,4},{24,8},{28,12},{1,17},{... | collective-permute-start | bytes 884744 | tf_op jit(solution)/shard_map/ppermute | solution.py:507
  80.2 15.2 %collective-permute-start.30 = (bf16[128,1152]{1,0:T(8,128)(2,1)S(1)}, bf16[128,1152]{1,0:T(8,128)(2,1)}, u32[]{:S(2)}, u32[]{:S(2)}) collective-permute-start(bf16[128,1152]{1,0:T(8,128)(2,1)S(1)} %get-tuple-element.80.refs_0_), channel_id=1, source_target_pairs={{0,16},{4,20},{8,24},{12,28},{16,0},{20,4},{24,8},{28,12},{1,17},{... | collective-permute-start | bytes 884744 | tf_op jit(solution)/shard_map/ppermute | solution.py:507
  81.0 14.3 %collective-permute-start.27 = (bf16[128,1152]{1,0:T(8,128)(2,1)S(1)}, bf16[128,1152]{1,0:T(8,128)(2,1)S(1)}, u32[]{:S(2)}, u32[]{:S(2)}) collective-permute-start(bf16[128,1152]{1,0:T(8,128)(2,1)S(1)} %get-tuple-element.81.refs_1_), channel_id=1, source_target_pairs={{0,8},{4,12},{8,0},{12,4},{16,24},{20,28},{24,16},{28,20},{1,9},{5... | collective-permute-start | bytes 884744 | tf_op jit(solution)/shard_map/ppermute | solution.py:507
  101.2 30.2 %all-to-all-start = ((bf16[8,256,512]{2,1,0:T(8,128)(2,1)}), bf16[8,256,512]{2,1,0:T(8,128)(2,1)S(1)}, u32[]{:S(2)}, u32[]{:S(2)}) async-start(bf16[8,256,512]{2,1,0:T(8,128)(2,1)} %get-tuple-element.85), calls=%async_computation | async-start | bytes 4194304 | tf_op jit(solution)/shard_map/all_to_all | solution.py:744
  136.4 21.2 %collective-permute-start.50 = (bf16[256,1024]{1,0:T(8,128)(2,1)S(1)}, bf16[256,1024]{1,0:T(8,128)(2,1)S(1)}, u32[]{:S(2)}, u32[]{:S(2)}) collective-permute-start(bf16[256,1024]{1,0:T(8,128)(2,1)S(1)} %get-tuple-element.103.refs_0_), channel_id=1, source_target_pairs={{0,16},{4,20},{8,24},{12,28},{16,0},{20,4},{24,8},{28,12},{1,17},{... | collective-permute-start | bytes 1572872 | tf_op jit(solution)/shard_map/ppermute | solution.py:507
  138.0 21.3 %collective-permute-start.48 = (bf16[256,1024]{1,0:T(8,128)(2,1)S(1)}, bf16[256,1024]{1,0:T(8,128)(2,1)S(1)}, u32[]{:S(2)}, u32[]{:S(2)}) collective-permute-start(bf16[256,1024]{1,0:T(8,128)(2,1)S(1)} %get-tuple-element.103.refs_0_), channel_id=1, source_target_pairs={{0,8},{4,12},{8,0},{12,4},{16,24},{20,28},{24,16},{28,20},{1,9},{5... | collective-permute-start | bytes 1572872 | tf_op jit(solution)/shard_map/ppermute | solution.py:507
  138.5 18.5 %collective-permute-start.45 = (bf16[128,1024]{1,0:T(8,128)(2,1)S(1)}, bf16[128,1024]{1,0:T(8,128)(2,1)S(1)}, u32[]{:S(2)}, u32[]{:S(2)}) collective-permute-start(bf16[128,1024]{1,0:T(8,128)(2,1)S(1)} %get-tuple-element.105), channel_id=1, source_target_pairs={{0,8},{4,12},{8,0},{12,4},{16,24},{20,28},{24,16},{28,20},{1,9},{5... | collective-permute-start | bytes 786440 | tf_op jit(solution)/shard_map/ppermute | solution.py:507
  140.0 19.8 %collective-permute-start.38 = (bf16[256,1024]{1,0:T(8,128)(2,1)S(1)}, bf16[256,1024]{1,0:T(8,128)(2,1)S(1)}, u32[]{:S(2)}, u32[]{:S(2)}) collective-permute-start(bf16[256,1024]{1,0:T(8,128)(2,1)S(1)} %copy-done.33), channel_id=1, source_target_pairs={{0,4},{4,0},{8,12},{12,8},{16,20},{20,16},{24,28},{28,24},{1,5},{5... | collective-permute-start | bytes 1572872 | tf_op jit(solution)/shard_map/ppermute | solution.py:507
  143.9 16.1 %collective-permute-start.47 = (bf16[128,1024]{1,0:T(8,128)(2,1)S(1)}, bf16[128,1024]{1,0:T(8,128)(2,1)S(1)}, u32[]{:S(2)}, u32[]{:S(2)}) collective-permute-start(bf16[128,1024]{1,0:T(8,128)(2,1)S(1)} %add_convert_fusion.1), channel_id=1, source_target_pairs={{0,16},{4,20},{8,24},{12,28},{16,0},{20,4},{24,8},{28,12},{1,17},{... | collective-permute-start | bytes 786440 | tf_op jit(solution)/shard_map/ppermute | solution.py:507
  157.7 14.2 %collective-permute-start.43 = (bf16[128,1024]{1,0:T(8,128)(2,1)S(1)}, bf16[128,1024]{1,0:T(8,128)(2,1)S(1)}, u32[]{:S(2)}, u32[]{:S(2)}) collective-permute-start(bf16[128,1024]{1,0:T(8,128)(2,1)S(1)} %add_convert_fusion.2), channel_id=1, source_target_pairs={{0,8},{4,12},{8,0},{12,4},{16,24},{20,28},{24,16},{28,20},{1,9},{5... | collective-permute-start | bytes 786440 | tf_op jit(solution)/shard_map/ppermute | solution.py:507
  159.3 12.6 %collective-permute-start.46 = (bf16[128,1024]{1,0:T(8,128)(2,1)S(1)}, bf16[128,1024]{1,0:T(8,128)(2,1)S(1)}, u32[]{:S(2)}, u32[]{:S(2)}) collective-permute-start(bf16[128,1024]{1,0:T(8,128)(2,1)S(1)} %add_convert_fusion), channel_id=1, source_target_pairs={{0,16},{4,20},{8,24},{12,28},{16,0},{20,4},{24,8},{28,12},{1,17},{... | collective-permute-start | bytes 786440 | tf_op jit(solution)/shard_map/ppermute | solution.py:507
  159.9 22.1 %collective-permute-start.54 = (bf16[256,1024]{1,0:T(8,128)(2,1)S(1)}, bf16[256,1024]{1,0:T(8,128)(2,1)S(1)}, u32[]{:S(2)}, u32[]{:S(2)}) collective-permute-start(bf16[256,1024]{1,0:T(8,128)(2,1)S(1)} %get-tuple-element.103.refs_0_), channel_id=1, source_target_pairs={{0,4},{4,0},{8,12},{12,8},{16,20},{20,16},{24,28},{28,24},{1,5},{5... | collective-permute-start | bytes 1572872 | tf_op jit(solution)/shard_map/ppermute | solution.py:507
  160.0 15.2 %collective-permute-start.51 = (bf16[128,1024]{1,0:T(8,128)(2,1)S(1)}, bf16[128,1024]{1,0:T(8,128)(2,1)S(1)}, u32[]{:S(2)}, u32[]{:S(2)}) collective-permute-start(bf16[128,1024]{1,0:T(8,128)(2,1)S(1)} %slice.78), channel_id=1, source_target_pairs={{0,8},{4,12},{8,0},{12,4},{16,24},{20,28},{24,16},{28,20},{1,9},{5... | collective-permute-start | bytes 786440 | tf_op jit(solution)/shard_map/ppermute | solution.py:507
  166.3 15.7 %collective-permute-start.56 = (bf16[256,1024]{1,0:T(8,128)(2,1)S(1)}, bf16[256,1024]{1,0:T(8,128)(2,1)S(1)}, u32[]{:S(2)}, u32[]{:S(2)}) collective-permute-start(bf16[256,1024]{1,0:T(8,128)(2,1)S(1)} %collective-permute-done.50.refs_4_), channel_id=1, source_target_pairs={{0,4},{4,0},{8,12},{12,8},{16,20},{20,16},{24,28},{28,24},{1,5},{5... | collective-permute-start | bytes 1572872 | tf_op jit(solution)/shard_map/ppermute | solution.py:507
  (68 other events, 469.0 us)

commit v17 on v16

--- a/solution.py
+++ b/solution.py
@@ -575,11 +575,10 @@
     x_sum, y_sum = both(3, top), both(3, low)
     x_far, y_far = swap(x_sum, 2), swap(y_sum, 4)
     x_sum, y_sum = both(1, top, None, x_sum), both(2, low, None, y_sum)
-    near_sums = [x_sum, y_sum]
     x_top, y_low = swap(x_sum, 2), swap(y_sum, 4)
     x_sum, y_sum = both(1, low, y_far, x_sum), both(2, top, x_far, y_sum)
     x_low, y_top = swap(x_sum, 2), swap(y_sum, 4)
-    return terms + [[x_top, x_low], [y_top, y_low]], near_sums
+    return terms + [[x_top, x_low], [y_top, y_low]], [x_top, y_low]
 
 
 def merge_chips(parts, received, heads, between):
@@ -773,8 +772,8 @@
     )(logits, hot, q_slots, probs, keys, values, *flat(grad_all))
     key_grad, value_grad = outs[chunks:]
     received = from_core(outs[:chunks], columns)
-    terms, near_sums = collect_chips(outs[:chunks], received)
-    attns = with_cores(spread_chips(after(attn_out, *near_sums), rows // 2))
+    terms, arrived = collect_chips(outs[:chunks], received)
+    attns = with_cores(spread_chips(after(attn_out, *arrived), rows // 2))
 
     def weight_part(chosen, first, when, *before):
         return pl.pallas_call(

time: 188 us -> 184 us (0.979)
  waiting for transfers between devices: 75.7 us -> 70.2 us
    ppermute x52, waiting for transfers between devices: 68.1 us -> 62.6 us  [swap(): return lax.ppermute(x, 'ctx', [(i, i ^ bits) for i in range(count)])]
    unnamed x69 -> x67, local copies, waits for them, and re-layouts: 7.43 us -> 7.46 us
  transfers between devices with their start and end apart: 58 -> 58, of which waited for: 27 -> 29; matrix products, arithmetic and copies ran while one was open for 2% -> 2% of each run, Pallas kernels for 24% -> 25%
where the time goes in v17:
time: 184 us; the launch traced here: 182 us
  waiting for transfers between devices  70.2 us (38%)
  Pallas kernels  50.3 us (27%)
  starting transfers between devices  49.4 us (27%)
  local copies, waits for them, and re-layouts  8.55 us (5%)
  other arithmetic  2.66 us (1%)
    ppermute x52, waiting for transfers between devices, swap(): return lax.ppermute(x, 'ctx', [(i, i ^ bits) for i in range(count)])  62.6 us
    ppermute x52, starting transfers between devices, swap(): return lax.ppermute(x, 'ctx', [(i, i ^ bits) for i in range(count)])  36.5 us
    pallas_call x1, Pallas kernels, body(): pl.pallas_call(functools.partial(backward_kernel, [len(pieces) for pieces...  18.7 us
    pallas_call x1, Pallas kernels, body(): pl.pallas_call(functools.partial(forward_kernel, [len(pieces) for pieces...  13.5 us
    pallas_call x1, Pallas kernels, body(): make_grad(after(line, *before), out_weight, out_grad, *ups, *downs)  7.66 us
    unnamed x67, local copies, waits for them, and re-layouts  7.46 us
    ppermute x2, starting transfers between devices, spread_line(): ups.append(lax.ppermute(ups[-1], 'head', up))  4.99 us
    ppermute x2, waiting for transfers between devices, spread_line(): downs.append(lax.ppermute(downs[-1], 'head', down))  4.78 us
  transfers between devices with their start and end apart: 58, of which 29 were waited for; matrix products, arithmetic and copies ran while one was open for 2% of the time, Pallas kernels for 25%

profile of v17, /device:TPU:0, one launch (start us, length us, event | category | flops | bytes accessed | tf_op | source)
XLA Modules:
  0.0 182.2 jit_solution(8812002354707445222)
XLA Ops:
  2.4 3.0 %collective-permute-start.1 = (bf16[272,1024]{1,0:T(8,128)(2,1)S(1)}, bf16[272,1024]{1,0:T(8,128)(2,1)S(1)}, u32[]{:S(2)}, u32[]{:S(2)}) collective-permute-start(bf16[272,1024]{1,0:T(8,128)(2,1)S(1)} %pack.1.refs_0_), channel_id=1, source_target_pairs={{0,8},{4,12},{8,0},{12,4},{16,24},{20,28},{24,16},{28,20},{1,9},{5... | collective-permute-start | bytes 1671176 | tf_op jit(solution)/shard_map/ppermute | solution.py:507
  6.9 4.3 %collective-permute-start.6 = (bf16[256,1024]{1,0:T(8,128)(2,1)}, bf16[256,1024]{1,0:T(8,128)(2,1)}, u32[]{:S(2)}, u32[]{:S(2)}) collective-permute-start(bf16[256,1024]{1,0:T(8,128)(2,1)} %refs_0_.1), channel_id=1, source_target_pairs={{0,1},{1,2},{2,3},{4,5},{5,6},{6,7},{8,9},{9,10},{10,11},{12,13},{... | collective-permute-start | bytes 1572872 | tf_op jit(solution)/shard_map/ppermute | solution.py:636
  12.6 5.4 %collective-permute-done.1.refs_2_ = bf16[272,1024]{1,0:T(8,128)(2,1)S(1)} collective-permute-done((bf16[272,1024]{1,0:T(8,128)(2,1)S(1)}, bf16[272,1024]{1,0:T(8,128)(2,1)S(1)}, u32[]{:S(2)}, u32[]{:S(2)}) %collective-permute-start.1) | collective-permute-done | bytes 557088 | tf_op jit(solution)/shard_map/ppermute | solution.py:507
  18.1 1.8 %collective-permute-start.5 = (bf16[128,1024]{1,0:T(8,128)(2,1)S(1)}, bf16[128,1024]{1,0:T(8,128)(2,1)S(1)}, u32[]{:S(2)}, u32[]{:S(2)}) collective-permute-start(bf16[128,1024]{1,0:T(8,128)(2,1)S(1)} %slice.69), channel_id=1, source_target_pairs={{0,16},{4,20},{8,24},{12,28},{16,0},{20,4},{24,8},{28,12},{1,17},{... | collective-permute-start | bytes 786440 | tf_op jit(solution)/shard_map/ppermute | solution.py:507
  21.5 4.8 %collective-permute-done.7.refs_4_ = bf16[256,1024]{1,0:T(8,128)(2,1)} collective-permute-done((bf16[256,1024]{1,0:T(8,128)(2,1)}, bf16[256,1024]{1,0:T(8,128)(2,1)}, u32[]{:S(2)}, u32[]{:S(2)}) %collective-permute-start.7) | collective-permute-done | bytes 524320 | tf_op jit(solution)/shard_map/ppermute | solution.py:637
  31.8 13.5 %forward.1 = (bf16[256,1152]{1,0:T(8,128)(2,1)}, bf16[256,1152]{1,0:T(8,128)(2,1)}, bf16[256,1152]{1,0:T(8,128)(2,1)}, bf16[256,1152]{1,0:T(8,128)(2,1)}, bf16[2...) custom-call(s32[1]{0:T(128)} %bitcast.me_ref, ...), custom_call_target="tpu_custom_call" | custom-call | tf_op jit(solution)/shard_map/forward/pallas_call | solution.py:680
  53.7 5.1 %collective-permute-done.18.refs_4_ = bf16[128,1152]{1,0:T(8,128)(2,1)S(1)} collective-permute-done((bf16[128,1152]{1,0:T(8,128)(2,1)S(1)}, bf16[128,1152]{1,0:T(8,128)(2,1)S(1)}, u32[]{:S(2)}, u32[]{:S(2)}) %collective-permute-start.18) | collective-permute-done | bytes 294944 | tf_op jit(solution)/shard_map/ppermute | solution.py:507
  65.6 7.7 %grad.1 = (bf16[256,1024]{1,0:T(8,128)(2,1)}, bf16[8,256,512]{2,1,0:T(8,128)(2,1)}) custom-call(s32[1]{0:T(128)} %bitcast.4.line_ref, bf16[4096,1024]{1,0:T(8,128)(2,1)} %w_ref.1, bf16[256,1024]{1,0:T(8,128)(2,1)} %refs_0_.1, bf16[256,1024]{1,0:T(8,128)(2,1)} %collective-permute-done.6.refs_1_, bf16[256,1024]{1,0:T(8,128)(2,1)} %copy-done.12, ...), custom_call_target="tpu_custom_call" | custom-call | tf_op jit(solution)/shard_map/grad/pallas_call | solution.py:730
  74.6 2.8 %finish.1 = (bf16[256,1024]{1,0:T(8,128)(2,1)S(1)}, bf16[128,1152]{1,0:T(8,128)(2,1)S(1)}, bf16[128,1152]{1,0:T(8,128)(2,1)S(1)}) custom-call(bf16[256,1152]{1,0:T(8,128)(2,1)S(1)} %copy-done.4, bf16[256,1152]{1,0:T(8,128)(2,1)S(1)} %collective-permute-done.13.refs_1_, bf16[128,1152]{1,0:T(8,128)(2,1)S(1)} %collective-permute-done.16.refs_2_, ...), custom_call_target="tpu_custom_call" | custom-call | tf_op jit(solution)/shard_map/finish/pallas_call | solution.py:732
  81.5 5.9 %collective-permute-done.26.refs_4_ = bf16[128,1152]{1,0:T(8,128)(2,1)S(1)} collective-permute-done((bf16[128,1152]{1,0:T(8,128)(2,1)S(1)}, bf16[128,1152]{1,0:T(8,128)(2,1)S(1)}, u32[]{:S(2)}, u32[]{:S(2)}) %collective-permute-start.26) | collective-permute-done | bytes 294944 | tf_op jit(solution)/shard_map/ppermute | solution.py:507
  90.1 5.2 %collective-permute-done.30.refs_8_ = bf16[128,1152]{1,0:T(8,128)(2,1)} collective-permute-done((bf16[128,1152]{1,0:T(8,128)(2,1)S(1)}, bf16[128,1152]{1,0:T(8,128)(2,1)}, u32[]{:S(2)}, u32[]{:S(2)}) %collective-permute-start.30) | collective-permute-done | bytes 294944 | tf_op jit(solution)/shard_map/ppermute | solution.py:507
  95.3 4.4 %collective-permute-done.34.refs_12_ = bf16[128,1152]{1,0:T(8,128)(2,1)S(1)} collective-permute-done((bf16[128,1152]{1,0:T(8,128)(2,1)S(1)}, bf16[128,1152]{1,0:T(8,128)(2,1)S(1)}, u32[]{:S(2)}, u32[]{:S(2)}) %collective-permute-start.34) | collective-permute-done | bytes 294944 | tf_op jit(solution)/shard_map/ppermute | solution.py:507
  101.1 3.8 %all-to-all-start = ((bf16[8,256,512]{2,1,0:T(8,128)(2,1)}), bf16[8,256,512]{2,1,0:T(8,128)(2,1)S(1)}, u32[]{:S(2)}, u32[]{:S(2)}) async-start(bf16[8,256,512]{2,1,0:T(8,128)(2,1)} %get-tuple-element.85), calls=%async_computation | async-start | bytes 4194304 | tf_op jit(solution)/shard_map/all_to_all | solution.py:743
  110.6 18.7 %backward.1 = (bf16[256,1024]{1,0:T(8,128)(2,1)}, bf16[256,1024]{1,0:T(8,128)(2,1)}, bf16[256,1024]{1,0:T(8,128)(2,1)}, bf16[256,1024]{1,0:T(8,128)(2,1)}, bf16[...) custom-call(f32[16,8,128]{2,1,0:T(8,128)} %get-tuple-element.56.logi, ...), custom_call_target="tpu_custom_call" | custom-call | tf_op jit(solution)/shard_map/backward/pallas_call | solution.py:747
  129.4 2.0 %all-to-all-done.cols_ref = bf16[8,256,512]{2,1,0:T(8,128)(2,1)S(1)} async-done(((bf16[8,256,512]{2,1,0:T(8,128)(2,1)}), bf16[8,256,512]{2,1,0:T(8,128)(2,1)S(1)}, u32[]{:S(2)}, u32[]{:S(2)}) %all-to-all-start) | async-done | bytes 2097184 | tf_op jit(solution)/shard_map/all_to_all | solution.py:743
  131.8 1.6 collective-permute-done.39
  140.0 4.9 %collective-permute-done.47.refs_5_ = bf16[128,1024]{1,0:T(8,128)(2,1)S(1)} collective-permute-done((bf16[128,1024]{1,0:T(8,128)(2,1)S(1)}, bf16[128,1024]{1,0:T(8,128)(2,1)S(1)}, u32[]{:S(2)}, u32[]{:S(2)}) %collective-permute-start.47) | collective-permute-done | bytes 262176 | tf_op jit(solution)/shard_map/ppermute | solution.py:507
  147.7 2.9 %collective-permute-done.42 = bf16[128,1024]{1,0:T(8,128)(2,1)S(1)} collective-permute-done((bf16[128,1024]{1,0:T(8,128)(2,1)S(1)}, bf16[128,1024]{1,0:T(8,128)(2,1)S(1)}, u32[]{:S(2)}, u32[]{:S(2)}) %collective-permute-start.42) | collective-permute-done | bytes 262176 | tf_op jit(solution)/shard_map/ppermute | solution.py:507
  153.0 8.8 %collective-permute-done.50.refs_4_ = bf16[256,1024]{1,0:T(8,128)(2,1)S(1)} collective-permute-done((bf16[256,1024]{1,0:T(8,128)(2,1)S(1)}, bf16[256,1024]{1,0:T(8,128)(2,1)S(1)}, u32[]{:S(2)}, u32[]{:S(2)}) %collective-permute-start.50) | collective-permute-done | bytes 524320 | tf_op jit(solution)/shard_map/ppermute | solution.py:507
  163.4 4.8 %collective-permute-done.43.refs_3_ = bf16[128,1024]{1,0:T(8,128)(2,1)S(1)} collective-permute-done((bf16[128,1024]{1,0:T(8,128)(2,1)S(1)}, bf16[128,1024]{1,0:T(8,128)(2,1)S(1)}, u32[]{:S(2)}, u32[]{:S(2)}) %collective-permute-start.43) | collective-permute-done | bytes 262176 | tf_op jit(solution)/shard_map/ppermute | solution.py:507
  169.7 3.0 %collective-permute-done.51.refs_1_ = bf16[128,1024]{1,0:T(8,128)(2,1)S(1)} collective-permute-done((bf16[128,1024]{1,0:T(8,128)(2,1)S(1)}, bf16[128,1024]{1,0:T(8,128)(2,1)S(1)}, u32[]{:S(2)}, u32[]{:S(2)}) %collective-permute-start.51) | collective-permute-done | bytes 262176 | tf_op jit(solution)/shard_map/ppermute | solution.py:507
  172.7 4.2 %collective-permute-done.49.refs_0_ = bf16[128,1024]{1,0:T(8,128)(2,1)S(1)} collective-permute-done((bf16[128,1024]{1,0:T(8,128)(2,1)S(1)}, bf16[128,1024]{1,0:T(8,128)(2,1)S(1)}, u32[]{:S(2)}, u32[]{:S(2)}) %collective-permute-start.49) | collective-permute-done | bytes 262176 | tf_op jit(solution)/shard_map/ppermute | solution.py:507
  178.3 1.8 weight.2.refs_4_
  180.1 2.1 %weight.3 = f32[512,1024]{1,0:T(8,128)} custom-call(s32[1]{0:T(128)} %bitcast.me_ref, bf16[8,256,512]{2,1,0:T(8,128)(2,1)S(1)} %all-to-all-done.cols_ref, bf16[128,1024]{1,0:T(8,128)(2,1)S(1)} %collective-permute-done.49.refs_0_, bf16[128,1024]{1,0:T(8,128)(2,1)S(1)} %collective-permute-done.51.refs_1_, ...), custom_call_target="tpu_custom_call" | custom-call | tf_op jit(solution)/shard_map/weight/pallas_call | solution.py:779
  (181 shorter events, 58.4 us)
Async XLA Ops:
  2.4 15.6 %collective-permute-start.1 = (bf16[272,1024]{1,0:T(8,128)(2,1)S(1)}, bf16[272,1024]{1,0:T(8,128)(2,1)S(1)}, u32[]{:S(2)}, u32[]{:S(2)}) collective-permute-start(bf16[272,1024]{1,0:T(8,128)(2,1)S(1)} %pack.1.refs_0_), channel_id=1, source_target_pairs={{0,8},{4,12},{8,0},{12,4},{16,24},{20,28},{24,16},{28,20},{1,9},{5... | collective-permute-start | bytes 1671176 | tf_op jit(solution)/shard_map/ppermute | solution.py:507
  5.4 14.5 %collective-permute-start.3 = (bf16[272,1024]{1,0:T(8,128)(2,1)S(1)}, bf16[272,1024]{1,0:T(8,128)(2,1)S(1)}, u32[]{:S(2)}, u32[]{:S(2)}) collective-permute-start(bf16[272,1024]{1,0:T(8,128)(2,1)S(1)} %pack.1.refs_0_), channel_id=1, source_target_pairs={{0,16},{4,20},{8,24},{12,28},{16,0},{20,4},{24,8},{28,12},{1,17},{... | collective-permute-start | bytes 1671176 | tf_op jit(solution)/shard_map/ppermute | solution.py:507
  6.9 14.6 %collective-permute-start.6 = (bf16[256,1024]{1,0:T(8,128)(2,1)}, bf16[256,1024]{1,0:T(8,128)(2,1)}, u32[]{:S(2)}, u32[]{:S(2)}) collective-permute-start(bf16[256,1024]{1,0:T(8,128)(2,1)} %refs_0_.1), channel_id=1, source_target_pairs={{0,1},{1,2},{2,3},{4,5},{5,6},{6,7},{8,9},{9,10},{10,11},{12,13},{... | collective-permute-start | bytes 1572872 | tf_op jit(solution)/shard_map/ppermute | solution.py:636
  11.2 15.0 %collective-permute-start.7 = (bf16[256,1024]{1,0:T(8,128)(2,1)}, bf16[256,1024]{1,0:T(8,128)(2,1)}, u32[]{:S(2)}, u32[]{:S(2)}) collective-permute-start(bf16[256,1024]{1,0:T(8,128)(2,1)} %refs_0_.1), channel_id=1, source_target_pairs={{1,0},{2,1},{3,2},{5,4},{6,5},{7,6},{9,8},{10,9},{11,10},{13,12},{... | collective-permute-start | bytes 1572872 | tf_op jit(solution)/shard_map/ppermute | solution.py:637
  12.5 14.3 %collective-permute-start = (bf16[272,1024]{1,0:T(8,128)(2,1)S(1)}, bf16[272,1024]{1,0:T(8,128)(2,1)S(1)}, u32[]{:S(2)}, u32[]{:S(2)}) collective-permute-start(bf16[272,1024]{1,0:T(8,128)(2,1)S(1)} %pack.1.refs_0_), channel_id=1, source_target_pairs={{0,4},{4,0},{8,12},{12,8},{16,20},{20,16},{24,28},{28,24},{1,5},{5... | collective-permute-start | bytes 1671176 | tf_op jit(solution)/shard_map/ppermute | solution.py:507
  26.8 18.5 %collective-permute-start.11 = (bf16[256,1024]{1,0:T(8,128)(2,1)}, bf16[256,1024]{1,0:T(8,128)(2,1)S(1)}, u32[]{:S(2)}, u32[]{:S(2)}) collective-permute-start(bf16[256,1024]{1,0:T(8,128)(2,1)} %collective-permute-done.6.refs_1_), channel_id=1, source_target_pairs={{1,2},{2,3},{5,6},{6,7},{9,10},{10,11},{13,14},{14,15},{17,18},{18... | collective-permute-start | bytes 1572872 | tf_op jit(solution)/shard_map/ppermute | solution.py:636
  27.8 17.5 %collective-permute-start.12 = (bf16[256,1024]{1,0:T(8,128)(2,1)}, bf16[256,1024]{1,0:T(8,128)(2,1)S(1)}, u32[]{:S(2)}, u32[]{:S(2)}) collective-permute-start(bf16[256,1024]{1,0:T(8,128)(2,1)} %collective-permute-done.7.refs_4_), channel_id=1, source_target_pairs={{1,0},{2,1},{5,4},{6,5},{9,8},{10,9},{13,12},{14,13},{17,16},{18,1... | collective-permute-start | bytes 1572872 | tf_op jit(solution)/shard_map/ppermute | solution.py:637
  46.3 17.7 %collective-permute-start.23 = (bf16[256,1024]{1,0:T(8,128)(2,1)S(1)}, bf16[256,1024]{1,0:T(8,128)(2,1)S(1)}, u32[]{:S(2)}, u32[]{:S(2)}) collective-permute-start(bf16[256,1024]{1,0:T(8,128)(2,1)S(1)} %broadcast_select_fusion), channel_id=1, source_target_pairs={{2,3},{1,0},{6,7},{5,4},{10,11},{9,8},{14,15},{13,12},{18,19},{17,... | collective-permute-start | bytes 1572872 | tf_op jit(solution)/shard_map/ppermute | solution.py:632
  52.4 20.9 %collective-permute-start.13 = (bf16[256,1152]{1,0:T(8,128)(2,1)}, bf16[256,1152]{1,0:T(8,128)(2,1)S(1)}, u32[]{:S(2)}, u32[]{:S(2)}) collective-permute-start(bf16[256,1152]{1,0:T(8,128)(2,1)} %get-tuple-element.62), channel_id=1, source_target_pairs={{0,4},{4,0},{8,12},{12,8},{16,20},{20,16},{24,28},{28,24},{1,5},{5... | collective-permute-start | bytes 1769480 | tf_op jit(solution)/shard_map/ppermute | solution.py:507
  53.1 20.2 %collective-permute-start.16 = (bf16[128,1152]{1,0:T(8,128)(2,1)S(1)}, bf16[128,1152]{1,0:T(8,128)(2,1)S(1)}, u32[]{:S(2)}, u32[]{:S(2)}) collective-permute-start(bf16[128,1152]{1,0:T(8,128)(2,1)S(1)} %get-tuple-element.69), channel_id=1, source_target_pairs={{0,8},{4,12},{8,0},{12,4},{16,24},{20,28},{24,16},{28,20},{1,9},{5... | collective-permute-start | bytes 884744 | tf_op jit(solution)/shard_map/ppermute | solution.py:507
  58.8 14.5 %collective-permute-start.22 = (bf16[128,1152]{1,0:T(8,128)(2,1)S(1)}, bf16[128,1152]{1,0:T(8,128)(2,1)S(1)}, u32[]{:S(2)}, u32[]{:S(2)}) collective-permute-start(bf16[128,1152]{1,0:T(8,128)(2,1)S(1)} %get-tuple-element.77), channel_id=1, source_target_pairs={{0,16},{4,20},{8,24},{12,28},{16,0},{20,4},{24,8},{28,12},{1,17},{... | collective-permute-start | bytes 884744 | tf_op jit(solution)/shard_map/ppermute | solution.py:507
  80.2 15.1 %collective-permute-start.30 = (bf16[128,1152]{1,0:T(8,128)(2,1)S(1)}, bf16[128,1152]{1,0:T(8,128)(2,1)}, u32[]{:S(2)}, u32[]{:S(2)}) collective-permute-start(bf16[128,1152]{1,0:T(8,128)(2,1)S(1)} %get-tuple-element.80.refs_0_), channel_id=1, source_target_pairs={{0,16},{4,20},{8,24},{12,28},{16,0},{20,4},{24,8},{28,12},{1,17},{... | collective-permute-start | bytes 884744 | tf_op jit(solution)/shard_map/ppermute | solution.py:507
  81.0 14.3 %collective-permute-start.27 = (bf16[128,1152]{1,0:T(8,128)(2,1)S(1)}, bf16[128,1152]{1,0:T(8,128)(2,1)}, u32[]{:S(2)}, u32[]{:S(2)}) collective-permute-start(bf16[128,1152]{1,0:T(8,128)(2,1)S(1)} %get-tuple-element.81.refs_1_), channel_id=1, source_target_pairs={{0,8},{4,12},{8,0},{12,4},{16,24},{20,28},{24,16},{28,20},{1,9},{5... | collective-permute-start | bytes 884744 | tf_op jit(solution)/shard_map/ppermute | solution.py:507
  87.4 12.3 %collective-permute-start.34 = (bf16[128,1152]{1,0:T(8,128)(2,1)S(1)}, bf16[128,1152]{1,0:T(8,128)(2,1)S(1)}, u32[]{:S(2)}, u32[]{:S(2)}) collective-permute-start(bf16[128,1152]{1,0:T(8,128)(2,1)S(1)} %collective-permute-done.26.refs_4_), channel_id=1, source_target_pairs={{0,16},{4,20},{8,24},{12,28},{16,0},{20,4},{24,8},{28,12},{1,17},{... | collective-permute-start | bytes 884744 | tf_op jit(solution)/shard_map/ppermute | solution.py:507
  101.1 30.2 %all-to-all-start = ((bf16[8,256,512]{2,1,0:T(8,128)(2,1)}), bf16[8,256,512]{2,1,0:T(8,128)(2,1)S(1)}, u32[]{:S(2)}, u32[]{:S(2)}) async-start(bf16[8,256,512]{2,1,0:T(8,128)(2,1)} %get-tuple-element.85), calls=%async_computation | async-start | bytes 4194304 | tf_op jit(solution)/shard_map/all_to_all | solution.py:743
  137.2 13.4 %collective-permute-start.42 = (bf16[128,1024]{1,0:T(8,128)(2,1)S(1)}, bf16[128,1024]{1,0:T(8,128)(2,1)S(1)}, u32[]{:S(2)}, u32[]{:S(2)}) collective-permute-start(bf16[128,1024]{1,0:T(8,128)(2,1)S(1)} %get-tuple-element.104), channel_id=1, source_target_pairs={{0,16},{4,20},{8,24},{12,28},{16,0},{20,4},{24,8},{28,12},{1,17},{... | collective-permute-start | bytes 786440 | tf_op jit(solution)/shard_map/ppermute | solution.py:507
  138.5 12.8 %collective-permute-start.45 = (bf16[128,1024]{1,0:T(8,128)(2,1)S(1)}, bf16[128,1024]{1,0:T(8,128)(2,1)S(1)}, u32[]{:S(2)}, u32[]{:S(2)}) collective-permute-start(bf16[128,1024]{1,0:T(8,128)(2,1)S(1)} %get-tuple-element.105), channel_id=1, source_target_pairs={{0,8},{4,12},{8,0},{12,4},{16,24},{20,28},{24,16},{28,20},{1,9},{5... | collective-permute-start | bytes 786440 | tf_op jit(solution)/shard_map/ppermute | solution.py:507
  140.0 23.2 %collective-permute-start.38 = (bf16[256,1024]{1,0:T(8,128)(2,1)S(1)}, bf16[256,1024]{1,0:T(8,128)(2,1)S(1)}, u32[]{:S(2)}, u32[]{:S(2)}) collective-permute-start(bf16[256,1024]{1,0:T(8,128)(2,1)S(1)} %copy-done.32), channel_id=1, source_target_pairs={{0,4},{4,0},{8,12},{12,8},{16,20},{20,16},{24,28},{28,24},{1,5},{5... | collective-permute-start | bytes 1572872 | tf_op jit(solution)/shard_map/ppermute | solution.py:507
  145.7 16.1 %collective-permute-start.50 = (bf16[256,1024]{1,0:T(8,128)(2,1)S(1)}, bf16[256,1024]{1,0:T(8,128)(2,1)S(1)}, u32[]{:S(2)}, u32[]{:S(2)}) collective-permute-start(bf16[256,1024]{1,0:T(8,128)(2,1)S(1)} %get-tuple-element.103.refs_0_), channel_id=1, source_target_pairs={{0,16},{4,20},{8,24},{12,28},{16,0},{20,4},{24,8},{28,12},{1,17},{... | collective-permute-start | bytes 1572872 | tf_op jit(solution)/shard_map/ppermute | solution.py:507
  147.2 15.4 %collective-permute-start.48 = (bf16[256,1024]{1,0:T(8,128)(2,1)S(1)}, bf16[256,1024]{1,0:T(8,128)(2,1)S(1)}, u32[]{:S(2)}, u32[]{:S(2)}) collective-permute-start(bf16[256,1024]{1,0:T(8,128)(2,1)S(1)} %get-tuple-element.103.refs_0_), channel_id=1, source_target_pairs={{0,8},{4,12},{8,0},{12,4},{16,24},{20,28},{24,16},{28,20},{1,9},{5... | collective-permute-start | bytes 1572872 | tf_op jit(solution)/shard_map/ppermute | solution.py:507
  150.7 17.4 %collective-permute-start.43 = (bf16[128,1024]{1,0:T(8,128)(2,1)S(1)}, bf16[128,1024]{1,0:T(8,128)(2,1)S(1)}, u32[]{:S(2)}, u32[]{:S(2)}) collective-permute-start(bf16[128,1024]{1,0:T(8,128)(2,1)S(1)} %add_convert_fusion.2), channel_id=1, source_target_pairs={{0,8},{4,12},{8,0},{12,4},{16,24},{20,28},{24,16},{28,20},{1,9},{5... | collective-permute-start | bytes 786440 | tf_op jit(solution)/shard_map/ppermute | solution.py:507
  151.5 16.7 %collective-permute-start.46 = (bf16[128,1024]{1,0:T(8,128)(2,1)S(1)}, bf16[128,1024]{1,0:T(8,128)(2,1)S(1)}, u32[]{:S(2)}, u32[]{:S(2)}) collective-permute-start(bf16[128,1024]{1,0:T(8,128)(2,1)S(1)} %add_convert_fusion), channel_id=1, source_target_pairs={{0,16},{4,20},{8,24},{12,28},{16,0},{20,4},{24,8},{28,12},{1,17},{... | collective-permute-start | bytes 786440 | tf_op jit(solution)/shard_map/ppermute | solution.py:507
  161.8 16.4 %collective-permute-start.54 = (bf16[256,1024]{1,0:T(8,128)(2,1)S(1)}, bf16[256,1024]{1,0:T(8,128)(2,1)S(1)}, u32[]{:S(2)}, u32[]{:S(2)}) collective-permute-start(bf16[256,1024]{1,0:T(8,128)(2,1)S(1)} %get-tuple-element.103.refs_0_), channel_id=1, source_target_pairs={{0,4},{4,0},{8,12},{12,8},{16,20},{20,16},{24,28},{28,24},{1,5},{5... | collective-permute-start | bytes 1572872 | tf_op jit(solution)/shard_map/ppermute | solution.py:507
  163.3 15.0 %collective-permute-start.56 = (bf16[256,1024]{1,0:T(8,128)(2,1)S(1)}, bf16[256,1024]{1,0:T(8,128)(2,1)S(1)}, u32[]{:S(2)}, u32[]{:S(2)}) collective-permute-start(bf16[256,1024]{1,0:T(8,128)(2,1)S(1)} %collective-permute-done.50.refs_4_), channel_id=1, source_target_pairs={{0,4},{4,0},{8,12},{12,8},{16,20},{20,16},{24,28},{28,24},{1,5},{5... | collective-permute-start | bytes 1572872 | tf_op jit(solution)/shard_map/ppermute | solution.py:507
  (67 other events, 463.2 us)

commit v18 on v13

--- a/solution.py
+++ b/solution.py
@@ -740,7 +740,7 @@
     grad_chips = spread_halves(*extended)
     grad_all = with_cores(grad_chips)
     arrived = flat(grad_chips[1:])
-    attns = spread_near(after(attn_out, *flat(grad_chips[1:3])))
+    attns = spread_near(after(attn_out, *arrived))
     columns = lax.all_to_all(
         after(blocks, *arrived), "ctx", split_axis=0, concat_axis=0, tiled=True
     )
@@ -774,8 +774,7 @@
     key_grad, value_grad = outs[chunks:]
     received = from_core(outs[:chunks], columns, *flat(attns[1:3]))
     terms, last_sums = collect_chips(outs[:chunks], received)
-    near = [[after(x, *last_sums) for x in pieces] for pieces in attns]
-    attns = with_cores(spread_far(near, rows // 2, terms[2][0], terms[-1][-1]))
+    attns = with_cores(spread_far(attns, rows // 2, *last_sums))
 
     def weight_part(chosen, first, when, *before):
         return pl.pallas_call(

time: 185 us -> 181 us (0.978)
    unnamed x71 -> x69, local copies, waits for them, and re-layouts: 7.43 us -> 7.44 us
  transfers between devices with their start and end apart: 58 -> 58, of which waited for: 26 -> 26; matrix products, arithmetic and copies ran while one was open for 2% -> 2% of each run, Pallas kernels for 25% -> 26%
where the time goes in v18:
time: 181 us; the launch traced here: 179 us
  waiting for transfers between devices  66.2 us (37%)
  Pallas kernels  51.8 us (29%)
  starting transfers between devices  50 us (28%)
  local copies, waits for them, and re-layouts  8.53 us (5%)
    ppermute x52, waiting for transfers between devices, swap(): return lax.ppermute(x, 'ctx', [(i, i ^ bits) for i in range(count)])  60.6 us
    ppermute x52, starting transfers between devices, swap(): return lax.ppermute(x, 'ctx', [(i, i ^ bits) for i in range(count)])  37.1 us
    pallas_call x1, Pallas kernels, body(): pl.pallas_call(functools.partial(backward_kernel, [len(pieces) for pieces...  18.7 us
    pallas_call x1, Pallas kernels, body(): pl.pallas_call(functools.partial(forward_kernel, [len(pieces) for pieces...  13.5 us
    pallas_call x1, Pallas kernels, body(): make_grad(after(line, *before), out_weight, out_grad, *ups, *downs)  7.68 us
    unnamed x69, local copies, waits for them, and re-layouts  7.44 us
    ppermute x2, starting transfers between devices, spread_line(): ups.append(lax.ppermute(ups[-1], 'head', up))  4.98 us
    pallas_call x2, Pallas kernels, weight_part(): pl.pallas_call(functools.partial(weight_kernel, [len(pieces) for pieces i...  4.92 us
  transfers between devices with their start and end apart: 58, of which 26 were waited for; matrix products, arithmetic and copies ran while one was open for 2% of the time, Pallas kernels for 26%

profile of v18, /device:TPU:0, one launch (start us, length us, event | category | flops | bytes accessed | tf_op | source)
XLA Modules:
  0.0 179.3 jit_solution(6253301749943805853)
XLA Ops:
  2.4 3.0 %collective-permute-start.1 = (bf16[272,1024]{1,0:T(8,128)(2,1)S(1)}, bf16[272,1024]{1,0:T(8,128)(2,1)S(1)}, u32[]{:S(2)}, u32[]{:S(2)}) collective-permute-start(bf16[272,1024]{1,0:T(8,128)(2,1)S(1)} %pack.1.refs_0_), channel_id=1, source_target_pairs={{0,8},{4,12},{8,0},{12,4},{16,24},{20,28},{24,16},{28,20},{1,9},{5... | collective-permute-start | bytes 1671176 | tf_op jit(solution)/shard_map/ppermute | solution.py:507
  6.9 4.3 %collective-permute-start.6 = (bf16[256,1024]{1,0:T(8,128)(2,1)}, bf16[256,1024]{1,0:T(8,128)(2,1)}, u32[]{:S(2)}, u32[]{:S(2)}) collective-permute-start(bf16[256,1024]{1,0:T(8,128)(2,1)} %refs_0_.1), channel_id=1, source_target_pairs={{0,1},{1,2},{2,3},{4,5},{5,6},{6,7},{8,9},{9,10},{10,11},{12,13},{... | collective-permute-start | bytes 1572872 | tf_op jit(solution)/shard_map/ppermute | solution.py:636
  12.6 5.4 %collective-permute-done.1.refs_2_ = bf16[272,1024]{1,0:T(8,128)(2,1)S(1)} collective-permute-done((bf16[272,1024]{1,0:T(8,128)(2,1)S(1)}, bf16[272,1024]{1,0:T(8,128)(2,1)S(1)}, u32[]{:S(2)}, u32[]{:S(2)}) %collective-permute-start.1) | collective-permute-done | bytes 557088 | tf_op jit(solution)/shard_map/ppermute | solution.py:507
  18.1 1.8 %collective-permute-start.5 = (bf16[128,1024]{1,0:T(8,128)(2,1)S(1)}, bf16[128,1024]{1,0:T(8,128)(2,1)S(1)}, u32[]{:S(2)}, u32[]{:S(2)}) collective-permute-start(bf16[128,1024]{1,0:T(8,128)(2,1)S(1)} %slice.69), channel_id=1, source_target_pairs={{0,16},{4,20},{8,24},{12,28},{16,0},{20,4},{24,8},{28,12},{1,17},{... | collective-permute-start | bytes 786440 | tf_op jit(solution)/shard_map/ppermute | solution.py:507
  19.9 1.6 collective-permute-start.8
  21.5 4.8 %collective-permute-done.7.refs_4_ = bf16[256,1024]{1,0:T(8,128)(2,1)} collective-permute-done((bf16[256,1024]{1,0:T(8,128)(2,1)}, bf16[256,1024]{1,0:T(8,128)(2,1)}, u32[]{:S(2)}, u32[]{:S(2)}) %collective-permute-start.7) | collective-permute-done | bytes 524320 | tf_op jit(solution)/shard_map/ppermute | solution.py:637
  31.8 13.5 %forward.1 = (bf16[256,1152]{1,0:T(8,128)(2,1)}, bf16[256,1152]{1,0:T(8,128)(2,1)}, bf16[256,1152]{1,0:T(8,128)(2,1)}, bf16[256,1152]{1,0:T(8,128)(2,1)}, bf16[2...) custom-call(s32[1]{0:T(128)} %bitcast.me_ref, ...), custom_call_target="tpu_custom_call" | custom-call | tf_op jit(solution)/shard_map/forward/pallas_call | solution.py:680
  53.7 5.1 %collective-permute-done.18.refs_4_ = bf16[128,1152]{1,0:T(8,128)(2,1)S(1)} collective-permute-done((bf16[128,1152]{1,0:T(8,128)(2,1)S(1)}, bf16[128,1152]{1,0:T(8,128)(2,1)S(1)}, u32[]{:S(2)}, u32[]{:S(2)}) %collective-permute-start.18) | collective-permute-done | bytes 294944 | tf_op jit(solution)/shard_map/ppermute | solution.py:507
  61.7 1.6 collective-permute-start.20
  65.6 7.7 %grad.1 = (bf16[256,1024]{1,0:T(8,128)(2,1)}, bf16[8,256,512]{2,1,0:T(8,128)(2,1)}) custom-call(s32[1]{0:T(128)} %bitcast.4.line_ref, bf16[4096,1024]{1,0:T(8,128)(2,1)} %w_ref.1, bf16[256,1024]{1,0:T(8,128)(2,1)} %refs_0_.1, bf16[256,1024]{1,0:T(8,128)(2,1)} %collective-permute-done.6.refs_1_, bf16[256,1024]{1,0:T(8,128)(2,1)} %copy-done.12, ...), custom_call_target="tpu_custom_call" | custom-call | tf_op jit(solution)/shard_map/grad/pallas_call | solution.py:730
  74.6 3.4 %finish.1 = (bf16[256,1024]{1,0:T(8,128)(2,1)}, bf16[128,1152]{1,0:T(8,128)(2,1)S(1)}, bf16[128,1152]{1,0:T(8,128)(2,1)S(1)}) custom-call(bf16[256,1152]{1,0:T(8,128)(2,1)S(1)} %copy-done.4, bf16[256,1152]{1,0:T(8,128)(2,1)S(1)} %collective-permute-done.13.refs_1_, bf16[128,1152]{1,0:T(8,128)(2,1)S(1)} %collective-permute-done.16.refs_2_, ...), custom_call_target="tpu_custom_call" | custom-call | tf_op jit(solution)/shard_map/finish/pallas_call | solution.py:732
  82.0 5.9 %collective-permute-done.26.refs_4_ = bf16[128,1152]{1,0:T(8,128)(2,1)S(1)} collective-permute-done((bf16[128,1152]{1,0:T(8,128)(2,1)S(1)}, bf16[128,1152]{1,0:T(8,128)(2,1)S(1)}, u32[]{:S(2)}, u32[]{:S(2)}) %collective-permute-start.26) | collective-permute-done | bytes 294944 | tf_op jit(solution)/shard_map/ppermute | solution.py:507
  90.6 5.2 %collective-permute-done.30.refs_8_ = bf16[128,1152]{1,0:T(8,128)(2,1)} collective-permute-done((bf16[128,1152]{1,0:T(8,128)(2,1)S(1)}, bf16[128,1152]{1,0:T(8,128)(2,1)}, u32[]{:S(2)}, u32[]{:S(2)}) %collective-permute-start.30) | collective-permute-done | bytes 294944 | tf_op jit(solution)/shard_map/ppermute | solution.py:507
  95.8 4.4 %collective-permute-done.34.refs_12_ = bf16[128,1152]{1,0:T(8,128)(2,1)S(1)} collective-permute-done((bf16[128,1152]{1,0:T(8,128)(2,1)S(1)}, bf16[128,1152]{1,0:T(8,128)(2,1)S(1)}, u32[]{:S(2)}, u32[]{:S(2)}) %collective-permute-start.34) | collective-permute-done | bytes 294944 | tf_op jit(solution)/shard_map/ppermute | solution.py:507
  101.6 3.8 %all-to-all-start = ((bf16[8,256,512]{2,1,0:T(8,128)(2,1)}), bf16[8,256,512]{2,1,0:T(8,128)(2,1)S(1)}, u32[]{:S(2)}, u32[]{:S(2)}) async-start(bf16[8,256,512]{2,1,0:T(8,128)(2,1)} %get-tuple-element.92), calls=%async_computation | async-start | bytes 4194304 | tf_op jit(solution)/shard_map/all_to_all | solution.py:744
  107.1 1.7 collective-permute-start.39
  113.6 18.7 %backward.1 = (bf16[256,1024]{1,0:T(8,128)(2,1)}, bf16[256,1024]{1,0:T(8,128)(2,1)}, bf16[256,1024]{1,0:T(8,128)(2,1)}, bf16[256,1024]{1,0:T(8,128)(2,1)}, bf16[...) custom-call(f32[16,8,128]{2,1,0:T(8,128)} %get-tuple-element.61.logi, ...), custom_call_target="tpu_custom_call" | custom-call | tf_op jit(solution)/shard_map/backward/pallas_call | solution.py:748
  132.4 9.8 %collective-permute-done.39.refs_4_ = bf16[256,1024]{1,0:T(8,128)(2,1)S(1)} collective-permute-done((bf16[256,1024]{1,0:T(8,128)(2,1)}, bf16[256,1024]{1,0:T(8,128)(2,1)S(1)}, u32[]{:S(2)}, u32[]{:S(2)}) %collective-permute-start.39) | collective-permute-done | bytes 524320 | tf_op jit(solution)/shard_map/ppermute | solution.py:507
  145.7 1.6 collective-permute-start.47
  148.1 6.3 %collective-permute-done.47 = bf16[128,1024]{1,0:T(8,128)(2,1)S(1)} collective-permute-done((bf16[128,1024]{1,0:T(8,128)(2,1)S(1)}, bf16[128,1024]{1,0:T(8,128)(2,1)S(1)}, u32[]{:S(2)}, u32[]{:S(2)}) %collective-permute-start.47) | collective-permute-done | bytes 262176 | tf_op jit(solution)/shard_map/ppermute | solution.py:507
  160.7 4.3 %collective-permute-done.42.refs_2_ = bf16[128,1024]{1,0:T(8,128)(2,1)S(1)} collective-permute-done((bf16[128,1024]{1,0:T(8,128)(2,1)S(1)}, bf16[128,1024]{1,0:T(8,128)(2,1)S(1)}, u32[]{:S(2)}, u32[]{:S(2)}) %collective-permute-start.42) | collective-permute-done | bytes 262176 | tf_op jit(solution)/shard_map/ppermute | solution.py:507
  165.8 4.8 %collective-permute-done.54.refs_1_ = bf16[128,1024]{1,0:T(8,128)(2,1)S(1)} collective-permute-done((bf16[128,1024]{1,0:T(8,128)(2,1)S(1)}, bf16[128,1024]{1,0:T(8,128)(2,1)S(1)}, u32[]{:S(2)}, u32[]{:S(2)}) %collective-permute-start.54) | collective-permute-done | bytes 262176 | tf_op jit(solution)/shard_map/ppermute | solution.py:507
  170.6 2.9 %weight.2.refs_4_ = f32[512,1024]{1,0:T(8,128)S(1)} custom-call(s32[1]{0:T(128)} %bitcast.me_ref, bf16[8,256,512]{2,1,0:T(8,128)(2,1)S(1)} %all-to-all-done.cols_ref, bf16[256,1024]{1,0:T(8,128)(2,1)} %get-tuple-element.94.refs_0_, bf16[256,1024]{1,0:T(8,128)(2,1)S(1)} %collective-permute-done.43.refs_1_, ...), custom_call_target="tpu_custom_call" | custom-call | tf_op jit(solution)/shard_map/weight/pallas_call | solution.py:780
  177.2 2.1 %weight.3 = f32[512,1024]{1,0:T(8,128)} custom-call(s32[1]{0:T(128)} %bitcast.me_ref, bf16[8,256,512]{2,1,0:T(8,128)(2,1)S(1)} %all-to-all-done.cols_ref, bf16[128,1024]{1,0:T(8,128)(2,1)S(1)} %collective-permute-done.53.refs_0_, bf16[128,1024]{1,0:T(8,128)(2,1)S(1)} %collective-permute-done.54.refs_1_, ...), custom_call_target="tpu_custom_call" | custom-call | tf_op jit(solution)/shard_map/weight/pallas_call | solution.py:780
  (183 shorter events, 54.6 us)
Async XLA Ops:
  2.4 15.6 %collective-permute-start.1 = (bf16[272,1024]{1,0:T(8,128)(2,1)S(1)}, bf16[272,1024]{1,0:T(8,128)(2,1)S(1)}, u32[]{:S(2)}, u32[]{:S(2)}) collective-permute-start(bf16[272,1024]{1,0:T(8,128)(2,1)S(1)} %pack.1.refs_0_), channel_id=1, source_target_pairs={{0,8},{4,12},{8,0},{12,4},{16,24},{20,28},{24,16},{28,20},{1,9},{5... | collective-permute-start | bytes 1671176 | tf_op jit(solution)/shard_map/ppermute | solution.py:507
  5.4 14.5 %collective-permute-start.3 = (bf16[272,1024]{1,0:T(8,128)(2,1)S(1)}, bf16[272,1024]{1,0:T(8,128)(2,1)S(1)}, u32[]{:S(2)}, u32[]{:S(2)}) collective-permute-start(bf16[272,1024]{1,0:T(8,128)(2,1)S(1)} %pack.1.refs_0_), channel_id=1, source_target_pairs={{0,16},{4,20},{8,24},{12,28},{16,0},{20,4},{24,8},{28,12},{1,17},{... | collective-permute-start | bytes 1671176 | tf_op jit(solution)/shard_map/ppermute | solution.py:507
  6.9 14.6 %collective-permute-start.6 = (bf16[256,1024]{1,0:T(8,128)(2,1)}, bf16[256,1024]{1,0:T(8,128)(2,1)}, u32[]{:S(2)}, u32[]{:S(2)}) collective-permute-start(bf16[256,1024]{1,0:T(8,128)(2,1)} %refs_0_.1), channel_id=1, source_target_pairs={{0,1},{1,2},{2,3},{4,5},{5,6},{6,7},{8,9},{9,10},{10,11},{12,13},{... | collective-permute-start | bytes 1572872 | tf_op jit(solution)/shard_map/ppermute | solution.py:636
  11.2 15.0 %collective-permute-start.7 = (bf16[256,1024]{1,0:T(8,128)(2,1)}, bf16[256,1024]{1,0:T(8,128)(2,1)}, u32[]{:S(2)}, u32[]{:S(2)}) collective-permute-start(bf16[256,1024]{1,0:T(8,128)(2,1)} %refs_0_.1), channel_id=1, source_target_pairs={{1,0},{2,1},{3,2},{5,4},{6,5},{7,6},{9,8},{10,9},{11,10},{13,12},{... | collective-permute-start | bytes 1572872 | tf_op jit(solution)/shard_map/ppermute | solution.py:637
  12.5 14.3 %collective-permute-start = (bf16[272,1024]{1,0:T(8,128)(2,1)S(1)}, bf16[272,1024]{1,0:T(8,128)(2,1)S(1)}, u32[]{:S(2)}, u32[]{:S(2)}) collective-permute-start(bf16[272,1024]{1,0:T(8,128)(2,1)S(1)} %pack.1.refs_0_), channel_id=1, source_target_pairs={{0,4},{4,0},{8,12},{12,8},{16,20},{20,16},{24,28},{28,24},{1,5},{5... | collective-permute-start | bytes 1671176 | tf_op jit(solution)/shard_map/ppermute | solution.py:507
  26.8 18.5 %collective-permute-start.11 = (bf16[256,1024]{1,0:T(8,128)(2,1)}, bf16[256,1024]{1,0:T(8,128)(2,1)S(1)}, u32[]{:S(2)}, u32[]{:S(2)}) collective-permute-start(bf16[256,1024]{1,0:T(8,128)(2,1)} %collective-permute-done.6.refs_1_), channel_id=1, source_target_pairs={{1,2},{2,3},{5,6},{6,7},{9,10},{10,11},{13,14},{14,15},{17,18},{18... | collective-permute-start | bytes 1572872 | tf_op jit(solution)/shard_map/ppermute | solution.py:636
  27.8 17.5 %collective-permute-start.12 = (bf16[256,1024]{1,0:T(8,128)(2,1)}, bf16[256,1024]{1,0:T(8,128)(2,1)S(1)}, u32[]{:S(2)}, u32[]{:S(2)}) collective-permute-start(bf16[256,1024]{1,0:T(8,128)(2,1)} %collective-permute-done.7.refs_4_), channel_id=1, source_target_pairs={{1,0},{2,1},{5,4},{6,5},{9,8},{10,9},{13,12},{14,13},{17,16},{18,1... | collective-permute-start | bytes 1572872 | tf_op jit(solution)/shard_map/ppermute | solution.py:637
  46.4 17.8 %collective-permute-start.23 = (bf16[256,1024]{1,0:T(8,128)(2,1)S(1)}, bf16[256,1024]{1,0:T(8,128)(2,1)S(1)}, u32[]{:S(2)}, u32[]{:S(2)}) collective-permute-start(bf16[256,1024]{1,0:T(8,128)(2,1)S(1)} %broadcast_select_fusion), channel_id=1, source_target_pairs={{2,3},{1,0},{6,7},{5,4},{10,11},{9,8},{14,15},{13,12},{18,19},{17,... | collective-permute-start | bytes 1572872 | tf_op jit(solution)/shard_map/ppermute | solution.py:632
  52.4 20.9 %collective-permute-start.13 = (bf16[256,1152]{1,0:T(8,128)(2,1)}, bf16[256,1152]{1,0:T(8,128)(2,1)S(1)}, u32[]{:S(2)}, u32[]{:S(2)}) collective-permute-start(bf16[256,1152]{1,0:T(8,128)(2,1)} %get-tuple-element.67), channel_id=1, source_target_pairs={{0,4},{4,0},{8,12},{12,8},{16,20},{20,16},{24,28},{28,24},{1,5},{5... | collective-permute-start | bytes 1769480 | tf_op jit(solution)/shard_map/ppermute | solution.py:507
  53.1 20.2 %collective-permute-start.16 = (bf16[128,1152]{1,0:T(8,128)(2,1)S(1)}, bf16[128,1152]{1,0:T(8,128)(2,1)S(1)}, u32[]{:S(2)}, u32[]{:S(2)}) collective-permute-start(bf16[128,1152]{1,0:T(8,128)(2,1)S(1)} %get-tuple-element.74), channel_id=1, source_target_pairs={{0,8},{4,12},{8,0},{12,4},{16,24},{20,28},{24,16},{28,20},{1,9},{5... | collective-permute-start | bytes 884744 | tf_op jit(solution)/shard_map/ppermute | solution.py:507
  58.9 14.5 %collective-permute-start.22 = (bf16[128,1152]{1,0:T(8,128)(2,1)S(1)}, bf16[128,1152]{1,0:T(8,128)(2,1)S(1)}, u32[]{:S(2)}, u32[]{:S(2)}) collective-permute-start(bf16[128,1152]{1,0:T(8,128)(2,1)S(1)} %get-tuple-element.82), channel_id=1, source_target_pairs={{0,16},{4,20},{8,24},{12,28},{16,0},{20,4},{24,8},{28,12},{1,17},{... | collective-permute-start | bytes 884744 | tf_op jit(solution)/shard_map/ppermute | solution.py:507
  61.7 11.7 %collective-permute-start.20 = (bf16[128,1152]{1,0:T(8,128)(2,1)S(1)}, bf16[128,1152]{1,0:T(8,128)(2,1)S(1)}, u32[]{:S(2)}, u32[]{:S(2)}) collective-permute-start(bf16[128,1152]{1,0:T(8,128)(2,1)S(1)} %get-tuple-element.80), channel_id=1, source_target_pairs={{0,8},{4,12},{8,0},{12,4},{16,24},{20,28},{24,16},{28,20},{1,9},{5... | collective-permute-start | bytes 884744 | tf_op jit(solution)/shard_map/ppermute | solution.py:507
  80.6 15.2 %collective-permute-start.30 = (bf16[128,1152]{1,0:T(8,128)(2,1)S(1)}, bf16[128,1152]{1,0:T(8,128)(2,1)}, u32[]{:S(2)}, u32[]{:S(2)}) collective-permute-start(bf16[128,1152]{1,0:T(8,128)(2,1)S(1)} %get-tuple-element.85.refs_0_), channel_id=1, source_target_pairs={{0,16},{4,20},{8,24},{12,28},{16,0},{20,4},{24,8},{28,12},{1,17},{... | collective-permute-start | bytes 884744 | tf_op jit(solution)/shard_map/ppermute | solution.py:507
  81.5 14.3 %collective-permute-start.27 = (bf16[128,1152]{1,0:T(8,128)(2,1)S(1)}, bf16[128,1152]{1,0:T(8,128)(2,1)S(1)}, u32[]{:S(2)}, u32[]{:S(2)}) collective-permute-start(bf16[128,1152]{1,0:T(8,128)(2,1)S(1)} %get-tuple-element.86.refs_1_), channel_id=1, source_target_pairs={{0,8},{4,12},{8,0},{12,4},{16,24},{20,28},{24,16},{28,20},{1,9},{5... | collective-permute-start | bytes 884744 | tf_op jit(solution)/shard_map/ppermute | solution.py:507
  87.9 12.2 %collective-permute-start.34 = (bf16[128,1152]{1,0:T(8,128)(2,1)S(1)}, bf16[128,1152]{1,0:T(8,128)(2,1)S(1)}, u32[]{:S(2)}, u32[]{:S(2)}) collective-permute-start(bf16[128,1152]{1,0:T(8,128)(2,1)S(1)} %collective-permute-done.26.refs_4_), channel_id=1, source_target_pairs={{0,16},{4,20},{8,24},{12,28},{16,0},{20,4},{24,8},{28,12},{1,17},{... | collective-permute-start | bytes 884744 | tf_op jit(solution)/shard_map/ppermute | solution.py:507
  101.6 40.5 %all-to-all-start = ((bf16[8,256,512]{2,1,0:T(8,128)(2,1)}), bf16[8,256,512]{2,1,0:T(8,128)(2,1)S(1)}, u32[]{:S(2)}, u32[]{:S(2)}) async-start(bf16[8,256,512]{2,1,0:T(8,128)(2,1)} %get-tuple-element.92), calls=%async_computation | async-start | bytes 4194304 | tf_op jit(solution)/shard_map/all_to_all | solution.py:744
  107.1 35.0 %collective-permute-start.39 = (bf16[256,1024]{1,0:T(8,128)(2,1)}, bf16[256,1024]{1,0:T(8,128)(2,1)S(1)}, u32[]{:S(2)}, u32[]{:S(2)}) collective-permute-start(bf16[256,1024]{1,0:T(8,128)(2,1)} %get-tuple-element.94.refs_0_), channel_id=1, source_target_pairs={{0,16},{4,20},{8,24},{12,28},{16,0},{20,4},{24,8},{28,12},{1,17},{... | collective-permute-start | bytes 1572872 | tf_op jit(solution)/shard_map/ppermute | solution.py:507
  108.8 33.4 %collective-permute-start.38 = (bf16[256,1024]{1,0:T(8,128)(2,1)}, bf16[256,1024]{1,0:T(8,128)(2,1)S(1)}, u32[]{:S(2)}, u32[]{:S(2)}) collective-permute-start(bf16[256,1024]{1,0:T(8,128)(2,1)} %get-tuple-element.94.refs_0_), channel_id=1, source_target_pairs={{0,8},{4,12},{8,0},{12,4},{16,24},{20,28},{24,16},{28,20},{1,9},{5... | collective-permute-start | bytes 1572872 | tf_op jit(solution)/shard_map/ppermute | solution.py:507
  142.8 13.7 %collective-permute-start.43 = (bf16[256,1024]{1,0:T(8,128)(2,1)}, bf16[256,1024]{1,0:T(8,128)(2,1)S(1)}, u32[]{:S(2)}, u32[]{:S(2)}) collective-permute-start(bf16[256,1024]{1,0:T(8,128)(2,1)} %get-tuple-element.94.refs_0_), channel_id=1, source_target_pairs={{0,4},{4,0},{8,12},{12,8},{16,20},{20,16},{24,28},{28,24},{1,5},{5... | collective-permute-start | bytes 1572872 | tf_op jit(solution)/shard_map/ppermute | solution.py:507
  143.3 14.6 %collective-permute-start.45 = (bf16[256,1024]{1,0:T(8,128)(2,1)S(1)}, bf16[256,1024]{1,0:T(8,128)(2,1)S(1)}, u32[]{:S(2)}, u32[]{:S(2)}) collective-permute-start(bf16[256,1024]{1,0:T(8,128)(2,1)S(1)} %collective-permute-done.39.refs_4_), channel_id=1, source_target_pairs={{0,4},{4,0},{8,12},{12,8},{16,20},{20,16},{24,28},{28,24},{1,5},{5... | collective-permute-start | bytes 1572872 | tf_op jit(solution)/shard_map/ppermute | solution.py:507
  144.4 14.3 %collective-permute-start.44 = (bf16[256,1024]{1,0:T(8,128)(2,1)S(1)}, bf16[256,1024]{1,0:T(8,128)(2,1)S(1)}, u32[]{:S(2)}, u32[]{:S(2)}) collective-permute-start(bf16[256,1024]{1,0:T(8,128)(2,1)S(1)} %collective-permute-done.38.refs_2_), channel_id=1, source_target_pairs={{0,4},{4,0},{8,12},{12,8},{16,20},{20,16},{24,28},{28,24},{1,5},{5... | collective-permute-start | bytes 1572872 | tf_op jit(solution)/shard_map/ppermute | solution.py:507
  157.9 12.7 %collective-permute-start.54 = (bf16[128,1024]{1,0:T(8,128)(2,1)S(1)}, bf16[128,1024]{1,0:T(8,128)(2,1)S(1)}, u32[]{:S(2)}, u32[]{:S(2)}) collective-permute-start(bf16[128,1024]{1,0:T(8,128)(2,1)S(1)} %slice.78), channel_id=1, source_target_pairs={{0,8},{4,12},{8,0},{12,4},{16,24},{20,28},{24,16},{28,20},{1,9},{5... | collective-permute-start | bytes 786440 | tf_op jit(solution)/shard_map/ppermute | solution.py:507
  158.7 14.8 %collective-permute-start.52 = (bf16[128,1024]{1,0:T(8,128)(2,1)S(1)}, bf16[128,1024]{1,0:T(8,128)(2,1)S(1)}, u32[]{:S(2)}, u32[]{:S(2)}) collective-permute-start(bf16[128,1024]{1,0:T(8,128)(2,1)S(1)} %add_convert_fusion.1), channel_id=1, source_target_pairs={{0,16},{4,20},{8,24},{12,28},{16,0},{20,4},{24,8},{28,12},{1,17},{... | collective-permute-start | bytes 786440 | tf_op jit(solution)/shard_map/ppermute | solution.py:507
  160.0 14.5 %collective-permute-start.48 = (bf16[128,1024]{1,0:T(8,128)(2,1)S(1)}, bf16[128,1024]{1,0:T(8,128)(2,1)S(1)}, u32[]{:S(2)}, u32[]{:S(2)}) collective-permute-start(bf16[128,1024]{1,0:T(8,128)(2,1)S(1)} %add_convert_fusion.2), channel_id=1, source_target_pairs={{0,8},{4,12},{8,0},{12,4},{16,24},{20,28},{24,16},{28,20},{1,9},{5... | collective-permute-start | bytes 786440 | tf_op jit(solution)/shard_map/ppermute | solution.py:507
  (68 other events, 447.2 us)

commit v19 on v18

--- a/solution.py
+++ b/solution.py
@@ -774,7 +774,8 @@
     key_grad, value_grad = outs[chunks:]
     received = from_core(outs[:chunks], columns, *flat(attns[1:3]))
     terms, last_sums = collect_chips(outs[:chunks], received)
-    attns = with_cores(spread_far(attns, rows // 2, *last_sums))
+    near = [[after(x, *last_sums) for x in pieces] for pieces in attns]
+    attns = with_cores(spread_far(near, rows // 2))
 
     def weight_part(chosen, first, when, *before):
         return pl.pallas_call(

time: 181 us -> 184 us (1.017)
  starting transfers between devices: 50 us -> 53.4 us
    ppermute x52, starting transfers between devices: 37.1 us -> 40.6 us  [swap(): return lax.ppermute(x, 'ctx', [(i, i ^ bits) for i in range(count)])]
  transfers between devices with their start and end apart: 58 -> 58, of which waited for: 26 -> 25; matrix products, arithmetic and copies ran while one was open for 2% -> 2% of each run, Pallas kernels for 26% -> 25%
where the time goes in v19:
time: 184 us; the launch traced here: 182 us
  waiting for transfers between devices  64.8 us (35%)
  starting transfers between devices  53.4 us (29%)
  Pallas kernels  51.8 us (28%)
  local copies, waits for them, and re-layouts  8.53 us (5%)
  other arithmetic  2.61 us (1%)
    ppermute x52, waiting for transfers between devices, swap(): return lax.ppermute(x, 'ctx', [(i, i ^ bits) for i in range(count)])  59.1 us
    ppermute x52, starting transfers between devices, swap(): return lax.ppermute(x, 'ctx', [(i, i ^ bits) for i in range(count)])  40.6 us
    pallas_call x1, Pallas kernels, body(): pl.pallas_call(functools.partial(backward_kernel, [len(pieces) for pieces...  18.7 us
    pallas_call x1, Pallas kernels, body(): pl.pallas_call(functools.partial(forward_kernel, [len(pieces) for pieces...  13.5 us
    pallas_call x1, Pallas kernels, body(): make_grad(after(line, *before), out_weight, out_grad, *ups, *downs)  7.68 us
    unnamed x69, local copies, waits for them, and re-layouts  7.43 us
    ppermute x2, starting transfers between devices, spread_line(): ups.append(lax.ppermute(ups[-1], 'head', up))  4.98 us
    pallas_call x2, Pallas kernels, weight_part(): pl.pallas_call(functools.partial(weight_kernel, [len(pieces) for pieces i...  4.91 us
  transfers between devices with their start and end apart: 58, of which 25 were waited for; matrix products, arithmetic and copies ran while one was open for 2% of the time, Pallas kernels for 25%

profile of v19, /device:TPU:0, one launch (start us, length us, event | category | flops | bytes accessed | tf_op | source)
XLA Modules:
  0.0 182.3 jit_solution(11968205299617011713)
XLA Ops:
  2.4 3.0 %collective-permute-start.1 = (bf16[272,1024]{1,0:T(8,128)(2,1)S(1)}, bf16[272,1024]{1,0:T(8,128)(2,1)S(1)}, u32[]{:S(2)}, u32[]{:S(2)}) collective-permute-start(bf16[272,1024]{1,0:T(8,128)(2,1)S(1)} %pack.1.refs_0_), channel_id=1, source_target_pairs={{0,8},{4,12},{8,0},{12,4},{16,24},{20,28},{24,16},{28,20},{1,9},{5... | collective-permute-start | bytes 1671176 | tf_op jit(solution)/shard_map/ppermute | solution.py:507
  6.9 4.3 %collective-permute-start.6 = (bf16[256,1024]{1,0:T(8,128)(2,1)}, bf16[256,1024]{1,0:T(8,128)(2,1)}, u32[]{:S(2)}, u32[]{:S(2)}) collective-permute-start(bf16[256,1024]{1,0:T(8,128)(2,1)} %refs_0_.1), channel_id=1, source_target_pairs={{0,1},{1,2},{2,3},{4,5},{5,6},{6,7},{8,9},{9,10},{10,11},{12,13},{... | collective-permute-start | bytes 1572872 | tf_op jit(solution)/shard_map/ppermute | solution.py:636
  12.6 5.4 %collective-permute-done.1.refs_2_ = bf16[272,1024]{1,0:T(8,128)(2,1)S(1)} collective-permute-done((bf16[272,1024]{1,0:T(8,128)(2,1)S(1)}, bf16[272,1024]{1,0:T(8,128)(2,1)S(1)}, u32[]{:S(2)}, u32[]{:S(2)}) %collective-permute-start.1) | collective-permute-done | bytes 557088 | tf_op jit(solution)/shard_map/ppermute | solution.py:507
  18.1 1.8 %collective-permute-start.5 = (bf16[128,1024]{1,0:T(8,128)(2,1)S(1)}, bf16[128,1024]{1,0:T(8,128)(2,1)S(1)}, u32[]{:S(2)}, u32[]{:S(2)}) collective-permute-start(bf16[128,1024]{1,0:T(8,128)(2,1)S(1)} %slice.69), channel_id=1, source_target_pairs={{0,16},{4,20},{8,24},{12,28},{16,0},{20,4},{24,8},{28,12},{1,17},{... | collective-permute-start | bytes 786440 | tf_op jit(solution)/shard_map/ppermute | solution.py:507
  21.5 4.8 %collective-permute-done.7.refs_4_ = bf16[256,1024]{1,0:T(8,128)(2,1)} collective-permute-done((bf16[256,1024]{1,0:T(8,128)(2,1)}, bf16[256,1024]{1,0:T(8,128)(2,1)}, u32[]{:S(2)}, u32[]{:S(2)}) %collective-permute-start.7) | collective-permute-done | bytes 524320 | tf_op jit(solution)/shard_map/ppermute | solution.py:637
  31.8 13.5 %forward.1 = (bf16[256,1152]{1,0:T(8,128)(2,1)}, bf16[256,1152]{1,0:T(8,128)(2,1)}, bf16[256,1152]{1,0:T(8,128)(2,1)}, bf16[256,1152]{1,0:T(8,128)(2,1)}, bf16[2...) custom-call(s32[1]{0:T(128)} %bitcast.me_ref, ...), custom_call_target="tpu_custom_call" | custom-call | tf_op jit(solution)/shard_map/forward/pallas_call | solution.py:680
  53.7 5.1 %collective-permute-done.18.refs_4_ = bf16[128,1152]{1,0:T(8,128)(2,1)S(1)} collective-permute-done((bf16[128,1152]{1,0:T(8,128)(2,1)S(1)}, bf16[128,1152]{1,0:T(8,128)(2,1)S(1)}, u32[]{:S(2)}, u32[]{:S(2)}) %collective-permute-start.18) | collective-permute-done | bytes 294944 | tf_op jit(solution)/shard_map/ppermute | solution.py:507
  65.6 7.7 %grad.1 = (bf16[256,1024]{1,0:T(8,128)(2,1)}, bf16[8,256,512]{2,1,0:T(8,128)(2,1)}) custom-call(s32[1]{0:T(128)} %bitcast.4.line_ref, bf16[4096,1024]{1,0:T(8,128)(2,1)} %w_ref.1, bf16[256,1024]{1,0:T(8,128)(2,1)} %refs_0_.1, bf16[256,1024]{1,0:T(8,128)(2,1)} %collective-permute-done.6.refs_1_, bf16[256,1024]{1,0:T(8,128)(2,1)} %copy-done.12, ...), custom_call_target="tpu_custom_call" | custom-call | tf_op jit(solution)/shard_map/grad/pallas_call | solution.py:730
  74.6 3.4 %finish.1 = (bf16[256,1024]{1,0:T(8,128)(2,1)}, bf16[128,1152]{1,0:T(8,128)(2,1)S(1)}, bf16[128,1152]{1,0:T(8,128)(2,1)S(1)}) custom-call(bf16[256,1152]{1,0:T(8,128)(2,1)S(1)} %copy-done.4, bf16[256,1152]{1,0:T(8,128)(2,1)S(1)} %collective-permute-done.13.refs_1_, bf16[128,1152]{1,0:T(8,128)(2,1)S(1)} %collective-permute-done.16.refs_2_, ...), custom_call_target="tpu_custom_call" | custom-call | tf_op jit(solution)/shard_map/finish/pallas_call | solution.py:732
  82.0 5.9 %collective-permute-done.26.refs_4_ = bf16[128,1152]{1,0:T(8,128)(2,1)S(1)} collective-permute-done((bf16[128,1152]{1,0:T(8,128)(2,1)S(1)}, bf16[128,1152]{1,0:T(8,128)(2,1)S(1)}, u32[]{:S(2)}, u32[]{:S(2)}) %collective-permute-start.26) | collective-permute-done | bytes 294944 | tf_op jit(solution)/shard_map/ppermute | solution.py:507
  90.6 5.1 %collective-permute-done.30.refs_8_ = bf16[128,1152]{1,0:T(8,128)(2,1)S(1)} collective-permute-done((bf16[128,1152]{1,0:T(8,128)(2,1)S(1)}, bf16[128,1152]{1,0:T(8,128)(2,1)S(1)}, u32[]{:S(2)}, u32[]{:S(2)}) %collective-permute-start.30) | collective-permute-done | bytes 294944 | tf_op jit(solution)/shard_map/ppermute | solution.py:507
  95.7 4.5 %collective-permute-done.34.refs_12_ = bf16[128,1152]{1,0:T(8,128)(2,1)S(1)} collective-permute-done((bf16[128,1152]{1,0:T(8,128)(2,1)S(1)}, bf16[128,1152]{1,0:T(8,128)(2,1)S(1)}, u32[]{:S(2)}, u32[]{:S(2)}) %collective-permute-start.34) | collective-permute-done | bytes 294944 | tf_op jit(solution)/shard_map/ppermute | solution.py:507
  101.6 3.8 %all-to-all-start = ((bf16[8,256,512]{2,1,0:T(8,128)(2,1)}), bf16[8,256,512]{2,1,0:T(8,128)(2,1)S(1)}, u32[]{:S(2)}, u32[]{:S(2)}) async-start(bf16[8,256,512]{2,1,0:T(8,128)(2,1)} %get-tuple-element.93), calls=%async_computation | async-start | bytes 4194304 | tf_op jit(solution)/shard_map/all_to_all | solution.py:744
  107.1 1.7 collective-permute-start.39
  113.6 18.7 %backward.1 = (bf16[256,1024]{1,0:T(8,128)(2,1)}, bf16[256,1024]{1,0:T(8,128)(2,1)}, bf16[256,1024]{1,0:T(8,128)(2,1)}, bf16[256,1024]{1,0:T(8,128)(2,1)}, bf16[...) custom-call(f32[16,8,128]{2,1,0:T(8,128)} %get-tuple-element.62.logi, ...), custom_call_target="tpu_custom_call" | custom-call | tf_op jit(solution)/shard_map/backward/pallas_call | solution.py:748
  132.4 9.8 %collective-permute-done.39.refs_4_ = bf16[256,1024]{1,0:T(8,128)(2,1)S(1)} collective-permute-done((bf16[256,1024]{1,0:T(8,128)(2,1)}, bf16[256,1024]{1,0:T(8,128)(2,1)S(1)}, u32[]{:S(2)}, u32[]{:S(2)}) %collective-permute-start.39) | collective-permute-done | bytes 524320 | tf_op jit(solution)/shard_map/ppermute | solution.py:507
  150.3 4.8 %collective-permute-done.43 = bf16[128,1024]{1,0:T(8,128)(2,1)S(1)} collective-permute-done((bf16[128,1024]{1,0:T(8,128)(2,1)S(1)}, bf16[128,1024]{1,0:T(8,128)(2,1)S(1)}, u32[]{:S(2)}, u32[]{:S(2)}) %collective-permute-start.43) | collective-permute-done | bytes 262176 | tf_op jit(solution)/shard_map/ppermute | solution.py:507
  157.1 2.8 %collective-permute-done.42.refs_2_ = bf16[128,1024]{1,0:T(8,128)(2,1)S(1)} collective-permute-done((bf16[128,1024]{1,0:T(8,128)(2,1)S(1)}, bf16[128,1024]{1,0:T(8,128)(2,1)S(1)}, u32[]{:S(2)}, u32[]{:S(2)}) %collective-permute-start.42) | collective-permute-done | bytes 262176 | tf_op jit(solution)/shard_map/ppermute | solution.py:507
  160.0 2.0 %collective-permute-start.53 = (bf16[128,1024]{1,0:T(8,128)(2,1)S(1)}, bf16[128,1024]{1,0:T(8,128)(2,1)S(1)}, u32[]{:S(2)}, u32[]{:S(2)}) collective-permute-start(bf16[128,1024]{1,0:T(8,128)(2,1)S(1)} %slice.66), channel_id=1, source_target_pairs={{0,16},{4,20},{8,24},{12,28},{16,0},{20,4},{24,8},{28,12},{1,17},{... | collective-permute-start | bytes 786440 | tf_op jit(solution)/shard_map/ppermute | solution.py:507
  161.9 3.3 %collective-permute-done.54.refs_1_ = bf16[128,1024]{1,0:T(8,128)(2,1)S(1)} collective-permute-done((bf16[128,1024]{1,0:T(8,128)(2,1)S(1)}, bf16[128,1024]{1,0:T(8,128)(2,1)S(1)}, u32[]{:S(2)}, u32[]{:S(2)}) %collective-permute-start.54) | collective-permute-done | bytes 262176 | tf_op jit(solution)/shard_map/ppermute | solution.py:507
  169.7 2.9 %weight.2.refs_4_ = f32[512,1024]{1,0:T(8,128)S(1)} custom-call(s32[1]{0:T(128)} %bitcast.me_ref, bf16[8,256,512]{2,1,0:T(8,128)(2,1)S(1)} %all-to-all-done.cols_ref, bf16[256,1024]{1,0:T(8,128)(2,1)} %get-tuple-element.107.refs_0_, bf16[256,1024]{1,0:T(8,128)(2,1)S(1)} %collective-permute-done.46.refs_1_, ...), custom_call_target="tpu_custom_call" | custom-call | tf_op jit(solution)/shard_map/weight/pallas_call | solution.py:781
  172.6 1.9 %collective-permute-done.52.refs_5_ = bf16[128,1024]{1,0:T(8,128)(2,1)S(1)} collective-permute-done((bf16[128,1024]{1,0:T(8,128)(2,1)S(1)}, bf16[128,1024]{1,0:T(8,128)(2,1)S(1)}, u32[]{:S(2)}, u32[]{:S(2)}) %collective-permute-start.52) | collective-permute-done | bytes 262176 | tf_op jit(solution)/shard_map/ppermute | solution.py:507
  174.5 4.4 %collective-permute-done.51.refs_4_ = bf16[128,1024]{1,0:T(8,128)(2,1)S(1)} collective-permute-done((bf16[128,1024]{1,0:T(8,128)(2,1)S(1)}, bf16[128,1024]{1,0:T(8,128)(2,1)S(1)}, u32[]{:S(2)}, u32[]{:S(2)}) %collective-permute-start.51) | collective-permute-done | bytes 262176 | tf_op jit(solution)/shard_map/ppermute | solution.py:507
  180.2 2.1 %weight.3 = f32[512,1024]{1,0:T(8,128)} custom-call(s32[1]{0:T(128)} %bitcast.me_ref, bf16[8,256,512]{2,1,0:T(8,128)(2,1)S(1)} %all-to-all-done.cols_ref, bf16[128,1024]{1,0:T(8,128)(2,1)S(1)} %collective-permute-done.53.refs_0_, bf16[128,1024]{1,0:T(8,128)(2,1)S(1)} %collective-permute-done.54.refs_1_, ...), custom_call_target="tpu_custom_call" | custom-call | tf_op jit(solution)/shard_map/weight/pallas_call | solution.py:781
  (183 shorter events, 58.5 us)
Async XLA Ops:
  2.4 15.6 %collective-permute-start.1 = (bf16[272,1024]{1,0:T(8,128)(2,1)S(1)}, bf16[272,1024]{1,0:T(8,128)(2,1)S(1)}, u32[]{:S(2)}, u32[]{:S(2)}) collective-permute-start(bf16[272,1024]{1,0:T(8,128)(2,1)S(1)} %pack.1.refs_0_), channel_id=1, source_target_pairs={{0,8},{4,12},{8,0},{12,4},{16,24},{20,28},{24,16},{28,20},{1,9},{5... | collective-permute-start | bytes 1671176 | tf_op jit(solution)/shard_map/ppermute | solution.py:507
  5.4 14.5 %collective-permute-start.3 = (bf16[272,1024]{1,0:T(8,128)(2,1)S(1)}, bf16[272,1024]{1,0:T(8,128)(2,1)S(1)}, u32[]{:S(2)}, u32[]{:S(2)}) collective-permute-start(bf16[272,1024]{1,0:T(8,128)(2,1)S(1)} %pack.1.refs_0_), channel_id=1, source_target_pairs={{0,16},{4,20},{8,24},{12,28},{16,0},{20,4},{24,8},{28,12},{1,17},{... | collective-permute-start | bytes 1671176 | tf_op jit(solution)/shard_map/ppermute | solution.py:507
  6.9 14.6 %collective-permute-start.6 = (bf16[256,1024]{1,0:T(8,128)(2,1)}, bf16[256,1024]{1,0:T(8,128)(2,1)}, u32[]{:S(2)}, u32[]{:S(2)}) collective-permute-start(bf16[256,1024]{1,0:T(8,128)(2,1)} %refs_0_.1), channel_id=1, source_target_pairs={{0,1},{1,2},{2,3},{4,5},{5,6},{6,7},{8,9},{9,10},{10,11},{12,13},{... | collective-permute-start | bytes 1572872 | tf_op jit(solution)/shard_map/ppermute | solution.py:636
  11.2 15.0 %collective-permute-start.7 = (bf16[256,1024]{1,0:T(8,128)(2,1)}, bf16[256,1024]{1,0:T(8,128)(2,1)}, u32[]{:S(2)}, u32[]{:S(2)}) collective-permute-start(bf16[256,1024]{1,0:T(8,128)(2,1)} %refs_0_.1), channel_id=1, source_target_pairs={{1,0},{2,1},{3,2},{5,4},{6,5},{7,6},{9,8},{10,9},{11,10},{13,12},{... | collective-permute-start | bytes 1572872 | tf_op jit(solution)/shard_map/ppermute | solution.py:637
  12.5 14.3 %collective-permute-start = (bf16[272,1024]{1,0:T(8,128)(2,1)S(1)}, bf16[272,1024]{1,0:T(8,128)(2,1)S(1)}, u32[]{:S(2)}, u32[]{:S(2)}) collective-permute-start(bf16[272,1024]{1,0:T(8,128)(2,1)S(1)} %pack.1.refs_0_), channel_id=1, source_target_pairs={{0,4},{4,0},{8,12},{12,8},{16,20},{20,16},{24,28},{28,24},{1,5},{5... | collective-permute-start | bytes 1671176 | tf_op jit(solution)/shard_map/ppermute | solution.py:507
  26.8 18.5 %collective-permute-start.11 = (bf16[256,1024]{1,0:T(8,128)(2,1)}, bf16[256,1024]{1,0:T(8,128)(2,1)S(1)}, u32[]{:S(2)}, u32[]{:S(2)}) collective-permute-start(bf16[256,1024]{1,0:T(8,128)(2,1)} %collective-permute-done.6.refs_1_), channel_id=1, source_target_pairs={{1,2},{2,3},{5,6},{6,7},{9,10},{10,11},{13,14},{14,15},{17,18},{18... | collective-permute-start | bytes 1572872 | tf_op jit(solution)/shard_map/ppermute | solution.py:636
  27.8 17.5 %collective-permute-start.12 = (bf16[256,1024]{1,0:T(8,128)(2,1)}, bf16[256,1024]{1,0:T(8,128)(2,1)S(1)}, u32[]{:S(2)}, u32[]{:S(2)}) collective-permute-start(bf16[256,1024]{1,0:T(8,128)(2,1)} %collective-permute-done.7.refs_4_), channel_id=1, source_target_pairs={{1,0},{2,1},{5,4},{6,5},{9,8},{10,9},{13,12},{14,13},{17,16},{18,1... | collective-permute-start | bytes 1572872 | tf_op jit(solution)/shard_map/ppermute | solution.py:637
  46.4 17.8 %collective-permute-start.23 = (bf16[256,1024]{1,0:T(8,128)(2,1)S(1)}, bf16[256,1024]{1,0:T(8,128)(2,1)S(1)}, u32[]{:S(2)}, u32[]{:S(2)}) collective-permute-start(bf16[256,1024]{1,0:T(8,128)(2,1)S(1)} %broadcast_select_fusion), channel_id=1, source_target_pairs={{2,3},{1,0},{6,7},{5,4},{10,11},{9,8},{14,15},{13,12},{18,19},{17,... | collective-permute-start | bytes 1572872 | tf_op jit(solution)/shard_map/ppermute | solution.py:632
  52.4 20.9 %collective-permute-start.13 = (bf16[256,1152]{1,0:T(8,128)(2,1)}, bf16[256,1152]{1,0:T(8,128)(2,1)S(1)}, u32[]{:S(2)}, u32[]{:S(2)}) collective-permute-start(bf16[256,1152]{1,0:T(8,128)(2,1)} %get-tuple-element.68), channel_id=1, source_target_pairs={{0,4},{4,0},{8,12},{12,8},{16,20},{20,16},{24,28},{28,24},{1,5},{5... | collective-permute-start | bytes 1769480 | tf_op jit(solution)/shard_map/ppermute | solution.py:507
  53.1 20.2 %collective-permute-start.16 = (bf16[128,1152]{1,0:T(8,128)(2,1)S(1)}, bf16[128,1152]{1,0:T(8,128)(2,1)S(1)}, u32[]{:S(2)}, u32[]{:S(2)}) collective-permute-start(bf16[128,1152]{1,0:T(8,128)(2,1)S(1)} %get-tuple-element.75), channel_id=1, source_target_pairs={{0,8},{4,12},{8,0},{12,4},{16,24},{20,28},{24,16},{28,20},{1,9},{5... | collective-permute-start | bytes 884744 | tf_op jit(solution)/shard_map/ppermute | solution.py:507
  58.9 14.5 %collective-permute-start.22 = (bf16[128,1152]{1,0:T(8,128)(2,1)S(1)}, bf16[128,1152]{1,0:T(8,128)(2,1)S(1)}, u32[]{:S(2)}, u32[]{:S(2)}) collective-permute-start(bf16[128,1152]{1,0:T(8,128)(2,1)S(1)} %get-tuple-element.83), channel_id=1, source_target_pairs={{0,16},{4,20},{8,24},{12,28},{16,0},{20,4},{24,8},{28,12},{1,17},{... | collective-permute-start | bytes 884744 | tf_op jit(solution)/shard_map/ppermute | solution.py:507
  61.7 11.7 %collective-permute-start.20 = (bf16[128,1152]{1,0:T(8,128)(2,1)S(1)}, bf16[128,1152]{1,0:T(8,128)(2,1)S(1)}, u32[]{:S(2)}, u32[]{:S(2)}) collective-permute-start(bf16[128,1152]{1,0:T(8,128)(2,1)S(1)} %get-tuple-element.81), channel_id=1, source_target_pairs={{0,8},{4,12},{8,0},{12,4},{16,24},{20,28},{24,16},{28,20},{1,9},{5... | collective-permute-start | bytes 884744 | tf_op jit(solution)/shard_map/ppermute | solution.py:507
  80.6 15.1 %collective-permute-start.30 = (bf16[128,1152]{1,0:T(8,128)(2,1)S(1)}, bf16[128,1152]{1,0:T(8,128)(2,1)S(1)}, u32[]{:S(2)}, u32[]{:S(2)}) collective-permute-start(bf16[128,1152]{1,0:T(8,128)(2,1)S(1)} %get-tuple-element.86.refs_0_), channel_id=1, source_target_pairs={{0,16},{4,20},{8,24},{12,28},{16,0},{20,4},{24,8},{28,12},{1,17},{... | collective-permute-start | bytes 884744 | tf_op jit(solution)/shard_map/ppermute | solution.py:507
  81.5 14.2 %collective-permute-start.27 = (bf16[128,1152]{1,0:T(8,128)(2,1)S(1)}, bf16[128,1152]{1,0:T(8,128)(2,1)S(1)}, u32[]{:S(2)}, u32[]{:S(2)}) collective-permute-start(bf16[128,1152]{1,0:T(8,128)(2,1)S(1)} %get-tuple-element.87.refs_1_), channel_id=1, source_target_pairs={{0,8},{4,12},{8,0},{12,4},{16,24},{20,28},{24,16},{28,20},{1,9},{5... | collective-permute-start | bytes 884744 | tf_op jit(solution)/shard_map/ppermute | solution.py:507
  87.9 12.2 %collective-permute-start.34 = (bf16[128,1152]{1,0:T(8,128)(2,1)S(1)}, bf16[128,1152]{1,0:T(8,128)(2,1)S(1)}, u32[]{:S(2)}, u32[]{:S(2)}) collective-permute-start(bf16[128,1152]{1,0:T(8,128)(2,1)S(1)} %collective-permute-done.26.refs_4_), channel_id=1, source_target_pairs={{0,16},{4,20},{8,24},{12,28},{16,0},{20,4},{24,8},{28,12},{1,17},{... | collective-permute-start | bytes 884744 | tf_op jit(solution)/shard_map/ppermute | solution.py:507
  101.6 40.5 %all-to-all-start = ((bf16[8,256,512]{2,1,0:T(8,128)(2,1)}), bf16[8,256,512]{2,1,0:T(8,128)(2,1)S(1)}, u32[]{:S(2)}, u32[]{:S(2)}) async-start(bf16[8,256,512]{2,1,0:T(8,128)(2,1)} %get-tuple-element.93), calls=%async_computation | async-start | bytes 4194304 | tf_op jit(solution)/shard_map/all_to_all | solution.py:744
  107.1 35.0 %collective-permute-start.39 = (bf16[256,1024]{1,0:T(8,128)(2,1)}, bf16[256,1024]{1,0:T(8,128)(2,1)S(1)}, u32[]{:S(2)}, u32[]{:S(2)}) collective-permute-start(bf16[256,1024]{1,0:T(8,128)(2,1)} %get-tuple-element.107.refs_0_), channel_id=1, source_target_pairs={{0,16},{4,20},{8,24},{12,28},{16,0},{20,4},{24,8},{28,12},{1,17},{... | collective-permute-start | bytes 1572872 | tf_op jit(solution)/shard_map/ppermute | solution.py:507
  108.8 33.4 %collective-permute-start.38 = (bf16[256,1024]{1,0:T(8,128)(2,1)}, bf16[256,1024]{1,0:T(8,128)(2,1)S(1)}, u32[]{:S(2)}, u32[]{:S(2)}) collective-permute-start(bf16[256,1024]{1,0:T(8,128)(2,1)} %get-tuple-element.107.refs_0_), channel_id=1, source_target_pairs={{0,8},{4,12},{8,0},{12,4},{16,24},{20,28},{24,16},{28,20},{1,9},{5... | collective-permute-start | bytes 1572872 | tf_op jit(solution)/shard_map/ppermute | solution.py:507
  142.8 13.3 %collective-permute-start.49 = (bf16[256,1024]{1,0:T(8,128)(2,1)}, bf16[256,1024]{1,0:T(8,128)(2,1)S(1)}, u32[]{:S(2)}, u32[]{:S(2)}) collective-permute-start(bf16[256,1024]{1,0:T(8,128)(2,1)} %get-tuple-element.112), channel_id=1, source_target_pairs={{0,4},{4,0},{8,12},{12,8},{16,20},{20,16},{24,28},{28,24},{1,5},{5... | collective-permute-start | bytes 1572872 | tf_op jit(solution)/shard_map/ppermute | solution.py:507
  148.7 11.2 %collective-permute-start.42 = (bf16[128,1024]{1,0:T(8,128)(2,1)S(1)}, bf16[128,1024]{1,0:T(8,128)(2,1)S(1)}, u32[]{:S(2)}, u32[]{:S(2)}) collective-permute-start(bf16[128,1024]{1,0:T(8,128)(2,1)S(1)} %add_convert_fusion.4), channel_id=1, source_target_pairs={{0,8},{4,12},{8,0},{12,4},{16,24},{20,28},{24,16},{28,20},{1,9},{5... | collective-permute-start | bytes 786440 | tf_op jit(solution)/shard_map/ppermute | solution.py:507
  155.4 13.1 %collective-permute-start.46 = (bf16[256,1024]{1,0:T(8,128)(2,1)}, bf16[256,1024]{1,0:T(8,128)(2,1)S(1)}, u32[]{:S(2)}, u32[]{:S(2)}) collective-permute-start(bf16[256,1024]{1,0:T(8,128)(2,1)} %get-tuple-element.107.refs_0_), channel_id=1, source_target_pairs={{0,4},{4,0},{8,12},{12,8},{16,20},{20,16},{24,28},{28,24},{1,5},{5... | collective-permute-start | bytes 1572872 | tf_op jit(solution)/shard_map/ppermute | solution.py:507
  155.5 13.7 %collective-permute-start.47 = (bf16[256,1024]{1,0:T(8,128)(2,1)S(1)}, bf16[256,1024]{1,0:T(8,128)(2,1)S(1)}, u32[]{:S(2)}, u32[]{:S(2)}) collective-permute-start(bf16[256,1024]{1,0:T(8,128)(2,1)S(1)} %collective-permute-done.38.refs_2_), channel_id=1, source_target_pairs={{0,4},{4,0},{8,12},{12,8},{16,20},{20,16},{24,28},{28,24},{1,5},{5... | collective-permute-start | bytes 1572872 | tf_op jit(solution)/shard_map/ppermute | solution.py:507
  156.0 13.2 %collective-permute-start.48 = (bf16[256,1024]{1,0:T(8,128)(2,1)S(1)}, bf16[256,1024]{1,0:T(8,128)(2,1)S(1)}, u32[]{:S(2)}, u32[]{:S(2)}) collective-permute-start(bf16[256,1024]{1,0:T(8,128)(2,1)S(1)} %collective-permute-done.39.refs_4_), channel_id=1, source_target_pairs={{0,4},{4,0},{8,12},{12,8},{16,20},{20,16},{24,28},{28,24},{1,5},{5... | collective-permute-start | bytes 1572872 | tf_op jit(solution)/shard_map/ppermute | solution.py:507
  169.2 11.0 %collective-permute-start.56 = (bf16[128,1024]{1,0:T(8,128)(2,1)S(1)}, bf16[128,1024]{1,0:T(8,128)(2,1)S(1)}, u32[]{:S(2)}, u32[]{:S(2)}) collective-permute-start(bf16[128,1024]{1,0:T(8,128)(2,1)S(1)} %collective-permute-done.54.refs_1_), channel_id=1, source_target_pairs={{0,4},{4,0},{8,12},{12,8},{16,20},{20,16},{24,28},{28,24},{1,5},{5... | collective-permute-start | bytes 786440 | tf_op jit(solution)/shard_map/ppermute | solution.py:507
  (68 other events, 460.2 us)
